TPU v7x, 32 devices: a whole 2x2x4 slice. The times are simulated.
32 devices in a mesh: section: 4 (over x, core), dp: 4 (over z), tensor: 2 (over y).
Axes of the slice: x: 2, y: 2, z: 4, core: 2. Of those that a mesh axis runs over, the one named last changes fastest.
Arguments:
- inputs: bfloat16 [8, 1024, 768], P('dp', ('section', 'tensor')), may hold values from -6 to 6
- cotangent: bfloat16 [8, 1024, 768], P('dp', ('section', 'tensor')), may hold values from -6 to 6
- subset_ids: int32 [8], P('dp'), may hold values from 0 to 21
- subset_weight: float32 [22], replicated, may hold values from 0.25 to 4
- ln_gain: float32 [4, 2, 2, 768], P('section'), may hold values from 0.5 to 1.5
- ln_bias: float32 [4, 2, 2, 768], P('section'), may hold values from -2 to 2
- w_query: bfloat16 [4, 2, 768, 768], P('section', None, None, 'tensor'), may hold values from -0.21875 to 0.21875
- b_query: float32 [4, 2, 768], P('section', None, 'tensor'), may hold values from -2 to 2
- w_kv: bfloat16 [4, 768, 128], P('section'), may hold values from -0.21875 to 0.21875
- b_kv: float32 [4, 128], P('section'), may hold values from -2 to 2
- w_out: bfloat16 [4, 2, 768, 768], P('section', None, 'tensor'), may hold values from -0.75 to 0.75
- out_bias: float32 [4, 2, 2, 768], P('section'), may hold values from -2 to 2
- w_in: bfloat16 [4, 2, 768, 3072], P('section', None, None, 'tensor'), may hold values from -0.21875 to 0.21875
- b_in: float32 [4, 2, 3072], P('section', None, 'tensor'), may hold values from -2 to 2
- w_hid_out: bfloat16 [4, 2, 3072, 768], P('section', None, 'tensor'), may hold values from -0.109375 to 0.109375
Outputs:
- final: bfloat16 [8, 1024, 768], P('dp', ('section', 'tensor'))
- input_grad: float32 [8, 1024, 768], P('dp', ('section', 'tensor'))
- grad_ln_gain: float32 [4, 2, 2, 768], P('section')
- grad_ln_bias: float32 [4, 2, 2, 768], P('section')
- grad_w_query: float32 [4, 2, 768, 768], P('section', None, None, 'tensor')
- grad_b_query: float32 [4, 2, 768], P('section', None, 'tensor')
- grad_w_kv: float32 [4, 768, 128], P('section')
- grad_b_kv: float32 [4, 128], P('section')
- grad_w_out: float32 [4, 2, 768, 768], P('section', None, 'tensor')
- grad_out_bias: float32 [4, 2, 2, 768], P('section')
- grad_w_in: float32 [4, 2, 768, 3072], P('section', None, None, 'tensor')
- grad_b_in: float32 [4, 2, 3072], P('section', None, 'tensor')
- grad_w_hid_out: float32 [4, 2, 3072, 768], P('section', None, 'tensor')
All inputs are finite; a program needn't handle non-finite values.
Results may differ from a plain program's by a relative error of at most 0.025.
Values may be sent and summed in bfloat16 or wider, within the bound.
No kernel may reach another device: no remote copies, remote signals or barrier semaphores. Data moves between devices by JAX's collectives and lax.ppermute only.
A program may use at most 320 MiB of HBM per device.

v0:
```python
import jax
import jax.numpy as jnp
from jax import lax
from jax.sharding import PartitionSpec as P

HD = 64
ROT = 16


EPS = 1e-05


def for_sending(shard):

    def short(part):
        return part.astype(jnp.bfloat16) if part.dtype == jnp.float32 else part

    return jax.tree.map(short, shard)


def shifted(shard, axis, by):
    size = lax.axis_size(axis)
    pairs = [(i, i + by) for i in range(size) if 0 <= i + by < size]
    return lax.ppermute(shard, axis, pairs)


def layer_norm(hidden, gain, bias):
    centre = jnp.mean(hidden, axis=-1, keepdims=True)
    centred = hidden - centre
    spread = jnp.mean(centred * centred, axis=-1, keepdims=True)
    return centred * lax.rsqrt(spread + EPS) * gain + bias


def normalize(hidden, gains, biases):
    return (layer_norm(hidden, gains[0], biases[0]), layer_norm(hidden, gains[1], biases[1]))


def rope_tables(length, width):
    column = jnp.arange(width) % HD
    half = ROT // 2
    freq = jnp.power(10000.0, -2.0 * (column % half).astype(jnp.float32) / ROT)
    angle = jnp.arange(length).astype(jnp.float32)[:, None] * freq[None, :]
    turning = (column < ROT)[None, :]
    return (jnp.where(turning, jnp.cos(angle), 1.0), jnp.where(turning, jnp.sin(angle), 0.0))


def rotate(values, cosines, sines):
    column = jnp.arange(values.shape[-1]) % HD
    half = ROT // 2
    ahead = jnp.roll(values, -half, axis=-1)
    behind = jnp.roll(values, half, axis=-1)
    turned = jnp.where(column < half, -ahead, jnp.where(column < ROT, behind, 0.0))
    return values * cosines + turned * sines


def matmul(left, right):
    return jnp.dot(left, right, preferred_element_type=jnp.float32)


def matmul_left(left, right):
    return lax.dot_general(
        left, right, (((0,), (0,)), ((), ())), preferred_element_type=jnp.float32
    )


def matmul_right(left, right):
    return lax.dot_general(
        left, right, (((1,), (1,)), ((), ())), preferred_element_type=jnp.float32
    )


def guarded(valid, action, *operands):

    def skipped(*inner):
        return jax.tree.map(jnp.zeros_like, action(*inner))

    return lax.cond(valid, action, skipped, *operands)


def visible_mask(number, block, heads, reach):
    query_pos = number * block + jnp.arange(block * heads) // heads
    return jnp.arange(reach)[None, :] <= query_pos[:, None]


def block_scores(query, keys, number, block, heads):
    reach = (number + 1) * block
    rows = query[number * block : reach].reshape(block * heads, HD)
    scores = matmul_right(rows, keys[:reach]) * HD ** (-0.5)
    return (rows, jnp.where(visible_mask(number, block, heads, reach), scores, -1e30))


def attend(query, keys, values, heads):
    length = query.shape[0]
    block = min(length, 512)
    outputs, totals = ([], [])
    for number in range(length // block):
        reach = (number + 1) * block
        rows, scores = block_scores(query, keys, number, block, heads)
        top = jnp.max(scores, axis=1, keepdims=True)
        expo = jnp.exp(scores - top)
        summed = jnp.sum(expo, axis=1, keepdims=True)
        probs = (expo / summed).astype(jnp.bfloat16)
        outputs.append(
            matmul(probs, values[:reach]).astype(jnp.bfloat16).reshape(block, heads * HD)
        )
        totals.append(top + jnp.log(summed))
    return (jnp.concatenate(outputs, axis=0), jnp.concatenate(totals, axis=0))


def attend_back(query, keys, values, grad_out, totals, heads):
    length = query.shape[0]
    block = min(length, 512)
    grad_query = []
    grad_keys = jnp.zeros((length, HD), jnp.float32)
    grad_values = jnp.zeros((length, HD), jnp.float32)
    for number in range(length // block):
        reach = (number + 1) * block
        rows, scores = block_scores(query, keys, number, block, heads)
        probs = jnp.exp(scores - totals[number * block * heads : reach * heads])
        grad_block = grad_out[number * block : reach].reshape(block * heads, HD)
        grad_probs = matmul_right(grad_block, values[:reach])
        inner_sum = jnp.sum(probs * grad_probs, axis=1, keepdims=True)
        grad_scores = (probs * (grad_probs - inner_sum)).astype(jnp.bfloat16)
        grad_query.append(
            (matmul(grad_scores, keys[:reach]) * HD ** (-0.5)).reshape(block, heads * HD)
        )
        grad_keys = grad_keys.at[:reach].add(matmul_left(grad_scores, rows) * HD ** (-0.5))
        grad_values = grad_values.at[:reach].add(
            matmul_left(probs.astype(jnp.bfloat16), grad_block)
        )
    return (jnp.concatenate(grad_query, axis=0), grad_keys, grad_values)


def layer_forward(hidden, slot, shared, kv_weights, tables, valid, need_branch):
    gains, biases, w_q, b_q, w_o, o_bias, w_i, b_i, w_h = slot
    heads = w_q.shape[1] // HD
    first, second = normalize(hidden, gains, biases)
    first_full, second_full = (
        lax.all_gather(first.astype(jnp.bfloat16), "tensor", axis=0, tiled=True),
        lax.all_gather(second.astype(jnp.bfloat16), "tensor", axis=0, tiled=True),
    )

    def inner(first_full, second_full, shared):
        if kv_weights is not None:
            kv_lin = matmul(first_full, kv_weights[0]) + kv_weights[1]
            shared = (
                rotate(kv_lin[:, :HD], tables[2], tables[3]).astype(jnp.bfloat16),
                kv_lin[:, HD:].astype(jnp.bfloat16),
            )
        query = rotate(matmul(first_full, w_q) + b_q, tables[0], tables[1]).astype(jnp.bfloat16)
        attended, totals = attend(query, shared[0], shared[1], heads)
        before = matmul(second_full, w_i) + b_i
        active = jax.nn.gelu(before, approximate=False).astype(jnp.bfloat16)
        return (shared, (query, attended, totals, before, active))

    shared, saved = guarded(valid, inner, first_full, second_full, shared)
    cache = (first_full, second_full) + saved
    if not need_branch:
        return (None, cache, shared)
    attended, active = (saved[1], saved[4])
    count = hidden.shape[0] * lax.axis_size("tensor")

    def branches(attended, active):
        return matmul(lax.slice_in_dim(attended, 0, count, axis=0), w_o) + matmul(
            lax.slice_in_dim(active, 0, count, axis=0), w_h
        )

    summed = lax.psum_scatter(
        guarded(valid, branches, attended, active).astype(jnp.bfloat16),
        "tensor",
        scatter_dimension=0,
        tiled=True,
    ).astype(jnp.float32)
    return (hidden + summed + o_bias[0] + o_bias[1], cache, shared)


def layer_backward(grad, slot, cache, shared, tables, valid):
    gains, biases, w_q, b_q, w_o, o_bias, w_i, b_i, w_h = slot
    heads = w_q.shape[1] // HD
    grad_full = lax.all_gather(grad.astype(jnp.bfloat16), "tensor", axis=0, tiled=True)

    def inner(grad_full, cache, shared):
        first_full, second_full, query, attended, totals, before, active = cache
        grad_wout = matmul_left(attended, grad_full)
        grad_whid = matmul_left(active, grad_full)
        grad_att = matmul_right(grad_full, w_o).astype(jnp.bfloat16)
        grad_act = matmul_right(grad_full, w_h)
        grad_before = jax.vjp(lambda inside: jax.nn.gelu(inside, approximate=False), before)[1](
            grad_act
        )[0].astype(jnp.bfloat16)
        grad_bin = jnp.sum(grad_before.astype(jnp.float32), axis=0)
        grad_win = matmul_left(second_full, grad_before)
        grad_second = matmul_right(grad_before, w_i)
        grad_query, grad_keys, grad_values = attend_back(
            query, shared[0], shared[1], grad_att, totals, heads
        )
        turned = jax.vjp(lambda inside: rotate(inside, tables[0], tables[1]), grad_query)[1](
            grad_query
        )[0]
        grad_lin = turned.astype(jnp.bfloat16)
        grad_bq = jnp.sum(grad_lin.astype(jnp.float32), axis=0)
        grad_wq = matmul_left(first_full, grad_lin)
        grad_first = matmul_right(grad_lin, w_q)
        return (
            (grad_first, grad_second),
            (grad_keys, grad_values),
            (grad_wq, grad_bq, grad_wout, grad_win, grad_bin, grad_whid),
        )

    parts, kv_part, grads = guarded(valid, inner, grad_full, cache, shared)
    grad_first, grad_second = jax.tree.map(
        lambda part: part.astype(jnp.float32),
        lax.psum_scatter(for_sending(parts), "tensor", scatter_dimension=0, tiled=True),
    )
    return (grad_first, grad_second, kv_part, grads)


def norm_back(hidden, gains, biases, grad_first, grad_second):
    return jax.vjp(normalize, hidden, gains, biases)[1]((grad_first, grad_second))


def reduce_grads(big, small):
    big_share = (
        lax.psum_scatter(big[0].astype(jnp.bfloat16), "dp", scatter_dimension=2, tiled=True).astype(
            jnp.float32
        ),
        lax.psum_scatter(big[1].astype(jnp.bfloat16), "dp", scatter_dimension=2, tiled=True).astype(
            jnp.float32
        ),
        lax.psum_scatter(big[2].astype(jnp.bfloat16), "dp", scatter_dimension=1, tiled=True).astype(
            jnp.float32
        ),
        lax.psum_scatter(big[3].astype(jnp.bfloat16), "dp", scatter_dimension=1, tiled=True).astype(
            jnp.float32
        ),
        lax.psum_scatter(big[4].astype(jnp.bfloat16), "dp", scatter_dimension=3, tiled=True).astype(
            jnp.float32
        ),
        lax.psum_scatter(big[5].astype(jnp.bfloat16), "dp", scatter_dimension=2, tiled=True).astype(
            jnp.float32
        ),
        lax.psum_scatter(big[6].astype(jnp.bfloat16), "dp", scatter_dimension=2, tiled=True).astype(
            jnp.float32
        ),
        lax.psum_scatter(big[7].astype(jnp.bfloat16), "dp", scatter_dimension=3, tiled=True).astype(
            jnp.float32
        ),
    )
    small_share = (
        lax.psum_scatter(small[0], ("dp", "tensor"), scatter_dimension=3, tiled=True),
        lax.psum_scatter(small[1], ("dp", "tensor"), scatter_dimension=3, tiled=True),
        lax.psum_scatter(small[2], ("dp", "tensor"), scatter_dimension=3, tiled=True),
    )
    return (big_share, small_share)


def local(
    inputs,
    cotangent,
    subset_ids,
    subset_weight,
    ln_gain,
    ln_bias,
    w_query,
    b_query,
    w_kv,
    b_kv,
    w_out,
    out_bias,
    w_in,
    b_in,
    w_hid_out,
):
    sections = lax.axis_size("section")
    section_id = lax.axis_index("section")
    part_id = lax.axis_index("tensor")
    whole_in, whole_cot = (
        lax.all_gather(inputs, ("section", "tensor"), axis=1, tiled=True),
        lax.all_gather(cotangent, ("section", "tensor"), axis=1, tiled=True),
    )
    micro, length, width = whole_in.shape
    rows = length // lax.axis_size("tensor")
    offset = part_id * rows
    mine_in = lax.dynamic_slice_in_dim(whole_in, offset, rows, 1)
    mine_cot = lax.dynamic_slice_in_dim(whole_cot, offset, rows, 1)
    matches = subset_ids[:, None] == jnp.arange(subset_weight.shape[0], dtype=jnp.int32)[None, :]
    seq_scale = jnp.sum(jnp.where(matches, subset_weight[None, :], 0.0), axis=1)
    slots = tuple(
        (
            (
                ln_gain[0, slot],
                ln_bias[0, slot],
                w_query[0, slot],
                b_query[0, slot],
                w_out[0, slot],
                out_bias[0, slot],
                w_in[0, slot],
                b_in[0, slot],
                w_hid_out[0, slot],
            )
            for slot in range(2)
        )
    )
    kv_weights = (w_kv[0], b_kv[0])
    tables = rope_tables(length, w_query.shape[3]) + rope_tables(length, HD)
    blank = (jnp.zeros((length, HD), jnp.bfloat16), jnp.zeros((length, HD), jnp.bfloat16))
    ticks = micro + sections - 1

    def forward_tick(tick, carry):
        arriving, kept_in, kept_mid, finals = carry
        number = tick - section_id
        valid = (number >= 0) & (number < micro)
        index = jnp.clip(number, 0, micro - 1)
        first_in = lax.dynamic_index_in_dim(mine_in, index, 0, keepdims=False).astype(jnp.float32)
        start = jnp.where(
            valid, jnp.where(section_id == 0, first_in, arriving.astype(jnp.float32)), 0.0
        )
        middle, unused, shared = layer_forward(
            start, slots[0], blank, kv_weights, tables, valid, True
        )
        leaving, unused, unused_kv = layer_forward(
            middle, slots[1], shared, None, tables, valid, True
        )
        kept_in = jnp.where(
            valid, lax.dynamic_update_index_in_dim(kept_in, start, index, 0), kept_in
        )
        finals = jnp.where(
            valid & (section_id == sections - 1),
            lax.dynamic_update_index_in_dim(finals, leaving, index, 0),
            finals,
        )
        arriving = shifted(leaving.astype(jnp.bfloat16), "section", 1)
        return (arriving, kept_in, kept_mid, finals)

    store = jnp.zeros((micro, rows, width), jnp.float32)
    start_carry = (jnp.zeros((rows, width), jnp.bfloat16), store, store, store)
    unused_arrival, kept_in, kept_mid, finals = lax.fori_loop(0, ticks, forward_tick, start_carry)
    big_items = (w_query, b_query, w_kv, b_kv, w_out, w_in, b_in, w_hid_out)
    small_items = (ln_gain, ln_bias, out_bias)
    big_zero = tuple((jnp.zeros(item.shape, jnp.float32) for item in big_items))
    small_zero = tuple((jnp.zeros(item.shape, jnp.float32) for item in small_items))

    def backward_tick(tick, carry):
        arriving, inputs_grad, big_acc, small_acc = carry
        number = micro - 1 - tick + (sections - 1 - section_id)
        valid = (number >= 0) & (number < micro)
        index = jnp.clip(number, 0, micro - 1)
        weighted = lax.dynamic_index_in_dim(mine_cot, index, 0, keepdims=False).astype(
            jnp.float32
        ) * lax.dynamic_index_in_dim(seq_scale, index, 0, keepdims=False)
        grad = jnp.where(
            valid,
            jnp.where(section_id == sections - 1, weighted, arriving.astype(jnp.float32)),
            0.0,
        )
        start = lax.dynamic_index_in_dim(kept_in, index, 0, keepdims=False)
        middle, cache_first, shared = layer_forward(
            start, slots[0], blank, kv_weights, tables, valid, True
        )
        unused, cache_second, unused_kv = layer_forward(
            middle, slots[1], shared, None, tables, valid, False
        )
        second_h1, second_h2, kv_second, grads_second = layer_backward(
            grad, slots[1], cache_second, shared, tables, valid
        )
        mid_grad, gain_second, bias_second = norm_back(
            middle, slots[1][0], slots[1][1], second_h1, second_h2
        )
        grad_mid = grad + mid_grad
        first_h1, first_h2, kv_first, grads_first = layer_backward(
            grad_mid, slots[0], cache_first, shared, tables, valid
        )
        grad_keys, grad_values = (
            lax.psum((kv_first[0] + kv_second[0]).astype(jnp.bfloat16), "tensor").astype(
                jnp.float32
            ),
            lax.psum((kv_first[1] + kv_second[1]).astype(jnp.bfloat16), "tensor").astype(
                jnp.float32
            ),
        )

        def kv_inner(grad_keys, grad_values, first_full):
            turned = jax.vjp(lambda inside: rotate(inside, tables[2], tables[3]), grad_keys)[1](
                grad_keys
            )[0]
            grad_kv = jnp.concatenate([turned, grad_values], axis=1).astype(jnp.bfloat16)
            mine = lax.dynamic_slice_in_dim(grad_kv, offset, rows, 0)
            return (
                matmul_left(first_full, grad_kv),
                jnp.sum(grad_kv.astype(jnp.float32), axis=0),
                matmul_right(mine, kv_weights[0]),
            )

        grad_wkv, grad_bkv, kv_rows = guarded(
            valid, kv_inner, grad_keys, grad_values, cache_first[0]
        )
        in_grad, gain_first, bias_first = norm_back(
            start, slots[0][0], slots[0][1], first_h1 + kv_rows, first_h2
        )
        leaving = grad_mid + in_grad
        sum_second = jnp.sum(grad, axis=0)
        sum_first = jnp.sum(grad_mid, axis=0)

        def paired(pick):
            return jnp.stack([grads_first[pick], grads_second[pick]])[None]

        big = (
            paired(0),
            paired(1),
            grad_wkv[None],
            grad_bkv[None],
            paired(2),
            paired(3),
            paired(4),
            paired(5),
        )
        small = (
            jnp.stack([gain_first, gain_second])[None],
            jnp.stack([bias_first, bias_second])[None],
            jnp.stack([jnp.stack([sum_first, sum_first]), jnp.stack([sum_second, sum_second])])[
                None
            ],
        )
        big_acc = jax.tree.map(jnp.add, big_acc, big)
        small_acc = jax.tree.map(jnp.add, small_acc, small)
        inputs_grad = jnp.where(
            valid & (section_id == 0),
            lax.dynamic_update_index_in_dim(inputs_grad, leaving, index, 0),
            inputs_grad,
        )
        arriving = shifted(leaving.astype(jnp.bfloat16), "section", -1)
        return (arriving, inputs_grad, big_acc, small_acc)

    back_carry = (jnp.zeros((rows, width), jnp.bfloat16), store, big_zero, small_zero)
    unused_arrival, inputs_grad, big_acc, small_acc = lax.fori_loop(
        0, ticks, backward_tick, back_carry
    )
    big_acc, small_acc = reduce_grads(big_acc, small_acc)
    big_full = (
        lax.all_gather(big_acc[0].astype(jnp.bfloat16), "dp", axis=2, tiled=True).astype(
            jnp.float32
        ),
        lax.all_gather(big_acc[1].astype(jnp.bfloat16), "dp", axis=2, tiled=True).astype(
            jnp.float32
        ),
        lax.all_gather(big_acc[2].astype(jnp.bfloat16), "dp", axis=1, tiled=True).astype(
            jnp.float32
        ),
        lax.all_gather(big_acc[3].astype(jnp.bfloat16), "dp", axis=1, tiled=True).astype(
            jnp.float32
        ),
        lax.all_gather(big_acc[4].astype(jnp.bfloat16), "dp", axis=3, tiled=True).astype(
            jnp.float32
        ),
        lax.all_gather(big_acc[5].astype(jnp.bfloat16), "dp", axis=2, tiled=True).astype(
            jnp.float32
        ),
        lax.all_gather(big_acc[6].astype(jnp.bfloat16), "dp", axis=2, tiled=True).astype(
            jnp.float32
        ),
        lax.all_gather(big_acc[7].astype(jnp.bfloat16), "dp", axis=3, tiled=True).astype(
            jnp.float32
        ),
    )
    small_full = (
        lax.all_gather(small_acc[0], ("dp", "tensor"), axis=3, tiled=True),
        lax.all_gather(small_acc[1], ("dp", "tensor"), axis=3, tiled=True),
        lax.all_gather(small_acc[2], ("dp", "tensor"), axis=3, tiled=True),
    )
    canvas = jnp.zeros((micro, length, width), jnp.float32)
    placed_final = lax.dynamic_update_slice_in_dim(canvas, finals, offset, 1)
    placed_grad = lax.dynamic_update_slice_in_dim(canvas, inputs_grad, offset, 1)
    final_sum, grad_share = (
        lax.psum_scatter(
            placed_final.astype(jnp.bfloat16),
            ("section", "tensor"),
            scatter_dimension=1,
            tiled=True,
        ).astype(jnp.float32),
        lax.psum_scatter(
            placed_grad.astype(jnp.bfloat16), ("section", "tensor"), scatter_dimension=1, tiled=True
        ).astype(jnp.float32),
    )
    final_share = final_sum.astype(jnp.bfloat16)
    return (
        final_share,
        grad_share,
        small_full[0],
        small_full[1],
        big_full[0],
        big_full[1],
        big_full[2],
        big_full[3],
        big_full[4],
        small_full[2],
        big_full[5],
        big_full[6],
        big_full[7],
    )


def solution(mesh):
    return jax.shard_map(
        local,
        mesh=mesh,
        in_specs=(
            P("dp", ("section", "tensor"), None),
            P("dp", ("section", "tensor"), None),
            P("dp"),
            P(),
            P("section", None, None, None),
            P("section", None, None, None),
            P("section", None, None, "tensor"),
            P("section", None, "tensor"),
            P("section", None, None),
            P("section", None),
            P("section", None, "tensor", None),
            P("section", None, None, None),
            P("section", None, None, "tensor"),
            P("section", None, "tensor"),
            P("section", None, "tensor", None),
        ),
        out_specs=(
            P("dp", ("section", "tensor"), None),
            P("dp", ("section", "tensor"), None),
            P("section", None, None, None),
            P("section", None, None, None),
            P("section", None, None, "tensor"),
            P("section", None, "tensor"),
            P("section", None, None),
            P("section", None),
            P("section", None, "tensor", None),
            P("section", None, None, None),
            P("section", None, None, "tensor"),
            P("section", None, "tensor"),
            P("section", None, "tensor", None),
        ),
        check_vma=False,
    )
```

profile of v0, /device:TPU:1, one launch (start us, length us, event | category | flops | bytes accessed | tf_op | source)
XLA Modules:
  0.0 6274.6 jit_solution(3110790000675619932)
XLA Ops:
  47.5 31.5 all-gather.19.cloned.1.call-done
  84.5 1716.3 %while.76 = (s32[]{:T(128)}, bf16[512,768]{1,0:T(8,128)(2,1)}, f32[2,512,768]{2,1,0:T(8,128)}, bf16[2,512,768]{2,1,0:T(8,128)(2,1)}, s32[]{:T(128)}, /*index=5*/...) while((s32[]{:T(128)}, bf16[512,768]{1,0:T(8,128)(2,1)}, ...), condition=%wide.region_23.24_spmd.clone.clone.clone, body=%wide.region_0.23_spmd.clone.clone.clone.sunk | while | flops 15067600896 | bytes 390926080 | solution.py:337
  119.5 28.6 all-gather.31.cloned.1.call-done
  161.9 90.4 %reduce-scatter.63.cloned.1.call-done = bf16[512,768]{1,0:T(8,128)(2,1)} async-done(((bf16[1024,768]{1,0:T(8,128)(2,1)}), bf16[512,768]{1,0:T(8,128)(2,1)}) %reduce-scatter.63.cloned.1.call-update) | async-done | bytes 786448 | tf_op jit(solution)/shard_map/while/body/eval_jaxpr/reduce_scatter | solution.py:168
  284.7 28.9 all-gather.35.cloned.1.call-done
  319.6 79.2 %reduce-scatter.65.cloned.1.call-done = bf16[512,768]{1,0:T(8,128)(2,1)} async-done(((bf16[1024,768]{1,0:T(8,128)(2,1)}), bf16[512,768]{1,0:T(8,128)(2,1)}) %reduce-scatter.65.cloned.1.call-update) | async-done | bytes 786448 | tf_op jit(solution)/shard_map/while/body/eval_jaxpr/reduce_scatter | solution.py:168
  452.6 28.6 all-gather.31.cloned.1.call-done
  481.3 80.0 %conditional.56 = (bf16[1024,64]{0,1:T(8,128)(2,1)}, bf16[1024,64]{0,1:T(8,128)(2,1)}, bf16[1024,384]{1,0:T(8,128)(2,1)}, bf16[1024,1536]{1,0:T(8,128)(2,1)S(1)}) conditional(s32[]{:T(128)} %convert_element_type.1022, () %tuple.521, (bf16[1024,768]{1,0:T(8,128)(2,1)}, bf16[768,128]{1,0:T(8,128)(2,1)}, f32[1,128]{1,0:T(1,128)}, ...), branch_computations={%region_3.3_spmd, %region_4.8_spmd.clone} | conditional | flops 4601260544 | bytes 102327216 | solution.py:77
  629.4 28.9 all-gather.35.cloned.1.call-done
  658.2 49.3 conditional.58
  797.2 28.6 all-gather.31.cloned.1.call-done
  825.9 80.0 %conditional.56 = (bf16[1024,64]{0,1:T(8,128)(2,1)}, bf16[1024,64]{0,1:T(8,128)(2,1)}, bf16[1024,384]{1,0:T(8,128)(2,1)}, bf16[1024,1536]{1,0:T(8,128)(2,1)S(1)}) conditional(s32[]{:T(128)} %convert_element_type.1022, () %tuple.521, (bf16[1024,768]{1,0:T(8,128)(2,1)}, bf16[768,128]{1,0:T(8,128)(2,1)}, f32[1,128]{1,0:T(1,128)}, ...), branch_computations={%region_3.3_spmd, %region_4.8_spmd.clone} | conditional | flops 4601260544 | bytes 102327216 | solution.py:77
  974.9 28.9 all-gather.35.cloned.1.call-done
  1003.7 49.3 conditional.58
  1143.6 28.8 all-gather.31.cloned.1.call-done
  1185.9 103.2 %reduce-scatter.63.cloned.1.call-done = bf16[512,768]{1,0:T(8,128)(2,1)} async-done(((bf16[1024,768]{1,0:T(8,128)(2,1)}), bf16[512,768]{1,0:T(8,128)(2,1)}) %reduce-scatter.63.cloned.1.call-update) | async-done | bytes 786448 | tf_op jit(solution)/shard_map/while/body/eval_jaxpr/reduce_scatter | solution.py:168
  1321.4 28.9 all-gather.35.cloned.1.call-done
  1352.8 83.6 %reduce-scatter.65.cloned.1.call-done = bf16[512,768]{1,0:T(8,128)(2,1)} async-done(((bf16[1024,768]{1,0:T(8,128)(2,1)}), bf16[512,768]{1,0:T(8,128)(2,1)}) %reduce-scatter.65.cloned.1.call-update) | async-done | bytes 786448 | tf_op jit(solution)/shard_map/while/body/eval_jaxpr/reduce_scatter | solution.py:168
  1490.1 28.8 all-gather.31.cloned.1.call-done
  1524.4 110.6 %reduce-scatter.63.cloned.1.call-done = bf16[512,768]{1,0:T(8,128)(2,1)} async-done(((bf16[1024,768]{1,0:T(8,128)(2,1)}), bf16[512,768]{1,0:T(8,128)(2,1)}) %reduce-scatter.63.cloned.1.call-update) | async-done | bytes 786448 | tf_op jit(solution)/shard_map/while/body/eval_jaxpr/reduce_scatter | solution.py:168
  1667.4 28.9 all-gather.35.cloned.1.call-done
  1698.8 83.1 %reduce-scatter.65.cloned.1.call-done = bf16[512,768]{1,0:T(8,128)(2,1)} async-done(((bf16[1024,768]{1,0:T(8,128)(2,1)}), bf16[512,768]{1,0:T(8,128)(2,1)}) %reduce-scatter.65.cloned.1.call-update) | async-done | bytes 786448 | tf_op jit(solution)/shard_map/while/body/eval_jaxpr/reduce_scatter | solution.py:168
  1801.8 3604.6 %while.77 = (s32[]{:T(128)}, bf16[512,768]{1,0:T(8,128)(2,1)}, bf16[2,512,768]{2,1,0:T(8,128)(2,1)}, f32[1,2,768,384]{2,3,1,0:T(8,128)}, f32[1,2,384]{2,1,0:T(2,...) while((s32[]{:T(128)}, bf16[512,768]{1,0:T(8,128)(2,1)}, ...), condition=%wide.region_85.86_spmd.clone.clone.clone.clone, body=%wide.region_26.85_spmd.clone.clone.clone.clone.sunk | while | flops 42937929728 | bytes 1885964544 | solution.py:435
  1845.7 28.8 all-gather.39.cloned.1.call-done
  1893.5 84.0 %reduce-scatter.67.cloned.1.call-done = bf16[512,768]{1,0:T(8,128)(2,1)} async-done(((bf16[1024,768]{1,0:T(8,128)(2,1)}), bf16[512,768]{1,0:T(8,128)(2,1)}) %reduce-scatter.67.cloned.1.call-update) | async-done | bytes 786448 | tf_op jit(solution)/shard_map/while/body/eval_jaxpr/reduce_scatter | solution.py:168
  2009.2 28.7 all-gather.43.cloned.1.call-done
  2084.4 156.7 %reduce-scatter.69.cloned.1.call-done = bf16[512,768]{1,0:T(8,128)(2,1)} async-done(((bf16[1024,768]{1,0:T(8,128)(2,1)}), bf16[512,768]{1,0:T(8,128)(2,1)}) %reduce-scatter.69.cloned.1.call-update) | async-done | bytes 786448 | tf_op jit(solution)/shard_map/while/body/eval_jaxpr/reduce_scatter | solution.py:213
  2241.1 28.4 reduce-scatter.71.cloned.1.call-done
  2355.2 89.9 %all-reduce.30.cloned.1.call-done = (bf16[1024,64]{0,1:T(8,128)(2,1)}, bf16[1024,64]{0,1:T(8,128)(2,1)}) async-done(((bf16[1024,64]{0,1:T(8,128)(2,1)}, bf16[1024,64]{0,1:T(8,128)(2,1)}), (bf16[1024,64]{0,1:T(8,128)(2,1)}, bf16[1024,64]{0,1:T(8,128)(2,1)})) %all-reduce.30.cloned.1.call-update) | async-done | bytes 262160 | tf_op jit(solution)/shard_map/while/body/eval_jaxpr/psum | solution.py:374
  2559.0 28.6 all-gather.39.cloned.1.call-done
  2606.4 84.7 %reduce-scatter.67.cloned.1.call-done = bf16[512,768]{1,0:T(8,128)(2,1)} async-done(((bf16[1024,768]{1,0:T(8,128)(2,1)}), bf16[512,768]{1,0:T(8,128)(2,1)}) %reduce-scatter.67.cloned.1.call-update) | async-done | bytes 786448 | tf_op jit(solution)/shard_map/while/body/eval_jaxpr/reduce_scatter | solution.py:168
  2722.8 28.7 all-gather.43.cloned.1.call-done
  2797.8 157.4 %reduce-scatter.69.cloned.1.call-done = bf16[512,768]{1,0:T(8,128)(2,1)} async-done(((bf16[1024,768]{1,0:T(8,128)(2,1)}), bf16[512,768]{1,0:T(8,128)(2,1)}) %reduce-scatter.69.cloned.1.call-update) | async-done | bytes 786448 | tf_op jit(solution)/shard_map/while/body/eval_jaxpr/reduce_scatter | solution.py:213
  2955.2 28.4 reduce-scatter.71.cloned.1.call-done
  3075.9 84.0 %all-reduce.30.cloned.1.call-done = (bf16[1024,64]{0,1:T(8,128)(2,1)}, bf16[1024,64]{0,1:T(8,128)(2,1)}) async-done(((bf16[1024,64]{0,1:T(8,128)(2,1)}, bf16[1024,64]{0,1:T(8,128)(2,1)}), (bf16[1024,64]{0,1:T(8,128)(2,1)}, bf16[1024,64]{0,1:T(8,128)(2,1)})) %all-reduce.30.cloned.1.call-update) | async-done | bytes 262160 | tf_op jit(solution)/shard_map/while/body/eval_jaxpr/psum | solution.py:374
  3273.6 28.6 all-gather.39.cloned.1.call-done
  3302.2 65.9 %conditional.60 = (bf16[1024,64]{0,1:T(8,128)(2,1)S(1)}, bf16[1024,64]{0,1:T(8,128)(2,1)S(1)}, bf16[1024,384]{0,1:T(8,128)(2,1)}, bf16[1024,384]{1,0:T(8,128)(2,...) conditional(s32[]{:T(128)} %convert_element_type.1034, () %tuple.553, ...), branch_computations={%region_29.29_spmd, %region_30.34_spmd} | conditional | flops 4601141760 | bytes 217269344 | solution.py:77
  3437.7 28.9 all-gather.43.cloned.1.call-done
  3466.6 61.4 conditional.62
  3528.1 115.9 %conditional.63 = (bf16[1024,768]{1,0:T(8,128)(2,1)}, bf16[1024,768]{1,0:T(8,128)(2,1)}, f32[1024,64]{0,1:T(8,128)}, f32[1024,64]{0,1:T(8,128)}, f32[1,768,384]{...) conditional(s32[]{:T(128)} %convert_element_type.1034, ...), branch_computations={%region_46.46_spmd, %region_47.51_spmd} | conditional | flops 15269246976 | bytes 531891200 | solution.py:77
  3670.2 28.2 reduce-scatter.71.cloned.1.call-done
  3736.0 112.1 %conditional.64 = (bf16[1024,768]{1,0:T(8,128)(2,1)}, bf16[1024,768]{1,0:T(8,128)(2,1)}, f32[1024,64]{0,1:T(8,128)}, f32[1024,64]{0,1:T(8,128)}, f32[1,768,384]{...) conditional(s32[]{:T(128)} %convert_element_type.1034, ...), branch_computations={%region_58.58_spmd, %region_59.63_spmd} | conditional | flops 15269246976 | bytes 551814144 | solution.py:77
  3988.3 28.6 all-gather.39.cloned.1.call-done
  4016.9 65.9 %conditional.60 = (bf16[1024,64]{0,1:T(8,128)(2,1)S(1)}, bf16[1024,64]{0,1:T(8,128)(2,1)S(1)}, bf16[1024,384]{0,1:T(8,128)(2,1)}, bf16[1024,384]{1,0:T(8,128)(2,...) conditional(s32[]{:T(128)} %convert_element_type.1034, () %tuple.553, ...), branch_computations={%region_29.29_spmd, %region_30.34_spmd} | conditional | flops 4601141760 | bytes 217269344 | solution.py:77
  4151.5 28.7 all-gather.43.cloned.1.call-done
  4180.2 61.2 conditional.62
  4241.5 126.4 %conditional.63 = (bf16[1024,768]{1,0:T(8,128)(2,1)}, bf16[1024,768]{1,0:T(8,128)(2,1)}, f32[1024,64]{0,1:T(8,128)}, f32[1024,64]{0,1:T(8,128)}, f32[1,768,384]{...) conditional(s32[]{:T(128)} %convert_element_type.1034, ...), branch_computations={%region_46.46_spmd, %region_47.51_spmd} | conditional | flops 15269246976 | bytes 531891200 | solution.py:77
  4392.8 28.2 reduce-scatter.71.cloned.1.call-done
  4458.5 112.3 %conditional.64 = (bf16[1024,768]{1,0:T(8,128)(2,1)}, bf16[1024,768]{1,0:T(8,128)(2,1)}, f32[1024,64]{0,1:T(8,128)}, f32[1024,64]{0,1:T(8,128)}, f32[1,768,384]{...) conditional(s32[]{:T(128)} %convert_element_type.1034, ...), branch_computations={%region_58.58_spmd, %region_59.63_spmd} | conditional | flops 15269246976 | bytes 551814144 | solution.py:77
  4710.1 28.6 all-gather.39.cloned.1.call-done
  4757.7 83.8 %reduce-scatter.67.cloned.1.call-done = bf16[512,768]{1,0:T(8,128)(2,1)} async-done(((bf16[1024,768]{1,0:T(8,128)(2,1)}), bf16[512,768]{1,0:T(8,128)(2,1)}) %reduce-scatter.67.cloned.1.call-update) | async-done | bytes 786448 | tf_op jit(solution)/shard_map/while/body/eval_jaxpr/reduce_scatter | solution.py:168
  4873.3 28.9 all-gather.43.cloned.1.call-done
  4948.4 166.9 %reduce-scatter.69.cloned.1.call-done = bf16[512,768]{1,0:T(8,128)(2,1)} async-done(((bf16[1024,768]{1,0:T(8,128)(2,1)}), bf16[512,768]{1,0:T(8,128)(2,1)}) %reduce-scatter.69.cloned.1.call-update) | async-done | bytes 786448 | tf_op jit(solution)/shard_map/while/body/eval_jaxpr/reduce_scatter | solution.py:213
  5115.2 28.2 reduce-scatter.71.cloned.1.call-done
  5235.5 83.6 %all-reduce.30.cloned.1.call-done = (bf16[1024,64]{0,1:T(8,128)(2,1)}, bf16[1024,64]{0,1:T(8,128)(2,1)}) async-done(((bf16[1024,64]{0,1:T(8,128)(2,1)}, bf16[1024,64]{0,1:T(8,128)(2,1)}), (bf16[1024,64]{0,1:T(8,128)(2,1)}, bf16[1024,64]{0,1:T(8,128)(2,1)})) %all-reduce.30.cloned.1.call-update) | async-done | bytes 262160 | tf_op jit(solution)/shard_map/while/body/eval_jaxpr/psum | solution.py:374
  5475.6 83.2 %reduce-scatter.61.cloned.1.call-done = bf16[192,3072]{1,0:T(8,128)(2,1)} async-done(((bf16[768,3072]{1,0:T(8,128)(2,1)}), bf16[192,3072]{1,0:T(8,128)(2,1)}) %reduce-scatter.61.cloned.1.call-update) | async-done | bytes 1179664
  5562.9 84.7 %reduce-scatter.45.cloned.1.call-done = bf16[1,2,192,1536]{3,2,1,0:T(8,128)(2,1)} async-done(((bf16[1,2,768,1536]{3,2,1,0:T(8,128)(2,1)}), bf16[1,2,192,1536]{3,2,1,0:T(8,128)(2,1)}) %reduce-scatter.45.cloned.1.call-update) | async-done | bytes 1179664 | tf_op jit(solution)/shard_map/reduce_scatter | solution.py:239
  5719.2 52.4 reduce-scatter.47.cloned.1.call-done
  5800.0 36.4 reduce-scatter.49.cloned.1.call-done
  5865.2 35.5 reduce-scatter.57.cloned.1.call-done
  5991.1 47.1 reduce-scatter.39.cloned.1.call-done
  6040.1 89.1 %all-gather.27.cloned.1.call-done = bf16[1,2,1536,768]{2,1,0,3:T(2,128)(2,1)} async-done(((bf16[1,2,1536,192]{2,1,0,3:T(2,128)(2,1)}), bf16[1,2,1536,768]{2,1,0,3:T(2,128)(2,1)}) %all-gather.27.cloned.1.call-update) | async-done | bytes 4718608 | tf_op jit(solution)/shard_map/all_gather | solution.py:461
  6143.0 75.8 %all-gather.25.cloned.1.call-done = bf16[1,2,768,1536]{3,2,1,0:T(8,128)(2,1)} async-done(((bf16[1,2,192,1536]{3,2,1,0:T(8,128)(2,1)}), bf16[1,2,768,1536]{3,2,1,0:T(8,128)(2,1)}) %all-gather.25.cloned.1.call-update) | async-done | bytes 4718608 | tf_op jit(solution)/shard_map/all_gather | solution.py:455
  6226.2 41.4 reduce-scatter.37.cloned.1.call-done
  (2498 shorter events, 3598.4 us)
Async XLA Ops:
  93.1 159.2 %reduce-scatter.63.cloned.1.call-start = ((), (), s32[]{:S(2)}) async-start(), calls=%async_computation.41 | async-start | bytes 2359296 | tf_op jit(solution)/shard_map/while/body/eval_jaxpr/reduce_scatter | solution.py:168
  160.2 124.4 %all-gather.33.cloned.1.call-start = ((), (), s32[]{:S(2)}) async-start(), calls=%async_computation.42 | async-start | bytes 2359296 | tf_op jit(solution)/shard_map/while/body/eval_jaxpr/all_gather | solution.py:139
  258.1 140.7 %reduce-scatter.65.cloned.1.call-start = ((), (), s32[]{:S(2)}) async-start(), calls=%async_computation.44 | async-start | bytes 2359296 | tf_op jit(solution)/shard_map/while/body/eval_jaxpr/reduce_scatter | solution.py:168
  425.0 172.0 %reduce-scatter.63.cloned.1.call-start = ((), (), s32[]{:S(2)}) async-start(), calls=%async_computation.41 | async-start | bytes 2359296 | tf_op jit(solution)/shard_map/while/body/eval_jaxpr/reduce_scatter | solution.py:168
  602.8 140.8 %reduce-scatter.65.cloned.1.call-start = ((), (), s32[]{:S(2)}) async-start(), calls=%async_computation.44 | async-start | bytes 2359296 | tf_op jit(solution)/shard_map/while/body/eval_jaxpr/reduce_scatter | solution.py:168
  769.7 172.8 %reduce-scatter.63.cloned.1.call-start = ((), (), s32[]{:S(2)}) async-start(), calls=%async_computation.41 | async-start | bytes 2359296 | tf_op jit(solution)/shard_map/while/body/eval_jaxpr/reduce_scatter | solution.py:168
  948.3 141.7 %reduce-scatter.65.cloned.1.call-start = ((), (), s32[]{:S(2)}) async-start(), calls=%async_computation.44 | async-start | bytes 2359296 | tf_op jit(solution)/shard_map/while/body/eval_jaxpr/reduce_scatter | solution.py:168
  1116.3 172.8 %reduce-scatter.63.cloned.1.call-start = ((), (), s32[]{:S(2)}) async-start(), calls=%async_computation.41 | async-start | bytes 2359296 | tf_op jit(solution)/shard_map/while/body/eval_jaxpr/reduce_scatter | solution.py:168
  1184.2 137.2 %all-gather.33.cloned.1.call-start = ((), (), s32[]{:S(2)}) async-start(), calls=%async_computation.42 | async-start | bytes 2359296 | tf_op jit(solution)/shard_map/while/body/eval_jaxpr/all_gather | solution.py:139
  1294.8 141.7 %reduce-scatter.65.cloned.1.call-start = ((), (), s32[]{:S(2)}) async-start(), calls=%async_computation.44 | async-start | bytes 2359296 | tf_op jit(solution)/shard_map/while/body/eval_jaxpr/reduce_scatter | solution.py:168
  1462.4 172.6 %reduce-scatter.63.cloned.1.call-start = ((), (), s32[]{:S(2)}) async-start(), calls=%async_computation.41 | async-start | bytes 2359296 | tf_op jit(solution)/shard_map/while/body/eval_jaxpr/reduce_scatter | solution.py:168
  1522.8 144.6 %all-gather.33.cloned.1.call-start = ((), (), s32[]{:S(2)}) async-start(), calls=%async_computation.42 | async-start | bytes 2359296 | tf_op jit(solution)/shard_map/while/body/eval_jaxpr/all_gather | solution.py:139
  1640.8 141.1 %reduce-scatter.65.cloned.1.call-start = ((), (), s32[]{:S(2)}) async-start(), calls=%async_computation.44 | async-start | bytes 2359296 | tf_op jit(solution)/shard_map/while/body/eval_jaxpr/reduce_scatter | solution.py:168
  1818.3 159.1 %reduce-scatter.67.cloned.1.call-start = ((), (), s32[]{:S(2)}) async-start(), calls=%async_computation.47 | async-start | bytes 2359296 | tf_op jit(solution)/shard_map/while/body/eval_jaxpr/reduce_scatter | solution.py:168
  1891.0 118.2 %all-gather.41.cloned.1.call-start = ((), (), s32[]{:S(2)}) async-start(), calls=%async_computation.48 | async-start | bytes 2359296 | tf_op jit(solution)/shard_map/while/body/eval_jaxpr/all_gather | solution.py:139
  1982.4 84.4 %all-gather.45.cloned.1.call-start = ((), (), s32[]{:S(2)}) async-start(), calls=%async_computation.50 | async-start | bytes 2359296 | tf_op jit(solution)/shard_map/while/body/eval_jaxpr/all_gather | solution.py:180
  1985.5 255.6 %reduce-scatter.69.cloned.1.call-start = ((), (), s32[]{:S(2)}) async-start(), calls=%async_computation.51 | async-start | bytes 2359296 | tf_op jit(solution)/shard_map/while/body/eval_jaxpr/reduce_scatter | solution.py:213
  2083.6 185.9 %reduce-scatter.71.cloned.1.call-start = ((), (), s32[]{:S(2)}) async-start(), calls=%async_computation.52 | async-start | bytes 2359296 | tf_op jit(solution)/shard_map/while/body/eval_jaxpr/reduce_scatter | solution.py:213
  2084.4 222.7 %all-gather.47.cloned.1.call-start = ((), (), s32[]{:S(2)}) async-start(), calls=%async_computation.53 | async-start | bytes 2359296 | tf_op jit(solution)/shard_map/while/body/eval_jaxpr/all_gather | solution.py:180
  2279.7 165.5 %all-reduce.30.cloned.1.call-start = ((), (), s32[]{:S(2)}) async-start(), calls=%async_computation.55 | async-start | bytes 524288 | tf_op jit(solution)/shard_map/while/body/eval_jaxpr/psum | solution.py:374
  2329.2 144.7 %reduce-scatter.73.cloned.1.call-start = ((), (), s32[]{:S(2)}) async-start(), calls=%async_computation.54 | async-start | bytes 2359296 | tf_op jit(solution)/shard_map/while/body/eval_jaxpr/reduce_scatter | solution.py:213
  2329.8 172.5 %reduce-scatter.75.cloned.1.call-start = ((), (), s32[]{:S(2)}) async-start(), calls=%async_computation.56 | async-start | bytes 2359296 | tf_op jit(solution)/shard_map/while/body/eval_jaxpr/reduce_scatter | solution.py:213
  2533.6 157.5 %reduce-scatter.67.cloned.1.call-start = ((), (), s32[]{:S(2)}) async-start(), calls=%async_computation.47 | async-start | bytes 2359296 | tf_op jit(solution)/shard_map/while/body/eval_jaxpr/reduce_scatter | solution.py:168
  2604.0 118.9 %all-gather.41.cloned.1.call-start = ((), (), s32[]{:S(2)}) async-start(), calls=%async_computation.48 | async-start | bytes 2359296 | tf_op jit(solution)/shard_map/while/body/eval_jaxpr/all_gather | solution.py:139
  2696.1 84.4 %all-gather.45.cloned.1.call-start = ((), (), s32[]{:S(2)}) async-start(), calls=%async_computation.50 | async-start | bytes 2359296 | tf_op jit(solution)/shard_map/while/body/eval_jaxpr/all_gather | solution.py:180
  2699.1 256.1 %reduce-scatter.69.cloned.1.call-start = ((), (), s32[]{:S(2)}) async-start(), calls=%async_computation.51 | async-start | bytes 2359296 | tf_op jit(solution)/shard_map/while/body/eval_jaxpr/reduce_scatter | solution.py:213
  2797.1 186.5 %reduce-scatter.71.cloned.1.call-start = ((), (), s32[]{:S(2)}) async-start(), calls=%async_computation.52 | async-start | bytes 2359296 | tf_op jit(solution)/shard_map/while/body/eval_jaxpr/reduce_scatter | solution.py:213
  2797.8 223.3 %all-gather.47.cloned.1.call-start = ((), (), s32[]{:S(2)}) async-start(), calls=%async_computation.53 | async-start | bytes 2359296 | tf_op jit(solution)/shard_map/while/body/eval_jaxpr/all_gather | solution.py:180
  2993.8 166.1 %all-reduce.30.cloned.1.call-start = ((), (), s32[]{:S(2)}) async-start(), calls=%async_computation.55 | async-start | bytes 524288 | tf_op jit(solution)/shard_map/while/body/eval_jaxpr/psum | solution.py:374
  3043.5 145.1 %reduce-scatter.73.cloned.1.call-start = ((), (), s32[]{:S(2)}) async-start(), calls=%async_computation.54 | async-start | bytes 2359296 | tf_op jit(solution)/shard_map/while/body/eval_jaxpr/reduce_scatter | solution.py:213
  3044.3 172.8 %reduce-scatter.75.cloned.1.call-start = ((), (), s32[]{:S(2)}) async-start(), calls=%async_computation.56 | async-start | bytes 2359296 | tf_op jit(solution)/shard_map/while/body/eval_jaxpr/reduce_scatter | solution.py:213
  3248.2 157.7 %reduce-scatter.67.cloned.1.call-start = ((), (), s32[]{:S(2)}) async-start(), calls=%async_computation.47 | async-start | bytes 2359296 | tf_op jit(solution)/shard_map/while/body/eval_jaxpr/reduce_scatter | solution.py:168
  3411.1 116.9 %all-gather.45.cloned.1.call-start = ((), (), s32[]{:S(2)}) async-start(), calls=%async_computation.50 | async-start | bytes 2359296 | tf_op jit(solution)/shard_map/while/body/eval_jaxpr/all_gather | solution.py:180
  3414.1 256.1 %reduce-scatter.69.cloned.1.call-start = ((), (), s32[]{:S(2)}) async-start(), calls=%async_computation.51 | async-start | bytes 2359296 | tf_op jit(solution)/shard_map/while/body/eval_jaxpr/reduce_scatter | solution.py:213
  3644.6 91.4 %all-gather.47.cloned.1.call-start = ((), (), s32[]{:S(2)}) async-start(), calls=%async_computation.53 | async-start | bytes 2359296 | tf_op jit(solution)/shard_map/while/body/eval_jaxpr/all_gather | solution.py:180
  3708.6 175.4 %all-reduce.30.cloned.1.call-start = ((), (), s32[]{:S(2)}) async-start(), calls=%async_computation.55 | async-start | bytes 524288 | tf_op jit(solution)/shard_map/while/body/eval_jaxpr/psum | solution.py:374
  3962.9 156.8 %reduce-scatter.67.cloned.1.call-start = ((), (), s32[]{:S(2)}) async-start(), calls=%async_computation.47 | async-start | bytes 2359296 | tf_op jit(solution)/shard_map/while/body/eval_jaxpr/reduce_scatter | solution.py:168
  4124.7 116.7 %all-gather.45.cloned.1.call-start = ((), (), s32[]{:S(2)}) async-start(), calls=%async_computation.50 | async-start | bytes 2359296 | tf_op jit(solution)/shard_map/while/body/eval_jaxpr/all_gather | solution.py:180
  4127.8 265.0 %reduce-scatter.69.cloned.1.call-start = ((), (), s32[]{:S(2)}) async-start(), calls=%async_computation.51 | async-start | bytes 2359296 | tf_op jit(solution)/shard_map/while/body/eval_jaxpr/reduce_scatter | solution.py:213
  4368.5 90.0 %all-gather.47.cloned.1.call-start = ((), (), s32[]{:S(2)}) async-start(), calls=%async_computation.53 | async-start | bytes 2359296 | tf_op jit(solution)/shard_map/while/body/eval_jaxpr/all_gather | solution.py:180
  4431.2 175.7 %all-reduce.30.cloned.1.call-start = ((), (), s32[]{:S(2)}) async-start(), calls=%async_computation.55 | async-start | bytes 524288 | tf_op jit(solution)/shard_map/while/body/eval_jaxpr/psum | solution.py:374
  4684.7 156.8 %reduce-scatter.67.cloned.1.call-start = ((), (), s32[]{:S(2)}) async-start(), calls=%async_computation.47 | async-start | bytes 2359296 | tf_op jit(solution)/shard_map/while/body/eval_jaxpr/reduce_scatter | solution.py:168
  4755.3 118.0 %all-gather.41.cloned.1.call-start = ((), (), s32[]{:S(2)}) async-start(), calls=%async_computation.48 | async-start | bytes 2359296 | tf_op jit(solution)/shard_map/while/body/eval_jaxpr/all_gather | solution.py:139
  4849.8 265.5 %reduce-scatter.69.cloned.1.call-start = ((), (), s32[]{:S(2)}) async-start(), calls=%async_computation.51 | async-start | bytes 2359296 | tf_op jit(solution)/shard_map/while/body/eval_jaxpr/reduce_scatter | solution.py:213
  4947.7 195.7 %reduce-scatter.71.cloned.1.call-start = ((), (), s32[]{:S(2)}) async-start(), calls=%async_computation.52 | async-start | bytes 2359296 | tf_op jit(solution)/shard_map/while/body/eval_jaxpr/reduce_scatter | solution.py:213
  4948.3 232.6 %all-gather.47.cloned.1.call-start = ((), (), s32[]{:S(2)}) async-start(), calls=%async_computation.53 | async-start | bytes 2359296 | tf_op jit(solution)/shard_map/while/body/eval_jaxpr/all_gather | solution.py:180
  5153.6 165.5 %all-reduce.30.cloned.1.call-start = ((), (), s32[]{:S(2)}) async-start(), calls=%async_computation.55 | async-start | bytes 524288 | tf_op jit(solution)/shard_map/while/body/eval_jaxpr/psum | solution.py:374
  5203.1 144.7 %reduce-scatter.73.cloned.1.call-start = ((), (), s32[]{:S(2)}) async-start(), calls=%async_computation.54 | async-start | bytes 2359296 | tf_op jit(solution)/shard_map/while/body/eval_jaxpr/reduce_scatter | solution.py:213
  5203.8 172.3 %reduce-scatter.75.cloned.1.call-start = ((), (), s32[]{:S(2)}) async-start(), calls=%async_computation.56 | async-start | bytes 2359296 | tf_op jit(solution)/shard_map/while/body/eval_jaxpr/reduce_scatter | solution.py:213
  5415.3 143.5 %reduce-scatter.61.cloned.1.call-start = ((), (), s32[]{:S(2)}) async-start(), calls=%async_computation.38 | async-start | bytes 5898240
  5440.0 207.6 %reduce-scatter.45.cloned.1.call-start = ((), (), s32[]{:S(2)}) async-start(), calls=%async_computation.28 | async-start | bytes 5898240 | tf_op jit(solution)/shard_map/reduce_scatter | solution.py:239
  5447.8 219.1 %reduce-scatter.53.cloned.1.call-start = ((), (), s32[]{:S(2)}) async-start(), calls=%async_computation.34 | async-start | bytes 40960
  5448.6 237.7 %reduce-scatter.51.cloned.1.call-start = ((), (), s32[]{:S(2)}) async-start(), calls=%async_computation.33 | async-start | bytes 122880
  5449.6 258.7 %reduce-scatter.59.cloned.1.call-start = ((), (), s32[]{:S(2)}) async-start(), calls=%async_computation.37 | async-start | bytes 491520
  5451.2 320.5 %reduce-scatter.47.cloned.1.call-start = ((), (), s32[]{:S(2)}) async-start(), calls=%async_computation.31 | async-start | bytes 442368
  5452.9 383.5 %reduce-scatter.49.cloned.1.call-start = ((), (), s32[]{:S(2)}) async-start(), calls=%async_computation.32 | async-start | bytes 442368
  5454.7 445.9 %reduce-scatter.57.cloned.1.call-start = ((), (), s32[]{:S(2)}) async-start(), calls=%async_computation.36 | async-start | bytes 442368
  5456.5 473.4 %reduce-scatter.43.cloned.1.call-start = ((), (), s32[]{:S(2)}) async-start(), calls=%async_computation.26 | async-start | bytes 245760 | tf_op jit(solution)/shard_map/reduce_scatter | solution.py:230
  5457.4 500.6 %all-gather.23.cloned.1.call-start = ((), (), s32[]{:S(2)}) async-start(), calls=%async_computation.27 | async-start | bytes 1474560 | tf_op jit(solution)/shard_map/all_gather | solution.py:452
  5459.3 529.0 %all-gather.21.cloned.1.call-start = ((), (), s32[]{:S(2)}) async-start(), calls=%async_computation.25 | async-start | bytes 1474560 | tf_op jit(solution)/shard_map/all_gather | solution.py:440
  5472.4 565.8 %reduce-scatter.39.cloned.1.call-start = ((), (), s32[]{:S(2)}) async-start(), calls=%async_computation.23 | async-start | bytes 3538944 | tf_op jit(solution)/shard_map/reduce_scatter | solution.py:480
  5475.6 653.7 %all-gather.27.cloned.1.call-start = ((), (), s32[]{:S(2)}) async-start(), calls=%async_computation.30 | async-start | bytes 5898240 | tf_op jit(solution)/shard_map/all_gather | solution.py:461
  5562.8 655.9 %all-gather.25.cloned.1.call-start = ((), (), s32[]{:S(2)}) async-start(), calls=%async_computation.29 | async-start | bytes 5898240 | tf_op jit(solution)/shard_map/all_gather | solution.py:455
  5647.6 620.0 %reduce-scatter.37.cloned.1.call-start = ((), (), s32[]{:S(2)}) async-start(), calls=%async_computation.21 | async-start | bytes 3538944 | tf_op jit(solution)/shard_map/reduce_scatter | solution.py:474
  (573 other events, 15740.8 us)
Sparse Core Ops, SparseCore 0:
  9.9 34.8 all-gather.16
  46.7 32.3 all-gather.18
  120.9 27.1 all-gather.30
  160.4 91.8 reduce-scatter.62
  286.3 27.1 all-gather.34
  319.7 79.0 reduce-scatter.64
  424.5 28.0 all-gather.28
  454.0 27.2 all-gather.30
  602.1 27.2 all-gather.32
  631.0 27.1 all-gather.34
  769.2 27.9 all-gather.28
  798.6 27.1 all-gather.30
  947.6 27.2 all-gather.32
  976.5 27.1 all-gather.34
  1115.6 27.9 all-gather.28
  1145.1 27.2 all-gather.30
  1184.3 104.6 reduce-scatter.62
  1294.1 27.2 all-gather.32
  1323.0 27.1 all-gather.34
  1352.9 83.4 reduce-scatter.64
  1461.8 28.3 all-gather.28
  1491.7 27.2 all-gather.30
  1522.9 112.1 reduce-scatter.62
  1669.0 27.1 all-gather.34
  1698.9 82.9 reduce-scatter.64
  1817.7 27.9 all-gather.36
  1891.1 86.2 reduce-scatter.66
  1981.9 27.2 all-gather.40
  2010.7 27.1 all-gather.42
  2083.7 157.3 reduce-scatter.68
  2279.8 27.2 all-gather.46
  2329.3 115.8 all-reduce.29
  2604.1 86.9 reduce-scatter.66
  2695.6 27.2 all-gather.40
  2724.3 27.2 all-gather.42
  2797.2 158.0 reduce-scatter.68
  2993.9 27.2 all-gather.46
  3043.6 116.1 all-reduce.29
  3410.4 27.2 all-gather.40
  3439.3 27.1 all-gather.42
  3468.2 27.1 all-gather.44
  3708.7 27.2 all-gather.46
  4124.2 27.2 all-gather.40
  4152.9 27.2 all-gather.42
  4181.7 27.1 all-gather.44
  4431.3 27.2 all-gather.46
  4755.4 86.0 reduce-scatter.66
  4903.6 27.1 all-gather.44
  4947.8 167.3 reduce-scatter.68
  5153.7 27.2 all-gather.46
  5203.2 115.7 all-reduce.29
  5413.9 27.5 reduce-scatter.54
  5444.4 27.8 reduce-scatter.40
  5474.6 84.1 reduce-scatter.60
  5561.7 85.7 reduce-scatter.44
  5712.3 59.2 reduce-scatter.46
  5775.8 60.6 reduce-scatter.48
  5840.1 60.5 reduce-scatter.56
  5924.3 33.6 all-gather.22
  5959.4 28.7 all-gather.20
  5992.2 45.9 reduce-scatter.38
  6039.7 89.4 all-gather.26
  6130.9 87.8 all-gather.24
  6222.9 44.6 reduce-scatter.36
  (45 shorter events, 1142.8 us)
where the time goes:
time: 6290 us; the launch traced here: 6270 us
  waiting for transfers between devices  4060 us (65%)
  other arithmetic  702 us (11%)
  matrix products  660 us (10%)
  local copies, waits for them, and re-layouts  554 us (9%)
  loops' own time  127 us (2%)
  blocking collectives  121 us (2%)
    reduce_scatter x15, waiting for transfers between devices, layer_forward(): lax.psum_scatter(guarded(valid, branches, attended, active).astype(jnp.bf...  949 us
    reduce_scatter x20, waiting for transfers between devices, layer_backward(): lax.psum_scatter(for_sending(parts), 'tensor', scatter_dimension=0, tiled...  891 us
    all_gather x20, waiting for transfers between devices, layer_forward(): lax.all_gather(second.astype(jnp.bfloat16), 'tensor', axis=0, tiled=True)  575 us
    all_gather x20, waiting for transfers between devices, layer_forward(): lax.all_gather(first.astype(jnp.bfloat16), 'tensor', axis=0, tiled=True)  427 us
    dot_general x56, matrix products, matmul(): return jnp.dot(left, right, preferred_element_type=jnp.float32)  323 us
    psum x5, waiting for transfers between devices, backward_tick(): lax.psum((kv_first[0] + kv_second[0]).astype(jnp.bfloat16), 'tensor')  257 us
    unnamed x27, waiting for transfers between devices  244 us
    dot_general x50, matrix products, matmul_right(): lax.dot_general(left, right, (((1,), (1,)), ((), ())), preferred_element_...  244 us
  transfers between devices with their start and end apart: 119, of which 113 were waited for; matrix products, arithmetic and copies ran while one was open for 10% of the time, Pallas kernels for 0%

commit v1 on v0

v1 whole, which is shorter than its diff:
```python
import functools
import jax
import jax.numpy as jnp
from jax import lax
from jax.experimental import pallas as pl
from jax.experimental.pallas import tpu as pltpu
from jax.sharding import PartitionSpec as P

HD = 64
ROT = 16
EPS = 1e-05
LANES = 128
TILE = 256
ROWS = 256
VMEM_LIMIT = 56 * 2**20
ANY = pl.BlockSpec(memory_space=pl.ANY)
SMEM = pl.BlockSpec(memory_space=pltpu.SMEM)
VMEM = pl.BlockSpec(memory_space=pltpu.VMEM)
BF16, F32 = jnp.bfloat16, jnp.float32


def dot(left, right, dims=((1,), (0,))):
    return lax.dot_general(left, right, (dims, ((), ())), preferred_element_type=F32)


def dot_nt(left, right):
    return dot(left, right, ((1,), (1,)))


def turn(values, cosines, ahead, behind):
    return (
        values * cosines
        + pltpu.roll(values, LANES - ROT // 2, axis=1) * ahead
        + pltpu.roll(values, ROT // 2, axis=1) * behind
    )


def normalized(rows):
    centred = rows - jnp.mean(rows, axis=-1, keepdims=True)
    scale = lax.rsqrt(jnp.mean(centred * centred, axis=-1, keepdims=True) + EPS)
    return centred * scale, scale


def split_pair(block):
    low = lax.broadcasted_iota(jnp.int32, block.shape, 1) < HD
    zero = jnp.zeros_like(block)
    return jnp.where(low, block, zero), jnp.where(low, zero, block)


def visible(rows):
    key = lax.broadcasted_iota(jnp.int32, (rows, rows), 0)
    return key <= lax.broadcasted_iota(jnp.int32, (rows, rows), 1)


class Copies:
    def __init__(self, sems):
        self.sems, self.used, self.open = sems, 0, []

    def start(self, source, target):
        copy = pltpu.make_async_copy(source, target, self.sems.at[self.used])
        self.used += 1
        copy.start()
        return copy

    def later(self, source, target):
        self.open.append(self.start(source, target))

    def finish(self):
        for copy in self.open:
            copy.wait()
        self.open = []


FWD_STATE = ("x0", "x1", "h1a", "h1b", "h2a", "h2b", "qa", "qb", "oa", "ob", "aa", "ab", "ga", "gb", "la", "lb", "kd", "vd", "kt", "vt", "y")
BWD_STATE = ("dba", "dbb", "dua", "dub", "dqa", "dqb", "dkv", "dkw", "dvw", "acc", "gin")


def state_shapes(length, width, hidden):
    pairs = width // LANES
    row, ff = ((length, width), BF16), ((length, hidden), BF16)
    lse, wide, tall = ((pairs, 8, length), F32), ((length, LANES), BF16), ((HD, length), BF16)
    fwd = dict(x0=row, x1=((length, width), F32), h1a=row, h1b=row, h2a=row, h2b=row, qa=row, qb=row, oa=row, ob=row, aa=ff, ab=ff, ga=ff, gb=ff, la=lse, lb=lse, kd=wide, vd=wide, kt=tall, vt=tall, y=row)
    total = ((length, LANES), F32)
    bwd = dict(dba=row, dbb=row, dua=ff, dub=ff, dqa=row, dqb=row, dkv=wide, dkw=total, dvw=total, acc=((24, width), F32), gin=row)
    return fwd, bwd


def make_struct(item):
    return jax.ShapeDtypeStruct(*item)


def fwd_kernel(rows, chunks, fresh, *refs):
    n_state = len(FWD_STATE)
    sc, hop_in, seq_in, common, bq_m, bq_t, bi_m, bi_t, cos, ahead, behind, wkv = refs[:12]
    weights = refs[12:20]
    at = 20 if fresh else 20 + n_state
    st = dict(zip(FWD_STATE, refs[at : at + n_state]))
    hop_out = refs[at + n_state]
    (x_s, xf_s, h1_s, h2_s, q_s, o_s, a_s, g_s, l_s, kd_s, vd_s, kt_s, vt_s, vtc_s, wq_s, wo_s, wi_s, wh_s, sems, wsems) = refs[at + n_state + 1 :]
    width = xf_s.shape[1]
    half, hid = wq_s.shape[3], wi_s.shape[3]
    biases = ((bq_m, bi_m), (bq_t, bi_t))

    @pl.when(sc[0] == 1)
    def _():
        m = sc[1]
        place = pl.ds(pl.multiple_of(m * rows, rows), rows)
        copies, loads = Copies(sems), Copies(wsems)

        @pl.when(sc[2] == 1)
        def _():
            pltpu.make_async_copy(seq_in.at[place], x_s, sems.at[50]).start()

        @pl.when(sc[2] == 0)
        def _():
            pltpu.make_async_copy(hop_in, x_s, sems.at[50]).start()

        kd_in = copies.start(st["kd"], kd_s)
        vt_in = copies.start(st["vt"], vt_s)
        got = {}
        for j in range(2):
            for n, (name, buf) in enumerate((("q", wq_s), ("o", wo_s), ("i", wi_s), ("h", wh_s))):
                for k in range(2):
                    got[name, k, j] = loads.start(weights[2 * n + k].at[j], buf.at[k, j])
        pltpu.make_async_copy(hop_in, x_s, sems.at[50]).wait()
        xf_s[...] = x_s[...].astype(F32)
        copies.later(x_s, st["x0"].at[place])
        tables = (cos[place, :], ahead[place, :], behind[place, :])
        for j in range(2):
            for r in range(0, rows, 64):
                hat, _ = normalized(xf_s[r : r + 64, :])
                h1_s[j, r : r + 64, :] = (hat * common[2 * j : 2 * j + 1, :] + common[4 + 2 * j : 5 + 2 * j, :]).astype(BF16)
                h2_s[j, r : r + 64, :] = (hat * common[2 * j + 1 : 2 * j + 2, :] + common[5 + 2 * j : 6 + 2 * j, :]).astype(BF16)
            copies.later(h1_s.at[j], st["h1" + "ab"[j]].at[place])
            copies.later(h2_s.at[j], st["h2" + "ab"[j]].at[place])
            h1 = h1_s[j]
            if j == 0:
                kv = dot(h1, wkv[...]) + common[12:13, :TILE]
                keys, values = turn(kv[:, :LANES], *tables), kv[:, LANES:]
                kd_in.wait()
                vt_in.wait()
                kd_s[place, :] = keys.astype(BF16)
                vd_s[...] = values.astype(BF16)
                kt_s[...] = jnp.transpose(keys)[:HD].astype(BF16)
                vtc_s[...] = jnp.transpose(values)[:HD].astype(BF16)
                vt_s[:, place] = vtc_s[...]
                copies.later(kd_s.at[place], st["kd"].at[place])
                copies.later(vd_s, st["vd"].at[place])
                copies.later(kt_s, st["kt"].at[:, place])
                copies.later(vtc_s, st["vt"].at[:, place])
            for k in range(2):
                got["q", k, j].wait()
                query = dot(h1, wq_s[k, j]) + biases[k][0][j : j + 1, :]
                for b in range(half // LANES):
                    block = turn(query[:, b * LANES : (b + 1) * LANES], *tables) * HD**-0.5
                    col = k * half + b * LANES
                    q_s[j, :, col : col + LANES] = block.astype(BF16)
            copies.later(q_s.at[j], st["q" + "ab"[j]].at[place])

            def attend(before):
                def pair(i, _):
                    cols = pl.ds(pl.multiple_of(i * LANES, LANES), LANES)
                    outs = []
                    for n, query in enumerate(split_pair(q_s[j, :, cols])):
                        diag = dot_nt(kd_s[before : before + rows, :], query)
                        diag = jnp.where(visible(rows), diag, -1e30)
                        top = jnp.max(diag, axis=0, keepdims=True)
                        if before:
                            past = dot_nt(kd_s[:before, :], query)
                            top = jnp.maximum(top, jnp.max(past, axis=0, keepdims=True))
                        expo = jnp.exp(diag - top)
                        summed = jnp.sum(expo, axis=0, keepdims=True)
                        out = dot(vt_s[:, before : before + rows], expo.astype(BF16))
                        if before:
                            expo = jnp.exp(past - top)
                            summed += jnp.sum(expo, axis=0, keepdims=True)
                            out += dot(vt_s[:, :before], expo.astype(BF16))
                        outs.append(out / summed)
                        l_s[j, i, n : n + 1, :] = top + jnp.log(summed)
                    o_s[j, :, cols] = jnp.transpose(jnp.concatenate(outs, axis=0)).astype(BF16)
                    return 0

                lax.fori_loop(0, width // LANES, pair, 0)

            for c in range(chunks):
                pl.when(m == c)(functools.partial(attend, c * rows))
            copies.later(o_s.at[j], st["o" + "ab"[j]].at[place])
            copies.later(l_s.at[j], st["l" + "ab"[j]].at[:, :, place])
            for k in range(2):
                got["i", k, j].wait()
                for n in range(hid // TILE):
                    cols = slice(n * TILE, (n + 1) * TILE)
                    before = dot(h2_s[j], wi_s[k, j, :, cols]) + biases[k][1][j : j + 1, cols]
                    normal = 0.5 + 0.5 * lax.erf(before * 0.5**0.5)
                    col = k * hid + n * TILE
                    a_s[j, :, col : col + TILE] = (before * normal).astype(BF16)
                    slope = normal + before * (jnp.exp(-0.5 * before * before) * 0.3989422804014327)
                    g_s[j, :, col : col + TILE] = slope.astype(BF16)
            copies.later(a_s.at[j], st["a" + "ab"[j]].at[place])
            copies.later(g_s.at[j], st["g" + "ab"[j]].at[place])
            for k in range(2):
                got["o", k, j].wait()
                got["h", k, j].wait()
                branch = dot(o_s[j, :, k * half : (k + 1) * half], wo_s[k, j])
                branch += dot(a_s[j, :, k * hid : (k + 1) * hid], wh_s[k, j])
                if k == 0:
                    branch += common[8 + 2 * j : 9 + 2 * j, :] + common[9 + 2 * j : 10 + 2 * j, :]
                if j == 1 and k == 0:
                    x1_out.wait()
                xf_s[...] += branch
            if j == 0:
                x1_out = copies.start(xf_s, st["x1"].at[place])
        copies.finish()
        x_s[...] = xf_s[...].astype(BF16)
        copies.later(x_s, st["y"].at[place])
        copies.later(x_s, hop_out)
        copies.finish()


def fwd_call(rows, chunks, state, sc, hop, seq, params, weights):
    common, bq_m, bq_t, bi_m, bi_t, cos, ahead, behind, wkv = params
    length, width = seq.shape
    half, hid = weights[0].shape[2], weights[4].shape[2]
    hidden = 2 * hid
    shapes, _ = state_shapes(length, width, hidden)
    fresh = state is None
    n = len(FWD_STATE)
    scratch = [
        pltpu.VMEM((rows, width), BF16),
        pltpu.VMEM((rows, width), F32),
        pltpu.VMEM((2, rows, width), BF16),
        pltpu.VMEM((2, rows, width), BF16),
        pltpu.VMEM((2, rows, width), BF16),
        pltpu.VMEM((2, rows, width), BF16),
        pltpu.VMEM((2, rows, hidden), BF16),
        pltpu.VMEM((2, rows, hidden), BF16),
        pltpu.VMEM((2, width // LANES, 8, rows), F32),
        pltpu.VMEM((length, LANES), BF16),
        pltpu.VMEM((rows, LANES), BF16),
        pltpu.VMEM((HD, rows), BF16),
        pltpu.VMEM((HD, length), BF16),
        pltpu.VMEM((HD, rows), BF16),
        pltpu.VMEM((2, 2, width, half), BF16),
        pltpu.VMEM((2, 2, half, width), BF16),
        pltpu.VMEM((2, 2, width, hid), BF16),
        pltpu.VMEM((2, 2, hid, width), BF16),
        pltpu.SemaphoreType.DMA((51,)),
        pltpu.SemaphoreType.DMA((16,)),
    ]
    outs = pl.pallas_call(
        functools.partial(fwd_kernel, rows, chunks, fresh),
        out_shape=[make_struct(shapes[k]) for k in FWD_STATE] + [jax.ShapeDtypeStruct((rows, width), BF16)],
        in_specs=[SMEM, ANY, ANY] + [VMEM] * 9 + [ANY] * (8 + (0 if fresh else n)),
        out_specs=[ANY] * (n + 1),
        scratch_shapes=scratch,
        input_output_aliases={} if fresh else {20 + i: i for i in range(n)},
        compiler_params=pltpu.CompilerParams(vmem_limit_bytes=VMEM_LIMIT),
        name="section_forward",
    )(sc, hop, seq, common, bq_m, bq_t, bi_m, bi_t, cos, ahead, behind, wkv, *weights, *([] if fresh else state))
    return outs[:n], outs[n]


READ = ("x0", "x1", "qa", "qb", "oa", "ob", "ga", "gb", "la", "lb", "kd", "vd", "kt")


def bwd_kernel(rows, chunks, fresh, *refs):
    n_read, n_state = len(READ), len(BWD_STATE)
    sc, scale, hop_in, cot, common, cos, ahead, behind, wkv = refs[:9]
    weights = refs[9:17]
    rd = dict(zip(READ, refs[17 : 17 + n_read]))
    at = 17 + n_read + (0 if fresh else n_state)
    st = dict(zip(BWD_STATE, refs[at : at + n_state]))
    hop_out = refs[at + n_state]
    (in_s, dy_s, x0_s, x1_s, q_s, o_s, g_s, l_s, kd_s, vd_s, kt_s, db_s, do_s, du_s, dql_s, dkv_s, dkw_s, dvw_s, dh1_s, dh2_s, acc_s, wq_s, wo_s, wi_s, wh_s, sems, wsems) = refs[at + n_state + 1 :]
    width = dy_s.shape[1]
    half, hid = wq_s.shape[3], wi_s.shape[3]

    @pl.when(sc[0] == 1)
    def _():
        m = sc[1]
        place = pl.ds(pl.multiple_of(m * rows, rows), rows)
        copies, loads = Copies(sems), Copies(wsems)

        @pl.when(sc[2] == 1)
        def _():
            pltpu.make_async_copy(cot.at[place], in_s, sems.at[50]).start()

        @pl.when(sc[2] == 0)
        def _():
            pltpu.make_async_copy(hop_in, in_s, sems.at[50]).start()

        got = {}
        for j in (1, 0):
            s = "ab"[j]
            for n, (name, buf) in enumerate((("q", wq_s), ("o", wo_s), ("i", wi_s), ("h", wh_s))[::-1]):
                for k in range(2):
                    got[name, k, j] = loads.start(weights[2 * (3 - n) + k].at[j], buf.at[k, j])
            got["g", j] = copies.start(rd["g" + s].at[place], g_s.at[j])
            got["o", j] = copies.start(rd["o" + s].at[place], o_s.at[j])
            got["q", j] = copies.start(rd["q" + s].at[place], q_s.at[j])
            got["l", j] = copies.start(rd["l" + s].at[:, :, place], l_s.at[j])
            if j == 1:
                early = [copies.start(rd["kd"], kd_s), copies.start(rd["vd"], vd_s), copies.start(rd["kt"], kt_s)]
                got["x", 1] = copies.start(rd["x1"].at[place], x1_s)
            else:
                got["x", 0] = copies.start(rd["x0"].at[place], x0_s)

        @pl.when(m == chunks - 1)
        def _():
            dkw_s[...] = jnp.zeros_like(dkw_s)
            dvw_s[...] = jnp.zeros_like(dvw_s)
            acc_s[...] = jnp.zeros_like(acc_s)

        @pl.when(m < chunks - 1)
        def _():
            for i, (source, target) in enumerate(((st["dkw"], dkw_s), (st["dvw"], dvw_s), (st["acc"], acc_s))):
                pltpu.make_async_copy(source, target, sems.at[47 + i]).start()
            for i, (source, target) in enumerate(((st["dkw"], dkw_s), (st["dvw"], dvw_s), (st["acc"], acc_s))):
                pltpu.make_async_copy(source, target, sems.at[47 + i]).wait()

        pltpu.make_async_copy(hop_in, in_s, sems.at[50]).wait()
        dy_s[...] = in_s[...].astype(F32) * scale[0]
        tables = (cos[place, :], -ahead[place, :], -behind[place, :])
        for j in (1, 0):
            base = 10 * j
            grad = dy_s[...]
            db_s[j] = grad.astype(BF16)
            acc_s[base : base + 1, :] += jnp.sum(grad, axis=0, keepdims=True)
            copies.later(db_s.at[j], st["db" + "ab"[j]].at[place])
            got["g", j].wait()
            for k in range(2):
                got["h", k, j].wait()
                for n in range(hid // TILE):
                    slope_col = k * hid + n * TILE
                    back = dot_nt(db_s[j], wh_s[k, j, n * TILE : (n + 1) * TILE, :])
                    back = (back * g_s[j, :, slope_col : slope_col + TILE].astype(F32)).astype(BF16)
                    du_s[j, :, slope_col : slope_col + TILE] = back
                    row, col = base + 6 + slope_col // width, slope_col % width
                    acc_s[row : row + 1, col : col + TILE] += jnp.sum(back.astype(F32), axis=0, keepdims=True)
            copies.later(du_s.at[j], st["du" + "ab"[j]].at[place])
            for k in range(2):
                got["i", k, j].wait()
                part = dot_nt(du_s[j, :, k * hid : (k + 1) * hid], wi_s[k, j])
                dh2_s[...] = part if k == 0 else dh2_s[...] + part
            for k in range(2):
                got["o", k, j].wait()
                do_s[:, k * half : (k + 1) * half] = dot_nt(db_s[j], wo_s[k, j]).astype(BF16)
            for name in ("o", "q", "l"):
                got[name, j].wait()
            if j == 1:
                for copy in early:
                    copy.wait()

            def attend(before):
                def pair(i, _):
                    cols = pl.ds(pl.multiple_of(i * LANES, LANES), LANES)
                    out_grad = do_s[:, cols]
                    inner = jnp.transpose(out_grad.astype(F32) * o_s[j, :, cols].astype(F32))
                    queries, grads = split_pair(q_s[j, :, cols]), split_pair(out_grad)
                    back = []
                    spans = ((before, before + rows, True),) + (((0, before, False),) if before else ())
                    sums = {}
                    for n in range(2):
                        lse = l_s[j, i, n : n + 1, :]
                        mean = jnp.sum(inner[n * HD : (n + 1) * HD], axis=0, keepdims=True)
                        total = None
                        for low, high, masked in spans:
                            scores = dot_nt(kd_s[low:high, :], queries[n])
                            probs = jnp.exp(scores - lse)
                            if masked:
                                probs = jnp.where(visible(rows), probs, 0.0)
                            prob_grad = dot_nt(vd_s[low:high, :], grads[n])
                            score_grad = (probs * (prob_grad - mean)).astype(BF16)
                            key_part = dot(score_grad, queries[n])
                            value_part = dot(probs.astype(BF16), grads[n])
                            query_part = dot(kt_s[:, low:high], score_grad)
                            total = query_part if total is None else total + query_part
                            if n == 0:
                                sums[low] = (key_part, value_part)
                            else:
                                dkw_s[low:high, :] += sums[low][0] + key_part
                                dvw_s[low:high, :] += sums[low][1] + value_part
                        back.append(total * HD**-0.5)
                    turned = turn(jnp.transpose(jnp.concatenate(back, axis=0)), *tables)
                    dql_s[j, :, cols] = turned.astype(BF16)
                    return 0

                lax.fori_loop(0, width // LANES, pair, 0)

            for c in range(chunks):
                pl.when(m == c)(functools.partial(attend, c * rows))
            copies.later(dql_s.at[j], st["dq" + "ab"[j]].at[place])
            acc_s[base + 5 : base + 6, :] += jnp.sum(dql_s[j].astype(F32), axis=0, keepdims=True)
            for k in range(2):
                got["q", k, j].wait()
                part = dot_nt(dql_s[j, :, k * half : (k + 1) * half], wq_s[k, j])
                dh1_s[...] = part if k == 0 else dh1_s[...] + part
            if j == 0:
                key_grad, value_grad = dkw_s[place, :], dvw_s[place, :]
                key_grad = turn(key_grad + pltpu.roll(key_grad, HD, axis=1), *tables)
                value_grad = value_grad + pltpu.roll(value_grad, HD, axis=1)
                low = lax.broadcasted_iota(jnp.int32, key_grad.shape, 1) < HD
                both = jnp.where(low, key_grad, value_grad).astype(BF16)
                dkv_s[...] = both
                copies.later(dkv_s, st["dkv"].at[place])
                acc_s[20:21, :LANES] += jnp.sum(both.astype(F32), axis=0, keepdims=True)
                dh1_s[...] += dot_nt(both, wkv[...])
            got["x", j].wait()
            gain1, gain2 = common[2 * j : 2 * j + 1, :], common[2 * j + 1 : 2 * j + 2, :]
            totals = None
            for r in range(0, rows, 64):
                span = slice(r, r + 64)
                hat, spread = normalized((x1_s if j else x0_s)[span, :].astype(F32))
                first, second = dh1_s[span, :], dh2_s[span, :]
                parts = [jnp.sum(v, axis=0, keepdims=True) for v in (first * hat, first, second * hat, second)]
                totals = parts if totals is None else [a + b for a, b in zip(totals, parts)]
                inside = first * gain1 + second * gain2
                shift = jnp.mean(inside, axis=-1, keepdims=True)
                tilt = jnp.mean(inside * hat, axis=-1, keepdims=True)
                dy_s[span, :] += spread * (inside - shift - hat * tilt)
            for i, v in enumerate(totals):
                acc_s[base + 1 + i : base + 2 + i, :] += v
        in_s[...] = dy_s[...].astype(BF16)
        copies.later(in_s, st["gin"].at[place])
        copies.later(in_s, hop_out)
        copies.later(dkw_s, st["dkw"])
        copies.later(dvw_s, st["dvw"])
        copies.later(acc_s, st["acc"])
        copies.finish()


def bwd_call(rows, chunks, state, sc, scale, hop, cot, params, weights, fwd):
    common, cos, ahead, behind, wkv = params
    length, width = cot.shape
    half, hid = weights[0].shape[2], weights[4].shape[2]
    hidden = 2 * hid
    _, shapes = state_shapes(length, width, hidden)
    fresh = state is None
    n = len(BWD_STATE)
    saved = dict(zip(FWD_STATE, fwd))
    scratch = [
        pltpu.VMEM((rows, width), BF16),
        pltpu.VMEM((rows, width), F32),
        pltpu.VMEM((rows, width), BF16),
        pltpu.VMEM((rows, width), F32),
        pltpu.VMEM((2, rows, width), BF16),
        pltpu.VMEM((2, rows, width), BF16),
        pltpu.VMEM((2, rows, hidden), BF16),
        pltpu.VMEM((2, width // LANES, 8, rows), F32),
        pltpu.VMEM((length, LANES), BF16),
        pltpu.VMEM((length, LANES), BF16),
        pltpu.VMEM((HD, length), BF16),
        pltpu.VMEM((2, rows, width), BF16),
        pltpu.VMEM((rows, width), BF16),
        pltpu.VMEM((2, rows, hidden), BF16),
        pltpu.VMEM((2, rows, width), BF16),
        pltpu.VMEM((rows, LANES), BF16),
        pltpu.VMEM((length, LANES), F32),
        pltpu.VMEM((length, LANES), F32),
        pltpu.VMEM((rows, width), F32),
        pltpu.VMEM((rows, width), F32),
        pltpu.VMEM((24, width), F32),
        pltpu.VMEM((2, 2, width, half), BF16),
        pltpu.VMEM((2, 2, half, width), BF16),
        pltpu.VMEM((2, 2, width, hid), BF16),
        pltpu.VMEM((2, 2, hid, width), BF16),
        pltpu.SemaphoreType.DMA((51,)),
        pltpu.SemaphoreType.DMA((16,)),
    ]
    first_state = 17 + len(READ)
    outs = pl.pallas_call(
        functools.partial(bwd_kernel, rows, chunks, fresh),
        out_shape=[make_struct(shapes[k]) for k in BWD_STATE] + [jax.ShapeDtypeStruct((rows, width), BF16)],
        in_specs=[SMEM, SMEM, ANY, ANY] + [VMEM] * 5 + [ANY] * (8 + len(READ) + (0 if fresh else n)),
        out_specs=[ANY] * (n + 1),
        scratch_shapes=scratch,
        input_output_aliases={} if fresh else {first_state + i: i for i in range(n)},
        compiler_params=pltpu.CompilerParams(vmem_limit_bytes=VMEM_LIMIT),
        name="section_backward",
    )(sc, scale, hop, cot, common, cos, ahead, behind, wkv, *weights, *[saved[k] for k in READ], *([] if fresh else state))
    return outs[:n], outs[n]


def turn_tables(length):
    column = jnp.arange(LANES) % HD
    half = ROT // 2
    freq = jnp.power(10000.0, -2.0 * (column % half).astype(F32) / ROT)
    angle = jnp.arange(length).astype(F32)[:, None] * freq[None, :]
    cosines = jnp.where((column < ROT)[None, :], jnp.cos(angle), 1.0)
    sines = jnp.sin(angle)
    ahead = jnp.where((column < half)[None, :], -sines, 0.0)
    behind = jnp.where(((column >= half) & (column < ROT))[None, :], sines, 0.0)
    return cosines, ahead, behind


def stage_place(stage):
    across = stage // 2
    return across, (stage % 2 if across == 0 else 1 - stage % 2)


def device(across, core, tensor):
    return (2 * across + core) * 2 + tensor


PLANE = ("section", "tensor")
SWAP = [(0, 1), (1, 0), (2, 3), (3, 2)]


def plane_routes():
    fetch, ahead = [], []
    for stage in range(4):
        across, tensor = stage_place(stage)
        for core in range(2):
            fetch.append((device(across, stage % 2, core), device(across, core, tensor)))
            if stage < 3:
                after, turned = stage_place(stage + 1)
                ahead.append((device(across, core, tensor), device(after, core, turned)))
    return fetch, [(b, a) for a, b in fetch], ahead, [(b, a) for a, b in ahead]


FETCH, DELIVER, AHEAD, BEHIND = plane_routes()


def other_core(value):
    return lax.ppermute(value, "section", SWAP)


def added(left, right):
    return (left.astype(F32) + right.astype(F32)).astype(BF16)


def after(value, *others):
    return lax.optimization_barrier((value, *others))[0]


def summed_over_line(pieces, make):
    position = lax.axis_index("dp")
    at_end = (position == 0) | (position == 3)
    first, second, third, done = [], [], [], []
    for r in range(len(pieces) + 3):
        if r < len(pieces):
            term = make(pieces[r])
            ties = [chain[-1] for chain in (first[:-1], second[:-1], third[:-1]) if chain]
            if ties:
                term = after(term, *ties)
            first.append(added(term, lax.ppermute(term, "dp", [(0, 1), (3, 2)])))
        if 0 <= r - 1 < len(pieces):
            part = first[r - 1]
            second.append(added(part, lax.ppermute(part, "dp", [(1, 2), (2, 1)])))
        if 0 <= r - 2 < len(pieces):
            whole = second[r - 2]
            third.append(jnp.where(at_end, lax.ppermute(whole, "dp", [(1, 0), (2, 3)]), whole))
        if 0 <= r - 3 < len(pieces):
            done.append(lax.ppermute(third[r - 3], PLANE, DELIVER))
    return done


def local(
    inputs,
    cotangent,
    subset_ids,
    subset_weight,
    ln_gain,
    ln_bias,
    w_query,
    b_query,
    w_kv,
    b_kv,
    w_out,
    out_bias,
    w_in,
    b_in,
    w_hid_out,
):
    section, tensor = lax.axis_index("section"), lax.axis_index("tensor")
    across, core = section // 2, section % 2
    stage = 2 * across + jnp.where(across == 0, tensor, 1 - tensor)
    micro, part, width = inputs.shape
    length = part * lax.axis_size(PLANE)
    half, hid = w_query.shape[3], w_in.shape[3]
    chunks = length // ROWS
    ticks = chunks + 3

    mine = [lax.ppermute(w[0], PLANE, FETCH) for w in (w_query, w_out, w_in, w_hid_out)]
    small = jnp.concatenate([v.reshape(-1) for v in (ln_gain, ln_bias, out_bias, b_kv, b_query, b_in)]).reshape(-1, LANES)
    small = lax.ppermute(small, PLANE, FETCH)
    own_kv = lax.ppermute(w_kv[0], PLANE, FETCH)
    weights = [w for pair in zip(mine, [other_core(w) for w in mine]) for w in pair]
    flat, flat_other = small.reshape(-1), other_core(small).reshape(-1)
    edge = 12 * width + LANES
    bkv = flat[12 * width : edge]
    bkv = jnp.concatenate([bkv[:HD], bkv[:HD], bkv[HD:], bkv[HD:]])
    common = jnp.concatenate([flat[: 12 * width].reshape(12, width), jnp.pad(bkv, (0, width - TILE))[None], jnp.zeros((3, width), F32)])
    bq = [f[edge : edge + 2 * half].reshape(2, half) for f in (flat, flat_other)]
    bi = [f[edge + 2 * half :].reshape(2, hid) for f in (flat, flat_other)]
    wide_kv = jnp.concatenate([own_kv[:, :HD], own_kv[:, :HD], own_kv[:, HD:], own_kv[:, HD:]], axis=1)

    whole_in = lax.all_gather(inputs, PLANE, axis=1, tiled=True)
    whole_cot = lax.all_gather(cotangent, PLANE, axis=1, tiled=True)
    my_in = lax.dynamic_index_in_dim(whole_in, core, 0, keepdims=False)
    my_cot = lax.dynamic_index_in_dim(whole_cot, core, 0, keepdims=False)
    my_id = lax.dynamic_index_in_dim(subset_ids, core, 0, keepdims=False)
    matches = my_id == jnp.arange(subset_weight.shape[0], dtype=jnp.int32)
    weight = jnp.sum(jnp.where(matches, subset_weight, 0.0))
    is_first, is_last = stage == 0, stage == 3
    scale = jnp.where(is_last, weight, 1.0).reshape(1)

    tables = turn_tables(length)
    forward_params = (common, *bq, *bi, *tables, wide_kv)
    hop = jnp.zeros((ROWS, width), BF16)
    saved = None
    for tick in range(ticks):
        number = tick - stage
        valid = (number >= 0) & (number < chunks)
        sc = jnp.stack([valid.astype(jnp.int32), jnp.clip(number, 0, chunks - 1), is_first.astype(jnp.int32)])
        saved, hop = fwd_call(ROWS, chunks, saved, sc, hop, my_in, forward_params, weights)
        if tick < ticks - 1:
            hop = lax.ppermute(hop, PLANE, AHEAD)
    kept = dict(zip(FWD_STATE, saved))

    def spread(mine_only, here):
        rows = jnp.where(here, mine_only, jnp.zeros_like(mine_only))[None]
        canvas = jnp.where((jnp.arange(micro) == core)[:, None, None], rows, jnp.zeros_like(rows))
        return lax.psum_scatter(canvas, PLANE, scatter_dimension=1, tiled=True)

    final = spread(kept["y"], is_last)

    backward_params = (common, *tables, own_kv)
    back = None
    for tick in range(ticks):
        number = chunks - 1 - tick + (3 - stage)
        valid = (number >= 0) & (number < chunks)
        sc = jnp.stack([valid.astype(jnp.int32), jnp.clip(number, 0, chunks - 1), is_last.astype(jnp.int32)])
        back, hop = bwd_call(ROWS, chunks, back, sc, scale, hop, my_cot, backward_params, weights, saved)
        if tick < ticks - 1:
            hop = lax.ppermute(hop, PLANE, BEHIND)
    got = dict(zip(BWD_STATE, back))
    input_grad = spread(got["gin"], is_first).astype(F32)

    def product(left, left_cols, right, right_cols):
        return dot(left[:, left_cols], right[:, right_cols], ((0,), (0,))).astype(BF16)

    everything = slice(None)

    def term(piece):
        name, slot, start, size = piece
        s = "ab"[slot]
        both = []
        for k in range(2):
            if name == "h":
                at = k * hid + start
                both.append(product(kept["a" + s], slice(at, at + size), got["db" + s], everything))
            elif name == "i":
                at = k * hid + start
                both.append(product(kept["h2" + s], everything, got["du" + s], slice(at, at + size)))
            elif name == "o":
                at = k * half + start
                both.append(product(kept["o" + s], slice(at, at + size), got["db" + s], everything))
            elif name == "q":
                at = k * half + start
                both.append(product(kept["h1" + s], everything, got["dq" + s], slice(at, at + size)))
        if name == "kv":
            one = product(kept["h1a"], everything, got["dkv"], everything)
            return added(one, other_core(one))
        return added(both[0], other_core(both[1]))

    pieces = []
    for slot in (1, 0):
        pieces.append(("o", slot, 0, half))
        pieces += [("h", slot, at, hid // 2) for at in (0, hid // 2)]
        pieces += [("i", slot, at, hid // 2) for at in (0, hid // 2)]
        pieces.append(("q", slot, 0, half))
    pieces.append(("kv", 0, 0, 0))
    if lax.axis_size("dp") == 4:
        done = summed_over_line(pieces, term)
    else:
        done = [lax.ppermute(lax.psum(term(piece), "dp"), PLANE, DELIVER) for piece in pieces]
    done = dict(zip(pieces, done))

    def joined(name, size, axis):
        slots = []
        for slot in range(2):
            parts = [done[p].astype(F32) for p in pieces if p[:2] == (name, slot)]
            slots.append(jnp.concatenate(parts, axis=axis))
        return jnp.stack(slots)[None]

    acc = got["acc"]
    rows = []
    for slot in range(2):
        base = 10 * slot
        query, first, second = acc[base + 5], acc[base + 6 : base + 8], acc[base + 8 : base + 10]
        query = jnp.where(core == 0, query, jnp.roll(query, half))
        rows += [acc[base : base + 5], query[None]]
        rows += [jnp.where(core == 0, first, second), jnp.where(core == 0, second, first)]
    rows.append(acc[20:])
    acc = jnp.concatenate(rows)
    acc = acc + other_core(acc)
    acc = lax.ppermute(lax.psum(acc, "dp"), PLANE, DELIVER)

    def per_slot(pick):
        return jnp.stack([pick(0), pick(10)])[None]

    gain_grad = per_slot(lambda b: jnp.stack([acc[b + 1], acc[b + 3]]))
    bias_grad = per_slot(lambda b: jnp.stack([acc[b + 2], acc[b + 4]]))
    out_bias_grad = per_slot(lambda b: jnp.stack([acc[b], acc[b]]))
    bq_grad = per_slot(lambda b: lax.dynamic_slice_in_dim(acc[b + 5], tensor * half, half))
    bi_grad = per_slot(lambda b: lax.dynamic_slice_in_dim(acc[b + 6 : b + 10].reshape(-1), tensor * hid, hid))
    return (
        final,
        input_grad,
        gain_grad,
        bias_grad,
        joined("q", half, 1),
        bq_grad,
        done["kv", 0, 0, 0].astype(F32)[None],
        acc[20, : 2 * HD][None],
        joined("o", half, 0),
        out_bias_grad,
        joined("i", hid, 1),
        bi_grad,
        joined("h", hid, 0),
    )


def solution(mesh):
    assert mesh.shape["section"] == 4 and mesh.shape["tensor"] == 2
    rows = P("dp", PLANE, None)
    weights = (
        P("section", None, None, None),
        P("section", None, None, None),
        P("section", None, None, "tensor"),
        P("section", None, "tensor"),
        P("section", None, None),
        P("section", None),
        P("section", None, "tensor", None),
        P("section", None, None, None),
        P("section", None, None, "tensor"),
        P("section", None, "tensor"),
        P("section", None, "tensor", None),
    )
    return jax.shard_map(
        local,
        mesh=mesh,
        in_specs=(rows, rows, P("dp"), P(), *weights),
        out_specs=(rows, rows, *weights),
        check_vma=False,
    )
```

time: 6290 us -> 1410 us (0.22)
  waiting for transfers between devices: 4060 us -> 548 us
  other arithmetic: 702 us -> 77.6 us
  matrix products: 660 us -> 63.9 us
  local copies, waits for them, and re-layouts: 554 us -> 36.9 us
  Pallas kernels: 0 us -> 372 us
  starting transfers between devices: 35.7 us -> 278 us
  loops' own time: 127 us -> 0 us
  blocking collectives: 121 us -> 0 us
    reduce_scatter x40 -> x2, waiting for transfers between devices: 2030 us -> 0.02 us  [spread(): return lax.psum_scatter(canvas, PLANE, scatter_dimension=1, tiled=True)]
    all_gather x56 -> x2, waiting for transfers between devices: 1450 us -> 0.01 us  [the longest x1 0.01 us: local(): whole_in = lax.all_gather(inputs, PLANE, axis=1, tiled=True)]
    dot_general x140 -> x25, matrix products: 660 us -> 63.9 us  [dot(): lax.dot_general(left, right, (dims, ((), ())), preferred_element_type=F32)]
    ppermute x10 -> x90, waiting for transfers between devices: 60 us -> 548 us  [the longest x6 197 us: local(): hop = lax.ppermute(hop, PLANE, BEHIND)]
    pallas_call x0 -> x14, Pallas kernels: none -> 372 us  [the longest x7 194 us: bwd_call(): pl.pallas_call(functools.partial(bwd_kernel, rows, chunks, fresh), out_sh...]
    psum x5 -> x1, waiting for transfers between devices: 257 us -> 0.01 us  [local(): acc = lax.ppermute(lax.psum(acc, 'dp'), PLANE, DELIVER)]
    ppermute x10 -> x90, starting transfers between devices: 31.2 us -> 278 us  [the longest x13 82.9 us: summed_over_line(): first.append(added(term, lax.ppermute(term, 'dp', [(0, 1), (3, 2)])))]
    unnamed x27 -> x5, waiting for transfers between devices: 244 us -> 0.08 us
  transfers between devices with their start and end apart: 119 -> 95, of which waited for: 113 -> 39; matrix products, arithmetic and copies ran while one was open for 10% -> 11% of each run, Pallas kernels for 0% -> 12%
where the time goes in v1:
time: 1410 us; the launch traced here: 1390 us
  waiting for transfers between devices  548 us (39%)
  Pallas kernels  372 us (26%)
  starting transfers between devices  278 us (20%)
  other arithmetic  77.6 us (6%)
  matrix products  63.9 us (5%)
  local copies, waits for them, and re-layouts  36.9 us (3%)
  between operations  16.5 us (1%)
    ppermute x6, waiting for transfers between devices, local(): hop = lax.ppermute(hop, PLANE, BEHIND)  197 us
    pallas_call x7, Pallas kernels, bwd_call(): pl.pallas_call(functools.partial(bwd_kernel, rows, chunks, fresh), out_sh...  194 us
    pallas_call x7, Pallas kernels, fwd_call(): pl.pallas_call(functools.partial(fwd_kernel, rows, chunks, fresh), out_sh...  178 us
    ppermute x4, waiting for transfers between devices, local(): lax.ppermute(w[0], PLANE, FETCH)  117 us
    ppermute x13, waiting for transfers between devices, summed_over_line(): lax.ppermute(whole, 'dp', [(1, 0), (2, 3)])  94.5 us
    ppermute x13, starting transfers between devices, summed_over_line(): first.append(added(term, lax.ppermute(term, 'dp', [(0, 1), (3, 2)])))  82.9 us
    ppermute x13, waiting for transfers between devices, summed_over_line(): first.append(added(term, lax.ppermute(term, 'dp', [(0, 1), (3, 2)])))  76.3 us
    dot_general x25, matrix products, dot(): lax.dot_general(left, right, (dims, ((), ())), preferred_element_type=F32)  63.9 us
  transfers between devices with their start and end apart: 95, of which 39 were waited for; matrix products, arithmetic and copies ran while one was open for 11% of the time, Pallas kernels for 12%

profile of v1, /device:TPU:1, one launch (start us, length us, event | category | flops | bytes accessed | tf_op | source)
XLA Modules:
  0.0 1392.7 jit_solution(205140342406877451)
XLA Ops:
  7.2 4.5 collective-permute-start.9
  13.8 50.1 %collective-permute-done.9.refs_18_.refs_15_ = bf16[2,1536,768]{2,1,0:T(8,128)(2,1)} collective-permute-done((bf16[2,1536,768]{2,1,0:T(8,128)(2,1)}, bf16[2,1536,768]{2,1,0:T(8,128)(2,1)}, u32[]{:S(2)}, u32[]{:S(2)}) %collective-permute-start.9) | collective-permute-done | bytes 4718624 | tf_op jit(solution)/shard_map/ppermute | solution.py:584
  63.9 17.0 %collective-permute-start.10 = (bf16[2,1536,768]{2,1,0:T(8,128)(2,1)}, bf16[2,1536,768]{2,1,0:T(8,128)(2,1)}, u32[]{:S(2)}, u32[]{:S(2)}) collective-permute-start(bf16[2,1536,768]{2,1,0:T(8,128)(2,1)} %collective-permute-done.9.refs_18_.refs_15_), channel_id=1, source_target_pairs={{0,8},{8,0},{16,24},{24,16},{1,9},{9,1},{17,25},{25,17},{2,10},{10... | collective-permute-start | bytes 14155784 | tf_op jit(solution)/shard_map/ppermute | solution.py:525
  80.9 46.2 %collective-permute-done.7.refs_16_.refs_13_ = bf16[2,768,1536]{2,1,0:T(8,128)(2,1)} collective-permute-done((bf16[2,768,1536]{2,1,0:T(8,128)(2,1)}, bf16[2,768,1536]{2,1,0:T(8,128)(2,1)}, u32[]{:S(2)}, u32[]{:S(2)}) %collective-permute-start.7) | collective-permute-done | bytes 4718624 | tf_op jit(solution)/shard_map/ppermute | solution.py:584
  149.1 21.1 %collective-permute-done.5.refs_14_.refs_11_ = bf16[2,384,768]{2,1,0:T(8,128)(2,1)S(1)} collective-permute-done((bf16[2,384,768]{2,1,0:T(8,128)(2,1)}, bf16[2,384,768]{2,1,0:T(8,128)(2,1)S(1)}, u32[]{:S(2)}, u32[]{:S(2)}) %collective-permute-start.5) | collective-permute-done | bytes 1179680 | tf_op jit(solution)/shard_map/ppermute | solution.py:584
  192.9 32.5 %section_forward.7 = (bf16[1024,768]{1,0:T(8,128)(2,1)}, f32[1024,768]{1,0:T(8,128)}, bf16[1024,768]{1,0:T(8,128)(2,1)}, bf16[1024,768]{1,0:T(8,128)(2,1)}, bf16...) custom-call(s32[3]{0:T(128)} %fusion.114.refs_0_, ...), custom_call_target="tpu_custom_call" | custom-call | tf_op jit(solution)/shard_map/section_forward/pallas_call | solution.py:250
  227.4 8.1 collective-permute-done.11.refs_1_
  236.3 36.9 %section_forward.8 = (bf16[1024,768]{1,0:T(8,128)(2,1)}, f32[1024,768]{1,0:T(8,128)}, bf16[1024,768]{1,0:T(8,128)(2,1)}, bf16[1024,768]{1,0:T(8,128)(2,1)}, bf16...) custom-call(s32[3]{0:T(128)} %fusion.116.refs_0_, ...), custom_call_target="tpu_custom_call", output_to_operand_aliasing={{0}: (20, {}), {1}: (21, {}), {2}: (22, {}), {3}: (23, {}),... | custom-call | tf_op jit(solution)/shard_map/section_forward/pallas_call | solution.py:250
  275.3 7.7 collective-permute-done.12.refs_1_
  283.8 39.9 %section_forward.9 = (bf16[1024,768]{1,0:T(8,128)(2,1)}, f32[1024,768]{1,0:T(8,128)}, bf16[1024,768]{1,0:T(8,128)(2,1)}, bf16[1024,768]{1,0:T(8,128)(2,1)}, bf16...) custom-call(s32[3]{0:T(128)} %fusion.118.refs_0_, ...), custom_call_target="tpu_custom_call", output_to_operand_aliasing={{0}: (20, {}), {1}: (21, {}), {2}: (22, {}), {3}: (23, {}),... | custom-call | tf_op jit(solution)/shard_map/section_forward/pallas_call | solution.py:250
  325.6 7.1 collective-permute-done.13.refs_1_
  333.5 39.6 %section_forward.10 = (bf16[1024,768]{1,0:T(8,128)(2,1)}, f32[1024,768]{1,0:T(8,128)}, bf16[1024,768]{1,0:T(8,128)(2,1)}, bf16[1024,768]{1,0:T(8,128)(2,1)}, bf1...) custom-call(s32[3]{0:T(128)} %fusion.120.refs_0_, ...), custom_call_target="tpu_custom_call", output_to_operand_aliasing={{0}: (20, {}), {1}: (21, {}), {2}: (22, {}), {3}: (23, {}),... | custom-call | tf_op jit(solution)/shard_map/section_forward/pallas_call | solution.py:250
  373.1 4.4 collective-permute-start.14
  378.2 6.2 collective-permute-done.14.refs_1_
  385.2 10.3 section_forward.11
  395.5 33.2 %collective-permute-start.15 = (bf16[256,768]{1,0:T(8,128)(2,1)}, bf16[256,768]{1,0:T(8,128)(2,1)S(1)}, u32[]{:S(2)}, u32[]{:S(2)}) collective-permute-start(bf16[256,768]{1,0:T(8,128)(2,1)} %get-tuple-element.346), channel_id=1, source_target_pairs={{0,1},{8,9},{1,17},{9,25},{17,16},{25,24},{2,3},{10,11},{3,19},{11... | collective-permute-start | bytes 1179656 | tf_op jit(solution)/shard_map/ppermute | solution.py:618
  430.0 4.7 collective-permute-done.15.refs_1_
  435.4 10.6 section_forward.12
  456.6 8.2 section_forward.13
  464.8 13.6 section_backward.7
  480.3 35.8 %collective-permute-done.17.refs_2_ = bf16[256,768]{1,0:T(8,128)(2,1)S(1)} collective-permute-done((bf16[256,768]{1,0:T(8,128)(2,1)}, bf16[256,768]{1,0:T(8,128)(2,1)S(1)}, u32[]{:S(2)}, u32[]{:S(2)}) %collective-permute-start.17) | collective-permute-done | bytes 393248 | tf_op jit(solution)/shard_map/ppermute | solution.py:636
  516.8 8.3 section_backward.8
  527.1 6.8 collective-permute-done.18.refs_2_
  534.6 8.1 section_backward.9
  544.7 130.0 %collective-permute-done.19.refs_2_ = bf16[256,768]{1,0:T(8,128)(2,1)S(1)} collective-permute-done((bf16[256,768]{1,0:T(8,128)(2,1)}, bf16[256,768]{1,0:T(8,128)(2,1)S(1)}, u32[]{:S(2)}, u32[]{:S(2)}) %collective-permute-start.19) | collective-permute-done | bytes 393248 | tf_op jit(solution)/shard_map/ppermute | solution.py:636
  675.4 41.0 %section_backward.10 = (bf16[1024,768]{1,0:T(8,128)(2,1)}, bf16[1024,768]{1,0:T(8,128)(2,1)}, bf16[1024,3072]{1,0:T(8,128)(2,1)}, bf16[1024,3072]{1,0:T(8,128)(2...) custom-call(s32[3]{0:T(128)} %fusion.119.refs_0_, ...), custom_call_target="tpu_custom_call", output_to_operand_aliasing={{0}: (30, {}), {1}: (31, {}), {2}: (32, {}), {3}: (33, {}),... | custom-call | tf_op jit(solution)/shard_map/section_backward/pallas_call | solution.py:471
  718.3 11.9 collective-permute-done.20.refs_2_
  730.9 43.5 %section_backward.11 = (bf16[1024,768]{1,0:T(8,128)(2,1)}, bf16[1024,768]{1,0:T(8,128)(2,1)}, bf16[1024,3072]{1,0:T(8,128)(2,1)}, bf16[1024,3072]{1,0:T(8,128)(2...) custom-call(s32[3]{0:T(128)} %fusion.117.refs_0_, ...), custom_call_target="tpu_custom_call", output_to_operand_aliasing={{0}: (30, {}), {1}: (31, {}), {2}: (32, {}), {3}: (33, {}),... | custom-call | tf_op jit(solution)/shard_map/section_backward/pallas_call | solution.py:471
  776.9 6.2 collective-permute-done.21.refs_2_
  783.9 42.1 %section_backward.12 = (bf16[1024,768]{1,0:T(8,128)(2,1)}, bf16[1024,768]{1,0:T(8,128)(2,1)}, bf16[1024,3072]{1,0:T(8,128)(2,1)}, bf16[1024,3072]{1,0:T(8,128)(2...) custom-call(s32[3]{0:T(128)} %fusion.115.refs_0_, ...), custom_call_target="tpu_custom_call", output_to_operand_aliasing={{0}: (30, {}), {1}: (31, {}), {2}: (32, {}), {3}: (33, {}),... | custom-call | tf_op jit(solution)/shard_map/section_backward/pallas_call | solution.py:471
  828.6 6.2 collective-permute-done.22.refs_2_
  835.5 37.1 %section_backward.13 = (bf16[1024,768]{1,0:T(8,128)(2,1)}, bf16[1024,768]{1,0:T(8,128)(2,1)}, bf16[1024,3072]{1,0:T(8,128)(2,1)}, bf16[1024,3072]{1,0:T(8,128)(2...) custom-call(s32[3]{0:T(128)} %fusion.113.refs_0_, ...), custom_call_target="tpu_custom_call", output_to_operand_aliasing={{0}: (30, {}), {1}: (31, {}), {2}: (32, {}), {3}: (33, {}),... | custom-call | tf_op jit(solution)/shard_map/section_backward/pallas_call | solution.py:471
  887.4 10.1 collective-permute-start.32
  904.6 5.1 broadcast_select_fusion
  913.6 4.1 fusion.52
  968.4 8.1 collective-permute-done.33
  983.1 12.1 collective-permute-start.37
  996.5 5.2 collective-permute-done.31
  1009.8 6.8 collective-permute-done.43
  1018.9 8.1 collective-permute-done.37
  1030.9 9.0 collective-permute-start.44
  1041.0 11.3 collective-permute-done.35
  1058.3 19.2 %collective-permute-done.44 = bf16[768,768]{1,0:T(8,128)(2,1)S(1)} collective-permute-done((bf16[768,768]{1,0:T(8,128)(2,1)S(1)}, bf16[768,768]{1,0:T(8,128)(2,1)S(1)}, u32[]{:S(2)}, u32[]{:S(2)}) %collective-permute-start.44) | collective-permute-done | bytes 1179680 | tf_op jit(solution)/shard_map/ppermute | solution.py:546
  1081.4 6.8 collective-permute-start.41
  1090.1 15.7 %collective-permute-done.50 = bf16[768,768]{1,0:T(8,128)(2,1)S(1)} collective-permute-done((bf16[768,768]{1,0:T(8,128)(2,1)S(1)}, bf16[768,768]{1,0:T(8,128)(2,1)S(1)}, u32[]{:S(2)}, u32[]{:S(2)}) %collective-permute-start.50) | collective-permute-done | bytes 1179680 | tf_op jit(solution)/shard_map/ppermute | solution.py:552
  1110.9 20.2 %collective-permute-done.47 = bf16[768,768]{1,0:T(8,128)(2,1)S(1)} collective-permute-done((bf16[768,768]{1,0:T(8,128)(2,1)S(1)}, bf16[768,768]{1,0:T(8,128)(2,1)S(1)}, u32[]{:S(2)}, u32[]{:S(2)}) %collective-permute-start.47) | collective-permute-done | bytes 1179680 | tf_op jit(solution)/shard_map/ppermute | solution.py:552
  1134.7 4.1 collective-permute-start.26
  1141.6 14.7 %collective-permute-done.57 = bf16[768,768]{1,0:T(8,128)(2,1)S(1)} collective-permute-done((bf16[768,768]{1,0:T(8,128)(2,1)S(1)}, bf16[768,768]{1,0:T(8,128)(2,1)S(1)}, u32[]{:S(2)}, u32[]{:S(2)}) %collective-permute-start.57) | collective-permute-done | bytes 1179680 | tf_op jit(solution)/shard_map/ppermute | solution.py:552
  1158.8 4.3 collective-permute-start.58
  1175.1 10.8 collective-permute-done.58
  1185.9 5.1 collective-permute-start.55
  1198.0 6.8 collective-permute-start.89
  1211.8 4.5 collective-permute-start.70
  1217.9 8.4 collective-permute-start.77
  1237.8 5.6 collective-permute-start.62
  1247.8 6.6 collective-permute-done.62
  1256.5 4.8 collective-permute-start.66
  1268.4 7.8 collective-permute-done.72
  1277.6 25.9 %collective-permute-start.73 = (bf16[768,128]{1,0:T(8,128)(2,1)S(1)}, bf16[768,128]{1,0:T(8,128)(2,1)S(1)}, u32[]{:S(2)}, u32[]{:S(2)}) collective-permute-start(bf16[768,128]{1,0:T(8,128)(2,1)S(1)} %copy-done.30), channel_id=1, source_target_pairs={{0,2},{6,4},{1,3},{7,5},{8,10},{14,12},{9,11},{15,13},{16,18},{22,... | collective-permute-start | bytes 589832 | tf_op jit(solution)/shard_map/ppermute | solution.py:546
  1316.7 26.1 %collective-permute-done.75 = bf16[768,128]{1,0:T(8,128)(2,1)S(1)} collective-permute-done((bf16[768,128]{1,0:T(8,128)(2,1)S(1)}, bf16[768,128]{1,0:T(8,128)(2,1)S(1)}, u32[]{:S(2)}, u32[]{:S(2)}) %collective-permute-start.75) | collective-permute-done | bytes 196640 | tf_op jit(solution)/shard_map/ppermute | solution.py:552
  1350.5 5.6 collective-permute-done.76
  1360.5 4.4 fusion.1
  1368.7 12.6 collective-permute-done.83
  1381.5 4.4 fusion
  (440 shorter events, 292.7 us)
Async XLA Ops:
  7.2 181.8 %all-gather.3.cloned.1.call-start = ((), (), s32[]{:S(2)}) async-start(), calls=%async_computation.2 | async-start | bytes 3538944 | tf_op jit(solution)/shard_map/all_gather | solution.py:598
  7.2 56.7 %collective-permute-start.9 = (bf16[2,1536,768]{2,1,0:T(8,128)(2,1)}, bf16[2,1536,768]{2,1,0:T(8,128)(2,1)}, u32[]{:S(2)}, u32[]{:S(2)}) collective-permute-start(bf16[2,1536,768]{2,1,0:T(8,128)(2,1)} %bitcast.128), channel_id=1, source_target_pairs={{0,0},{1,8},{8,1},{9,9},{16,17},{17,25},{24,16},{25,24},{2,2},{3,1... | collective-permute-start | bytes 14155784 | tf_op jit(solution)/shard_map/ppermute | solution.py:584
  11.8 115.3 %collective-permute-start.7 = (bf16[2,768,1536]{2,1,0:T(8,128)(2,1)}, bf16[2,768,1536]{2,1,0:T(8,128)(2,1)}, u32[]{:S(2)}, u32[]{:S(2)}) collective-permute-start(bf16[2,768,1536]{2,1,0:T(8,128)(2,1)} %bitcast.129), channel_id=1, source_target_pairs={{0,0},{1,8},{8,1},{9,9},{16,17},{17,25},{24,16},{25,24},{2,2},{3,1... | collective-permute-start | bytes 14155784 | tf_op jit(solution)/shard_map/ppermute | solution.py:584
  13.7 439.4 %all-gather.5.cloned.1.call-start = ((), (), s32[]{:S(2)}) async-start(), calls=%async_computation.4 | async-start | bytes 3538944 | tf_op jit(solution)/shard_map/all_gather | solution.py:599
  63.9 127.8 %collective-permute-start.10 = (bf16[2,1536,768]{2,1,0:T(8,128)(2,1)}, bf16[2,1536,768]{2,1,0:T(8,128)(2,1)}, u32[]{:S(2)}, u32[]{:S(2)}) collective-permute-start(bf16[2,1536,768]{2,1,0:T(8,128)(2,1)} %collective-permute-done.9.refs_18_.refs_15_), channel_id=1, source_target_pairs={{0,8},{8,0},{16,24},{24,16},{1,9},{9,1},{17,25},{25,17},{2,10},{10... | collective-permute-start | bytes 14155784 | tf_op jit(solution)/shard_map/ppermute | solution.py:525
  127.1 64.6 %collective-permute-start.8 = (bf16[2,768,1536]{2,1,0:T(8,128)(2,1)}, bf16[2,768,1536]{2,1,0:T(8,128)(2,1)}, u32[]{:S(2)}, u32[]{:S(2)}) collective-permute-start(bf16[2,768,1536]{2,1,0:T(8,128)(2,1)} %collective-permute-done.7.refs_16_.refs_13_), channel_id=1, source_target_pairs={{0,8},{8,0},{16,24},{24,16},{1,9},{9,1},{17,25},{25,17},{2,10},{10... | collective-permute-start | bytes 14155784 | tf_op jit(solution)/shard_map/ppermute | solution.py:525
  127.1 823.7 %all-reduce.3.cloned.1.call-start = ((), (), s32[]{:S(2)}) async-start(), calls=%async_computation.6 | async-start | bytes 147456 | tf_op jit(solution)/shard_map/psum | solution.py:698
  130.8 39.4 %collective-permute-start.5 = (bf16[2,384,768]{2,1,0:T(8,128)(2,1)}, bf16[2,384,768]{2,1,0:T(8,128)(2,1)S(1)}, u32[]{:S(2)}, u32[]{:S(2)}) collective-permute-start(bf16[2,384,768]{2,1,0:T(8,128)(2,1)} %bitcast.131), channel_id=1, source_target_pairs={{0,0},{1,8},{8,1},{9,9},{16,17},{17,25},{24,16},{25,24},{2,2},{3,1... | collective-permute-start | bytes 3538952 | tf_op jit(solution)/shard_map/ppermute | solution.py:584
  142.1 29.4 %collective-permute-start = (f32[103,128]{1,0:T(8,128)}, f32[103,128]{1,0:T(8,128)}, u32[]{:S(2)}, u32[]{:S(2)}) collective-permute-start(f32[103,128]{1,0:T(8,128)} %bitcast.17), channel_id=1, source_target_pairs={{0,0},{1,8},{8,1},{9,9},{16,17},{17,25},{24,16},{25,24},{2,2},{3,1... | collective-permute-start | bytes 158216 | tf_op jit(solution)/shard_map/ppermute | solution.py:586
  149.1 42.6 %collective-permute-start.4 = (bf16[2,768,384]{2,1,0:T(8,128)(2,1)S(1)}, bf16[2,768,384]{2,1,0:T(8,128)(2,1)S(1)}, u32[]{:S(2)}, u32[]{:S(2)}) collective-permute-start(bf16[2,768,384]{2,1,0:T(8,128)(2,1)S(1)} %collective-permute-done.3.refs_12_.refs_9_), channel_id=1, source_target_pairs={{0,8},{8,0},{16,24},{24,16},{1,9},{9,1},{17,25},{25,17},{2,10},{10... | collective-permute-start | bytes 3538952 | tf_op jit(solution)/shard_map/ppermute | solution.py:525
  395.5 39.1 %collective-permute-start.15 = (bf16[256,768]{1,0:T(8,128)(2,1)}, bf16[256,768]{1,0:T(8,128)(2,1)S(1)}, u32[]{:S(2)}, u32[]{:S(2)}) collective-permute-start(bf16[256,768]{1,0:T(8,128)(2,1)} %get-tuple-element.346), channel_id=1, source_target_pairs={{0,1},{8,9},{1,17},{9,25},{17,16},{25,24},{2,3},{10,11},{3,19},{11... | collective-permute-start | bytes 1179656 | tf_op jit(solution)/shard_map/ppermute | solution.py:618
  478.4 37.7 %collective-permute-start.17 = (bf16[256,768]{1,0:T(8,128)(2,1)}, bf16[256,768]{1,0:T(8,128)(2,1)S(1)}, u32[]{:S(2)}, u32[]{:S(2)}) collective-permute-start(bf16[256,768]{1,0:T(8,128)(2,1)} %get-tuple-element.405), channel_id=1, source_target_pairs={{1,0},{9,8},{17,1},{25,9},{16,17},{24,25},{3,2},{11,10},{19,3},{27... | collective-permute-start | bytes 1179656 | tf_op jit(solution)/shard_map/ppermute | solution.py:636
  542.8 131.8 %collective-permute-start.19 = (bf16[256,768]{1,0:T(8,128)(2,1)}, bf16[256,768]{1,0:T(8,128)(2,1)S(1)}, u32[]{:S(2)}, u32[]{:S(2)}) collective-permute-start(bf16[256,768]{1,0:T(8,128)(2,1)} %get-tuple-element.429), channel_id=1, source_target_pairs={{1,0},{9,8},{17,1},{25,9},{16,17},{24,25},{3,2},{11,10},{19,3},{27... | collective-permute-start | bytes 1179656 | tf_op jit(solution)/shard_map/ppermute | solution.py:636
  887.4 71.3 %collective-permute-start.32 = (bf16[384,768]{1,0:T(8,128)(2,1)}, bf16[384,768]{1,0:T(8,128)(2,1)}, u32[]{:S(2)}, u32[]{:S(2)}) collective-permute-start(bf16[384,768]{1,0:T(8,128)(2,1)} %convolution_convert_fusion.2), channel_id=1, source_target_pairs={{0,8},{8,0},{16,24},{24,16},{1,9},{9,1},{17,25},{25,17},{2,10},{10... | collective-permute-start | bytes 1769480 | tf_op jit(solution)/shard_map/ppermute | solution.py:525
  897.5 107.2 %collective-permute-start.42 = (bf16[768,768]{1,0:T(8,128)(2,1)}, bf16[768,768]{1,0:T(8,128)(2,1)}, u32[]{:S(2)}, u32[]{:S(2)}) collective-permute-start(bf16[768,768]{1,0:T(8,128)(2,1)} %fusion.67), channel_id=1, source_target_pairs={{0,8},{8,0},{16,24},{24,16},{1,9},{9,1},{17,25},{25,17},{2,10},{10... | collective-permute-start | bytes 3538952 | tf_op jit(solution)/shard_map/ppermute | solution.py:525
  897.5 66.8 %collective-permute-start.30 = (bf16[768,768]{1,0:T(8,128)(2,1)}, bf16[768,768]{1,0:T(8,128)(2,1)}, u32[]{:S(2)}, u32[]{:S(2)}) collective-permute-start(bf16[768,768]{1,0:T(8,128)(2,1)} %fusion.55), channel_id=1, source_target_pairs={{0,8},{8,0},{16,24},{24,16},{1,9},{9,1},{17,25},{25,17},{2,10},{10... | collective-permute-start | bytes 3538952 | tf_op jit(solution)/shard_map/ppermute | solution.py:525
  898.0 80.9 %collective-permute-start.36 = (bf16[768,768]{1,0:T(8,128)(2,1)}, bf16[768,768]{1,0:T(8,128)(2,1)}, u32[]{:S(2)}, u32[]{:S(2)}) collective-permute-start(bf16[768,768]{1,0:T(8,128)(2,1)} %fusion.61), channel_id=1, source_target_pairs={{0,8},{8,0},{16,24},{24,16},{1,9},{9,1},{17,25},{25,17},{2,10},{10... | collective-permute-start | bytes 3538952 | tf_op jit(solution)/shard_map/ppermute | solution.py:525
  903.7 47.1 %collective-permute-start.67 = (bf16[768,128]{1,0:T(8,128)(2,1)S(1)}, bf16[768,128]{1,0:T(8,128)(2,1)}, u32[]{:S(2)}, u32[]{:S(2)}) collective-permute-start(bf16[768,128]{1,0:T(8,128)(2,1)S(1)} %convolution_convert_fusion.8), channel_id=1, source_target_pairs={{0,8},{8,0},{16,24},{24,16},{1,9},{9,1},{17,25},{25,17},{2,10},{10... | collective-permute-start | bytes 589832 | tf_op jit(solution)/shard_map/ppermute | solution.py:525
  904.5 291.5 %reduce-scatter.5.cloned.1.call-start = ((), (), s32[]{:S(2)}) async-start(), calls=%async_computation.5 | async-start | bytes 3538944 | tf_op jit(solution)/shard_map/reduce_scatter | solution.py:624
  909.8 476.1 %reduce-scatter.3.cloned.1.call-start = ((), (), s32[]{:S(2)}) async-start(), calls=%async_computation.3 | async-start | bytes 3538944 | tf_op jit(solution)/shard_map/reduce_scatter | solution.py:624
  956.7 177.9 %collective-permute-start.56 = (bf16[768,768]{1,0:T(8,128)(2,1)}, bf16[768,768]{1,0:T(8,128)(2,1)}, u32[]{:S(2)}, u32[]{:S(2)}) collective-permute-start(bf16[768,768]{1,0:T(8,128)(2,1)} %fusion.73), channel_id=1, source_target_pairs={{0,8},{8,0},{16,24},{24,16},{1,9},{9,1},{17,25},{25,17},{2,10},{10... | collective-permute-start | bytes 3538952 | tf_op jit(solution)/shard_map/ppermute | solution.py:525
  966.0 35.7 %collective-permute-start.31 = (bf16[768,768]{1,0:T(8,128)(2,1)S(1)}, bf16[768,768]{1,0:T(8,128)(2,1)}, u32[]{:S(2)}, u32[]{:S(2)}) collective-permute-start(bf16[768,768]{1,0:T(8,128)(2,1)S(1)} %add_convert_fusion.20), channel_id=1, source_target_pairs={{0,2},{6,4},{1,3},{7,5},{8,10},{14,12},{9,11},{15,13},{16,18},{22,... | collective-permute-start | bytes 3538952 | tf_op jit(solution)/shard_map/ppermute | solution.py:546
  978.9 28.3 %collective-permute-start.29 = (bf16[768,768]{1,0:T(8,128)(2,1)}, bf16[768,768]{1,0:T(8,128)(2,1)S(1)}, u32[]{:S(2)}, u32[]{:S(2)}) collective-permute-start(bf16[768,768]{1,0:T(8,128)(2,1)} %fusion.49), channel_id=1, source_target_pairs={{0,8},{8,0},{16,24},{24,16},{1,9},{9,1},{17,25},{25,17},{2,10},{10... | collective-permute-start | bytes 3538952 | tf_op jit(solution)/shard_map/ppermute | solution.py:525
  983.1 43.9 %collective-permute-start.37 = (bf16[768,768]{1,0:T(8,128)(2,1)S(1)}, bf16[768,768]{1,0:T(8,128)(2,1)S(1)}, u32[]{:S(2)}, u32[]{:S(2)}) collective-permute-start(bf16[768,768]{1,0:T(8,128)(2,1)S(1)} %add_convert_fusion.17), channel_id=1, source_target_pairs={{0,2},{6,4},{1,3},{7,5},{8,10},{14,12},{9,11},{15,13},{16,18},{22,... | collective-permute-start | bytes 3538952 | tf_op jit(solution)/shard_map/ppermute | solution.py:546
  1007.2 46.7 %collective-permute-start.49 = (bf16[384,768]{1,0:T(8,128)(2,1)S(1)}, bf16[384,768]{1,0:T(8,128)(2,1)S(1)}, u32[]{:S(2)}, u32[]{:S(2)}) collective-permute-start(bf16[384,768]{1,0:T(8,128)(2,1)S(1)} %copy-done.49), channel_id=1, source_target_pairs={{0,8},{8,0},{16,24},{24,16},{1,9},{9,1},{17,25},{25,17},{2,10},{10... | collective-permute-start | bytes 1769480 | tf_op jit(solution)/shard_map/ppermute | solution.py:525
  1016.7 35.6 %collective-permute-start.35 = (bf16[768,768]{1,0:T(8,128)(2,1)S(1)}, bf16[768,768]{1,0:T(8,128)(2,1)S(1)}, u32[]{:S(2)}, u32[]{:S(2)}) collective-permute-start(bf16[768,768]{1,0:T(8,128)(2,1)S(1)} %add_convert_fusion.21), channel_id=1, source_target_pairs={{0,2},{6,4},{1,3},{7,5},{8,10},{14,12},{9,11},{15,13},{16,18},{22,... | collective-permute-start | bytes 3538952 | tf_op jit(solution)/shard_map/ppermute | solution.py:546
  1029.6 26.0 %collective-permute-start.38 = (bf16[768,768]{1,0:T(8,128)(2,1)S(1)}, bf16[768,768]{1,0:T(8,128)(2,1)S(1)}, u32[]{:S(2)}, u32[]{:S(2)}) collective-permute-start(bf16[768,768]{1,0:T(8,128)(2,1)S(1)} %add_convert_fusion.16), channel_id=1, source_target_pairs={{2,4},{4,2},{3,5},{5,3},{10,12},{12,10},{11,13},{13,11},{18,20},{2... | collective-permute-start | bytes 3538952 | tf_op jit(solution)/shard_map/ppermute | solution.py:549
  1030.9 46.6 %collective-permute-start.44 = (bf16[768,768]{1,0:T(8,128)(2,1)S(1)}, bf16[768,768]{1,0:T(8,128)(2,1)S(1)}, u32[]{:S(2)}, u32[]{:S(2)}) collective-permute-start(bf16[768,768]{1,0:T(8,128)(2,1)S(1)} %add_convert_fusion.13), channel_id=1, source_target_pairs={{0,2},{6,4},{1,3},{7,5},{8,10},{14,12},{9,11},{15,13},{16,18},{22,... | collective-permute-start | bytes 3538952 | tf_op jit(solution)/shard_map/ppermute | solution.py:546
  1052.3 27.3 %collective-permute-start.40 = (bf16[768,768]{1,0:T(8,128)(2,1)S(1)}, bf16[768,768]{1,0:T(8,128)(2,1)S(1)}, u32[]{:S(2)}, u32[]{:S(2)}) collective-permute-start(bf16[768,768]{1,0:T(8,128)(2,1)S(1)} %add_convert_fusion.14), channel_id=1, source_target_pairs={{2,0},{4,6},{3,1},{5,7},{10,8},{12,14},{11,9},{13,15},{18,16},{20,... | collective-permute-start | bytes 3538952 | tf_op jit(solution)/shard_map/ppermute | solution.py:552
  1053.9 27.5 %collective-permute-start.46 = (bf16[768,768]{1,0:T(8,128)(2,1)S(1)}, bf16[768,768]{1,0:T(8,128)(2,1)S(1)}, u32[]{:S(2)}, u32[]{:S(2)}) collective-permute-start(bf16[768,768]{1,0:T(8,128)(2,1)S(1)} %add_convert_fusion.18), channel_id=1, source_target_pairs={{2,4},{4,2},{3,5},{5,3},{10,12},{12,10},{11,13},{13,11},{18,20},{2... | collective-permute-start | bytes 3538952 | tf_op jit(solution)/shard_map/ppermute | solution.py:549
  1055.6 32.9 %collective-permute-start.27 = (bf16[768,768]{1,0:T(8,128)(2,1)S(1)}, bf16[768,768]{1,0:T(8,128)(2,1)S(1)}, u32[]{:S(2)}, u32[]{:S(2)}) collective-permute-start(bf16[768,768]{1,0:T(8,128)(2,1)S(1)} %copy-done.47), channel_id=1, source_target_pairs={{0,8},{8,0},{16,24},{24,16},{1,9},{9,1},{17,25},{25,17},{2,10},{10... | collective-permute-start | bytes 3538952 | tf_op jit(solution)/shard_map/ppermute | solution.py:525
  1077.6 28.2 %collective-permute-start.50 = (bf16[768,768]{1,0:T(8,128)(2,1)S(1)}, bf16[768,768]{1,0:T(8,128)(2,1)S(1)}, u32[]{:S(2)}, u32[]{:S(2)}) collective-permute-start(bf16[768,768]{1,0:T(8,128)(2,1)S(1)} %add_convert_fusion.15), channel_id=1, source_target_pairs={{2,0},{4,6},{3,1},{5,7},{10,8},{12,14},{11,9},{13,15},{18,16},{20,... | collective-permute-start | bytes 3538952 | tf_op jit(solution)/shard_map/ppermute | solution.py:552
  1079.5 29.6 %collective-permute-start.45 = (bf16[768,768]{1,0:T(8,128)(2,1)S(1)}, bf16[768,768]{1,0:T(8,128)(2,1)S(1)}, u32[]{:S(2)}, u32[]{:S(2)}) collective-permute-start(bf16[768,768]{1,0:T(8,128)(2,1)S(1)} %add_convert_fusion.12), channel_id=1, source_target_pairs={{2,4},{4,2},{3,5},{5,3},{10,12},{12,10},{11,13},{13,11},{18,20},{2... | collective-permute-start | bytes 3538952 | tf_op jit(solution)/shard_map/ppermute | solution.py:549
  1081.4 26.8 %collective-permute-start.41 = (bf16[768,384]{1,0:T(8,128)(2,1)S(1)}, bf16[768,384]{1,0:T(8,128)(2,1)S(1)}, u32[]{:S(2)}, u32[]{:S(2)}) collective-permute-start(bf16[768,384]{1,0:T(8,128)(2,1)S(1)} %fusion.90), channel_id=1, source_target_pairs={{0,2},{6,4},{1,3},{7,5},{8,10},{14,12},{9,11},{15,13},{16,18},{22,... | collective-permute-start | bytes 1769480 | tf_op jit(solution)/shard_map/ppermute | solution.py:546
  1088.5 42.6 %collective-permute-start.47 = (bf16[768,768]{1,0:T(8,128)(2,1)S(1)}, bf16[768,768]{1,0:T(8,128)(2,1)S(1)}, u32[]{:S(2)}, u32[]{:S(2)}) collective-permute-start(bf16[768,768]{1,0:T(8,128)(2,1)S(1)} %add_convert_fusion.10), channel_id=1, source_target_pairs={{2,0},{4,6},{3,1},{5,7},{10,8},{12,14},{11,9},{13,15},{18,16},{20,... | collective-permute-start | bytes 3538952 | tf_op jit(solution)/shard_map/ppermute | solution.py:552
  1106.9 33.5 %collective-permute-start.51 = (bf16[384,768]{1,0:T(8,128)(2,1)S(1)}, bf16[384,768]{1,0:T(8,128)(2,1)S(1)}, u32[]{:S(2)}, u32[]{:S(2)}) collective-permute-start(bf16[384,768]{1,0:T(8,128)(2,1)S(1)} %fusion.84), channel_id=1, source_target_pairs={{0,2},{6,4},{1,3},{7,5},{8,10},{14,12},{9,11},{15,13},{16,18},{22,... | collective-permute-start | bytes 1769480 | tf_op jit(solution)/shard_map/ppermute | solution.py:546
  1108.4 32.3 %collective-permute-start.53 = (bf16[768,384]{1,0:T(8,128)(2,1)S(1)}, bf16[768,384]{1,0:T(8,128)(2,1)S(1)}, u32[]{:S(2)}, u32[]{:S(2)}) collective-permute-start(bf16[768,384]{1,0:T(8,128)(2,1)S(1)} %add_convert_fusion.29), channel_id=1, source_target_pairs={{2,4},{4,2},{3,5},{5,3},{10,12},{12,10},{11,13},{13,11},{18,20},{2... | collective-permute-start | bytes 1769480 | tf_op jit(solution)/shard_map/ppermute | solution.py:549
  1109.5 46.9 %collective-permute-start.57 = (bf16[768,768]{1,0:T(8,128)(2,1)S(1)}, bf16[768,768]{1,0:T(8,128)(2,1)S(1)}, u32[]{:S(2)}, u32[]{:S(2)}) collective-permute-start(bf16[768,768]{1,0:T(8,128)(2,1)S(1)} %add_convert_fusion.11), channel_id=1, source_target_pairs={{2,0},{4,6},{3,1},{5,7},{10,8},{12,14},{11,9},{13,15},{18,16},{20,... | collective-permute-start | bytes 3538952 | tf_op jit(solution)/shard_map/ppermute | solution.py:552
  1132.2 26.6 %collective-permute-start.48 = (bf16[768,768]{1,0:T(8,128)(2,1)S(1)}, bf16[768,768]{1,0:T(8,128)(2,1)S(1)}, u32[]{:S(2)}, u32[]{:S(2)}) collective-permute-start(bf16[768,768]{1,0:T(8,128)(2,1)S(1)} %add_convert_fusion.22), channel_id=1, source_target_pairs={{0,2},{6,4},{1,3},{7,5},{8,10},{14,12},{9,11},{15,13},{16,18},{22,... | collective-permute-start | bytes 3538952 | tf_op jit(solution)/shard_map/ppermute | solution.py:546
  1134.7 31.6 %collective-permute-start.26 = (bf16[768,768]{1,0:T(8,128)(2,1)S(1)}, bf16[768,768]{1,0:T(8,128)(2,1)S(1)}, u32[]{:S(2)}, u32[]{:S(2)}) collective-permute-start(bf16[768,768]{1,0:T(8,128)(2,1)S(1)} %copy-done.46), channel_id=1, source_target_pairs={{0,8},{8,0},{16,24},{24,16},{1,9},{9,1},{17,25},{25,17},{2,10},{10... | collective-permute-start | bytes 3538952 | tf_op jit(solution)/shard_map/ppermute | solution.py:525
  1140.7 28.6 %collective-permute-start.52 = (bf16[384,768]{1,0:T(8,128)(2,1)S(1)}, bf16[384,768]{1,0:T(8,128)(2,1)S(1)}, u32[]{:S(2)}, u32[]{:S(2)}) collective-permute-start(bf16[384,768]{1,0:T(8,128)(2,1)S(1)} %add_convert_fusion.28), channel_id=1, source_target_pairs={{2,4},{4,2},{3,5},{5,3},{10,12},{12,10},{11,13},{13,11},{18,20},{2... | collective-permute-start | bytes 1769480 | tf_op jit(solution)/shard_map/ppermute | solution.py:549
  1158.8 27.1 %collective-permute-start.58 = (bf16[768,768]{1,0:T(8,128)(2,1)S(1)}, bf16[768,768]{1,0:T(8,128)(2,1)S(1)}, u32[]{:S(2)}, u32[]{:S(2)}) collective-permute-start(bf16[768,768]{1,0:T(8,128)(2,1)S(1)} %add_convert_fusion.7), channel_id=1, source_target_pairs={{0,2},{6,4},{1,3},{7,5},{8,10},{14,12},{9,11},{15,13},{16,18},{22,... | collective-permute-start | bytes 3538952 | tf_op jit(solution)/shard_map/ppermute | solution.py:546
  1163.5 27.8 %collective-permute-start.60 = (bf16[768,768]{1,0:T(8,128)(2,1)S(1)}, bf16[768,768]{1,0:T(8,128)(2,1)S(1)}, u32[]{:S(2)}, u32[]{:S(2)}) collective-permute-start(bf16[768,768]{1,0:T(8,128)(2,1)S(1)} %add_convert_fusion.9), channel_id=1, source_target_pairs={{2,4},{4,2},{3,5},{5,3},{10,12},{12,10},{11,13},{13,11},{18,20},{2... | collective-permute-start | bytes 3538952 | tf_op jit(solution)/shard_map/ppermute | solution.py:549
  1166.3 28.1 %collective-permute-start.68 = (bf16[768,768]{1,0:T(8,128)(2,1)S(1)}, bf16[768,768]{1,0:T(8,128)(2,1)S(1)}, u32[]{:S(2)}, u32[]{:S(2)}) collective-permute-start(bf16[768,768]{1,0:T(8,128)(2,1)S(1)} %copy-done.45), channel_id=1, source_target_pairs={{0,8},{8,0},{16,24},{24,16},{1,9},{9,1},{17,25},{25,17},{2,10},{10... | collective-permute-start | bytes 3538952 | tf_op jit(solution)/shard_map/ppermute | solution.py:525
  1169.3 28.7 %collective-permute-start.78 = (bf16[384,768]{1,0:T(8,128)(2,1)}, bf16[384,768]{1,0:T(8,128)(2,1)}, u32[]{:S(2)}, u32[]{:S(2)}) collective-permute-start(bf16[384,768]{1,0:T(8,128)(2,1)} %broadcast_select_fusion.13), channel_id=1, source_target_pairs={{0,0},{8,1},{1,8},{9,9},{17,16},{25,17},{16,24},{24,25},{2,2},{10,... | collective-permute-start | bytes 1769480 | tf_op jit(solution)/shard_map/ppermute | solution.py:554
  1172.9 31.9 %collective-permute-start.69 = (bf16[384,768]{1,0:T(8,128)(2,1)}, bf16[384,768]{1,0:T(8,128)(2,1)}, u32[]{:S(2)}, u32[]{:S(2)}) collective-permute-start(bf16[384,768]{1,0:T(8,128)(2,1)} %add_convert_fusion.27), channel_id=1, source_target_pairs={{2,0},{4,6},{3,1},{5,7},{10,8},{12,14},{11,9},{13,15},{18,16},{20,... | collective-permute-start | bytes 1769480 | tf_op jit(solution)/shard_map/ppermute | solution.py:552
  1185.9 26.0 %collective-permute-start.55 = (bf16[768,768]{1,0:T(8,128)(2,1)S(1)}, bf16[768,768]{1,0:T(8,128)(2,1)}, u32[]{:S(2)}, u32[]{:S(2)}) collective-permute-start(bf16[768,768]{1,0:T(8,128)(2,1)S(1)} %add_convert_fusion.23), channel_id=1, source_target_pairs={{0,2},{6,4},{1,3},{7,5},{8,10},{14,12},{9,11},{15,13},{16,18},{22,... | collective-permute-start | bytes 3538952 | tf_op jit(solution)/shard_map/ppermute | solution.py:546
  1191.3 26.6 %collective-permute-start.59 = (bf16[768,768]{1,0:T(8,128)(2,1)S(1)}, bf16[768,768]{1,0:T(8,128)(2,1)}, u32[]{:S(2)}, u32[]{:S(2)}) collective-permute-start(bf16[768,768]{1,0:T(8,128)(2,1)S(1)} %add_convert_fusion.6), channel_id=1, source_target_pairs={{2,4},{4,2},{3,5},{5,3},{10,12},{12,10},{11,13},{13,11},{18,20},{2... | collective-permute-start | bytes 3538952 | tf_op jit(solution)/shard_map/ppermute | solution.py:549
  1194.4 33.5 %collective-permute-start.61 = (bf16[768,768]{1,0:T(8,128)(2,1)}, bf16[768,768]{1,0:T(8,128)(2,1)}, u32[]{:S(2)}, u32[]{:S(2)}) collective-permute-start(bf16[768,768]{1,0:T(8,128)(2,1)} %add_convert_fusion.4), channel_id=1, source_target_pairs={{2,0},{4,6},{3,1},{5,7},{10,8},{12,14},{11,9},{13,15},{18,16},{20,... | collective-permute-start | bytes 3538952 | tf_op jit(solution)/shard_map/ppermute | solution.py:552
  1198.0 32.2 %collective-permute-start.89 = (bf16[768,768]{1,0:T(8,128)(2,1)}, bf16[768,768]{1,0:T(8,128)(2,1)S(1)}, u32[]{:S(2)}, u32[]{:S(2)}) collective-permute-start(bf16[768,768]{1,0:T(8,128)(2,1)} %broadcast_select_fusion.9), channel_id=1, source_target_pairs={{0,0},{8,1},{1,8},{9,9},{17,16},{25,17},{16,24},{24,25},{2,2},{10,... | collective-permute-start | bytes 3538952 | tf_op jit(solution)/shard_map/ppermute | solution.py:554
  1204.8 27.3 %collective-permute-start.88 = (bf16[768,768]{1,0:T(8,128)(2,1)}, bf16[768,768]{1,0:T(8,128)(2,1)S(1)}, u32[]{:S(2)}, u32[]{:S(2)}) collective-permute-start(bf16[768,768]{1,0:T(8,128)(2,1)} %broadcast_select_fusion.11), channel_id=1, source_target_pairs={{0,0},{8,1},{1,8},{9,9},{17,16},{25,17},{16,24},{24,25},{2,2},{10,... | collective-permute-start | bytes 3538952 | tf_op jit(solution)/shard_map/ppermute | solution.py:554
  1211.8 34.4 %collective-permute-start.70 = (bf16[768,768]{1,0:T(8,128)(2,1)S(1)}, bf16[768,768]{1,0:T(8,128)(2,1)S(1)}, u32[]{:S(2)}, u32[]{:S(2)}) collective-permute-start(bf16[768,768]{1,0:T(8,128)(2,1)S(1)} %add_convert_fusion.3), channel_id=1, source_target_pairs={{0,2},{6,4},{1,3},{7,5},{8,10},{14,12},{9,11},{15,13},{16,18},{22,... | collective-permute-start | bytes 3538952 | tf_op jit(solution)/shard_map/ppermute | solution.py:546
  1227.9 27.5 %collective-permute-start.71 = (bf16[768,768]{1,0:T(8,128)(2,1)S(1)}, bf16[768,768]{1,0:T(8,128)(2,1)S(1)}, u32[]{:S(2)}, u32[]{:S(2)}) collective-permute-start(bf16[768,768]{1,0:T(8,128)(2,1)S(1)} %add_convert_fusion.8), channel_id=1, source_target_pairs={{2,4},{4,2},{3,5},{5,3},{10,12},{12,10},{11,13},{13,11},{18,20},{2... | collective-permute-start | bytes 3538952 | tf_op jit(solution)/shard_map/ppermute | solution.py:549
  1230.2 26.3 %collective-permute-start.84 = (bf16[768,768]{1,0:T(8,128)(2,1)S(1)}, bf16[768,768]{1,0:T(8,128)(2,1)S(1)}, u32[]{:S(2)}, u32[]{:S(2)}) collective-permute-start(bf16[768,768]{1,0:T(8,128)(2,1)S(1)} %copy-done.28), channel_id=1, source_target_pairs={{0,0},{8,1},{1,8},{9,9},{17,16},{25,17},{16,24},{24,25},{2,2},{10,... | collective-permute-start | bytes 3538952 | tf_op jit(solution)/shard_map/ppermute | solution.py:554
  1232.1 31.3 %collective-permute-start.85 = (bf16[768,768]{1,0:T(8,128)(2,1)S(1)}, bf16[768,768]{1,0:T(8,128)(2,1)S(1)}, u32[]{:S(2)}, u32[]{:S(2)}) collective-permute-start(bf16[768,768]{1,0:T(8,128)(2,1)S(1)} %copy-done.29), channel_id=1, source_target_pairs={{0,0},{8,1},{1,8},{9,9},{17,16},{25,17},{16,24},{24,25},{2,2},{10,... | collective-permute-start | bytes 3538952 | tf_op jit(solution)/shard_map/ppermute | solution.py:554
  1246.3 29.9 %collective-permute-start.72 = (bf16[768,768]{1,0:T(8,128)(2,1)S(1)}, bf16[768,768]{1,0:T(8,128)(2,1)S(1)}, u32[]{:S(2)}, u32[]{:S(2)}) collective-permute-start(bf16[768,768]{1,0:T(8,128)(2,1)S(1)} %add_convert_fusion.5), channel_id=1, source_target_pairs={{2,0},{4,6},{3,1},{5,7},{10,8},{12,14},{11,9},{13,15},{18,16},{20,... | collective-permute-start | bytes 3538952 | tf_op jit(solution)/shard_map/ppermute | solution.py:552
  1256.5 92.0 %collective-permute-start.66 = (bf16[768,384]{1,0:T(8,128)(2,1)S(1)}, bf16[768,384]{1,0:T(8,128)(2,1)S(1)}, u32[]{:S(2)}, u32[]{:S(2)}) collective-permute-start(bf16[768,384]{1,0:T(8,128)(2,1)S(1)} %copy-done.32), channel_id=1, source_target_pairs={{0,0},{8,1},{1,8},{9,9},{17,16},{25,17},{16,24},{24,25},{2,2},{10,... | collective-permute-start | bytes 1769480 | tf_op jit(solution)/shard_map/ppermute | solution.py:554
  1263.4 44.8 %collective-permute-start.79 = (bf16[768,768]{1,0:T(8,128)(2,1)S(1)}, bf16[768,768]{1,0:T(8,128)(2,1)S(1)}, u32[]{:S(2)}, u32[]{:S(2)}) collective-permute-start(bf16[768,768]{1,0:T(8,128)(2,1)S(1)} %add_convert_fusion.1), channel_id=1, source_target_pairs={{2,0},{4,6},{3,1},{5,7},{10,8},{12,14},{11,9},{13,15},{18,16},{20,... | collective-permute-start | bytes 3538952 | tf_op jit(solution)/shard_map/ppermute | solution.py:552
  1264.9 95.5 %collective-permute-start.86 = (bf16[768,768]{1,0:T(8,128)(2,1)S(1)}, bf16[768,768]{1,0:T(8,128)(2,1)S(1)}, u32[]{:S(2)}, u32[]{:S(2)}) collective-permute-start(bf16[768,768]{1,0:T(8,128)(2,1)S(1)} %broadcast_select_fusion.7), channel_id=1, source_target_pairs={{0,0},{8,1},{1,8},{9,9},{17,16},{25,17},{16,24},{24,25},{2,2},{10,... | collective-permute-start | bytes 3538952 | tf_op jit(solution)/shard_map/ppermute | solution.py:554
  1276.2 39.2 %collective-permute-start.64 = (bf16[768,384]{1,0:T(8,128)(2,1)S(1)}, bf16[768,384]{1,0:T(8,128)(2,1)S(1)}, u32[]{:S(2)}, u32[]{:S(2)}) collective-permute-start(bf16[768,384]{1,0:T(8,128)(2,1)S(1)} %add_convert_fusion.24), channel_id=1, source_target_pairs={{2,0},{4,6},{3,1},{5,7},{10,8},{12,14},{11,9},{13,15},{18,16},{20,... | collective-permute-start | bytes 1769480 | tf_op jit(solution)/shard_map/ppermute | solution.py:552
  1277.6 29.2 %collective-permute-start.73 = (bf16[768,128]{1,0:T(8,128)(2,1)S(1)}, bf16[768,128]{1,0:T(8,128)(2,1)S(1)}, u32[]{:S(2)}, u32[]{:S(2)}) collective-permute-start(bf16[768,128]{1,0:T(8,128)(2,1)S(1)} %copy-done.30), channel_id=1, source_target_pairs={{0,2},{6,4},{1,3},{7,5},{8,10},{14,12},{9,11},{15,13},{16,18},{22,... | collective-permute-start | bytes 589832 | tf_op jit(solution)/shard_map/ppermute | solution.py:546
  1306.8 37.9 %collective-permute-start.82 = (bf16[768,768]{1,0:T(8,128)(2,1)S(1)}, bf16[768,768]{1,0:T(8,128)(2,1)S(1)}, u32[]{:S(2)}, u32[]{:S(2)}) collective-permute-start(bf16[768,768]{1,0:T(8,128)(2,1)S(1)} %add_convert_fusion), channel_id=1, source_target_pairs={{2,0},{4,6},{3,1},{5,7},{10,8},{12,14},{11,9},{13,15},{18,16},{20,... | collective-permute-start | bytes 3538952 | tf_op jit(solution)/shard_map/ppermute | solution.py:552
  1309.0 51.3 %collective-permute-start.87 = (bf16[768,768]{1,0:T(8,128)(2,1)S(1)}, bf16[768,768]{1,0:T(8,128)(2,1)S(1)}, u32[]{:S(2)}, u32[]{:S(2)}) collective-permute-start(bf16[768,768]{1,0:T(8,128)(2,1)S(1)} %broadcast_select_fusion.6), channel_id=1, source_target_pairs={{0,0},{8,1},{1,8},{9,9},{17,16},{25,17},{16,24},{24,25},{2,2},{10,... | collective-permute-start | bytes 3538952 | tf_op jit(solution)/shard_map/ppermute | solution.py:554
  1315.4 27.4 %collective-permute-start.75 = (bf16[768,128]{1,0:T(8,128)(2,1)S(1)}, bf16[768,128]{1,0:T(8,128)(2,1)S(1)}, u32[]{:S(2)}, u32[]{:S(2)}) collective-permute-start(bf16[768,128]{1,0:T(8,128)(2,1)S(1)} %add_convert_fusion.32), channel_id=1, source_target_pairs={{2,0},{4,6},{3,1},{5,7},{10,8},{12,14},{11,9},{13,15},{18,16},{20,... | collective-permute-start | bytes 589832 | tf_op jit(solution)/shard_map/ppermute | solution.py:552
  (92 other events, 913.4 us)
Sparse Core Ops, SparseCore 0:
  13.8 106.7 all-gather.2
  127.2 41.0 all-gather.4
  904.7 30.9 all-reduce.2
  939.3 48.1 reduce-scatter.4
  991.3 46.2 reduce-scatter.2

commit v2 on v1

v2 whole, which is shorter than its diff:
```python
import functools
import jax
import jax.numpy as jnp
from jax import lax
from jax.experimental import pallas as pl
from jax.experimental.pallas import tpu as pltpu
from jax.sharding import PartitionSpec as P

HD = 64
ROT = 16
EPS = 1e-05
LANES = 128
ROWS = 256
NORM_ROWS = 64
SPAN = 512
VMEM_LIMIT = 60 * 2**20
ANY = pl.BlockSpec(memory_space=pl.ANY)
SMEM = pl.BlockSpec(memory_space=pltpu.SMEM)
VMEM = pl.BlockSpec(memory_space=pltpu.VMEM)
BF16, F32 = jnp.bfloat16, jnp.float32


def dot(left, right, dims=((1,), (0,))):
    return lax.dot_general(left, right, (dims, ((), ())), preferred_element_type=F32)


def dot_nt(left, right):
    return dot(left, right, ((1,), (1,)))


def turn(values, cosines, ahead, behind):
    return (
        values * cosines
        + pltpu.roll(values, LANES - ROT // 2, axis=1) * ahead
        + pltpu.roll(values, ROT // 2, axis=1) * behind
    )


def normalized(rows):
    centred = rows - jnp.mean(rows, axis=-1, keepdims=True)
    scale = lax.rsqrt(jnp.mean(centred * centred, axis=-1, keepdims=True) + EPS)
    return centred * scale, scale


def hidden_from(span, rows, m):
    key = lax.broadcasted_iota(jnp.int32, (SPAN, 2 * rows), 0)
    query = lax.broadcasted_iota(jnp.int32, (SPAN, 2 * rows), 1) & (rows - 1)
    return key > query + (m * rows - span * SPAN)


def side_by_side(pair):
    return jnp.concatenate([pair[:HD], pair[HD:]], axis=1)


def staged(total, stages):
    def turns(t):
        for half in range(2):
            for k, stage in enumerate(stages):
                u = 2 * t + half - k
                stage(jnp.clip(u, 0, total - 1), (half - k) % 2, u >= 0)

    steps((total + len(stages)) // 2, turns)


def fold(values):
    return jnp.sum(values.reshape(values.shape[0] // 8, 8, values.shape[1]), axis=0)


def steps(size, body):
    def step(i, _):
        body(i)
        return 0

    lax.fori_loop(0, size, step, 0)


def block_of(i, size):
    return pl.ds(pl.multiple_of(i * size, size), size)


FWD_STATE = ("x", "h1", "h2", "q", "qt", "o", "ot", "a", "g", "l", "kd", "vd", "kt", "vt", "y")
BWD_STATE = ("db", "du", "dq", "dkv", "dkw", "acc", "accu", "gin")
READ = ("x", "q", "qt", "ot", "g", "l", "kd", "vd", "kt")
N_W = 8


def state_shapes(length, width, hidden):
    pairs, tiles = width // LANES, hidden // width
    row, ff, one = ((2, length, width), BF16), ((2, length, hidden), BF16), ((length, width), BF16)
    full, chunks = ((2, length, width), F32), length // ROWS
    lse, turned = ((2, chunks, pairs, 1, 2 * ROWS), F32), (2, chunks, pairs, HD, 2 * ROWS)
    wide, tall, total = ((length, LANES), BF16), ((HD, length), BF16), ((length, LANES), F32)
    fwd = dict(x=full, h1=row, h2=row, q=row, qt=(turned, BF16), o=row, ot=(turned, F32), a=ff, g=ff, l=lse, kd=wide, vd=wide, kt=tall, vt=tall, y=one)
    bwd = dict(db=row, du=ff, dq=row, dkv=wide, dkw=total, acc=((2, 8, 8, width), F32), accu=((2, tiles, 8, width), F32), gin=one)
    return fwd, bwd


def weight_copies(stored, weights, wsems, slot):
    copies = {}
    for n, name in enumerate("qoih"):
        copies[name] = [pltpu.make_async_copy(stored[2 * n + k].at[slot], weights[2 * n + k].at[slot], wsems.at[slot, 2 * n + k]) for k in range(2)]
    return copies


def weight_scratch(weights):
    return [pltpu.VMEM(w.shape, BF16) for w in weights]


def make_struct(item):
    return jax.ShapeDtypeStruct(*item)


def fwd_kernel(rows, fresh, *refs):
    n_state = len(FWD_STATE)
    sc, hop_in, seq_in, small, bi, cos, ahead, behind, wkv = refs[:9]
    stored = refs[9 : 9 + N_W]
    at = 9 + N_W + (0 if fresh else n_state)
    st = dict(zip(FWD_STATE, refs[at : at + n_state]))
    hop_out = refs[at + n_state]
    (x_s, xf_s, h1_s, h2_s, q_s, qt_s, o_s, ot_s, a_s, g_s, l_s, kd_s, vd_s, kt_s, vt_s, vtc_s, s0_s, s1_s, e0_s, e1_s, top_s, sum_s, part_s, *weights, sems, once, wsems) = refs[at + n_state + 1 :]
    wq, wo, wi, wh = (weights[2 * i : 2 * i + 2] for i in range(4))
    width = xf_s.shape[2]
    half, hid = wq[0].shape[2], wi[0].shape[2]
    pairs, tiles, length = width // LANES, hid // width, kd_s.shape[0]

    @pl.when(sc[0] == 1)
    def _():
        m = sc[1]
        place = block_of(m, rows)

        @pl.when(sc[2] == 1)
        def _():
            pltpu.make_async_copy(seq_in.at[place], x_s, once.at[0]).start()

        @pl.when(sc[2] == 0)
        def _():
            pltpu.make_async_copy(hop_in, x_s, once.at[0]).start()

        for j in range(2):
            copies = weight_copies(stored, weights, wsems, j ^ sc[3])
            for name in "qioh":
                for copy in copies[name]:
                    copy.start()
        kd_in = pltpu.make_async_copy(st["kd"], kd_s, once.at[1])
        vt_in = pltpu.make_async_copy(st["vt"], vt_s, once.at[2])
        kd_in.start()
        vt_in.start()
        pltpu.make_async_copy(hop_in, x_s, once.at[0]).wait()
        xf_s[0] = x_s[...].astype(F32)
        tables = (cos[place, :], ahead[place, :], behind[place, :])

        def saves(j):
            pairs_of = (("x", xf_s), ("h1", h1_s), ("h2", h2_s), ("q", q_s), ("o", o_s), ("a", a_s), ("g", g_s))
            out = {n: pltpu.make_async_copy(b.at[j], st[n].at[j, place], sems.at[j, i]) for i, (n, b) in enumerate(pairs_of)}
            for i, (n, b) in enumerate((("l", l_s), ("qt", qt_s), ("ot", ot_s))):
                out[n] = pltpu.make_async_copy(b.at[j], st[n].at[j, m], sems.at[j, 7 + i])
            return out

        kv_saves = (
            pltpu.make_async_copy(kd_s.at[place], st["kd"].at[place], once.at[3]),
            pltpu.make_async_copy(vd_s, st["vd"].at[place], once.at[4]),
            pltpu.make_async_copy(kt_s, st["kt"].at[:, place], once.at[5]),
            pltpu.make_async_copy(vtc_s, st["vt"].at[:, place], once.at[6]),
        )

        def layer(j):
            w = j ^ sc[3]
            loads = weight_copies(stored, weights, wsems, w)
            save = saves(j)
            save["x"].start()

            def norm(r):
                span = block_of(r, NORM_ROWS)
                hat, _ = normalized(xf_s[j, span, :])
                h1_s[j, span, :] = (hat * small[j, 0:1, :] + small[j, 2:3, :]).astype(BF16)
                h2_s[j, span, :] = (hat * small[j, 1:2, :] + small[j, 3:4, :]).astype(BF16)

            steps(rows // NORM_ROWS, norm)
            save["h1"].start()
            save["h2"].start()

            @pl.when(j == 0)
            def _():
                kv = dot(h1_s[j], wkv[...]) + small[j, 7:8, : 2 * LANES]
                keys, values = turn(kv[:, :LANES], *tables), kv[:, LANES:]
                kd_in.wait()
                vt_in.wait()
                kd_s[place, :] = keys.astype(BF16)
                vd_s[...] = values.astype(BF16)
                kt_s[...] = jnp.transpose(keys)[:HD].astype(BF16)
                vtc_s[...] = jnp.transpose(values)[:HD].astype(BF16)
                vt_s[:, place] = vtc_s[...]
                for c in range(1, length // rows):

                    @pl.when(m < c)
                    def _():
                        vt_s[:, c * rows : (c + 1) * rows] = jnp.zeros((HD, rows), BF16)

                for copy in kv_saves:
                    copy.start()

            for k in range(2):
                loads["q"][k].wait()
                query = dot(h1_s[j], wq[k][w]) + small[j, 6:7, k * half : (k + 1) * half]
                for b in range(half // LANES):
                    block = turn(query[:, b * LANES : (b + 1) * LANES], *tables) * HD**-0.5
                    col = k * half + b * LANES
                    q_s[j, :, col : col + LANES] = block.astype(BF16)
                    qt_s[j, col // LANES] = side_by_side(jnp.transpose(block)).astype(BF16)
            save["q"].start()
            save["qt"].start()

            many = m * rows >= SPAN

            def unit(u):
                return (u >= pairs).astype(jnp.int32), jnp.where(u >= pairs, u - pairs, u)

            def scores(u, slot, live):
                span, i = unit(u)
                (s0_s, s1_s)[slot][...] = dot(kd_s[block_of(span, SPAN), :HD], qt_s[j, i])

            def soften(u, slot, live):
                span, i = unit(u)
                score = jnp.where(hidden_from(span, rows, m), -1e30, (s0_s, s1_s)[slot][...])
                top = jnp.max(score, axis=0, keepdims=True)
                expo = jnp.exp(score - top)
                top_s[u] = top
                sum_s[u] = jnp.sum(expo, axis=0, keepdims=True)
                (e0_s, e1_s)[slot][...] = expo.astype(BF16)

            def weigh(u, slot, live):
                span, i = unit(u)
                part_s[u] = dot(vt_s[:, block_of(span, SPAN)], (e0_s, e1_s)[slot][...])

            staged(jnp.where(many, 2 * pairs, pairs), (scores, soften, weigh))

            def gather(i):
                first, second = top_s[i], jnp.where(many, top_s[pairs + i], -1e30)
                top = jnp.maximum(first, second)
                first, second = jnp.exp(first - top), jnp.exp(second - top)
                summed = first * sum_s[i] + jnp.where(many, second * sum_s[pairs + i], 0.0)
                out = first * part_s[i] + jnp.where(many, second * part_s[pairs + i], 0.0)
                out = out / summed
                l_s[j, i] = top + jnp.log(summed)
                ot_s[j, i] = out
                out = jnp.concatenate([out[:, :rows], out[:, rows:]], axis=0)
                o_s[j, :, block_of(i, LANES)] = jnp.transpose(out).astype(BF16)

            steps(pairs, gather)
            for name in ("o", "ot", "l"):
                save[name].start()

            for copy in loads["i"]:
                copy.wait()

            def hidden(t):
                for k in range(2):
                    before = dot(h2_s[j], wi[k][w, :, block_of(t, width)]) + bi[j, k * tiles + t]
                    normal = 0.5 + 0.5 * lax.erf(before * 0.5**0.5)
                    cols = pl.ds(pl.multiple_of(k * hid + t * width, width), width)
                    a_s[j, :, cols] = (before * normal).astype(BF16)
                    slope = normal + before * (jnp.exp(-0.5 * before * before) * 0.3989422804014327)
                    g_s[j, :, cols] = slope.astype(BF16)

            steps(tiles, hidden)
            save["a"].start()
            save["g"].start()
            for copy in loads["o"] + loads["h"]:
                copy.wait()
            branch = dot(a_s[j, :, :hid], wh[0][w]) + dot(a_s[j, :, hid:], wh[1][w])
            branch += dot(o_s[j, :, :half], wo[0][w]) + dot(o_s[j, :, half:], wo[1][w])
            xf_s[j + 1] = xf_s[j] + (branch + small[j, 4:5, :] + small[j, 5:6, :])

        steps(2, layer)
        x_s[...] = xf_s[2].astype(BF16)
        ends = (
            pltpu.make_async_copy(x_s, st["y"].at[place], once.at[7]),
            pltpu.make_async_copy(x_s, hop_out, once.at[8]),
        )
        for copy in ends:
            copy.start()
        for j in range(2):
            for copy in saves(j).values():
                copy.wait()
        for copy in kv_saves + ends:
            copy.wait()


def fwd_call(rows, state, sc, hop, seq, params, weights):
    small, bi, cos, ahead, behind, wkv = params
    length, width = seq.shape
    half, hid = weights[0].shape[2], weights[4].shape[2]
    hidden, pairs = 2 * hid, width // LANES
    shapes, _ = state_shapes(length, width, hidden)
    fresh = state is None
    n = len(FWD_STATE)
    scratch = [
        pltpu.VMEM((rows, width), BF16),
        pltpu.VMEM((3, rows, width), F32),
        pltpu.VMEM((2, rows, width), BF16),
        pltpu.VMEM((2, rows, width), BF16),
        pltpu.VMEM((2, rows, width), BF16),
        pltpu.VMEM((2, pairs, HD, 2 * rows), BF16),
        pltpu.VMEM((2, rows, width), BF16),
        pltpu.VMEM((2, pairs, HD, 2 * rows), F32),
        pltpu.VMEM((2, rows, hidden), BF16),
        pltpu.VMEM((2, rows, hidden), BF16),
        pltpu.VMEM((2, pairs, 1, 2 * rows), F32),
        pltpu.VMEM((length, LANES), BF16),
        pltpu.VMEM((rows, LANES), BF16),
        pltpu.VMEM((HD, rows), BF16),
        pltpu.VMEM((HD, length), BF16),
        pltpu.VMEM((HD, rows), BF16),
        pltpu.VMEM((SPAN, 2 * rows), F32),
        pltpu.VMEM((SPAN, 2 * rows), F32),
        pltpu.VMEM((SPAN, 2 * rows), BF16),
        pltpu.VMEM((SPAN, 2 * rows), BF16),
        pltpu.VMEM((2 * pairs, 1, 2 * rows), F32),
        pltpu.VMEM((2 * pairs, 1, 2 * rows), F32),
        pltpu.VMEM((2 * pairs, HD, 2 * rows), F32),
        *weight_scratch(weights),
        pltpu.SemaphoreType.DMA((2, 10)),
        pltpu.SemaphoreType.DMA((9,)),
        pltpu.SemaphoreType.DMA((2, N_W)),
    ]
    outs = pl.pallas_call(
        functools.partial(fwd_kernel, rows, fresh),
        out_shape=[make_struct(shapes[k]) for k in FWD_STATE] + [jax.ShapeDtypeStruct((rows, width), BF16)],
        in_specs=[SMEM, ANY, ANY] + [VMEM] * 6 + [ANY] * (N_W + (0 if fresh else n)),
        out_specs=[ANY] * (n + 1),
        scratch_shapes=scratch,
        input_output_aliases={} if fresh else {9 + N_W + i: i for i in range(n)},
        compiler_params=pltpu.CompilerParams(vmem_limit_bytes=VMEM_LIMIT),
        name="section_forward",
    )(sc, hop, seq, small, bi, cos, ahead, behind, wkv, *weights, *([] if fresh else state))
    return outs[:n], outs[n]


def bwd_kernel(rows, chunks, fresh, *refs):
    n_read, n_state = len(READ), len(BWD_STATE)
    sc, scale, hop_in, cot, small, cos, ahead, behind, wkv = refs[:9]
    stored = refs[9 : 9 + N_W]
    at = 9 + N_W
    rd = dict(zip(READ, refs[at : at + n_read]))
    at += n_read + (0 if fresh else n_state)
    st = dict(zip(BWD_STATE, refs[at : at + n_state]))
    hop_out = refs[at + n_state]
    (in_s, dy_s, x_s, q_s, qt_s, ot_s, g_s, l_s, kd_s, vd_s, kt_s, db_s, do_s, du_s, dq_s, dqt_s, dkv_s, dkw_s, dh1_s, dh2_s, acc_s, accu_s, two_s, dot_s, d_s, s0_s, s1_s, dp0_s, dp1_s, both0_s, both1_s, *weights, sems, outs, once, wsems) = refs[at + n_state + 1 :]
    wq, wo, wi, wh = (weights[2 * i : 2 * i + 2] for i in range(4))
    width = dy_s.shape[1]
    half, hid = wq[0].shape[2], wi[0].shape[2]
    pairs, tiles, length = width // LANES, hid // width, kd_s.shape[0]

    @pl.when(sc[0] == 1)
    def _():
        m = sc[1]
        place = block_of(m, rows)

        @pl.when(sc[2] == 1)
        def _():
            pltpu.make_async_copy(cot.at[place], in_s, once.at[0]).start()

        @pl.when(sc[2] == 0)
        def _():
            pltpu.make_async_copy(hop_in, in_s, once.at[0]).start()

        def gets(j):
            named = (("g", g_s), ("q", q_s), ("x", x_s))
            got = {n: pltpu.make_async_copy(rd[n].at[j, place], b.at[j], sems.at[j, i]) for i, (n, b) in enumerate(named)}
            for i, (n, b) in enumerate((("l", l_s), ("qt", qt_s), ("ot", ot_s))):
                got[n] = pltpu.make_async_copy(rd[n].at[j, m], b.at[j], sems.at[j, 3 + i])
            return got

        shared = [pltpu.make_async_copy(rd[n], b, once.at[1 + i]) for i, (n, b) in enumerate((("kd", kd_s), ("vd", vd_s), ("kt", kt_s)))]
        for j in (1, 0):
            copies = weight_copies(stored, weights, wsems, j ^ sc[3])
            for copy in copies["o"] + list(gets(j).values()):
                copy.start()
            for copy in shared if j == 1 else ():
                copy.start()
            for copy in copies["q"] + copies["h"] + copies["i"]:
                copy.start()
        running = (("dkw", dkw_s), ("acc", acc_s), ("accu", accu_s))

        @pl.when(m == chunks - 1)
        def _():
            for _, buf in running:
                buf[...] = jnp.zeros_like(buf)

        @pl.when(m < chunks - 1)
        def _():
            copies = [pltpu.make_async_copy(st[n], b, once.at[4 + i]) for i, (n, b) in enumerate(running)]
            for copy in copies:
                copy.start()
            for copy in copies:
                copy.wait()

        pltpu.make_async_copy(hop_in, in_s, once.at[0]).wait()
        dy_s[...] = in_s[...].astype(F32) * scale[0]
        tables = (cos[place, :], -ahead[place, :], -behind[place, :])

        def saves(j):
            named = (("db", db_s), ("du", du_s), ("dq", dq_s))
            return {n: pltpu.make_async_copy(b.at[j], st[n].at[j, place], outs.at[j, i]) for i, (n, b) in enumerate(named)}

        kv_save = pltpu.make_async_copy(dkv_s, st["dkv"].at[place], once.at[8])

        def layer(step):
            j = 1 - step
            w = j ^ sc[3]
            loads = weight_copies(stored, weights, wsems, w)
            got, save = gets(j), saves(j)
            grad = dy_s[...]
            db_s[j] = grad.astype(BF16)
            acc_s[j, 0] += fold(grad)
            save["db"].start()
            for k in range(2):
                loads["o"][k].wait()
                do_s[:, k * half : (k + 1) * half] = dot_nt(db_s[j], wo[k][w]).astype(BF16)
            for name in ("ot", "q", "qt", "l"):
                got[name].wait()

            @pl.when(j == 1)
            def _():
                for copy in shared:
                    copy.wait()

            def ready(i):
                cols = block_of(i, LANES)
                out_grad = do_s[:, cols].astype(F32)
                turned = side_by_side(jnp.transpose(out_grad))
                d_s[i] = jnp.sum(turned * ot_s[j, i], axis=0, keepdims=True)
                dot_s[i] = turned.astype(BF16)
                query = q_s[j, :, cols].astype(F32)
                low = lax.broadcasted_iota(jnp.int32, query.shape, 1) < HD
                parts = (
                    jnp.where(low, query, 0.0),
                    jnp.where(low, pltpu.roll(query, HD, axis=1), 0.0),
                    jnp.where(low, 0.0, pltpu.roll(out_grad, HD, axis=1)),
                    jnp.where(low, 0.0, out_grad),
                )
                for n, part in enumerate(parts):
                    two_s[i, n * rows : (n + 1) * rows, :] = part.astype(BF16)

            steps(pairs, ready)

            def unit(u):
                return (u >= pairs).astype(jnp.int32), jnp.where(u >= pairs, u - pairs, u)

            def scores(u, slot, live):
                span, i = unit(u)
                (s0_s, s1_s)[slot][...] = dot(kd_s[block_of(span, SPAN), :HD], qt_s[j, i])
                (dp0_s, dp1_s)[slot][...] = dot(vd_s[block_of(span, SPAN), :HD], dot_s[i])

            def soften(u, slot, live):
                span, i = unit(u)
                probs = jnp.where(hidden_from(span, rows, m), 0.0, jnp.exp((s0_s, s1_s)[slot][...] - l_s[j, i]))
                both = (both0_s, both1_s)[slot]
                both[:, : 2 * rows] = (probs * ((dp0_s, dp1_s)[slot][...] - d_s[i])).astype(BF16)
                both[:, 2 * rows :] = probs.astype(BF16)

            def weigh(u, slot, live):
                span, i = unit(u)
                place = block_of(span, SPAN)
                dqt_s[u] = dot(kt_s[:, place], (both0_s, both1_s)[slot][:, : 2 * rows])
                part = dot((both0_s, both1_s)[slot][...], two_s[i])

                dkw_s[place, :] += jnp.where(live, part, 0.0)

            many = m * rows >= SPAN
            staged(jnp.where(many, 2 * pairs, pairs), (scores, soften, weigh))

            def finish(i):
                grad = dqt_s[i] + jnp.where(many, dqt_s[pairs + i], 0.0)
                grad = jnp.concatenate([grad[:, :rows], grad[:, rows:]], axis=0)
                turned = turn(jnp.transpose(grad) * HD**-0.5, *tables)
                dq_s[j, :, block_of(i, LANES)] = turned.astype(BF16)

            steps(pairs, finish)
            save["dq"].start()
            acc_s[j, 5] += fold(dq_s[j].astype(F32))
            for copy in loads["q"]:
                copy.wait()
            dh1_s[...] = dot_nt(dq_s[j, :, :half], wq[0][w]) + dot_nt(dq_s[j, :, half:], wq[1][w])

            @pl.when(j == 0)
            def _():
                both = dkw_s[place, :]
                low = lax.broadcasted_iota(jnp.int32, both.shape, 1) < HD
                both = jnp.where(low, turn(both, *tables), both).astype(BF16)
                dkv_s[...] = both
                kv_save.start()
                acc_s[j, 6, :, :LANES] += fold(both.astype(F32))
                dh1_s[...] += dot_nt(both, wkv[...])

            got["g"].wait()
            for copy in loads["h"] + loads["i"]:
                copy.wait()

            def hidden(t):
                for k in range(2):
                    cols = pl.ds(pl.multiple_of(k * hid + t * width, width), width)
                    back = dot_nt(db_s[j], wh[k][w, block_of(t, width), :])
                    back = (back * g_s[j, :, cols].astype(F32)).astype(BF16)
                    du_s[j, :, cols] = back
                    accu_s[j, k * tiles + t] += fold(back.astype(F32))

            steps(tiles, hidden)
            save["du"].start()
            dh2_s[...] = dot_nt(du_s[j, :, :hid], wi[0][w]) + dot_nt(du_s[j, :, hid:], wi[1][w])
            got["x"].wait()

            def norm(r):
                span = block_of(r, NORM_ROWS)
                hat, spread = normalized(x_s[j, span, :])
                first, second = dh1_s[span, :], dh2_s[span, :]
                for i, v in enumerate((first * hat, first, second * hat, second)):
                    acc_s[j, 1 + i] += fold(v)
                inside = first * small[j, 0:1, :] + second * small[j, 1:2, :]
                shift = jnp.mean(inside, axis=-1, keepdims=True)
                tilt = jnp.mean(inside * hat, axis=-1, keepdims=True)
                dy_s[span, :] += spread * (inside - shift - hat * tilt)

            steps(rows // NORM_ROWS, norm)

        steps(2, layer)
        in_s[...] = dy_s[...].astype(BF16)
        ends = [pltpu.make_async_copy(in_s, st["gin"].at[place], once.at[9]), pltpu.make_async_copy(in_s, hop_out, once.at[10])]
        ends += [pltpu.make_async_copy(b, st[n], once.at[4 + i]) for i, (n, b) in enumerate(running)]
        for copy in ends:
            copy.start()
        for j in range(2):
            for copy in saves(j).values():
                copy.wait()
        for copy in ends + [kv_save]:
            copy.wait()


def bwd_call(rows, chunks, state, sc, scale, hop, cot, params, weights, fwd):
    small, cos, ahead, behind, wkv = params
    length, width = cot.shape
    half, hid = weights[0].shape[2], weights[4].shape[2]
    hidden, pairs, tiles = 2 * hid, width // LANES, 2 * hid // width
    _, shapes = state_shapes(length, width, hidden)
    fresh = state is None
    n = len(BWD_STATE)
    saved = dict(zip(FWD_STATE, fwd))
    scratch = [
        pltpu.VMEM((rows, width), BF16),
        pltpu.VMEM((rows, width), F32),
        pltpu.VMEM((2, rows, width), F32),
        pltpu.VMEM((2, rows, width), BF16),
        pltpu.VMEM((2, pairs, HD, 2 * rows), BF16),
        pltpu.VMEM((2, pairs, HD, 2 * rows), F32),
        pltpu.VMEM((2, rows, hidden), BF16),
        pltpu.VMEM((2, pairs, 1, 2 * rows), F32),
        pltpu.VMEM((length, LANES), BF16),
        pltpu.VMEM((length, LANES), BF16),
        pltpu.VMEM((HD, length), BF16),
        pltpu.VMEM((2, rows, width), BF16),
        pltpu.VMEM((rows, width), BF16),
        pltpu.VMEM((2, rows, hidden), BF16),
        pltpu.VMEM((2, rows, width), BF16),
        pltpu.VMEM((2 * pairs, HD, 2 * rows), F32),
        pltpu.VMEM((rows, LANES), BF16),
        pltpu.VMEM((length, LANES), F32),
        pltpu.VMEM((rows, width), F32),
        pltpu.VMEM((rows, width), F32),
        pltpu.VMEM((2, 8, 8, width), F32),
        pltpu.VMEM((2, tiles, 8, width), F32),
        pltpu.VMEM((pairs, 4 * rows, LANES), BF16),
        pltpu.VMEM((pairs, HD, 2 * rows), BF16),
        pltpu.VMEM((pairs, 1, 2 * rows), F32),
        pltpu.VMEM((SPAN, 2 * rows), F32),
        pltpu.VMEM((SPAN, 2 * rows), F32),
        pltpu.VMEM((SPAN, 2 * rows), F32),
        pltpu.VMEM((SPAN, 2 * rows), F32),
        pltpu.VMEM((SPAN, 4 * rows), BF16),
        pltpu.VMEM((SPAN, 4 * rows), BF16),
        *weight_scratch(weights),
        pltpu.SemaphoreType.DMA((2, 6)),
        pltpu.SemaphoreType.DMA((2, 3)),
        pltpu.SemaphoreType.DMA((11,)),
        pltpu.SemaphoreType.DMA((2, N_W)),
    ]
    first_state = 9 + N_W + len(READ)
    outs = pl.pallas_call(
        functools.partial(bwd_kernel, rows, chunks, fresh),
        out_shape=[make_struct(shapes[k]) for k in BWD_STATE] + [jax.ShapeDtypeStruct((rows, width), BF16)],
        in_specs=[SMEM, SMEM, ANY, ANY] + [VMEM] * 5 + [ANY] * (N_W + len(READ) + (0 if fresh else n)),
        out_specs=[ANY] * (n + 1),
        scratch_shapes=scratch,
        input_output_aliases={} if fresh else {first_state + i: i for i in range(n)},
        compiler_params=pltpu.CompilerParams(vmem_limit_bytes=VMEM_LIMIT),
        name="section_backward",
    )(sc, scale, hop, cot, small, cos, ahead, behind, wkv, *weights, *[saved[k] for k in READ], *([] if fresh else state))
    return outs[:n], outs[n]


def turn_tables(length):
    column = jnp.arange(LANES) % HD
    half = ROT // 2
    freq = jnp.power(10000.0, -2.0 * (column % half).astype(F32) / ROT)
    angle = jnp.arange(length).astype(F32)[:, None] * freq[None, :]
    cosines = jnp.where((column < ROT)[None, :], jnp.cos(angle), 1.0)
    sines = jnp.sin(angle)
    ahead = jnp.where((column < half)[None, :], -sines, 0.0)
    behind = jnp.where(((column >= half) & (column < ROT))[None, :], sines, 0.0)
    return cosines, ahead, behind


def stage_place(stage):
    across = stage // 2
    return across, (stage % 2 if across == 0 else 1 - stage % 2)


def device(across, core, tensor):
    return (2 * across + core) * 2 + tensor


PLANE = ("section", "tensor")
SWAP = [(0, 1), (1, 0), (2, 3), (3, 2)]


def plane_routes():
    fetch, ahead = [], []
    for stage in range(4):
        across, tensor = stage_place(stage)
        for core in range(2):
            fetch.append((device(across, stage % 2, core), device(across, core, tensor)))
            if stage < 3:
                after, turned = stage_place(stage + 1)
                ahead.append((device(across, core, tensor), device(after, core, turned)))
    return fetch, [(b, a) for a, b in fetch], ahead, [(b, a) for a, b in ahead]


FETCH, DELIVER, AHEAD, BEHIND = plane_routes()


def other_core(value):
    return lax.ppermute(value, "section", SWAP)


def added(left, right):
    return (left.astype(F32) + right.astype(F32)).astype(BF16)


def after(value, *others):
    return lax.optimization_barrier((value, *others))[0]


def line_sums(pieces, make):
    position = lax.axis_index("dp")
    at_end = (position == 0) | (position == 3)
    count = len(pieces)
    own, first, second, third, done = [], [], [], [], []
    for r in range(count + 5):
        if r < count:
            ties = [chain[n] for chain, n in ((first, r - 3), (second, r - 4), (third, r - 5), (done, r - 6)) if n >= 0]
            mine, theirs = make(pieces[r], ties)
            own.append((mine, other_core(theirs)))
        if 0 <= r - 1 < count:
            term = added(*own[r - 1])
            first.append(added(term, lax.ppermute(term, "dp", [(0, 1), (3, 2)])))
        if 0 <= r - 2 < count:
            part = first[r - 2]
            second.append(added(part, lax.ppermute(part, "dp", [(1, 2), (2, 1)])))
        if 0 <= r - 3 < count:
            whole = second[r - 3]
            third.append(jnp.where(at_end, lax.ppermute(whole, "dp", [(1, 0), (2, 3)]), whole))
        if 0 <= r - 4 < count:
            done.append(lax.ppermute(third[r - 4], PLANE, DELIVER))
    return done


def local(
    inputs,
    cotangent,
    subset_ids,
    subset_weight,
    ln_gain,
    ln_bias,
    w_query,
    b_query,
    w_kv,
    b_kv,
    w_out,
    out_bias,
    w_in,
    b_in,
    w_hid_out,
):
    section, tensor = lax.axis_index("section"), lax.axis_index("tensor")
    across, core = section // 2, section % 2
    stage = 2 * across + jnp.where(across == 0, tensor, 1 - tensor)
    micro, part, width = inputs.shape
    length = part * lax.axis_size(PLANE)
    half, hid = w_query.shape[3], w_in.shape[3]
    chunks = length // ROWS
    ticks = chunks + 3

    parity = lax.axis_index("dp") % 2
    pairs = [(i, i ^ 1) for i in range(lax.axis_size("dp"))]
    halves = {}
    for name, whole in (("h", w_hid_out), ("i", w_in), ("o", w_out), ("q", w_query)):
        fetched = lax.ppermute(lax.dynamic_index_in_dim(whole[0], parity, 0, keepdims=False), PLANE, FETCH)
        swapped = lax.ppermute(fetched, "dp", pairs)
        mine = jnp.stack([fetched, swapped])
        halves[name] = [mine, other_core(mine)]
    weights = [w for name in "qoih" for w in halves[name]]
    vectors = jnp.concatenate([v.reshape(-1) for v in (ln_gain, ln_bias, out_bias, b_kv, b_query, b_in)]).reshape(-1, LANES)
    vectors = lax.ppermute(vectors, PLANE, FETCH)
    own_kv = lax.ppermute(w_kv[0], PLANE, FETCH)
    flat, flat_other = vectors.reshape(-1), other_core(vectors).reshape(-1)
    edge = 12 * width + LANES
    bkv = flat[12 * width : edge]
    bkv = jnp.pad(jnp.concatenate([bkv[:HD], bkv[:HD], bkv[HD:], bkv[HD:]]), (0, width - 2 * LANES))
    bq = jnp.concatenate([f[edge : edge + 2 * half].reshape(2, 1, half) for f in (flat, flat_other)], axis=2)
    bi = jnp.concatenate([f[edge + 2 * half :].reshape(2, hid // width, 1, width) for f in (flat, flat_other)], axis=1)
    norms = [flat[n * 4 * width : (n + 1) * 4 * width].reshape(2, 2, width) for n in range(3)]
    small = jnp.concatenate([*norms, bq, jnp.broadcast_to(bkv, (2, 1, width))], axis=1)
    wide_kv = jnp.concatenate([own_kv[:, :HD], own_kv[:, :HD], own_kv[:, HD:], own_kv[:, HD:]], axis=1)

    whole_in = lax.all_gather(inputs, PLANE, axis=1, tiled=True)
    my_in = lax.dynamic_index_in_dim(whole_in, core, 0, keepdims=False)
    my_id = lax.dynamic_index_in_dim(subset_ids, core, 0, keepdims=False)
    matches = my_id == jnp.arange(subset_weight.shape[0], dtype=jnp.int32)
    weight = jnp.sum(jnp.where(matches, subset_weight, 0.0))
    is_first, is_last = stage == 0, stage == 3
    scale = jnp.where(is_last, weight, 1.0).reshape(1)

    tables = turn_tables(length)
    forward_params = (small, bi, *tables, wide_kv)
    hop = jnp.zeros((ROWS, width), BF16)
    saved = None
    for tick in range(ticks):
        number = tick - stage
        valid = (number >= 0) & (number < chunks)
        sc = jnp.stack([valid.astype(jnp.int32), jnp.clip(number, 0, chunks - 1), is_first.astype(jnp.int32), parity])
        saved, hop = fwd_call(ROWS, saved, sc, hop, my_in, forward_params, weights)
        if tick == 0:
            whole_cot = lax.all_gather(after(cotangent, hop), PLANE, axis=1, tiled=True)
        if tick < ticks - 1:
            hop = lax.ppermute(hop, PLANE, AHEAD)
    my_cot = lax.dynamic_index_in_dim(whole_cot, core, 0, keepdims=False)
    kept = dict(zip(FWD_STATE, saved))

    def spread(mine_only, here):
        rows = jnp.where(here, mine_only, jnp.zeros_like(mine_only))[None]
        canvas = jnp.where((jnp.arange(micro) == core)[:, None, None], rows, jnp.zeros_like(rows))
        return lax.psum_scatter(canvas, PLANE, scatter_dimension=1, tiled=True)

    final = spread(kept["y"], is_last)

    backward_params = (small, *tables, own_kv)
    back = None
    for tick in range(ticks):
        number = chunks - 1 - tick + (3 - stage)
        valid = (number >= 0) & (number < chunks)
        sc = jnp.stack([valid.astype(jnp.int32), jnp.clip(number, 0, chunks - 1), is_last.astype(jnp.int32), parity])
        back, hop = bwd_call(ROWS, chunks, back, sc, scale, hop, my_cot, backward_params, weights, saved)
        if tick < ticks - 1:
            hop = lax.ppermute(hop, PLANE, BEHIND)
    got = dict(zip(BWD_STATE, back))
    input_grad = spread(got["gin"], is_first).astype(F32)

    sources = {"h": ("a", "db"), "i": ("h2", "du"), "o": ("o", "db"), "q": ("h1", "dq"), "kv": ("h1", "dkv")}

    def terms(piece, ties):
        name, slot, start, size = piece
        left, right = kept[sources[name][0]][slot], got[sources[name][1]]
        right = after(right, *ties) if ties else right
        if name == "kv":
            one = dot(left, right, ((0,), (0,))).astype(BF16)
            return one, one
        right = right[slot]
        both = []
        for k in range(2):
            if name in "ho":
                at = k * (hid if name == "h" else half) + start
                both.append(dot(left[:, at : at + size], right, ((0,), (0,))).astype(BF16))
            else:
                at = k * (hid if name == "i" else half) + start
                both.append(dot(left, right[:, at : at + size], ((0,), (0,))).astype(BF16))
        return both

    pieces = [("q", 1, 0, half)]
    for slot in (1, 0):
        for name in "hi":
            pieces += [(name, slot, at, hid // 2) for at in (0, hid // 2)]
    pieces += [("o", 1, 0, half), ("o", 0, 0, half), ("q", 0, 0, half), ("kv", 0, 0, 0)]
    if lax.axis_size("dp") == 4:
        done = line_sums(pieces, terms)
    else:
        done = []
        for piece in pieces:
            mine, theirs = terms(piece, [])
            done.append(lax.ppermute(lax.psum(added(mine, other_core(theirs)), "dp"), PLANE, DELIVER))
    done = dict(zip(pieces, done))

    def joined(name, size, axis):
        slots = []
        for slot in range(2):
            parts = [done[p].astype(F32) for p in pieces if p[:2] == (name, slot)]
            slots.append(jnp.concatenate(parts, axis=axis))
        return jnp.stack(slots)[None]

    query = jnp.sum(got["acc"], axis=2)
    inner = jnp.sum(got["accu"], axis=2)
    rolled = jnp.roll(query[:, 5], half, axis=1)
    query = query.at[:, 5].set(jnp.where(core == 0, query[:, 5], rolled))
    inner = jnp.where(core == 0, inner, jnp.roll(inner, hid // width, axis=1))
    acc = jnp.concatenate([query, inner], axis=1)
    acc = acc + other_core(acc)
    acc = lax.ppermute(lax.psum(acc, "dp"), PLANE, DELIVER)
    gain_grad = jnp.stack([acc[:, 1], acc[:, 3]], axis=1)[None]
    bias_grad = jnp.stack([acc[:, 2], acc[:, 4]], axis=1)[None]
    out_bias_grad = jnp.stack([acc[:, 0], acc[:, 0]], axis=1)[None]
    bq_grad = lax.dynamic_slice_in_dim(acc[:, 5], tensor * half, half, axis=1)[None]
    bi_grad = lax.dynamic_slice_in_dim(acc[:, 8:].reshape(2, 2 * hid), tensor * hid, hid, axis=1)[None]
    return (
        final,
        input_grad,
        gain_grad,
        bias_grad,
        joined("q", half, 1),
        bq_grad,
        done["kv", 0, 0, 0].astype(F32)[None],
        acc[0, 6, : 2 * HD][None],
        joined("o", half, 0),
        out_bias_grad,
        joined("i", hid, 1),
        bi_grad,
        joined("h", hid, 0),
    )


def solution(mesh):
    assert mesh.shape["section"] == 4 and mesh.shape["tensor"] == 2
    rows = P("dp", PLANE, None)
    weights = (
        P("section", None, None, None),
        P("section", None, None, None),
        P("section", None, None, "tensor"),
        P("section", None, "tensor"),
        P("section", None, None),
        P("section", None),
        P("section", None, "tensor", None),
        P("section", None, None, None),
        P("section", None, None, "tensor"),
        P("section", None, "tensor"),
        P("section", None, "tensor", None),
    )
    return jax.shard_map(
        local,
        mesh=mesh,
        in_specs=(rows, rows, P("dp"), P(), *weights),
        out_specs=(rows, rows, *weights),
        check_vma=False,
    )
```

time: 1410 us -> 1500 us (1.064)
  waiting for transfers between devices: 548 us -> 629 us
  local copies, waits for them, and re-layouts: 36.9 us -> 68.6 us
  Pallas kernels: 372 us -> 349 us
  other arithmetic: 77.6 us -> 96.5 us
    ppermute x6, waiting for transfers between devices: 197 us -> 264 us  [local(): hop = lax.ppermute(hop, PLANE, BEHIND)]
    squeeze x0 -> x12, local copies, waits for them, and re-layouts: none -> 27.6 us  [the longest x6 13 us: terms(): right = right[slot]]
    pallas_call x7, Pallas kernels: 178 us -> 153 us  [fwd_call(): pl.pallas_call(functools.partial(fwd_kernel, rows, fresh), out_shape=[mak...]
    ppermute x57 -> x61, waiting for transfers between devices: 315 us -> 333 us  [the longest x13 109 us: line_sums(): lax.ppermute(whole, 'dp', [(1, 0), (2, 3)])]
    ppermute x19, starting transfers between devices: 45.1 us -> 29.8 us  [other_core(): return lax.ppermute(value, 'section', SWAP)]
    ppermute x57 -> x61, starting transfers between devices: 174 us -> 159 us  [the longest x13 59.1 us: line_sums(): first.append(added(term, lax.ppermute(term, 'dp', [(0, 1), (3, 2)])))]
  transfers between devices with their start and end apart: 95 -> 99, of which waited for: 39 -> 44; matrix products, arithmetic and copies ran while one was open for 11% -> 14% of each run, Pallas kernels for 12% -> 8%
where the time goes in v2:
time: 1500 us; the launch traced here: 1490 us
  waiting for transfers between devices  629 us (42%)
  Pallas kernels  349 us (23%)
  starting transfers between devices  265 us (18%)
  other arithmetic  96.5 us (6%)
  local copies, waits for them, and re-layouts  68.6 us (5%)
  matrix products  61.8 us (4%)
  between operations  16.8 us (1%)
    ppermute x6, waiting for transfers between devices, local(): hop = lax.ppermute(hop, PLANE, BEHIND)  264 us
    pallas_call x7, Pallas kernels, bwd_call(): pl.pallas_call(functools.partial(bwd_kernel, rows, chunks, fresh), out_sh...  196 us
    pallas_call x7, Pallas kernels, fwd_call(): pl.pallas_call(functools.partial(fwd_kernel, rows, fresh), out_shape=[mak...  153 us
    ppermute x13, waiting for transfers between devices, line_sums(): lax.ppermute(whole, 'dp', [(1, 0), (2, 3)])  109 us
    ppermute x13, waiting for transfers between devices, line_sums(): first.append(added(term, lax.ppermute(term, 'dp', [(0, 1), (3, 2)])))  108 us
    dot_general x25, matrix products, dot(): lax.dot_general(left, right, (dims, ((), ())), preferred_element_type=F32)  61.8 us
    ppermute x6, starting transfers between devices, local(): hop = lax.ppermute(hop, PLANE, AHEAD)  60.3 us
    ppermute x13, starting transfers between devices, line_sums(): first.append(added(term, lax.ppermute(term, 'dp', [(0, 1), (3, 2)])))  59.1 us
  transfers between devices with their start and end apart: 99, of which 44 were waited for; matrix products, arithmetic and copies ran while one was open for 14% of the time, Pallas kernels for 8%

profile of v2, /device:TPU:1, one launch (start us, length us, event | category | flops | bytes accessed | tf_op | source)
XLA Modules:
  0.0 1486.7 jit_solution(10839213858043402574)
XLA Ops:
  9.2 4.7 collective-permute-start.9
  16.0 24.8 %collective-permute-done.9 = bf16[768,1536]{1,0:T(8,128)(2,1)} collective-permute-done((bf16[768,1536]{1,0:T(8,128)(2,1)S(1)}, bf16[768,1536]{1,0:T(8,128)(2,1)}, u32[]{:S(2)}, u32[]{:S(2)}) %collective-permute-start.9) | collective-permute-done | bytes 2359328 | tf_op jit(solution)/shard_map/ppermute | solution.py:706
  42.1 24.0 %collective-permute-done.12 = bf16[1536,768]{1,0:T(8,128)(2,1)S(1)} collective-permute-done((bf16[1536,768]{1,0:T(8,128)(2,1)S(1)}, bf16[1536,768]{1,0:T(8,128)(2,1)S(1)}, u32[]{:S(2)}, u32[]{:S(2)}) %collective-permute-start.12) | collective-permute-done | bytes 2359328 | tf_op jit(solution)/shard_map/ppermute | solution.py:706
  67.5 25.5 %collective-permute-done.10 = bf16[768,1536]{1,0:T(8,128)(2,1)} collective-permute-done((bf16[768,1536]{1,0:T(8,128)(2,1)}, bf16[768,1536]{1,0:T(8,128)(2,1)}, u32[]{:S(2)}, u32[]{:S(2)}) %collective-permute-start.10) | collective-permute-done | bytes 2359328 | tf_op jit(solution)/shard_map/ppermute | solution.py:707
  92.9 5.0 pad_maximum_fusion.refs_13_
  97.9 20.0 %collective-permute-done.13 = bf16[1536,768]{1,0:T(8,128)(2,1)} collective-permute-done((bf16[1536,768]{1,0:T(8,128)(2,1)S(1)}, bf16[1536,768]{1,0:T(8,128)(2,1)}, u32[]{:S(2)}, u32[]{:S(2)}) %collective-permute-start.13) | collective-permute-done | bytes 2359328 | tf_op jit(solution)/shard_map/ppermute | solution.py:707
  135.8 4.6 collective-permute-done.6
  182.2 33.4 %section_forward.7 = (f32[2,1024,768]{2,1,0:T(8,128)}, bf16[2,1024,768]{2,1,0:T(8,128)(2,1)}, bf16[2,1024,768]{2,1,0:T(8,128)(2,1)}, bf16[2,1024,768]{2,1,0:T(8,...) custom-call(s32[4]{0:T(128)} %add_add_fusion.6.refs_0_, ...), custom_call_target="tpu_custom_call" | custom-call | tf_op jit(solution)/shard_map/section_forward/pallas_call | solution.py:326
  217.6 7.7 collective-permute-done.15.refs_1_
  226.0 33.6 %section_forward.8 = (f32[2,1024,768]{2,1,0:T(8,128)}, bf16[2,1024,768]{2,1,0:T(8,128)(2,1)}, bf16[2,1024,768]{2,1,0:T(8,128)(2,1)}, bf16[2,1024,768]{2,1,0:T(8,...) custom-call(s32[4]{0:T(128)} %add_add_fusion.5.refs_0_, ...), custom_call_target="tpu_custom_call", output_to_operand_aliasing={{0}: (17, {}), {1}: (18, {}), {2}: (19, {}), {3}: (20, {}),... | custom-call | tf_op jit(solution)/shard_map/section_forward/pallas_call | solution.py:326
  259.6 8.6 collective-permute-start.16
  268.9 6.6 collective-permute-done.16.refs_1_
  276.3 39.6 %section_forward.9 = (f32[2,1024,768]{2,1,0:T(8,128)}, bf16[2,1024,768]{2,1,0:T(8,128)(2,1)}, bf16[2,1024,768]{2,1,0:T(8,128)(2,1)}, bf16[2,1024,768]{2,1,0:T(8,...) custom-call(s32[4]{0:T(128)} %add_add_fusion.4.refs_0_, ...), custom_call_target="tpu_custom_call", output_to_operand_aliasing={{0}: (17, {}), {1}: (18, {}), {2}: (19, {}), {3}: (20, {}),... | custom-call | tf_op jit(solution)/shard_map/section_forward/pallas_call | solution.py:326
  317.8 6.0 collective-permute-done.17.refs_1_
  324.5 40.0 %section_forward.10 = (f32[2,1024,768]{2,1,0:T(8,128)}, bf16[2,1024,768]{2,1,0:T(8,128)(2,1)}, bf16[2,1024,768]{2,1,0:T(8,128)(2,1)}, bf16[2,1024,768]{2,1,0:T(8...) custom-call(s32[4]{0:T(128)} %add_add_fusion.3.refs_0_, ...), custom_call_target="tpu_custom_call", output_to_operand_aliasing={{0}: (17, {}), {1}: (18, {}), {2}: (19, {}), {3}: (20, {}),... | custom-call | tf_op jit(solution)/shard_map/section_forward/pallas_call | solution.py:326
  369.0 5.1 collective-permute-done.18.refs_1_
  376.7 41.5 %collective-permute-start.19 = (bf16[256,768]{1,0:T(8,128)(2,1)}, bf16[256,768]{1,0:T(8,128)(2,1)S(1)}, u32[]{:S(2)}, u32[]{:S(2)}) collective-permute-start(bf16[256,768]{1,0:T(8,128)(2,1)} %get-tuple-element.272), channel_id=1, source_target_pairs={{0,1},{8,9},{1,17},{9,25},{17,16},{25,24},{2,3},{10,11},{3,19},{11... | collective-permute-start | bytes 1179656 | tf_op jit(solution)/shard_map/ppermute | solution.py:744
  418.8 4.4 collective-permute-done.19.refs_1_
  444.1 43.5 %collective-permute-done.21.refs_2_ = bf16[256,768]{1,0:T(8,128)(2,1)S(1)} collective-permute-done((bf16[256,768]{1,0:T(8,128)(2,1)}, bf16[256,768]{1,0:T(8,128)(2,1)S(1)}, u32[]{:S(2)}, u32[]{:S(2)}) %collective-permute-start.21) | collective-permute-done | bytes 393248 | tf_op jit(solution)/shard_map/ppermute | solution.py:763
  492.1 7.2 collective-permute-done.22.refs_2_
  503.7 189.4 %collective-permute-done.23.refs_2_ = bf16[256,768]{1,0:T(8,128)(2,1)S(1)} collective-permute-done((bf16[256,768]{1,0:T(8,128)(2,1)}, bf16[256,768]{1,0:T(8,128)(2,1)S(1)}, u32[]{:S(2)}, u32[]{:S(2)}) %collective-permute-start.23) | collective-permute-done | bytes 393248 | tf_op jit(solution)/shard_map/ppermute | solution.py:763
  693.9 50.9 %section_backward.10 = (bf16[2,1024,768]{2,1,0:T(8,128)(2,1)}, bf16[2,1024,3072]{2,1,0:T(8,128)(2,1)}, bf16[2,1024,768]{2,1,0:T(8,128)(2,1)}, bf16[1024,128]{1,0...) custom-call(s32[4]{0:T(128)} %add_add_fusion.10.refs_0_, ...), custom_call_target="tpu_custom_call", output_to_operand_aliasing={{0}: (26, {}), {1}: (27, {}), {2}: (28, {}), {3}: (29, {}),... | custom-call | tf_op jit(solution)/shard_map/section_backward/pallas_call | solution.py:587
  746.7 11.2 collective-permute-done.24.refs_2_
  758.6 53.0 %section_backward.11 = (bf16[2,1024,768]{2,1,0:T(8,128)(2,1)}, bf16[2,1024,3072]{2,1,0:T(8,128)(2,1)}, bf16[2,1024,768]{2,1,0:T(8,128)(2,1)}, bf16[1024,128]{1,0...) custom-call(s32[4]{0:T(128)} %add_add_fusion.9.refs_0_, ...), custom_call_target="tpu_custom_call", output_to_operand_aliasing={{0}: (26, {}), {1}: (27, {}), {2}: (28, {}), {3}: (29, {}),... | custom-call | tf_op jit(solution)/shard_map/section_backward/pallas_call | solution.py:587
  813.5 6.8 collective-permute-done.25.refs_2_
  821.1 43.3 %section_backward.12 = (bf16[2,1024,768]{2,1,0:T(8,128)(2,1)}, bf16[2,1024,3072]{2,1,0:T(8,128)(2,1)}, bf16[2,1024,768]{2,1,0:T(8,128)(2,1)}, bf16[1024,128]{1,0...) custom-call(s32[4]{0:T(128)} %add_add_fusion.8.refs_0_, ...), custom_call_target="tpu_custom_call", output_to_operand_aliasing={{0}: (26, {}), {1}: (27, {}), {2}: (28, {}), {3}: (29, {}),... | custom-call | tf_op jit(solution)/shard_map/section_backward/pallas_call | solution.py:587
  867.5 5.6 collective-permute-done.26.refs_2_
  873.8 43.4 %section_backward.13 = (bf16[2,1024,768]{2,1,0:T(8,128)(2,1)}, bf16[2,1024,3072]{2,1,0:T(8,128)(2,1)}, bf16[2,1024,768]{2,1,0:T(8,128)(2,1)}, bf16[1024,128]{1,0...) custom-call(s32[4]{0:T(128)} %add_add_fusion.7.refs_0_, ...), custom_call_target="tpu_custom_call", output_to_operand_aliasing={{0}: (26, {}), {1}: (27, {}), {2}: (28, {}), {3}: (29, {}),... | custom-call | tf_op jit(solution)/shard_map/section_backward/pallas_call | solution.py:587
  919.6 11.6 collective-permute-start.27
  934.7 4.5 broadcast_select_fusion
  943.0 8.5 slice_bitcast_fusion.4
  965.5 5.7 collective-permute-start.28
  971.2 4.4 fusion.83
  984.6 10.3 collective-permute-done.35
  1004.8 6.8 collective-permute-start.32
  1017.9 5.4 collective-permute-start.30
  1023.3 4.4 collective-permute-done.37
  1031.2 5.7 collective-permute-done.32
  1047.4 14.8 collective-permute-done.30
  1064.5 22.9 %collective-permute-done.44 = bf16[768,768]{1,0:T(8,128)(2,1)} collective-permute-done((bf16[768,768]{1,0:T(8,128)(2,1)S(1)}, bf16[768,768]{1,0:T(8,128)(2,1)}, u32[]{:S(2)}, u32[]{:S(2)}) %collective-permute-start.44) | collective-permute-done | bytes 1179680 | tf_op jit(solution)/shard_map/ppermute | solution.py:664
  1100.0 7.3 collective-permute-start.41
  1122.0 9.6 collective-permute-done.41
  1140.5 19.7 %collective-permute-done.48 = bf16[768,768]{1,0:T(8,128)(2,1)} collective-permute-done((bf16[768,768]{1,0:T(8,128)(2,1)}, bf16[768,768]{1,0:T(8,128)(2,1)}, u32[]{:S(2)}, u32[]{:S(2)}) %collective-permute-start.48) | collective-permute-done | bytes 1179680 | tf_op jit(solution)/shard_map/ppermute | solution.py:670
  1160.2 7.9 collective-permute-start.53
  1180.8 4.6 collective-permute-done.46
  1185.4 5.2 collective-permute-start.58
  1210.0 6.1 collective-permute-start.54
  1221.6 6.3 collective-permute-start.59
  1236.1 16.1 %collective-permute-done.59 = bf16[768,768]{1,0:T(8,128)(2,1)} collective-permute-done((bf16[768,768]{1,0:T(8,128)(2,1)S(1)}, bf16[768,768]{1,0:T(8,128)(2,1)}, u32[]{:S(2)}, u32[]{:S(2)}) %collective-permute-start.59) | collective-permute-done | bytes 1179680 | tf_op jit(solution)/shard_map/ppermute | solution.py:664
  1272.9 4.4 collective-permute-start.51
  1286.5 10.7 collective-permute-done.63
  1301.8 16.9 %collective-permute-done.73 = bf16[384,768]{1,0:T(8,128)(2,1)S(1)} collective-permute-done((bf16[384,768]{1,0:T(8,128)(2,1)S(1)}, bf16[384,768]{1,0:T(8,128)(2,1)S(1)}, u32[]{:S(2)}, u32[]{:S(2)}) %collective-permute-start.73) | collective-permute-done | bytes 589856 | tf_op jit(solution)/shard_map/ppermute | solution.py:664
  1319.5 4.9 collective-permute-start.64
  1326.3 8.3 collective-permute-start.84
  1349.9 10.9 collective-permute-done.89
  1362.1 4.7 collective-permute-start.90
  1368.6 4.5 collective-permute-done.66
  1374.5 11.5 collective-permute-done.75
  1386.8 4.5 collective-permute-start.91
  1392.0 31.9 %collective-permute-done.86 = bf16[384,768]{1,0:T(8,128)(2,1)S(1)} collective-permute-done((bf16[384,768]{1,0:T(8,128)(2,1)S(1)}, bf16[384,768]{1,0:T(8,128)(2,1)S(1)}, u32[]{:S(2)}, u32[]{:S(2)}) %collective-permute-start.86) | collective-permute-done | bytes 589856 | tf_op jit(solution)/shard_map/ppermute | solution.py:670
  1439.0 11.8 collective-permute-done.80
  1455.8 4.4 fusion.1
  1468.2 4.4 fusion
  1472.5 4.7 collective-permute-done.69
  (450 shorter events, 354.6 us)
Async XLA Ops:
  7.2 171.1 %all-gather.3.cloned.1.call-start = ((), (), s32[]{:S(2)}) async-start(), calls=%async_computation.2 | async-start | bytes 3538944 | tf_op jit(solution)/shard_map/all_gather | solution.py:724
  9.2 31.6 %collective-permute-start.9 = (bf16[768,1536]{1,0:T(8,128)(2,1)S(1)}, bf16[768,1536]{1,0:T(8,128)(2,1)}, u32[]{:S(2)}, u32[]{:S(2)}) collective-permute-start(bf16[768,1536]{1,0:T(8,128)(2,1)S(1)} %dynamic-slice_bitcast_fusion.1), channel_id=1, source_target_pairs={{0,0},{1,8},{8,1},{9,9},{16,17},{17,25},{24,16},{25,24},{2,2},{3,1... | collective-permute-start | bytes 7077896 | tf_op jit(solution)/shard_map/ppermute | solution.py:706
  14.1 52.0 %collective-permute-start.12 = (bf16[1536,768]{1,0:T(8,128)(2,1)S(1)}, bf16[1536,768]{1,0:T(8,128)(2,1)S(1)}, u32[]{:S(2)}, u32[]{:S(2)}) collective-permute-start(bf16[1536,768]{1,0:T(8,128)(2,1)S(1)} %dynamic-slice_bitcast_fusion), channel_id=1, source_target_pairs={{0,0},{1,8},{8,1},{9,9},{16,17},{17,25},{24,16},{25,24},{2,2},{3,1... | collective-permute-start | bytes 7077896 | tf_op jit(solution)/shard_map/ppermute | solution.py:706
  40.8 52.1 %collective-permute-start.10 = (bf16[768,1536]{1,0:T(8,128)(2,1)}, bf16[768,1536]{1,0:T(8,128)(2,1)}, u32[]{:S(2)}, u32[]{:S(2)}) collective-permute-start(bf16[768,1536]{1,0:T(8,128)(2,1)} %collective-permute-done.9), channel_id=1, source_target_pairs={{0,2},{2,0},{4,6},{6,4},{1,3},{3,1},{5,7},{7,5},{8,10},{10,8},{12,... | collective-permute-start | bytes 7077896 | tf_op jit(solution)/shard_map/ppermute | solution.py:707
  66.1 51.8 %collective-permute-start.13 = (bf16[1536,768]{1,0:T(8,128)(2,1)S(1)}, bf16[1536,768]{1,0:T(8,128)(2,1)}, u32[]{:S(2)}, u32[]{:S(2)}) collective-permute-start(bf16[1536,768]{1,0:T(8,128)(2,1)S(1)} %collective-permute-done.12), channel_id=1, source_target_pairs={{0,2},{2,0},{4,6},{6,4},{1,3},{3,1},{5,7},{7,5},{8,10},{10,8},{12,... | collective-permute-start | bytes 7077896 | tf_op jit(solution)/shard_map/ppermute | solution.py:707
  67.4 370.1 %all-gather.5.cloned.1.call-start = ((), (), s32[]{:S(2)}) async-start(), calls=%async_computation.4 | async-start | bytes 3538944 | tf_op jit(solution)/shard_map/all_gather | solution.py:742
  97.9 83.0 %collective-permute-start.11 = (bf16[2,768,1536]{2,1,0:T(8,128)(2,1)}, bf16[2,768,1536]{2,1,0:T(8,128)(2,1)}, u32[]{:S(2)}, u32[]{:S(2)}) collective-permute-start(bf16[2,768,1536]{2,1,0:T(8,128)(2,1)} %pad_maximum_fusion.refs_13_), channel_id=1, source_target_pairs={{0,8},{8,0},{16,24},{24,16},{1,9},{9,1},{17,25},{25,17},{2,10},{10... | collective-permute-start | bytes 14155784 | tf_op jit(solution)/shard_map/ppermute | solution.py:641
  122.3 58.7 %collective-permute-start.14 = (bf16[2,1536,768]{2,1,0:T(8,128)(2,1)}, bf16[2,1536,768]{2,1,0:T(8,128)(2,1)}, u32[]{:S(2)}, u32[]{:S(2)}) collective-permute-start(bf16[2,1536,768]{2,1,0:T(8,128)(2,1)} %pad_maximum_fusion.1.refs_15_), channel_id=1, source_target_pairs={{0,8},{8,0},{16,24},{24,16},{1,9},{9,1},{17,25},{25,17},{2,10},{10... | collective-permute-start | bytes 14155784 | tf_op jit(solution)/shard_map/ppermute | solution.py:641
  149.9 31.1 %collective-permute-start.5 = (bf16[2,768,384]{2,1,0:T(8,128)(2,1)S(1)}, bf16[2,768,384]{2,1,0:T(8,128)(2,1)S(1)}, u32[]{:S(2)}, u32[]{:S(2)}) collective-permute-start(bf16[2,768,384]{2,1,0:T(8,128)(2,1)S(1)} %pad_maximum_fusion.2.refs_9_), channel_id=1, source_target_pairs={{0,8},{8,0},{16,24},{24,16},{1,9},{9,1},{17,25},{25,17},{2,10},{10... | collective-permute-start | bytes 3538952 | tf_op jit(solution)/shard_map/ppermute | solution.py:641
  156.3 24.6 %collective-permute-start.8 = (bf16[2,384,768]{2,1,0:T(8,128)(2,1)S(1)}, bf16[2,384,768]{2,1,0:T(8,128)(2,1)}, u32[]{:S(2)}, u32[]{:S(2)}) collective-permute-start(bf16[2,384,768]{2,1,0:T(8,128)(2,1)S(1)} %pad_maximum_fusion.3.refs_11_), channel_id=1, source_target_pairs={{0,8},{8,0},{16,24},{24,16},{1,9},{9,1},{17,25},{25,17},{2,10},{10... | collective-permute-start | bytes 3538952 | tf_op jit(solution)/shard_map/ppermute | solution.py:641
  215.6 749.9 %all-reduce.3.cloned.1.call-start = ((), (), s32[]{:S(2)}) async-start(), calls=%async_computation.6 | async-start | bytes 196608 | tf_op jit(solution)/shard_map/psum | solution.py:815
  376.7 46.5 %collective-permute-start.19 = (bf16[256,768]{1,0:T(8,128)(2,1)}, bf16[256,768]{1,0:T(8,128)(2,1)S(1)}, u32[]{:S(2)}, u32[]{:S(2)}) collective-permute-start(bf16[256,768]{1,0:T(8,128)(2,1)} %get-tuple-element.272), channel_id=1, source_target_pairs={{0,1},{8,9},{1,17},{9,25},{17,16},{25,24},{2,3},{10,11},{3,19},{11... | collective-permute-start | bytes 1179656 | tf_op jit(solution)/shard_map/ppermute | solution.py:744
  442.2 45.4 %collective-permute-start.21 = (bf16[256,768]{1,0:T(8,128)(2,1)}, bf16[256,768]{1,0:T(8,128)(2,1)S(1)}, u32[]{:S(2)}, u32[]{:S(2)}) collective-permute-start(bf16[256,768]{1,0:T(8,128)(2,1)} %get-tuple-element.316), channel_id=1, source_target_pairs={{1,0},{9,8},{17,1},{25,9},{16,17},{24,25},{3,2},{11,10},{19,3},{27... | collective-permute-start | bytes 1179656 | tf_op jit(solution)/shard_map/ppermute | solution.py:763
  501.8 191.3 %collective-permute-start.23 = (bf16[256,768]{1,0:T(8,128)(2,1)}, bf16[256,768]{1,0:T(8,128)(2,1)S(1)}, u32[]{:S(2)}, u32[]{:S(2)}) collective-permute-start(bf16[256,768]{1,0:T(8,128)(2,1)} %get-tuple-element.334), channel_id=1, source_target_pairs={{1,0},{9,8},{17,1},{25,9},{16,17},{24,25},{3,2},{11,10},{19,3},{27... | collective-permute-start | bytes 1179656 | tf_op jit(solution)/shard_map/ppermute | solution.py:763
  934.6 180.5 %reduce-scatter.5.cloned.1.call-start = ((), (), s32[]{:S(2)}) async-start(), calls=%async_computation.5 | async-start | bytes 3538944 | tf_op jit(solution)/shard_map/reduce_scatter | solution.py:751
  939.2 540.8 %reduce-scatter.3.cloned.1.call-start = ((), (), s32[]{:S(2)}) async-start(), calls=%async_computation.3 | async-start | bytes 3538944 | tf_op jit(solution)/shard_map/reduce_scatter | solution.py:751
  956.7 20.0 %collective-permute-start.34 = (bf16[768,384]{1,0:T(8,128)(2,1)S(1)}, bf16[768,384]{1,0:T(8,128)(2,1)S(1)}, u32[]{:S(2)}, u32[]{:S(2)}) collective-permute-start(bf16[768,384]{1,0:T(8,128)(2,1)S(1)} %fusion.185), channel_id=1, source_target_pairs={{0,8},{8,0},{16,24},{24,16},{1,9},{9,1},{17,25},{25,17},{2,10},{10... | collective-permute-start | bytes 1769480 | tf_op jit(solution)/shard_map/ppermute | solution.py:641
  975.5 40.7 %collective-permute-start.29 = (bf16[768,768]{1,0:T(8,128)(2,1)}, bf16[768,768]{1,0:T(8,128)(2,1)}, u32[]{:S(2)}, u32[]{:S(2)}) collective-permute-start(bf16[768,768]{1,0:T(8,128)(2,1)} %fusion.78), channel_id=1, source_target_pairs={{0,8},{8,0},{16,24},{24,16},{1,9},{9,1},{17,25},{25,17},{2,10},{10... | collective-permute-start | bytes 3538952 | tf_op jit(solution)/shard_map/ppermute | solution.py:641
  975.6 27.7 %collective-permute-start.31 = (bf16[768,768]{1,0:T(8,128)(2,1)}, bf16[768,768]{1,0:T(8,128)(2,1)}, u32[]{:S(2)}, u32[]{:S(2)}) collective-permute-start(bf16[768,768]{1,0:T(8,128)(2,1)} %fusion.88), channel_id=1, source_target_pairs={{0,8},{8,0},{16,24},{24,16},{1,9},{9,1},{17,25},{25,17},{2,10},{10... | collective-permute-start | bytes 3538952 | tf_op jit(solution)/shard_map/ppermute | solution.py:641
  1002.4 26.2 %collective-permute-start.43 = (bf16[768,768]{1,0:T(8,128)(2,1)S(1)}, bf16[768,768]{1,0:T(8,128)(2,1)S(1)}, u32[]{:S(2)}, u32[]{:S(2)}) collective-permute-start(bf16[768,768]{1,0:T(8,128)(2,1)S(1)} %fusion.113), channel_id=1, source_target_pairs={{0,8},{8,0},{16,24},{24,16},{1,9},{9,1},{17,25},{25,17},{2,10},{10... | collective-permute-start | bytes 3538952 | tf_op jit(solution)/shard_map/ppermute | solution.py:641
  1004.8 32.1 %collective-permute-start.32 = (bf16[768,768]{1,0:T(8,128)(2,1)S(1)}, bf16[768,768]{1,0:T(8,128)(2,1)S(1)}, u32[]{:S(2)}, u32[]{:S(2)}) collective-permute-start(bf16[768,768]{1,0:T(8,128)(2,1)S(1)} %add_convert_fusion.21), channel_id=1, source_target_pairs={{0,2},{6,4},{1,3},{7,5},{8,10},{14,12},{9,11},{15,13},{16,18},{22,... | collective-permute-start | bytes 3538952 | tf_op jit(solution)/shard_map/ppermute | solution.py:664
  1017.9 44.3 %collective-permute-start.30 = (bf16[768,768]{1,0:T(8,128)(2,1)S(1)}, bf16[768,768]{1,0:T(8,128)(2,1)}, u32[]{:S(2)}, u32[]{:S(2)}) collective-permute-start(bf16[768,768]{1,0:T(8,128)(2,1)S(1)} %add_convert_fusion.23), channel_id=1, source_target_pairs={{0,2},{6,4},{1,3},{7,5},{8,10},{14,12},{9,11},{15,13},{16,18},{22,... | collective-permute-start | bytes 3538952 | tf_op jit(solution)/shard_map/ppermute | solution.py:664
  1028.9 58.6 %collective-permute-start.44 = (bf16[768,768]{1,0:T(8,128)(2,1)S(1)}, bf16[768,768]{1,0:T(8,128)(2,1)}, u32[]{:S(2)}, u32[]{:S(2)}) collective-permute-start(bf16[768,768]{1,0:T(8,128)(2,1)S(1)} %add_convert_fusion.13), channel_id=1, source_target_pairs={{0,2},{6,4},{1,3},{7,5},{8,10},{14,12},{9,11},{15,13},{16,18},{22,... | collective-permute-start | bytes 3538952 | tf_op jit(solution)/shard_map/ppermute | solution.py:664
  1038.3 51.9 %collective-permute-start.33 = (bf16[768,768]{1,0:T(8,128)(2,1)}, bf16[768,768]{1,0:T(8,128)(2,1)}, u32[]{:S(2)}, u32[]{:S(2)}) collective-permute-start(bf16[768,768]{1,0:T(8,128)(2,1)} %add_convert_fusion.20), channel_id=1, source_target_pairs={{2,4},{4,2},{3,5},{5,3},{10,12},{12,10},{11,13},{13,11},{18,20},{2... | collective-permute-start | bytes 3538952 | tf_op jit(solution)/shard_map/ppermute | solution.py:667
  1046.5 53.2 %collective-permute-start.40 = (bf16[768,768]{1,0:T(8,128)(2,1)S(1)}, bf16[768,768]{1,0:T(8,128)(2,1)S(1)}, u32[]{:S(2)}, u32[]{:S(2)}) collective-permute-start(bf16[768,768]{1,0:T(8,128)(2,1)S(1)} %fusion.103), channel_id=1, source_target_pairs={{0,8},{8,0},{16,24},{24,16},{1,9},{9,1},{17,25},{25,17},{2,10},{10... | collective-permute-start | bytes 3538952 | tf_op jit(solution)/shard_map/ppermute | solution.py:641
  1063.8 46.0 %collective-permute-start.47 = (bf16[768,768]{1,0:T(8,128)(2,1)S(1)}, bf16[768,768]{1,0:T(8,128)(2,1)S(1)}, u32[]{:S(2)}, u32[]{:S(2)}) collective-permute-start(bf16[768,768]{1,0:T(8,128)(2,1)S(1)} %add_convert_fusion.22), channel_id=1, source_target_pairs={{2,4},{4,2},{3,5},{5,3},{10,12},{12,10},{11,13},{13,11},{18,20},{2... | collective-permute-start | bytes 3538952 | tf_op jit(solution)/shard_map/ppermute | solution.py:667
  1089.1 23.4 %collective-permute-start.45 = (bf16[768,768]{1,0:T(8,128)(2,1)S(1)}, bf16[768,768]{1,0:T(8,128)(2,1)S(1)}, u32[]{:S(2)}, u32[]{:S(2)}) collective-permute-start(bf16[768,768]{1,0:T(8,128)(2,1)S(1)} %add_convert_fusion.12), channel_id=1, source_target_pairs={{2,4},{4,2},{3,5},{5,3},{10,12},{12,10},{11,13},{13,11},{18,20},{2... | collective-permute-start | bytes 3538952 | tf_op jit(solution)/shard_map/ppermute | solution.py:667
  1096.0 21.0 %collective-permute-start.38 = (bf16[768,768]{1,0:T(8,128)(2,1)}, bf16[768,768]{1,0:T(8,128)(2,1)}, u32[]{:S(2)}, u32[]{:S(2)}) collective-permute-start(bf16[768,768]{1,0:T(8,128)(2,1)} %fusion.93), channel_id=1, source_target_pairs={{0,8},{8,0},{16,24},{24,16},{1,9},{9,1},{17,25},{25,17},{2,10},{10... | collective-permute-start | bytes 3538952 | tf_op jit(solution)/shard_map/ppermute | solution.py:641
  1100.0 31.6 %collective-permute-start.41 = (bf16[768,768]{1,0:T(8,128)(2,1)S(1)}, bf16[768,768]{1,0:T(8,128)(2,1)}, u32[]{:S(2)}, u32[]{:S(2)}) collective-permute-start(bf16[768,768]{1,0:T(8,128)(2,1)S(1)} %add_convert_fusion.16), channel_id=1, source_target_pairs={{0,2},{6,4},{1,3},{7,5},{8,10},{14,12},{9,11},{15,13},{16,18},{22,... | collective-permute-start | bytes 3538952 | tf_op jit(solution)/shard_map/ppermute | solution.py:664
  1107.9 62.8 %collective-permute-start.57 = (bf16[768,384]{1,0:T(8,128)(2,1)}, bf16[768,384]{1,0:T(8,128)(2,1)}, u32[]{:S(2)}, u32[]{:S(2)}) collective-permute-start(bf16[768,384]{1,0:T(8,128)(2,1)} %broadcast_select_fusion.15), channel_id=1, source_target_pairs={{0,0},{8,1},{1,8},{9,9},{17,16},{25,17},{16,24},{24,25},{2,2},{10,... | collective-permute-start | bytes 1769480 | tf_op jit(solution)/shard_map/ppermute | solution.py:672
  1109.8 27.7 %collective-permute-start.52 = (bf16[768,768]{1,0:T(8,128)(2,1)S(1)}, bf16[768,768]{1,0:T(8,128)(2,1)}, u32[]{:S(2)}, u32[]{:S(2)}) collective-permute-start(bf16[768,768]{1,0:T(8,128)(2,1)S(1)} %add_convert_fusion.19), channel_id=1, source_target_pairs={{2,0},{4,6},{3,1},{5,7},{10,8},{12,14},{11,9},{13,15},{18,16},{20,... | collective-permute-start | bytes 3538952 | tf_op jit(solution)/shard_map/ppermute | solution.py:670
  1112.5 47.8 %collective-permute-start.48 = (bf16[768,768]{1,0:T(8,128)(2,1)}, bf16[768,768]{1,0:T(8,128)(2,1)}, u32[]{:S(2)}, u32[]{:S(2)}) collective-permute-start(bf16[768,768]{1,0:T(8,128)(2,1)} %add_convert_fusion.10), channel_id=1, source_target_pairs={{2,0},{4,6},{3,1},{5,7},{10,8},{12,14},{11,9},{13,15},{18,16},{20,... | collective-permute-start | bytes 3538952 | tf_op jit(solution)/shard_map/ppermute | solution.py:670
  1117.0 68.4 %collective-permute-start.46 = (bf16[768,768]{1,0:T(8,128)(2,1)}, bf16[768,768]{1,0:T(8,128)(2,1)S(1)}, u32[]{:S(2)}, u32[]{:S(2)}) collective-permute-start(bf16[768,768]{1,0:T(8,128)(2,1)} %add_convert_fusion.11), channel_id=1, source_target_pairs={{2,0},{4,6},{3,1},{5,7},{10,8},{12,14},{11,9},{13,15},{18,16},{20,... | collective-permute-start | bytes 3538952 | tf_op jit(solution)/shard_map/ppermute | solution.py:670
  1131.6 67.6 %collective-permute-start.39 = (bf16[768,768]{1,0:T(8,128)(2,1)S(1)}, bf16[768,768]{1,0:T(8,128)(2,1)S(1)}, u32[]{:S(2)}, u32[]{:S(2)}) collective-permute-start(bf16[768,768]{1,0:T(8,128)(2,1)S(1)} %add_convert_fusion.18), channel_id=1, source_target_pairs={{0,2},{6,4},{1,3},{7,5},{8,10},{14,12},{9,11},{15,13},{16,18},{22,... | collective-permute-start | bytes 3538952 | tf_op jit(solution)/shard_map/ppermute | solution.py:664
  1137.4 63.9 %collective-permute-start.42 = (bf16[768,768]{1,0:T(8,128)(2,1)S(1)}, bf16[768,768]{1,0:T(8,128)(2,1)}, u32[]{:S(2)}, u32[]{:S(2)}) collective-permute-start(bf16[768,768]{1,0:T(8,128)(2,1)S(1)} %add_convert_fusion.15), channel_id=1, source_target_pairs={{2,4},{4,2},{3,5},{5,3},{10,12},{12,10},{11,13},{13,11},{18,20},{2... | collective-permute-start | bytes 3538952 | tf_op jit(solution)/shard_map/ppermute | solution.py:667
  1160.2 31.5 %collective-permute-start.53 = (bf16[768,768]{1,0:T(8,128)(2,1)S(1)}, bf16[768,768]{1,0:T(8,128)(2,1)}, u32[]{:S(2)}, u32[]{:S(2)}) collective-permute-start(bf16[768,768]{1,0:T(8,128)(2,1)S(1)} %broadcast_select_fusion.9), channel_id=1, source_target_pairs={{0,0},{8,1},{1,8},{9,9},{17,16},{25,17},{16,24},{24,25},{2,2},{10,... | collective-permute-start | bytes 3538952 | tf_op jit(solution)/shard_map/ppermute | solution.py:672
  1170.6 35.0 %collective-permute-start.49 = (bf16[768,768]{1,0:T(8,128)(2,1)}, bf16[768,768]{1,0:T(8,128)(2,1)S(1)}, u32[]{:S(2)}, u32[]{:S(2)}) collective-permute-start(bf16[768,768]{1,0:T(8,128)(2,1)} %broadcast_select_fusion.10), channel_id=1, source_target_pairs={{0,0},{8,1},{1,8},{9,9},{17,16},{25,17},{16,24},{24,25},{2,2},{10,... | collective-permute-start | bytes 3538952 | tf_op jit(solution)/shard_map/ppermute | solution.py:672
  1185.4 34.6 %collective-permute-start.58 = (bf16[768,768]{1,0:T(8,128)(2,1)}, bf16[768,768]{1,0:T(8,128)(2,1)}, u32[]{:S(2)}, u32[]{:S(2)}) collective-permute-start(bf16[768,768]{1,0:T(8,128)(2,1)} %fusion.143), channel_id=1, source_target_pairs={{0,8},{8,0},{16,24},{24,16},{1,9},{9,1},{17,25},{25,17},{2,10},{10... | collective-permute-start | bytes 3538952 | tf_op jit(solution)/shard_map/ppermute | solution.py:641
  1191.8 70.3 %collective-permute-start.71 = (bf16[768,768]{1,0:T(8,128)(2,1)}, bf16[768,768]{1,0:T(8,128)(2,1)}, u32[]{:S(2)}, u32[]{:S(2)}) collective-permute-start(bf16[768,768]{1,0:T(8,128)(2,1)} %broadcast_select_fusion.11), channel_id=1, source_target_pairs={{0,0},{8,1},{1,8},{9,9},{17,16},{25,17},{16,24},{24,25},{2,2},{10,... | collective-permute-start | bytes 3538952 | tf_op jit(solution)/shard_map/ppermute | solution.py:672
  1199.5 58.5 %collective-permute-start.62 = (bf16[768,768]{1,0:T(8,128)(2,1)S(1)}, bf16[768,768]{1,0:T(8,128)(2,1)}, u32[]{:S(2)}, u32[]{:S(2)}) collective-permute-start(bf16[768,768]{1,0:T(8,128)(2,1)S(1)} %add_convert_fusion.17), channel_id=1, source_target_pairs={{2,4},{4,2},{3,5},{5,3},{10,12},{12,10},{11,13},{13,11},{18,20},{2... | collective-permute-start | bytes 3538952 | tf_op jit(solution)/shard_map/ppermute | solution.py:667
  1203.9 56.6 %collective-permute-start.70 = (bf16[768,768]{1,0:T(8,128)(2,1)}, bf16[768,768]{1,0:T(8,128)(2,1)}, u32[]{:S(2)}, u32[]{:S(2)}) collective-permute-start(bf16[768,768]{1,0:T(8,128)(2,1)} %add_convert_fusion.14), channel_id=1, source_target_pairs={{2,0},{4,6},{3,1},{5,7},{10,8},{12,14},{11,9},{13,15},{18,16},{20,... | collective-permute-start | bytes 3538952 | tf_op jit(solution)/shard_map/ppermute | solution.py:670
  1210.0 24.0 %collective-permute-start.54 = (bf16[768,768]{1,0:T(8,128)(2,1)}, bf16[768,768]{1,0:T(8,128)(2,1)}, u32[]{:S(2)}, u32[]{:S(2)}) collective-permute-start(bf16[768,768]{1,0:T(8,128)(2,1)} %fusion.133), channel_id=1, source_target_pairs={{0,8},{8,0},{16,24},{24,16},{1,9},{9,1},{17,25},{25,17},{2,10},{10... | collective-permute-start | bytes 3538952 | tf_op jit(solution)/shard_map/ppermute | solution.py:641
  1221.6 30.6 %collective-permute-start.59 = (bf16[768,768]{1,0:T(8,128)(2,1)S(1)}, bf16[768,768]{1,0:T(8,128)(2,1)}, u32[]{:S(2)}, u32[]{:S(2)}) collective-permute-start(bf16[768,768]{1,0:T(8,128)(2,1)S(1)} %add_convert_fusion.4), channel_id=1, source_target_pairs={{0,2},{6,4},{1,3},{7,5},{8,10},{14,12},{9,11},{15,13},{16,18},{22,... | collective-permute-start | bytes 3538952 | tf_op jit(solution)/shard_map/ppermute | solution.py:664
  1234.0 35.0 %collective-permute-start.50 = (bf16[768,768]{1,0:T(8,128)(2,1)S(1)}, bf16[768,768]{1,0:T(8,128)(2,1)S(1)}, u32[]{:S(2)}, u32[]{:S(2)}) collective-permute-start(bf16[768,768]{1,0:T(8,128)(2,1)S(1)} %fusion.123), channel_id=1, source_target_pairs={{0,8},{8,0},{16,24},{24,16},{1,9},{9,1},{17,25},{25,17},{2,10},{10... | collective-permute-start | bytes 3538952 | tf_op jit(solution)/shard_map/ppermute | solution.py:641
  1252.2 28.6 %collective-permute-start.55 = (bf16[768,768]{1,0:T(8,128)(2,1)S(1)}, bf16[768,768]{1,0:T(8,128)(2,1)S(1)}, u32[]{:S(2)}, u32[]{:S(2)}) collective-permute-start(bf16[768,768]{1,0:T(8,128)(2,1)S(1)} %add_convert_fusion.7), channel_id=1, source_target_pairs={{0,2},{6,4},{1,3},{7,5},{8,10},{14,12},{9,11},{15,13},{16,18},{22,... | collective-permute-start | bytes 3538952 | tf_op jit(solution)/shard_map/ppermute | solution.py:664
  1258.1 27.2 %collective-permute-start.60 = (bf16[768,768]{1,0:T(8,128)(2,1)S(1)}, bf16[768,768]{1,0:T(8,128)(2,1)S(1)}, u32[]{:S(2)}, u32[]{:S(2)}) collective-permute-start(bf16[768,768]{1,0:T(8,128)(2,1)S(1)} %add_convert_fusion.3), channel_id=1, source_target_pairs={{2,4},{4,2},{3,5},{5,3},{10,12},{12,10},{11,13},{13,11},{18,20},{2... | collective-permute-start | bytes 3538952 | tf_op jit(solution)/shard_map/ppermute | solution.py:667
  1267.7 29.5 %collective-permute-start.63 = (bf16[768,768]{1,0:T(8,128)(2,1)S(1)}, bf16[768,768]{1,0:T(8,128)(2,1)S(1)}, u32[]{:S(2)}, u32[]{:S(2)}) collective-permute-start(bf16[768,768]{1,0:T(8,128)(2,1)S(1)} %add_convert_fusion.1), channel_id=1, source_target_pairs={{2,0},{4,6},{3,1},{5,7},{10,8},{12,14},{11,9},{13,15},{18,16},{20,... | collective-permute-start | bytes 3538952 | tf_op jit(solution)/shard_map/ppermute | solution.py:670
  1269.0 28.3 %collective-permute-start.82 = (bf16[768,768]{1,0:T(8,128)(2,1)S(1)}, bf16[768,768]{1,0:T(8,128)(2,1)S(1)}, u32[]{:S(2)}, u32[]{:S(2)}) collective-permute-start(bf16[768,768]{1,0:T(8,128)(2,1)S(1)} %broadcast_select_fusion.6), channel_id=1, source_target_pairs={{0,0},{8,1},{1,8},{9,9},{17,16},{25,17},{16,24},{24,25},{2,2},{10,... | collective-permute-start | bytes 3538952 | tf_op jit(solution)/shard_map/ppermute | solution.py:672
  1272.9 46.7 %collective-permute-start.51 = (bf16[768,768]{1,0:T(8,128)(2,1)S(1)}, bf16[768,768]{1,0:T(8,128)(2,1)S(1)}, u32[]{:S(2)}, u32[]{:S(2)}) collective-permute-start(bf16[768,768]{1,0:T(8,128)(2,1)S(1)} %add_convert_fusion.9), channel_id=1, source_target_pairs={{0,2},{6,4},{1,3},{7,5},{8,10},{14,12},{9,11},{15,13},{16,18},{22,... | collective-permute-start | bytes 3538952 | tf_op jit(solution)/shard_map/ppermute | solution.py:664
  1280.8 37.9 %collective-permute-start.73 = (bf16[384,768]{1,0:T(8,128)(2,1)S(1)}, bf16[384,768]{1,0:T(8,128)(2,1)S(1)}, u32[]{:S(2)}, u32[]{:S(2)}) collective-permute-start(bf16[384,768]{1,0:T(8,128)(2,1)S(1)} %fusion.197), channel_id=1, source_target_pairs={{0,2},{6,4},{1,3},{7,5},{8,10},{14,12},{9,11},{15,13},{16,18},{22,... | collective-permute-start | bytes 1769480 | tf_op jit(solution)/shard_map/ppermute | solution.py:664
  1285.2 41.1 %collective-permute-start.56 = (bf16[768,768]{1,0:T(8,128)(2,1)S(1)}, bf16[768,768]{1,0:T(8,128)(2,1)S(1)}, u32[]{:S(2)}, u32[]{:S(2)}) collective-permute-start(bf16[768,768]{1,0:T(8,128)(2,1)S(1)} %add_convert_fusion.6), channel_id=1, source_target_pairs={{2,4},{4,2},{3,5},{5,3},{10,12},{12,10},{11,13},{13,11},{18,20},{2... | collective-permute-start | bytes 3538952 | tf_op jit(solution)/shard_map/ppermute | solution.py:667
  1298.2 26.6 %collective-permute-start.83 = (bf16[384,768]{1,0:T(8,128)(2,1)S(1)}, bf16[384,768]{1,0:T(8,128)(2,1)S(1)}, u32[]{:S(2)}, u32[]{:S(2)}) collective-permute-start(bf16[384,768]{1,0:T(8,128)(2,1)S(1)} %fusion.215), channel_id=1, source_target_pairs={{0,8},{8,0},{16,24},{24,16},{1,9},{9,1},{17,25},{25,17},{2,10},{10... | collective-permute-start | bytes 1769480 | tf_op jit(solution)/shard_map/ppermute | solution.py:641
  1300.5 34.5 %collective-permute-start.61 = (bf16[768,768]{1,0:T(8,128)(2,1)S(1)}, bf16[768,768]{1,0:T(8,128)(2,1)S(1)}, u32[]{:S(2)}, u32[]{:S(2)}) collective-permute-start(bf16[768,768]{1,0:T(8,128)(2,1)S(1)} %add_convert_fusion.2), channel_id=1, source_target_pairs={{2,0},{4,6},{3,1},{5,7},{10,8},{12,14},{11,9},{13,15},{18,16},{20,... | collective-permute-start | bytes 3538952 | tf_op jit(solution)/shard_map/ppermute | solution.py:670
  1318.8 22.2 %collective-permute-start.88 = (bf16[384,768]{1,0:T(8,128)(2,1)S(1)}, bf16[384,768]{1,0:T(8,128)(2,1)S(1)}, u32[]{:S(2)}, u32[]{:S(2)}) collective-permute-start(bf16[384,768]{1,0:T(8,128)(2,1)S(1)} %add_convert_fusion.27), channel_id=1, source_target_pairs={{2,4},{4,2},{3,5},{5,3},{10,12},{12,10},{11,13},{13,11},{18,20},{2... | collective-permute-start | bytes 1769480 | tf_op jit(solution)/shard_map/ppermute | solution.py:667
  1324.8 37.4 %collective-permute-start.74 = (bf16[768,768]{1,0:T(8,128)(2,1)S(1)}, bf16[768,768]{1,0:T(8,128)(2,1)S(1)}, u32[]{:S(2)}, u32[]{:S(2)}) collective-permute-start(bf16[768,768]{1,0:T(8,128)(2,1)S(1)} %add_convert_fusion.8), channel_id=1, source_target_pairs={{2,4},{4,2},{3,5},{5,3},{10,12},{12,10},{11,13},{13,11},{18,20},{2... | collective-permute-start | bytes 3538952 | tf_op jit(solution)/shard_map/ppermute | solution.py:667
  1342.4 43.6 %collective-permute-start.75 = (bf16[768,768]{1,0:T(8,128)(2,1)S(1)}, bf16[768,768]{1,0:T(8,128)(2,1)S(1)}, u32[]{:S(2)}, u32[]{:S(2)}) collective-permute-start(bf16[768,768]{1,0:T(8,128)(2,1)S(1)} %add_convert_fusion.5), channel_id=1, source_target_pairs={{2,0},{4,6},{3,1},{5,7},{10,8},{12,14},{11,9},{13,15},{18,16},{20,... | collective-permute-start | bytes 3538952 | tf_op jit(solution)/shard_map/ppermute | solution.py:670
  1346.1 40.8 %collective-permute-start.76 = (bf16[768,768]{1,0:T(8,128)(2,1)S(1)}, bf16[768,768]{1,0:T(8,128)(2,1)S(1)}, u32[]{:S(2)}, u32[]{:S(2)}) collective-permute-start(bf16[768,768]{1,0:T(8,128)(2,1)S(1)} %broadcast_select_fusion.8), channel_id=1, source_target_pairs={{0,0},{8,1},{1,8},{9,9},{17,16},{25,17},{16,24},{24,25},{2,2},{10,... | collective-permute-start | bytes 3538952 | tf_op jit(solution)/shard_map/ppermute | solution.py:672
  1362.1 89.9 %collective-permute-start.90 = (bf16[384,768]{1,0:T(8,128)(2,1)S(1)}, bf16[384,768]{1,0:T(8,128)(2,1)S(1)}, u32[]{:S(2)}, u32[]{:S(2)}) collective-permute-start(bf16[384,768]{1,0:T(8,128)(2,1)S(1)} %broadcast_select_fusion.12), channel_id=1, source_target_pairs={{0,0},{8,1},{1,8},{9,9},{17,16},{25,17},{16,24},{24,25},{2,2},{10,... | collective-permute-start | bytes 1769480 | tf_op jit(solution)/shard_map/ppermute | solution.py:672
  1367.1 62.6 %collective-permute-start.92 = (bf16[768,768]{1,0:T(8,128)(2,1)S(1)}, bf16[768,768]{1,0:T(8,128)(2,1)S(1)}, u32[]{:S(2)}, u32[]{:S(2)}) collective-permute-start(bf16[768,768]{1,0:T(8,128)(2,1)S(1)} %add_convert_fusion), channel_id=1, source_target_pairs={{2,0},{4,6},{3,1},{5,7},{10,8},{12,14},{11,9},{13,15},{18,16},{20,... | collective-permute-start | bytes 3538952 | tf_op jit(solution)/shard_map/ppermute | solution.py:670
  1373.1 50.8 %collective-permute-start.86 = (bf16[384,768]{1,0:T(8,128)(2,1)S(1)}, bf16[384,768]{1,0:T(8,128)(2,1)S(1)}, u32[]{:S(2)}, u32[]{:S(2)}) collective-permute-start(bf16[384,768]{1,0:T(8,128)(2,1)S(1)} %add_convert_fusion.25), channel_id=1, source_target_pairs={{2,0},{4,6},{3,1},{5,7},{10,8},{12,14},{11,9},{13,15},{18,16},{20,... | collective-permute-start | bytes 1769480 | tf_op jit(solution)/shard_map/ppermute | solution.py:670
  1386.0 51.5 %collective-permute-start.67 = (bf16[768,384]{1,0:T(8,128)(2,1)S(1)}, bf16[768,384]{1,0:T(8,128)(2,1)S(1)}, u32[]{:S(2)}, u32[]{:S(2)}) collective-permute-start(bf16[768,384]{1,0:T(8,128)(2,1)S(1)} %add_convert_fusion.29), channel_id=1, source_target_pairs={{2,4},{4,2},{3,5},{5,3},{10,12},{12,10},{11,13},{13,11},{18,20},{2... | collective-permute-start | bytes 1769480 | tf_op jit(solution)/shard_map/ppermute | solution.py:667
  1386.8 81.1 %collective-permute-start.91 = (bf16[768,768]{1,0:T(8,128)(2,1)S(1)}, bf16[768,768]{1,0:T(8,128)(2,1)S(1)}, u32[]{:S(2)}, u32[]{:S(2)}) collective-permute-start(bf16[768,768]{1,0:T(8,128)(2,1)S(1)} %broadcast_select_fusion.5), channel_id=1, source_target_pairs={{0,0},{8,1},{1,8},{9,9},{17,16},{25,17},{16,24},{24,25},{2,2},{10,... | collective-permute-start | bytes 3538952 | tf_op jit(solution)/shard_map/ppermute | solution.py:672
  1426.0 34.1 %collective-permute-start.87 = (bf16[384,768]{1,0:T(8,128)(2,1)S(1)}, bf16[384,768]{1,0:T(8,128)(2,1)S(1)}, u32[]{:S(2)}, u32[]{:S(2)}) collective-permute-start(bf16[384,768]{1,0:T(8,128)(2,1)S(1)} %broadcast_select_fusion.13), channel_id=1, source_target_pairs={{0,0},{8,1},{1,8},{9,9},{17,16},{25,17},{16,24},{24,25},{2,2},{10,... | collective-permute-start | bytes 1769480 | tf_op jit(solution)/shard_map/ppermute | solution.py:672
  1434.6 33.4 %collective-permute-start.93 = (bf16[768,768]{1,0:T(8,128)(2,1)S(1)}, bf16[768,768]{1,0:T(8,128)(2,1)S(1)}, u32[]{:S(2)}, u32[]{:S(2)}) collective-permute-start(bf16[768,768]{1,0:T(8,128)(2,1)S(1)} %broadcast_select_fusion.4), channel_id=1, source_target_pairs={{0,0},{8,1},{1,8},{9,9},{17,16},{25,17},{16,24},{24,25},{2,2},{10,... | collective-permute-start | bytes 3538952 | tf_op jit(solution)/shard_map/ppermute | solution.py:672
  (94 other events, 1008.9 us)
Sparse Core Ops, SparseCore 0:
  67.6 38.6 all-gather.2
  215.7 36.8 all-gather.4
  934.7 30.7 all-reduce.2
  969.1 49.0 reduce-scatter.4
  1022.0 46.2 reduce-scatter.2

commit v3 on v2

--- a/solution.py
+++ b/solution.py
@@ -81,7 +81,7 @@
 FWD_STATE = ("x", "h1", "h2", "q", "qt", "o", "ot", "a", "g", "l", "kd", "vd", "kt", "vt", "y")
 BWD_STATE = ("db", "du", "dq", "dkv", "dkw", "acc", "accu", "gin")
 READ = ("x", "q", "qt", "ot", "g", "l", "kd", "vd", "kt")
-N_W = 8
+N_W = 16
 
 
 def state_shapes(length, width, hidden):
@@ -95,15 +95,26 @@
     return fwd, bwd
 
 
-def weight_copies(stored, weights, wsems, slot):
-    copies = {}
-    for n, name in enumerate("qoih"):
-        copies[name] = [pltpu.make_async_copy(stored[2 * n + k].at[slot], weights[2 * n + k].at[slot], wsems.at[slot, 2 * n + k]) for k in range(2)]
-    return copies
+def weight_waits(stored, weights, wsems, place):
+    return {
+        name: [pltpu.make_async_copy(stored[4 * n + 2 * k], weights[2 * n + k].at[place], wsems.at[place, 2 * n + k]) for k in range(2)]
+        for n, name in enumerate("qoih")
+    }
+
+
+def start_weights(stored, weights, wsems, place, names):
+    for held in range(2):
+
+        @pl.when(place == held)
+        def _():
+            for name in names:
+                n = "qoih".index(name)
+                for k in range(2):
+                    pltpu.make_async_copy(stored[4 * n + 2 * k + held], weights[2 * n + k].at[held], wsems.at[held, 2 * n + k]).start()
 
 
 def weight_scratch(weights):
-    return [pltpu.VMEM(w.shape, BF16) for w in weights]
+    return [pltpu.VMEM((2, *w.shape), BF16) for w in weights[::2]]
 
 
 def make_struct(item):
@@ -130,17 +141,14 @@
 
         @pl.when(sc[2] == 1)
         def _():
-            pltpu.make_async_copy(seq_in.at[place], x_s, once.at[0]).start()
+            pltpu.make_async_copy(seq_in.at[sc[4], place], x_s, once.at[0]).start()
 
         @pl.when(sc[2] == 0)
         def _():
             pltpu.make_async_copy(hop_in, x_s, once.at[0]).start()
 
         for j in range(2):
-            copies = weight_copies(stored, weights, wsems, j ^ sc[3])
-            for name in "qioh":
-                for copy in copies[name]:
-                    copy.start()
+            start_weights(stored, weights, wsems, j ^ sc[3], "qioh")
         kd_in = pltpu.make_async_copy(st["kd"], kd_s, once.at[1])
         vt_in = pltpu.make_async_copy(st["vt"], vt_s, once.at[2])
         kd_in.start()
@@ -165,7 +173,7 @@
 
         def layer(j):
             w = j ^ sc[3]
-            loads = weight_copies(stored, weights, wsems, w)
+            loads = weight_waits(stored, weights, wsems, w)
             save = saves(j)
             save["x"].start()
 
@@ -288,8 +296,8 @@
 
 def fwd_call(rows, state, sc, hop, seq, params, weights):
     small, bi, cos, ahead, behind, wkv = params
-    length, width = seq.shape
-    half, hid = weights[0].shape[2], weights[4].shape[2]
+    _, length, width = seq.shape
+    half, hid = weights[0].shape[1], weights[8].shape[1]
     hidden, pairs = 2 * hid, width // LANES
     shapes, _ = state_shapes(length, width, hidden)
     fresh = state is None
@@ -358,7 +366,7 @@
 
         @pl.when(sc[2] == 1)
         def _():
-            pltpu.make_async_copy(cot.at[place], in_s, once.at[0]).start()
+            pltpu.make_async_copy(cot.at[sc[4], place], in_s, once.at[0]).start()
 
         @pl.when(sc[2] == 0)
         def _():
@@ -373,13 +381,10 @@
 
         shared = [pltpu.make_async_copy(rd[n], b, once.at[1 + i]) for i, (n, b) in enumerate((("kd", kd_s), ("vd", vd_s), ("kt", kt_s)))]
         for j in (1, 0):
-            copies = weight_copies(stored, weights, wsems, j ^ sc[3])
-            for copy in copies["o"] + list(gets(j).values()):
+            start_weights(stored, weights, wsems, j ^ sc[3], "o")
+            for copy in list(gets(j).values()) + (shared if j == 1 else []):
                 copy.start()
-            for copy in shared if j == 1 else ():
-                copy.start()
-            for copy in copies["q"] + copies["h"] + copies["i"]:
-                copy.start()
+            start_weights(stored, weights, wsems, j ^ sc[3], "qhi")
         running = (("dkw", dkw_s), ("acc", acc_s), ("accu", accu_s))
 
         @pl.when(m == chunks - 1)
@@ -408,7 +413,7 @@
         def layer(step):
             j = 1 - step
             w = j ^ sc[3]
-            loads = weight_copies(stored, weights, wsems, w)
+            loads = weight_waits(stored, weights, wsems, w)
             got, save = gets(j), saves(j)
             grad = dy_s[...]
             db_s[j] = grad.astype(BF16)
@@ -538,8 +543,8 @@
 
 def bwd_call(rows, chunks, state, sc, scale, hop, cot, params, weights, fwd):
     small, cos, ahead, behind, wkv = params
-    length, width = cot.shape
-    half, hid = weights[0].shape[2], weights[4].shape[2]
+    _, length, width = cot.shape
+    half, hid = weights[0].shape[1], weights[8].shape[1]
     hidden, pairs, tiles = 2 * hid, width // LANES, 2 * hid // width
     _, shapes = state_shapes(length, width, hidden)
     fresh = state is None
@@ -649,28 +654,25 @@
     return lax.optimization_barrier((value, *others))[0]
 
 
-def line_sums(pieces, make):
+def line_sums(count, make):
     position = lax.axis_index("dp")
     at_end = (position == 0) | (position == 3)
-    count = len(pieces)
     own, first, second, third, done = [], [], [], [], []
-    for r in range(count + 5):
+    for r in range(count + 4):
         if r < count:
-            ties = [chain[n] for chain, n in ((first, r - 3), (second, r - 4), (third, r - 5), (done, r - 6)) if n >= 0]
-            mine, theirs = make(pieces[r], ties)
-            own.append((mine, other_core(theirs)))
+            ties = [chain[n] for chain, n in ((first, r - 2), (second, r - 3), (third, r - 4), (done, r - 5)) if n >= 0]
+            mine, theirs = make(r, ties)
+            term = added(mine, other_core(theirs))
+            first.append(added(term, lax.ppermute(term, "dp", [(0, 1), (3, 2)])))
         if 0 <= r - 1 < count:
-            term = added(*own[r - 1])
-            first.append(added(term, lax.ppermute(term, "dp", [(0, 1), (3, 2)])))
+            part = first[r - 1]
+            second.append(added(part, lax.ppermute(part, "dp", [(1, 2), (2, 1)])))
         if 0 <= r - 2 < count:
-            part = first[r - 2]
-            second.append(added(part, lax.ppermute(part, "dp", [(1, 2), (2, 1)])))
+            whole = second[r - 2]
+            third.append(jnp.where(at_end, lax.ppermute(whole, "dp", [(1, 0), (2, 3)]), whole))
         if 0 <= r - 3 < count:
-            whole = second[r - 3]
-            third.append(jnp.where(at_end, lax.ppermute(whole, "dp", [(1, 0), (2, 3)]), whole))
-        if 0 <= r - 4 < count:
-            done.append(lax.ppermute(third[r - 4], PLANE, DELIVER))
-    return done
+            done.append(lax.ppermute(third[r - 3], PLANE, DELIVER))
+    return done, first
 
 
 def local(
@@ -701,16 +703,17 @@
 
     parity = lax.axis_index("dp") % 2
     pairs = [(i, i ^ 1) for i in range(lax.axis_size("dp"))]
-    halves = {}
-    for name, whole in (("h", w_hid_out), ("i", w_in), ("o", w_out), ("q", w_query)):
-        fetched = lax.ppermute(lax.dynamic_index_in_dim(whole[0], parity, 0, keepdims=False), PLANE, FETCH)
-        swapped = lax.ppermute(fetched, "dp", pairs)
-        mine = jnp.stack([fetched, swapped])
-        halves[name] = [mine, other_core(mine)]
-    weights = [w for name in "qoih" for w in halves[name]]
+    wholes = (w_in, w_query, w_out, w_hid_out)
+    fetched = [lax.ppermute(lax.dynamic_index_in_dim(w[0], parity, 0, keepdims=False), PLANE, FETCH) for w in wholes]
+    swapped = [lax.ppermute(w, "dp", pairs) for w in fetched]
+    held = dict(zip("iqoh", zip(fetched, [after(w, fetched[3]) for w in fetched], swapped, [after(w, swapped[3]) for w in swapped])))
+    weights = []
+    for name in "qoih":
+        near, tied_near, far, tied_far = held[name]
+        weights += [near, far, other_core(tied_near), other_core(tied_far)]
     vectors = jnp.concatenate([v.reshape(-1) for v in (ln_gain, ln_bias, out_bias, b_kv, b_query, b_in)]).reshape(-1, LANES)
-    vectors = lax.ppermute(vectors, PLANE, FETCH)
-    own_kv = lax.ppermute(w_kv[0], PLANE, FETCH)
+    vectors = lax.ppermute(after(vectors, fetched[3]), PLANE, FETCH)
+    own_kv = lax.ppermute(after(w_kv[0], fetched[3]), PLANE, FETCH)
     flat, flat_other = vectors.reshape(-1), other_core(vectors).reshape(-1)
     edge = 12 * width + LANES
     bkv = flat[12 * width : edge]
@@ -721,8 +724,7 @@
     small = jnp.concatenate([*norms, bq, jnp.broadcast_to(bkv, (2, 1, width))], axis=1)
     wide_kv = jnp.concatenate([own_kv[:, :HD], own_kv[:, :HD], own_kv[:, HD:], own_kv[:, HD:]], axis=1)
 
-    whole_in = lax.all_gather(inputs, PLANE, axis=1, tiled=True)
-    my_in = lax.dynamic_index_in_dim(whole_in, core, 0, keepdims=False)
+    whole_in = lax.all_gather(after(inputs, fetched[3]), PLANE, axis=1, tiled=True)
     my_id = lax.dynamic_index_in_dim(subset_ids, core, 0, keepdims=False)
     matches = my_id == jnp.arange(subset_weight.shape[0], dtype=jnp.int32)
     weight = jnp.sum(jnp.where(matches, subset_weight, 0.0))
@@ -736,13 +738,12 @@
     for tick in range(ticks):
         number = tick - stage
         valid = (number >= 0) & (number < chunks)
-        sc = jnp.stack([valid.astype(jnp.int32), jnp.clip(number, 0, chunks - 1), is_first.astype(jnp.int32), parity])
-        saved, hop = fwd_call(ROWS, saved, sc, hop, my_in, forward_params, weights)
+        sc = jnp.stack([valid.astype(jnp.int32), jnp.clip(number, 0, chunks - 1), is_first.astype(jnp.int32), parity, core])
+        saved, hop = fwd_call(ROWS, saved, sc, hop, whole_in, forward_params, weights)
         if tick == 0:
             whole_cot = lax.all_gather(after(cotangent, hop), PLANE, axis=1, tiled=True)
         if tick < ticks - 1:
             hop = lax.ppermute(hop, PLANE, AHEAD)
-    my_cot = lax.dynamic_index_in_dim(whole_cot, core, 0, keepdims=False)
     kept = dict(zip(FWD_STATE, saved))
 
     def spread(mine_only, here):
@@ -757,53 +758,63 @@
     for tick in range(ticks):
         number = chunks - 1 - tick + (3 - stage)
         valid = (number >= 0) & (number < chunks)
-        sc = jnp.stack([valid.astype(jnp.int32), jnp.clip(number, 0, chunks - 1), is_last.astype(jnp.int32), parity])
-        back, hop = bwd_call(ROWS, chunks, back, sc, scale, hop, my_cot, backward_params, weights, saved)
+        sc = jnp.stack([valid.astype(jnp.int32), jnp.clip(number, 0, chunks - 1), is_last.astype(jnp.int32), parity, core])
+        back, hop = bwd_call(ROWS, chunks, back, sc, scale, hop, whole_cot, backward_params, weights, saved)
         if tick < ticks - 1:
             hop = lax.ppermute(hop, PLANE, BEHIND)
     got = dict(zip(BWD_STATE, back))
-    input_grad = spread(got["gin"], is_first).astype(F32)
-
-    sources = {"h": ("a", "db"), "i": ("h2", "du"), "o": ("o", "db"), "q": ("h1", "dq"), "kv": ("h1", "dkv")}
-
-    def terms(piece, ties):
-        name, slot, start, size = piece
-        left, right = kept[sources[name][0]][slot], got[sources[name][1]]
-        right = after(right, *ties) if ties else right
-        if name == "kv":
-            one = dot(left, right, ((0,), (0,))).astype(BF16)
-            return one, one
-        right = right[slot]
+
+    def part(values, slot, start, size):
+        return lax.slice(values, (slot, 0, start), (slot + 1, length, start + size)).reshape(length, size)
+
+    def product(left, right):
+        return dot(left, right, ((0,), (0,))).astype(BF16)
+
+    def outer(slot, ties):
+        grad = after(got["db"], *ties) if ties else got["db"]
         both = []
         for k in range(2):
-            if name in "ho":
-                at = k * (hid if name == "h" else half) + start
-                both.append(dot(left[:, at : at + size], right, ((0,), (0,))).astype(BF16))
-            else:
-                at = k * (hid if name == "i" else half) + start
-                both.append(dot(left, right[:, at : at + size], ((0,), (0,))).astype(BF16))
+            rows = [
+                product(part(kept["o"], slot, k * half, half), part(grad, slot, 0, width)),
+                product(part(got["dq"], slot, k * half, half), part(kept["h1"], slot, 0, width)),
+            ]
+            if slot == 0:
+                rows.append(product(got["dkv"], part(kept["h1"], slot, 0, width)))
+            both.append(jnp.concatenate(rows))
         return both
 
-    pieces = [("q", 1, 0, half)]
-    for slot in (1, 0):
-        for name in "hi":
-            pieces += [(name, slot, at, hid // 2) for at in (0, hid // 2)]
-    pieces += [("o", 1, 0, half), ("o", 0, 0, half), ("q", 0, 0, half), ("kv", 0, 0, 0)]
+    def inner_out(slot, ties):
+        grad = after(got["db"], *ties) if ties else got["db"]
+        return [product(part(kept["a"], slot, k * hid, hid), part(grad, slot, 0, width)) for k in range(2)]
+
+    def inner_in(slot, ties):
+        grad = after(got["du"], *ties) if ties else got["du"]
+        return [product(part(kept["h2"], slot, 0, width), part(grad, slot, k * hid, hid)) for k in range(2)]
+
+    makers = (
+        lambda ties: outer(1, ties),
+        lambda ties: inner_out(1, ties),
+        lambda ties: inner_in(1, ties),
+        lambda ties: inner_out(0, ties),
+        lambda ties: inner_in(0, ties),
+        lambda ties: outer(0, ties),
+    )
     if lax.axis_size("dp") == 4:
-        done = line_sums(pieces, terms)
+        done, sent = line_sums(len(makers), lambda n, ties: makers[n](ties))
+        later = after(got["gin"], sent[0])
     else:
         done = []
-        for piece in pieces:
-            mine, theirs = terms(piece, [])
+        for make in makers:
+            mine, theirs = make([])
             done.append(lax.ppermute(lax.psum(added(mine, other_core(theirs)), "dp"), PLANE, DELIVER))
-    done = dict(zip(pieces, done))
-
-    def joined(name, size, axis):
-        slots = []
-        for slot in range(2):
-            parts = [done[p].astype(F32) for p in pieces if p[:2] == (name, slot)]
-            slots.append(jnp.concatenate(parts, axis=axis))
-        return jnp.stack(slots)[None]
+        later = got["gin"]
+    input_grad = spread(later, is_first).astype(F32)
+    out_grad = jnp.stack([done[5][:half], done[0][:half]])[None].astype(F32)
+    query_grad = jnp.stack([done[5][half : 2 * half], done[0][half : 2 * half]]).astype(F32)
+    query_grad = jnp.swapaxes(query_grad, 1, 2)[None]
+    kv_grad = jnp.swapaxes(done[5][2 * half :].astype(F32), 0, 1)[None]
+    in_grad = jnp.stack([done[4], done[2]])[None].astype(F32)
+    hid_out_grad = jnp.stack([done[3], done[1]])[None].astype(F32)
 
     query = jnp.sum(got["acc"], axis=2)
     inner = jnp.sum(got["accu"], axis=2)
@@ -823,15 +834,15 @@
         input_grad,
         gain_grad,
         bias_grad,
-        joined("q", half, 1),
+        query_grad,
         bq_grad,
-        done["kv", 0, 0, 0].astype(F32)[None],
+        kv_grad,
         acc[0, 6, : 2 * HD][None],
-        joined("o", half, 0),
+        out_grad,
         out_bias_grad,
-        joined("i", hid, 1),
+        in_grad,
         bi_grad,
-        joined("h", hid, 0),
+        hid_out_grad,
     )
 
 

time: 1500 us -> 1510 us (level)
  waiting for transfers between devices: 629 us -> 750 us
  starting transfers between devices: 265 us -> 168 us
    ppermute x13 -> x6, waiting for transfers between devices: 108 us -> 170 us  [line_sums(): first.append(added(term, lax.ppermute(term, 'dp', [(0, 1), (3, 2)])))]
    ppermute x23 -> x16, starting transfers between devices: 71.8 us -> 35.7 us  [the longest x6 13.3 us: line_sums(): done.append(lax.ppermute(third[r - 3], PLANE, DELIVER))]
    ppermute x23 -> x16, waiting for transfers between devices: 115 us -> 146 us  [the longest x4 67.1 us: local(): lax.ppermute(lax.dynamic_index_in_dim(w[0], parity, 0, keepdims=False), P...]
    ppermute x13 -> x6, starting transfers between devices: 59.1 us -> 30.1 us  [line_sums(): first.append(added(term, lax.ppermute(term, 'dp', [(0, 1), (3, 2)])))]
    squeeze x14 -> x4, local copies, waits for them, and re-layouts: 32.9 us -> 6.33 us  [local(): lax.dynamic_index_in_dim(w[0], parity, 0, keepdims=False)]
    another operation x22 -> x0, other arithmetic: 23.2 us -> none  [the longest x4 11.8 us: local(): mine = jnp.stack([fetched, swapped])]
    ppermute x13 -> x6, waiting for transfers between devices: 109 us -> 131 us  [line_sums(): lax.ppermute(whole, 'dp', [(1, 0), (2, 3)])]
    convert_element_type x1 -> x4, other arithmetic: 1.93 us -> 17 us  [the longest x1 6.82 us: local(): in_grad = jnp.stack([done[4], done[2]])[None].astype(F32)]
  transfers between devices with their start and end apart: 99 -> 68, of which waited for: 44 -> 36; matrix products, arithmetic and copies ran while one was open for 14% -> 13% of each run, Pallas kernels for 8% -> 8%
where the time goes in v3:
time: 1510 us; the launch traced here: 1500 us
  waiting for transfers between devices  750 us (50%)
  Pallas kernels  352 us (23%)
  starting transfers between devices  168 us (11%)
  other arithmetic  97.5 us (6%)
  matrix products  58.9 us (4%)
  local copies, waits for them, and re-layouts  54.7 us (4%)
  between operations  16.1 us (1%)
    ppermute x6, waiting for transfers between devices, local(): hop = lax.ppermute(hop, PLANE, BEHIND)  265 us
    pallas_call x7, Pallas kernels, bwd_call(): pl.pallas_call(functools.partial(bwd_kernel, rows, chunks, fresh), out_sh...  198 us
    ppermute x6, waiting for transfers between devices, line_sums(): first.append(added(term, lax.ppermute(term, 'dp', [(0, 1), (3, 2)])))  170 us
    pallas_call x7, Pallas kernels, fwd_call(): pl.pallas_call(functools.partial(fwd_kernel, rows, fresh), out_shape=[mak...  154 us
    ppermute x6, waiting for transfers between devices, line_sums(): lax.ppermute(whole, 'dp', [(1, 0), (2, 3)])  131 us
    ppermute x4, waiting for transfers between devices, local(): lax.ppermute(lax.dynamic_index_in_dim(w[0], parity, 0, keepdims=False), P...  67.1 us
    dot_general x17, matrix products, dot(): lax.dot_general(left, right, (dims, ((), ())), preferred_element_type=F32)  58.9 us
    ppermute x6, starting transfers between devices, local(): hop = lax.ppermute(hop, PLANE, AHEAD)  56.2 us
  transfers between devices with their start and end apart: 68, of which 36 were waited for; matrix products, arithmetic and copies ran while one was open for 13% of the time, Pallas kernels for 8%

profile of v3, /device:TPU:1, one launch (start us, length us, event | category | flops | bytes accessed | tf_op | source)
XLA Modules:
  0.0 1497.2 jit_solution(16028199453267904650)
XLA Ops:
  9.2 4.7 collective-permute-start
  17.4 23.4 %collective-permute-done.refs_21_ = bf16[1536,768]{1,0:T(8,128)(2,1)S(1)} collective-permute-done((bf16[1536,768]{1,0:T(8,128)(2,1)S(1)}, bf16[1536,768]{1,0:T(8,128)(2,1)S(1)}, u32[]{:S(2)}, u32[]{:S(2)}) %collective-permute-start) | collective-permute-done | bytes 2359328 | tf_op jit(solution)/shard_map/ppermute | solution.py:707
  42.3 35.5 %collective-permute-done.13.refs_17_ = bf16[768,1536]{1,0:T(8,128)(2,1)} collective-permute-done((bf16[768,1536]{1,0:T(8,128)(2,1)}, bf16[768,1536]{1,0:T(8,128)(2,1)}, u32[]{:S(2)}, u32[]{:S(2)}) %collective-permute-start.13) | collective-permute-done | bytes 2359328 | tf_op jit(solution)/shard_map/ppermute | solution.py:707
  79.6 4.7 collective-permute-start.4
  94.2 4.6 collective-permute-done.9.refs_13_
  106.5 38.5 %collective-permute-done.14.refs_18_ = bf16[768,1536]{1,0:T(8,128)(2,1)} collective-permute-done((bf16[768,1536]{1,0:T(8,128)(2,1)}, bf16[768,1536]{1,0:T(8,128)(2,1)}, u32[]{:S(2)}, u32[]{:S(2)}) %collective-permute-start.14) | collective-permute-done | bytes 2359328 | tf_op jit(solution)/shard_map/ppermute | solution.py:708
  145.0 10.4 collective-permute-done.5.refs_10_
  156.7 5.0 collective-permute-done.10.refs_14_
  171.6 4.3 collective-permute-done.3.refs_8_
  198.3 33.6 %section_forward.7 = (f32[2,1024,768]{2,1,0:T(8,128)}, bf16[2,1024,768]{2,1,0:T(8,128)(2,1)}, bf16[2,1024,768]{2,1,0:T(8,128)(2,1)}, bf16[2,1024,768]{2,1,0:T(8,...) custom-call(s32[5]{0:T(128)} %stack.251.refs_0_, ...), custom_call_target="tpu_custom_call" | custom-call | tf_op jit(solution)/shard_map/section_forward/pallas_call | solution.py:334
  233.8 9.1 collective-permute-done.19.refs_1_
  243.7 33.8 %section_forward.8 = (f32[2,1024,768]{2,1,0:T(8,128)}, bf16[2,1024,768]{2,1,0:T(8,128)(2,1)}, bf16[2,1024,768]{2,1,0:T(8,128)(2,1)}, bf16[2,1024,768]{2,1,0:T(8,...) custom-call(s32[5]{0:T(128)} %stack.247.refs_0_, ...), custom_call_target="tpu_custom_call", output_to_operand_aliasing={{0}: (25, {}), {1}: (26, {}), {2}: (27, {}), {3}: (28, {}),... | custom-call | tf_op jit(solution)/shard_map/section_forward/pallas_call | solution.py:334
  277.4 4.1 collective-permute-start.20
  282.2 6.1 collective-permute-done.20.refs_1_
  289.0 39.7 %section_forward.9 = (f32[2,1024,768]{2,1,0:T(8,128)}, bf16[2,1024,768]{2,1,0:T(8,128)(2,1)}, bf16[2,1024,768]{2,1,0:T(8,128)(2,1)}, bf16[2,1024,768]{2,1,0:T(8,...) custom-call(s32[5]{0:T(128)} %stack.243.refs_0_, ...), custom_call_target="tpu_custom_call", output_to_operand_aliasing={{0}: (25, {}), {1}: (26, {}), {2}: (27, {}), {3}: (28, {}),... | custom-call | tf_op jit(solution)/shard_map/section_forward/pallas_call | solution.py:334
  330.7 5.5 collective-permute-done.21.refs_1_
  336.9 40.2 %section_forward.10 = (f32[2,1024,768]{2,1,0:T(8,128)}, bf16[2,1024,768]{2,1,0:T(8,128)(2,1)}, bf16[2,1024,768]{2,1,0:T(8,128)(2,1)}, bf16[2,1024,768]{2,1,0:T(8...) custom-call(s32[5]{0:T(128)} %stack.239.refs_0_, ...), custom_call_target="tpu_custom_call", output_to_operand_aliasing={{0}: (25, {}), {1}: (26, {}), {2}: (27, {}), {3}: (28, {}),... | custom-call | tf_op jit(solution)/shard_map/section_forward/pallas_call | solution.py:334
  377.1 4.0 collective-permute-start.22
  381.7 4.5 collective-permute-done.22.refs_1_
  389.1 41.7 %collective-permute-start.23 = (bf16[256,768]{1,0:T(8,128)(2,1)}, bf16[256,768]{1,0:T(8,128)(2,1)S(1)}, u32[]{:S(2)}, u32[]{:S(2)}) collective-permute-start(bf16[256,768]{1,0:T(8,128)(2,1)} %get-tuple-element.289), channel_id=1, source_target_pairs={{0,1},{8,9},{1,17},{9,25},{17,16},{25,24},{2,3},{10,11},{3,19},{11... | collective-permute-start | bytes 1179656 | tf_op jit(solution)/shard_map/ppermute | solution.py:746
  431.4 4.4 collective-permute-done.23.refs_1_
  438.8 3.7 collective-permute-start.24
  454.5 43.3 %collective-permute-done.25.refs_2_ = bf16[256,768]{1,0:T(8,128)(2,1)S(1)} collective-permute-done((bf16[256,768]{1,0:T(8,128)(2,1)}, bf16[256,768]{1,0:T(8,128)(2,1)S(1)}, u32[]{:S(2)}, u32[]{:S(2)}) %collective-permute-start.25) | collective-permute-done | bytes 393248 | tf_op jit(solution)/shard_map/ppermute | solution.py:764
  502.4 7.2 collective-permute-done.26.refs_2_
  514.3 192.3 %collective-permute-done.27.refs_2_ = bf16[256,768]{1,0:T(8,128)(2,1)S(1)} collective-permute-done((bf16[256,768]{1,0:T(8,128)(2,1)}, bf16[256,768]{1,0:T(8,128)(2,1)S(1)}, u32[]{:S(2)}, u32[]{:S(2)}) %collective-permute-start.27) | collective-permute-done | bytes 393248 | tf_op jit(solution)/shard_map/ppermute | solution.py:764
  707.3 52.1 %section_backward.10 = (bf16[2,1024,768]{2,1,0:T(8,128)(2,1)}, bf16[2,1024,3072]{2,1,0:T(8,128)(2,1)}, bf16[2,1024,768]{2,1,0:T(8,128)(2,1)}, bf16[1024,128]{1,0...) custom-call(s32[5]{0:T(128)} %stack.257.refs_0_, ...), custom_call_target="tpu_custom_call", output_to_operand_aliasing={{0}: (34, {}), {1}: (35, {}), {2}: (36, {}), {3}: (37, {}),... | custom-call | tf_op jit(solution)/shard_map/section_backward/pallas_call | solution.py:592
  761.2 9.0 collective-permute-done.28.refs_2_
  771.0 52.9 %section_backward.11 = (bf16[2,1024,768]{2,1,0:T(8,128)(2,1)}, bf16[2,1024,3072]{2,1,0:T(8,128)(2,1)}, bf16[2,1024,768]{2,1,0:T(8,128)(2,1)}, bf16[1024,128]{1,0...) custom-call(s32[5]{0:T(128)} %stack.256.refs_0_, ...), custom_call_target="tpu_custom_call", output_to_operand_aliasing={{0}: (34, {}), {1}: (35, {}), {2}: (36, {}), {3}: (37, {}),... | custom-call | tf_op jit(solution)/shard_map/section_backward/pallas_call | solution.py:592
  825.8 6.8 collective-permute-done.29.refs_2_
  833.4 43.3 %section_backward.12 = (bf16[2,1024,768]{2,1,0:T(8,128)(2,1)}, bf16[2,1024,3072]{2,1,0:T(8,128)(2,1)}, bf16[2,1024,768]{2,1,0:T(8,128)(2,1)}, bf16[1024,128]{1,0...) custom-call(s32[5]{0:T(128)} %stack.255.refs_0_, ...), custom_call_target="tpu_custom_call", output_to_operand_aliasing={{0}: (34, {}), {1}: (35, {}), {2}: (36, {}), {3}: (37, {}),... | custom-call | tf_op jit(solution)/shard_map/section_backward/pallas_call | solution.py:592
  878.6 6.8 collective-permute-done.30.refs_2_
  886.2 43.7 %section_backward.13 = (bf16[2,1024,768]{2,1,0:T(8,128)(2,1)}, bf16[2,1024,3072]{2,1,0:T(8,128)(2,1)}, bf16[2,1024,768]{2,1,0:T(8,128)(2,1)}, bf16[1024,128]{1,0...) custom-call(s32[5]{0:T(128)} %stack.254.refs_0_, ...), custom_call_target="tpu_custom_call", output_to_operand_aliasing={{0}: (34, {}), {1}: (35, {}), {2}: (36, {}), {3}: (37, {}),... | custom-call | tf_op jit(solution)/shard_map/section_backward/pallas_call | solution.py:592
  929.9 5.2 convolution_convert_fusion.6
  935.1 12.2 collective-permute-start.35
  951.9 4.6 convolution_convert_fusion.7
  956.8 8.5 collective-permute-start.32
  969.0 21.1 %collective-permute-done.32 = bf16[768,768]{1,0:T(8,128)(2,1)S(1)} collective-permute-done((bf16[768,768]{1,0:T(8,128)(2,1)S(1)}, bf16[768,768]{1,0:T(8,128)(2,1)S(1)}, u32[]{:S(2)}, u32[]{:S(2)}) %collective-permute-start.32) | collective-permute-done | bytes 1179680 | tf_op jit(solution)/shard_map/ppermute | solution.py:666
  992.2 5.8 convolution_convert_fusion.2
  1002.9 37.7 %collective-permute-done.36 = bf16[1536,768]{1,0:T(8,128)(2,1)} collective-permute-done((bf16[1536,768]{1,0:T(8,128)(2,1)S(1)}, bf16[1536,768]{1,0:T(8,128)(2,1)}, u32[]{:S(2)}, u32[]{:S(2)}) %collective-permute-start.36) | collective-permute-done | bytes 2359328 | tf_op jit(solution)/shard_map/ppermute | solution.py:666
  1042.9 6.1 convolution_convert_fusion.4
  1055.2 7.1 add_convert_fusion.7
  1062.4 7.2 collective-permute-start.41
  1070.2 5.1 convolution_convert_fusion.5
  1075.3 6.7 collective-permute-done.45
  1091.0 3.7 add_convert_fusion.4
  1096.2 22.5 %collective-permute-done.41 = bf16[768,1536]{1,0:T(8,128)(2,1)} collective-permute-done((bf16[768,1536]{1,0:T(8,128)(2,1)}, bf16[768,1536]{1,0:T(8,128)(2,1)}, u32[]{:S(2)}, u32[]{:S(2)}) %collective-permute-start.41) | collective-permute-done | bytes 2359328 | tf_op jit(solution)/shard_map/ppermute | solution.py:666
  1121.7 5.8 convolution_convert_fusion
  1133.6 35.7 %collective-permute-done.39 = bf16[1536,768]{1,0:T(8,128)(2,1)} collective-permute-done((bf16[1536,768]{1,0:T(8,128)(2,1)}, bf16[1536,768]{1,0:T(8,128)(2,1)}, u32[]{:S(2)}, u32[]{:S(2)}) %collective-permute-start.39) | collective-permute-done | bytes 2359328 | tf_op jit(solution)/shard_map/ppermute | solution.py:666
  1171.2 4.4 add_convert_fusion.8
  1179.1 6.1 add_convert_fusion.3
  1185.2 5.8 collective-permute-start.53
  1199.8 4.6 broadcast_select_fusion
  1212.2 31.6 %collective-permute-done.53 = bf16[768,1536]{1,0:T(8,128)(2,1)} collective-permute-done((bf16[768,1536]{1,0:T(8,128)(2,1)}, bf16[768,1536]{1,0:T(8,128)(2,1)}, u32[]{:S(2)}, u32[]{:S(2)}) %collective-permute-start.53) | collective-permute-done | bytes 2359328 | tf_op jit(solution)/shard_map/ppermute | solution.py:666
  1243.8 4.7 add_convert_fusion.2
  1251.9 21.3 %collective-permute-done.48 = bf16[896,768]{1,0:T(8,128)(2,1)S(1)} collective-permute-done((bf16[896,768]{1,0:T(8,128)(2,1)S(1)}, bf16[896,768]{1,0:T(8,128)(2,1)S(1)}, u32[]{:S(2)}, u32[]{:S(2)}) %collective-permute-start.48) | collective-permute-done | bytes 1376288 | tf_op jit(solution)/shard_map/ppermute | solution.py:666
  1283.5 4.6 collective-permute-done.34
  1288.2 4.4 add_convert_fusion.1
  1300.9 4.0 collective-permute-done.57
  1310.1 45.3 %collective-permute-done.60 = bf16[1536,768]{1,0:T(8,128)(2,1)} collective-permute-done((bf16[1536,768]{1,0:T(8,128)(2,1)}, bf16[1536,768]{1,0:T(8,128)(2,1)}, u32[]{:S(2)}, u32[]{:S(2)}) %collective-permute-start.60) | collective-permute-done | bytes 2359328 | tf_op jit(solution)/shard_map/ppermute | solution.py:672
  1360.9 74.6 %collective-permute-done.50 = bf16[896,768]{1,0:T(8,128)(2,1)} collective-permute-done((bf16[896,768]{1,0:T(8,128)(2,1)}, bf16[896,768]{1,0:T(8,128)(2,1)}, u32[]{:S(2)}, u32[]{:S(2)}) %collective-permute-start.50) | collective-permute-done | bytes 1376288 | tf_op jit(solution)/shard_map/ppermute | solution.py:672
  1452.1 5.9 collective-permute-done.51
  1464.9 6.7 maximum_convert_fusion.1
  1471.6 11.8 collective-permute-done.56
  1483.4 6.8 maximum_convert_fusion
  (323 shorter events, 225.0 us)
Async XLA Ops:
  7.2 190.3 %all-gather.3.cloned.1.call-start = ((), (), s32[]{:S(2)}) async-start(), calls=%async_computation.2 | async-start | bytes 3538944 | tf_op jit(solution)/shard_map/all_gather | solution.py:727
  9.2 31.6 %collective-permute-start = (bf16[1536,768]{1,0:T(8,128)(2,1)S(1)}, bf16[1536,768]{1,0:T(8,128)(2,1)S(1)}, u32[]{:S(2)}, u32[]{:S(2)}) collective-permute-start(bf16[1536,768]{1,0:T(8,128)(2,1)S(1)} %dynamic-slice_bitcast_fusion.1), channel_id=1, source_target_pairs={{0,0},{1,8},{8,1},{9,9},{16,17},{17,25},{24,16},{25,24},{2,2},{3,1... | collective-permute-start | bytes 7077896 | tf_op jit(solution)/shard_map/ppermute | solution.py:707
  15.5 62.3 %collective-permute-start.13 = (bf16[768,1536]{1,0:T(8,128)(2,1)}, bf16[768,1536]{1,0:T(8,128)(2,1)}, u32[]{:S(2)}, u32[]{:S(2)}) collective-permute-start(bf16[768,1536]{1,0:T(8,128)(2,1)} %dynamic-slice_bitcast_fusion), channel_id=1, source_target_pairs={{0,0},{1,8},{8,1},{9,9},{16,17},{17,25},{24,16},{25,24},{2,2},{3,1... | collective-permute-start | bytes 7077896 | tf_op jit(solution)/shard_map/ppermute | solution.py:707
  40.9 409.5 %all-gather.5.cloned.1.call-start = ((), (), s32[]{:S(2)}) async-start(), calls=%async_computation.4 | async-start | bytes 3538944 | tf_op jit(solution)/shard_map/all_gather | solution.py:744
  40.9 65.5 %collective-permute-start.7 = (bf16[1536,768]{1,0:T(8,128)(2,1)S(1)}, bf16[1536,768]{1,0:T(8,128)(2,1)}, u32[]{:S(2)}, u32[]{:S(2)}) collective-permute-start(bf16[1536,768]{1,0:T(8,128)(2,1)S(1)} %collective-permute-done.refs_21_), channel_id=1, source_target_pairs={{0,2},{2,0},{4,6},{6,4},{1,3},{3,1},{5,7},{7,5},{8,10},{10,8},{12,... | collective-permute-start | bytes 7077896 | tf_op jit(solution)/shard_map/ppermute | solution.py:708
  77.8 67.2 %collective-permute-start.14 = (bf16[768,1536]{1,0:T(8,128)(2,1)}, bf16[768,1536]{1,0:T(8,128)(2,1)}, u32[]{:S(2)}, u32[]{:S(2)}) collective-permute-start(bf16[768,1536]{1,0:T(8,128)(2,1)} %collective-permute-done.13.refs_17_), channel_id=1, source_target_pairs={{0,2},{2,0},{4,6},{6,4},{1,3},{3,1},{5,7},{7,5},{8,10},{10,8},{12,... | collective-permute-start | bytes 7077896 | tf_op jit(solution)/shard_map/ppermute | solution.py:708
  79.6 12.8 collective-permute-start.4
  86.2 12.6 collective-permute-start.9
  92.5 62.9 %collective-permute-start.5 = (bf16[768,384]{1,0:T(8,128)(2,1)S(1)}, bf16[768,384]{1,0:T(8,128)(2,1)}, u32[]{:S(2)}, u32[]{:S(2)}) collective-permute-start(bf16[768,384]{1,0:T(8,128)(2,1)S(1)} %collective-permute-done.4.refs_9_), channel_id=1, source_target_pairs={{0,2},{2,0},{4,6},{6,4},{1,3},{3,1},{5,7},{7,5},{8,10},{10,8},{12,... | collective-permute-start | bytes 1769480 | tf_op jit(solution)/shard_map/ppermute | solution.py:708
  92.9 91.9 %collective-permute-start.15 = (bf16[768,1536]{1,0:T(8,128)(2,1)}, bf16[768,1536]{1,0:T(8,128)(2,1)}, u32[]{:S(2)}, u32[]{:S(2)}) collective-permute-start(bf16[768,1536]{1,0:T(8,128)(2,1)} %collective-permute-done.13.refs_17_), channel_id=1, source_target_pairs={{0,8},{8,0},{16,24},{24,16},{1,9},{9,1},{17,25},{25,17},{2,10},{10... | collective-permute-start | bytes 7077896 | tf_op jit(solution)/shard_map/ppermute | solution.py:646
  98.8 62.9 %collective-permute-start.10 = (bf16[384,768]{1,0:T(8,128)(2,1)S(1)}, bf16[384,768]{1,0:T(8,128)(2,1)}, u32[]{:S(2)}, u32[]{:S(2)}) collective-permute-start(bf16[384,768]{1,0:T(8,128)(2,1)S(1)} %collective-permute-done.9.refs_13_), channel_id=1, source_target_pairs={{0,2},{2,0},{4,6},{6,4},{1,3},{3,1},{5,7},{7,5},{8,10},{10,8},{12,... | collective-permute-start | bytes 1769480 | tf_op jit(solution)/shard_map/ppermute | solution.py:708
  106.5 91.0 %collective-permute-start.17 = (bf16[1536,768]{1,0:T(8,128)(2,1)S(1)}, bf16[1536,768]{1,0:T(8,128)(2,1)}, u32[]{:S(2)}, u32[]{:S(2)}) collective-permute-start(bf16[1536,768]{1,0:T(8,128)(2,1)S(1)} %collective-permute-done.refs_21_), channel_id=1, source_target_pairs={{0,8},{8,0},{16,24},{24,16},{1,9},{9,1},{17,25},{25,17},{2,10},{10... | collective-permute-start | bytes 7077896 | tf_op jit(solution)/shard_map/ppermute | solution.py:646
  145.0 52.5 %collective-permute-start.16 = (bf16[768,1536]{1,0:T(8,128)(2,1)}, bf16[768,1536]{1,0:T(8,128)(2,1)}, u32[]{:S(2)}, u32[]{:S(2)}) collective-permute-start(bf16[768,1536]{1,0:T(8,128)(2,1)} %collective-permute-done.14.refs_18_), channel_id=1, source_target_pairs={{0,8},{8,0},{16,24},{24,16},{1,9},{9,1},{17,25},{25,17},{2,10},{10... | collective-permute-start | bytes 7077896 | tf_op jit(solution)/shard_map/ppermute | solution.py:646
  155.4 42.1 %collective-permute-start.18 = (bf16[1536,768]{1,0:T(8,128)(2,1)}, bf16[1536,768]{1,0:T(8,128)(2,1)}, u32[]{:S(2)}, u32[]{:S(2)}) collective-permute-start(bf16[1536,768]{1,0:T(8,128)(2,1)} %collective-permute-done.7.refs_22_), channel_id=1, source_target_pairs={{0,8},{8,0},{16,24},{24,16},{1,9},{9,1},{17,25},{25,17},{2,10},{10... | collective-permute-start | bytes 7077896 | tf_op jit(solution)/shard_map/ppermute | solution.py:646
  168.6 7.3 collective-permute-start.3
  184.4 13.1 collective-permute-start.8
  184.7 12.7 collective-permute-start.12
  231.8 1049.7 %all-reduce.3.cloned.1.call-start = ((), (), s32[]{:S(2)}) async-start(), calls=%async_computation.6 | async-start | bytes 196608 | tf_op jit(solution)/shard_map/psum | solution.py:826
  231.9 11.0 collective-permute-start.19
  277.4 10.8 collective-permute-start.20
  328.8 7.4 collective-permute-start.21
  377.1 9.2 collective-permute-start.22
  389.1 46.7 %collective-permute-start.23 = (bf16[256,768]{1,0:T(8,128)(2,1)}, bf16[256,768]{1,0:T(8,128)(2,1)S(1)}, u32[]{:S(2)}, u32[]{:S(2)}) collective-permute-start(bf16[256,768]{1,0:T(8,128)(2,1)} %get-tuple-element.289), channel_id=1, source_target_pairs={{0,1},{8,9},{1,17},{9,25},{17,16},{25,24},{2,3},{10,11},{3,19},{11... | collective-permute-start | bytes 1179656 | tf_op jit(solution)/shard_map/ppermute | solution.py:746
  438.8 8.7 collective-permute-start.24
  452.6 45.2 %collective-permute-start.25 = (bf16[256,768]{1,0:T(8,128)(2,1)}, bf16[256,768]{1,0:T(8,128)(2,1)S(1)}, u32[]{:S(2)}, u32[]{:S(2)}) collective-permute-start(bf16[256,768]{1,0:T(8,128)(2,1)} %get-tuple-element.333), channel_id=1, source_target_pairs={{1,0},{9,8},{17,1},{25,9},{16,17},{24,25},{3,2},{11,10},{19,3},{27... | collective-permute-start | bytes 1179656 | tf_op jit(solution)/shard_map/ppermute | solution.py:764
  500.5 9.1 collective-permute-start.26
  512.4 194.2 %collective-permute-start.27 = (bf16[256,768]{1,0:T(8,128)(2,1)}, bf16[256,768]{1,0:T(8,128)(2,1)S(1)}, u32[]{:S(2)}, u32[]{:S(2)}) collective-permute-start(bf16[256,768]{1,0:T(8,128)(2,1)} %get-tuple-element.351), channel_id=1, source_target_pairs={{1,0},{9,8},{17,1},{25,9},{16,17},{24,25},{3,2},{11,10},{19,3},{27... | collective-permute-start | bytes 1179656 | tf_op jit(solution)/shard_map/ppermute | solution.py:764
  759.3 10.9 collective-permute-start.28
  823.9 8.7 collective-permute-start.29
  876.7 8.7 collective-permute-start.30
  935.1 30.1 %collective-permute-start.35 = (bf16[1536,768]{1,0:T(8,128)(2,1)S(1)}, bf16[1536,768]{1,0:T(8,128)(2,1)S(1)}, u32[]{:S(2)}, u32[]{:S(2)}) collective-permute-start(bf16[1536,768]{1,0:T(8,128)(2,1)S(1)} %convolution_convert_fusion.6), channel_id=1, source_target_pairs={{0,8},{8,0},{16,24},{24,16},{1,9},{9,1},{17,25},{25,17},{2,10},{10... | collective-permute-start | bytes 7077896 | tf_op jit(solution)/shard_map/ppermute | solution.py:646
  950.2 6.3 collective-permute-start.31
  956.8 33.3 %collective-permute-start.32 = (bf16[768,768]{1,0:T(8,128)(2,1)S(1)}, bf16[768,768]{1,0:T(8,128)(2,1)S(1)}, u32[]{:S(2)}, u32[]{:S(2)}) collective-permute-start(bf16[768,768]{1,0:T(8,128)(2,1)S(1)} %add_convert_fusion.17), channel_id=1, source_target_pairs={{0,2},{6,4},{1,3},{7,5},{8,10},{14,12},{9,11},{15,13},{16,18},{22,... | collective-permute-start | bytes 3538952 | tf_op jit(solution)/shard_map/ppermute | solution.py:666
  965.9 74.7 %collective-permute-start.36 = (bf16[1536,768]{1,0:T(8,128)(2,1)S(1)}, bf16[1536,768]{1,0:T(8,128)(2,1)}, u32[]{:S(2)}, u32[]{:S(2)}) collective-permute-start(bf16[1536,768]{1,0:T(8,128)(2,1)S(1)} %add_convert_fusion.11), channel_id=1, source_target_pairs={{0,2},{6,4},{1,3},{7,5},{8,10},{14,12},{9,11},{15,13},{16,18},{22,... | collective-permute-start | bytes 7077896 | tf_op jit(solution)/shard_map/ppermute | solution.py:666
  990.3 9.9 collective-permute-start.37
  997.9 57.3 %collective-permute-start.40 = (bf16[768,1536]{1,0:T(8,128)(2,1)}, bf16[768,1536]{1,0:T(8,128)(2,1)}, u32[]{:S(2)}, u32[]{:S(2)}) collective-permute-start(bf16[768,1536]{1,0:T(8,128)(2,1)} %convolution_convert_fusion.2), channel_id=1, source_target_pairs={{0,8},{8,0},{16,24},{24,16},{1,9},{9,1},{17,25},{25,17},{2,10},{10... | collective-permute-start | bytes 7077896 | tf_op jit(solution)/shard_map/ppermute | solution.py:646
  1048.9 35.5 %collective-permute-start.38 = (bf16[1536,768]{1,0:T(8,128)(2,1)}, bf16[1536,768]{1,0:T(8,128)(2,1)}, u32[]{:S(2)}, u32[]{:S(2)}) collective-permute-start(bf16[1536,768]{1,0:T(8,128)(2,1)} %convolution_convert_fusion.4), channel_id=1, source_target_pairs={{0,8},{8,0},{16,24},{24,16},{1,9},{9,1},{17,25},{25,17},{2,10},{10... | collective-permute-start | bytes 7077896 | tf_op jit(solution)/shard_map/ppermute | solution.py:646
  1051.7 30.3 %collective-permute-start.45 = (bf16[768,768]{1,0:T(8,128)(2,1)}, bf16[768,768]{1,0:T(8,128)(2,1)}, u32[]{:S(2)}, u32[]{:S(2)}) collective-permute-start(bf16[768,768]{1,0:T(8,128)(2,1)} %add_convert_fusion.15), channel_id=1, source_target_pairs={{2,0},{4,6},{3,1},{5,7},{10,8},{12,14},{11,9},{13,15},{18,16},{20,... | collective-permute-start | bytes 3538952 | tf_op jit(solution)/shard_map/ppermute | solution.py:672
  1053.1 37.9 %collective-permute-start.43 = (bf16[1536,768]{1,0:T(8,128)(2,1)S(1)}, bf16[1536,768]{1,0:T(8,128)(2,1)}, u32[]{:S(2)}, u32[]{:S(2)}) collective-permute-start(bf16[1536,768]{1,0:T(8,128)(2,1)S(1)} %add_convert_fusion.10), channel_id=1, source_target_pairs={{2,4},{4,2},{3,5},{5,3},{10,12},{12,10},{11,13},{13,11},{18,20},{2... | collective-permute-start | bytes 7077896 | tf_op jit(solution)/shard_map/ppermute | solution.py:669
  1062.4 56.4 %collective-permute-start.41 = (bf16[768,1536]{1,0:T(8,128)(2,1)}, bf16[768,1536]{1,0:T(8,128)(2,1)}, u32[]{:S(2)}, u32[]{:S(2)}) collective-permute-start(bf16[768,1536]{1,0:T(8,128)(2,1)} %add_convert_fusion.7), channel_id=1, source_target_pairs={{0,2},{6,4},{1,3},{7,5},{8,10},{14,12},{9,11},{15,13},{16,18},{22,... | collective-permute-start | bytes 7077896 | tf_op jit(solution)/shard_map/ppermute | solution.py:666
  1088.1 81.2 %collective-permute-start.39 = (bf16[1536,768]{1,0:T(8,128)(2,1)}, bf16[1536,768]{1,0:T(8,128)(2,1)}, u32[]{:S(2)}, u32[]{:S(2)}) collective-permute-start(bf16[1536,768]{1,0:T(8,128)(2,1)} %add_convert_fusion.9), channel_id=1, source_target_pairs={{0,2},{6,4},{1,3},{7,5},{8,10},{14,12},{9,11},{15,13},{16,18},{22,... | collective-permute-start | bytes 7077896 | tf_op jit(solution)/shard_map/ppermute | solution.py:666
  1094.7 80.9 %collective-permute-start.44 = (bf16[1536,768]{1,0:T(8,128)(2,1)}, bf16[1536,768]{1,0:T(8,128)(2,1)}, u32[]{:S(2)}, u32[]{:S(2)}) collective-permute-start(bf16[1536,768]{1,0:T(8,128)(2,1)} %add_convert_fusion.4), channel_id=1, source_target_pairs={{2,0},{4,6},{3,1},{5,7},{10,8},{12,14},{11,9},{13,15},{18,16},{20,... | collective-permute-start | bytes 7077896 | tf_op jit(solution)/shard_map/ppermute | solution.py:672
  1127.5 51.6 %collective-permute-start.52 = (bf16[768,1536]{1,0:T(8,128)(2,1)}, bf16[768,1536]{1,0:T(8,128)(2,1)}, u32[]{:S(2)}, u32[]{:S(2)}) collective-permute-start(bf16[768,1536]{1,0:T(8,128)(2,1)} %convolution_convert_fusion), channel_id=1, source_target_pairs={{0,8},{8,0},{16,24},{24,16},{1,9},{9,1},{17,25},{25,17},{2,10},{10... | collective-permute-start | bytes 7077896 | tf_op jit(solution)/shard_map/ppermute | solution.py:646
  1129.6 69.3 %collective-permute-start.33 = (f32[2,12,768]{2,1,0:T(8,128)S(1)}, f32[2,12,768]{2,1,0:T(8,128)S(1)}, u32[]{:S(2)}, u32[]{:S(2)}) collective-permute-start(f32[2,12,768]{2,1,0:T(8,128)S(1)} %pad_maximum_fusion.4), channel_id=1, source_target_pairs={{0,8},{8,0},{16,24},{24,16},{1,9},{9,1},{17,25},{25,17},{2,10},{10... | collective-permute-start | bytes 221192 | tf_op jit(solution)/shard_map/ppermute | solution.py:646
  1132.3 58.7 %collective-permute-start.42 = (bf16[768,1536]{1,0:T(8,128)(2,1)S(1)}, bf16[768,1536]{1,0:T(8,128)(2,1)S(1)}, u32[]{:S(2)}, u32[]{:S(2)}) collective-permute-start(bf16[768,1536]{1,0:T(8,128)(2,1)S(1)} %add_convert_fusion.6), channel_id=1, source_target_pairs={{2,4},{4,2},{3,5},{5,3},{10,12},{12,10},{11,13},{13,11},{18,20},{2... | collective-permute-start | bytes 7077896 | tf_op jit(solution)/shard_map/ppermute | solution.py:669
  1169.3 23.8 %collective-permute-start.46 = (bf16[768,768]{1,0:T(8,128)(2,1)S(1)}, bf16[768,768]{1,0:T(8,128)(2,1)S(1)}, u32[]{:S(2)}, u32[]{:S(2)}) collective-permute-start(bf16[768,768]{1,0:T(8,128)(2,1)S(1)} %copy-done.30), channel_id=1, source_target_pairs={{0,0},{8,1},{1,8},{9,9},{17,16},{25,17},{16,24},{24,25},{2,2},{10,... | collective-permute-start | bytes 3538952 | tf_op jit(solution)/shard_map/ppermute | solution.py:674
  1185.2 58.5 %collective-permute-start.53 = (bf16[768,1536]{1,0:T(8,128)(2,1)}, bf16[768,1536]{1,0:T(8,128)(2,1)}, u32[]{:S(2)}, u32[]{:S(2)}) collective-permute-start(bf16[768,1536]{1,0:T(8,128)(2,1)} %add_convert_fusion.3), channel_id=1, source_target_pairs={{0,2},{6,4},{1,3},{7,5},{8,10},{14,12},{9,11},{15,13},{16,18},{22,... | collective-permute-start | bytes 7077896 | tf_op jit(solution)/shard_map/ppermute | solution.py:666
  1196.6 11.2 collective-permute-start.47
  1199.7 250.5 %reduce-scatter.5.cloned.1.call-start = ((), (), s32[]{:S(2)}) async-start(), calls=%async_computation.5 | async-start | bytes 3538944 | tf_op jit(solution)/shard_map/reduce_scatter | solution.py:752
  1204.5 285.8 %reduce-scatter.3.cloned.1.call-start = ((), (), s32[]{:S(2)}) async-start(), calls=%async_computation.3 | async-start | bytes 3538944 | tf_op jit(solution)/shard_map/reduce_scatter | solution.py:752
  1204.5 72.1 %collective-permute-start.59 = (bf16[1536,768]{1,0:T(8,128)(2,1)}, bf16[1536,768]{1,0:T(8,128)(2,1)S(1)}, u32[]{:S(2)}, u32[]{:S(2)}) collective-permute-start(bf16[1536,768]{1,0:T(8,128)(2,1)} %add_convert_fusion.8), channel_id=1, source_target_pairs={{2,4},{4,2},{3,5},{5,3},{10,12},{12,10},{11,13},{13,11},{18,20},{2... | collective-permute-start | bytes 7077896 | tf_op jit(solution)/shard_map/ppermute | solution.py:669
  1209.5 63.6 %collective-permute-start.48 = (bf16[896,768]{1,0:T(8,128)(2,1)S(1)}, bf16[896,768]{1,0:T(8,128)(2,1)S(1)}, u32[]{:S(2)}, u32[]{:S(2)}) collective-permute-start(bf16[896,768]{1,0:T(8,128)(2,1)S(1)} %add_convert_fusion.14), channel_id=1, source_target_pairs={{0,2},{6,4},{1,3},{7,5},{8,10},{14,12},{9,11},{15,13},{16,18},{22,... | collective-permute-start | bytes 4128776 | tf_op jit(solution)/shard_map/ppermute | solution.py:666
  1248.5 39.7 %collective-permute-start.54 = (bf16[768,1536]{1,0:T(8,128)(2,1)}, bf16[768,1536]{1,0:T(8,128)(2,1)}, u32[]{:S(2)}, u32[]{:S(2)}) collective-permute-start(bf16[768,1536]{1,0:T(8,128)(2,1)} %add_convert_fusion.2), channel_id=1, source_target_pairs={{2,4},{4,2},{3,5},{5,3},{10,12},{12,10},{11,13},{13,11},{18,20},{2... | collective-permute-start | bytes 7077896 | tf_op jit(solution)/shard_map/ppermute | solution.py:669
  1250.6 54.3 %collective-permute-start.57 = (bf16[768,1536]{1,0:T(8,128)(2,1)S(1)}, bf16[768,1536]{1,0:T(8,128)(2,1)}, u32[]{:S(2)}, u32[]{:S(2)}) collective-permute-start(bf16[768,1536]{1,0:T(8,128)(2,1)S(1)} %copy-done.21), channel_id=1, source_target_pairs={{2,0},{4,6},{3,1},{5,7},{10,8},{12,14},{11,9},{13,15},{18,16},{20,... | collective-permute-start | bytes 7077896 | tf_op jit(solution)/shard_map/ppermute | solution.py:672
  1274.6 19.3 %collective-permute-start.49 = (bf16[896,768]{1,0:T(8,128)(2,1)}, bf16[896,768]{1,0:T(8,128)(2,1)}, u32[]{:S(2)}, u32[]{:S(2)}) collective-permute-start(bf16[896,768]{1,0:T(8,128)(2,1)} %add_convert_fusion.13), channel_id=1, source_target_pairs={{2,4},{4,2},{3,5},{5,3},{10,12},{12,10},{11,13},{13,11},{18,20},{2... | collective-permute-start | bytes 4128776 | tf_op jit(solution)/shard_map/ppermute | solution.py:669
  1280.3 75.2 %collective-permute-start.60 = (bf16[1536,768]{1,0:T(8,128)(2,1)}, bf16[1536,768]{1,0:T(8,128)(2,1)}, u32[]{:S(2)}, u32[]{:S(2)}) collective-permute-start(bf16[1536,768]{1,0:T(8,128)(2,1)} %add_convert_fusion), channel_id=1, source_target_pairs={{2,0},{4,6},{3,1},{5,7},{10,8},{12,14},{11,9},{13,15},{18,16},{20,... | collective-permute-start | bytes 7077896 | tf_op jit(solution)/shard_map/ppermute | solution.py:672
  1281.6 6.5 collective-permute-start.34
  1292.5 147.6 %collective-permute-start.55 = (bf16[768,1536]{1,0:T(8,128)(2,1)}, bf16[768,1536]{1,0:T(8,128)(2,1)}, u32[]{:S(2)}, u32[]{:S(2)}) collective-permute-start(bf16[768,1536]{1,0:T(8,128)(2,1)} %add_convert_fusion.1), channel_id=1, source_target_pairs={{2,0},{4,6},{3,1},{5,7},{10,8},{12,14},{11,9},{13,15},{18,16},{20,... | collective-permute-start | bytes 7077896 | tf_op jit(solution)/shard_map/ppermute | solution.py:672
  1297.0 138.5 %collective-permute-start.50 = (bf16[896,768]{1,0:T(8,128)(2,1)}, bf16[896,768]{1,0:T(8,128)(2,1)}, u32[]{:S(2)}, u32[]{:S(2)}) collective-permute-start(bf16[896,768]{1,0:T(8,128)(2,1)} %add_convert_fusion.12), channel_id=1, source_target_pairs={{2,0},{4,6},{3,1},{5,7},{10,8},{12,14},{11,9},{13,15},{18,16},{20,... | collective-permute-start | bytes 4128776 | tf_op jit(solution)/shard_map/ppermute | solution.py:672
  1299.0 165.9 %collective-permute-start.62 = (bf16[1536,768]{1,0:T(8,128)(2,1)}, bf16[1536,768]{1,0:T(8,128)(2,1)}, u32[]{:S(2)}, u32[]{:S(2)}) collective-permute-start(bf16[1536,768]{1,0:T(8,128)(2,1)} %broadcast_select_fusion.5), channel_id=1, source_target_pairs={{0,0},{8,1},{1,8},{9,9},{17,16},{25,17},{16,24},{24,25},{2,2},{10,... | collective-permute-start | bytes 7077896 | tf_op jit(solution)/shard_map/ppermute | solution.py:674
  1308.2 163.4 %collective-permute-start.58 = (bf16[768,1536]{1,0:T(8,128)(2,1)}, bf16[768,1536]{1,0:T(8,128)(2,1)}, u32[]{:S(2)}, u32[]{:S(2)}) collective-permute-start(bf16[768,1536]{1,0:T(8,128)(2,1)} %broadcast_select_fusion.2), channel_id=1, source_target_pairs={{0,0},{8,1},{1,8},{9,9},{17,16},{25,17},{16,24},{24,25},{2,2},{10,... | collective-permute-start | bytes 7077896 | tf_op jit(solution)/shard_map/ppermute | solution.py:674
  1359.0 105.9 %collective-permute-start.61 = (bf16[1536,768]{1,0:T(8,128)(2,1)}, bf16[1536,768]{1,0:T(8,128)(2,1)}, u32[]{:S(2)}, u32[]{:S(2)}) collective-permute-start(bf16[1536,768]{1,0:T(8,128)(2,1)} %broadcast_select_fusion.4), channel_id=1, source_target_pairs={{0,0},{8,1},{1,8},{9,9},{17,16},{25,17},{16,24},{24,25},{2,2},{10,... | collective-permute-start | bytes 7077896 | tf_op jit(solution)/shard_map/ppermute | solution.py:674
  1438.1 20.0 %collective-permute-start.51 = (bf16[896,768]{1,0:T(8,128)(2,1)}, bf16[896,768]{1,0:T(8,128)(2,1)S(1)}, u32[]{:S(2)}, u32[]{:S(2)}) collective-permute-start(bf16[896,768]{1,0:T(8,128)(2,1)} %broadcast_select_fusion.8), channel_id=1, source_target_pairs={{0,0},{8,1},{1,8},{9,9},{17,16},{25,17},{16,24},{24,25},{2,2},{10,... | collective-permute-start | bytes 4128776 | tf_op jit(solution)/shard_map/ppermute | solution.py:674
  1443.5 39.9 %collective-permute-start.56 = (bf16[768,1536]{1,0:T(8,128)(2,1)}, bf16[768,1536]{1,0:T(8,128)(2,1)}, u32[]{:S(2)}, u32[]{:S(2)}) collective-permute-start(bf16[768,1536]{1,0:T(8,128)(2,1)} %broadcast_select_fusion.3), channel_id=1, source_target_pairs={{0,0},{8,1},{1,8},{9,9},{17,16},{25,17},{16,24},{24,25},{2,2},{10,... | collective-permute-start | bytes 7077896 | tf_op jit(solution)/shard_map/ppermute | solution.py:674
  (54 other events, 899.7 us)
Sparse Core Ops, SparseCore 0:
  41.0 39.4 all-gather.2
  232.0 34.8 all-gather.4
  1199.8 32.0 all-reduce.2
  1236.1 49.7 reduce-scatter.4
  1299.1 97.1 reduce-scatter.2

commit v4 on v3

--- a/solution.py
+++ b/solution.py
@@ -11,6 +11,7 @@
 EPS = 1e-05
 LANES = 128
 ROWS = 256
+OFFLOADED = 0
 NORM_ROWS = 64
 SPAN = 512
 VMEM_LIMIT = 60 * 2**20
@@ -147,8 +148,7 @@
         def _():
             pltpu.make_async_copy(hop_in, x_s, once.at[0]).start()
 
-        for j in range(2):
-            start_weights(stored, weights, wsems, j ^ sc[3], "qioh")
+        start_weights(stored, weights, wsems, sc[3], "q")
         kd_in = pltpu.make_async_copy(st["kd"], kd_s, once.at[1])
         vt_in = pltpu.make_async_copy(st["vt"], vt_s, once.at[2])
         kd_in.start()
@@ -207,8 +207,10 @@
                 for copy in kv_saves:
                     copy.start()
 
+            for copy in loads["q"]:
+                copy.wait()
+            start_weights(stored, weights, wsems, w, "ioh")
             for k in range(2):
-                loads["q"][k].wait()
                 query = dot(h1_s[j], wq[k][w]) + small[j, 6:7, k * half : (k + 1) * half]
                 for b in range(half // LANES):
                     block = turn(query[:, b * LANES : (b + 1) * LANES], *tables) * HD**-0.5
@@ -271,6 +273,11 @@
                     g_s[j, :, cols] = slope.astype(BF16)
 
             steps(tiles, hidden)
+
+            @pl.when(j == 0)
+            def _():
+                start_weights(stored, weights, wsems, 1 ^ sc[3], "q")
+
             save["a"].start()
             save["g"].start()
             for copy in loads["o"] + loads["h"]:
@@ -380,11 +387,14 @@
             return got
 
         shared = [pltpu.make_async_copy(rd[n], b, once.at[1 + i]) for i, (n, b) in enumerate((("kd", kd_s), ("vd", vd_s), ("kt", kt_s)))]
-        for j in (1, 0):
+        def fetch(j):
             start_weights(stored, weights, wsems, j ^ sc[3], "o")
-            for copy in list(gets(j).values()) + (shared if j == 1 else []):
+            for copy in gets(j).values():
                 copy.start()
-            start_weights(stored, weights, wsems, j ^ sc[3], "qhi")
+
+        fetch(1)
+        for copy in shared:
+            copy.start()
         running = (("dkw", dkw_s), ("acc", acc_s), ("accu", accu_s))
 
         @pl.when(m == chunks - 1)
@@ -419,8 +429,10 @@
             db_s[j] = grad.astype(BF16)
             acc_s[j, 0] += fold(grad)
             save["db"].start()
+            for copy in loads["o"]:
+                copy.wait()
+            start_weights(stored, weights, wsems, w, "qhi")
             for k in range(2):
-                loads["o"][k].wait()
                 do_s[:, k * half : (k + 1) * half] = dot_nt(db_s[j], wo[k][w]).astype(BF16)
             for name in ("ot", "q", "qt", "l"):
                 got[name].wait()
@@ -486,6 +498,11 @@
             acc_s[j, 5] += fold(dq_s[j].astype(F32))
             for copy in loads["q"]:
                 copy.wait()
+
+            @pl.when(j == 1)
+            def _():
+                fetch(0)
+
             dh1_s[...] = dot_nt(dq_s[j, :, :half], wq[0][w]) + dot_nt(dq_s[j, :, half:], wq[1][w])
 
             @pl.when(j == 0)
@@ -642,6 +659,21 @@
 FETCH, DELIVER, AHEAD, BEHIND = plane_routes()
 
 
+def end_routes():
+    def place(plane_index, z):
+        section, tensor = plane_index // 2, plane_index % 2
+        return (section * 4 + z) * 2 + tensor
+
+    return [(place(a, z), place(b, end)) for a, b in DELIVER for z, end in ((1, 0), (2, 3))]
+
+
+def routed(value, routes):
+    moved = lax.ppermute(value, PLANE, [(a, b) for a, b in routes if a != b])
+    here = lax.axis_index(PLANE)
+    stays = sum((here == a).astype(jnp.int32) for a, b in routes if a == b) > 0
+    return jnp.where(stays, value, moved)
+
+
 def other_core(value):
     return lax.ppermute(value, "section", SWAP)
 
@@ -654,25 +686,45 @@
     return lax.optimization_barrier((value, *others))[0]
 
 
-def line_sums(count, make):
+def line_sums(count, offloaded, make):
     position = lax.axis_index("dp")
     at_end = (position == 0) | (position == 3)
-    own, first, second, third, done = [], [], [], [], []
-    for r in range(count + 4):
-        if r < count:
-            ties = [chain[n] for chain, n in ((first, r - 2), (second, r - 3), (third, r - 4), (done, r - 5)) if n >= 0]
-            mine, theirs = make(r, ties)
-            term = added(mine, other_core(theirs))
-            first.append(added(term, lax.ppermute(term, "dp", [(0, 1), (3, 2)])))
-        if 0 <= r - 1 < count:
-            part = first[r - 1]
-            second.append(added(part, lax.ppermute(part, "dp", [(1, 2), (2, 1)])))
-        if 0 <= r - 2 < count:
-            whole = second[r - 2]
-            third.append(jnp.where(at_end, lax.ppermute(whole, "dp", [(1, 0), (2, 3)]), whole))
-        if 0 <= r - 3 < count:
-            done.append(lax.ppermute(third[r - 3], PLANE, DELIVER))
-    return done, first
+    owners = end_routes()
+    sums, terms, first, second, done = [], [], [], [], []
+
+    def finish(n):
+        whole = second[n]
+        near = routed(whole, DELIVER)
+        far = lax.ppermute(whole, ("section", "dp", "tensor"), owners)
+        done.append(jnp.where(at_end, far, near))
+
+    steps_left = count - offloaded
+
+    def middle(n):
+        part = first[n]
+        if n >= 2:
+            finish(n - 2)
+        if n >= 3:
+            part = after(part, done[n - 3])
+        second.append(added(part, lax.ppermute(part, "dp", [(1, 2), (2, 1)])))
+
+    for r in range(count):
+        n = r - offloaded
+        ties = terms[:] if n == 0 else [chain[i] for chain, i in ((first, n - 2), (second, n - 3), (done, n - 4)) if i >= 0]
+        mine, theirs = make(r, ties)
+        term = added(mine, other_core(theirs))
+        if n < 0:
+            terms.append(term)
+            sums.append(lax.psum(term, "dp"))
+            continue
+        first.append(added(term, lax.ppermute(term, "dp", [(0, 1), (3, 2)])))
+        if n >= 1:
+            middle(n - 1)
+    for n in range(len(second), steps_left):
+        middle(n)
+    while len(done) < steps_left:
+        finish(len(done))
+    return [routed(value, DELIVER) for value in sums] + done, first[1]
 
 
 def local(
@@ -704,16 +756,16 @@
     parity = lax.axis_index("dp") % 2
     pairs = [(i, i ^ 1) for i in range(lax.axis_size("dp"))]
     wholes = (w_in, w_query, w_out, w_hid_out)
-    fetched = [lax.ppermute(lax.dynamic_index_in_dim(w[0], parity, 0, keepdims=False), PLANE, FETCH) for w in wholes]
+    fetched = [routed(lax.dynamic_index_in_dim(w[0], parity, 0, keepdims=False), FETCH) for w in wholes]
     swapped = [lax.ppermute(w, "dp", pairs) for w in fetched]
-    held = dict(zip("iqoh", zip(fetched, [after(w, fetched[3]) for w in fetched], swapped, [after(w, swapped[3]) for w in swapped])))
+    vectors = jnp.concatenate([v.reshape(-1) for v in (ln_gain, ln_bias, out_bias, b_kv, b_query, b_in)]).reshape(-1, LANES)
+    vectors, own_kv = routed(vectors, FETCH), routed(w_kv[0], FETCH)
+    early = (fetched[3], vectors, own_kv)
+    held = dict(zip("iqoh", zip(fetched, [after(w, *early) for w in fetched], swapped, [after(w, swapped[3]) for w in swapped])))
     weights = []
     for name in "qoih":
         near, tied_near, far, tied_far = held[name]
         weights += [near, far, other_core(tied_near), other_core(tied_far)]
-    vectors = jnp.concatenate([v.reshape(-1) for v in (ln_gain, ln_bias, out_bias, b_kv, b_query, b_in)]).reshape(-1, LANES)
-    vectors = lax.ppermute(after(vectors, fetched[3]), PLANE, FETCH)
-    own_kv = lax.ppermute(after(w_kv[0], fetched[3]), PLANE, FETCH)
     flat, flat_other = vectors.reshape(-1), other_core(vectors).reshape(-1)
     edge = 12 * width + LANES
     bkv = flat[12 * width : edge]
@@ -792,16 +844,16 @@
         return [product(part(kept["h2"], slot, 0, width), part(grad, slot, k * hid, hid)) for k in range(2)]
 
     makers = (
-        lambda ties: outer(1, ties),
         lambda ties: inner_out(1, ties),
         lambda ties: inner_in(1, ties),
         lambda ties: inner_out(0, ties),
         lambda ties: inner_in(0, ties),
+        lambda ties: outer(1, ties),
         lambda ties: outer(0, ties),
     )
     if lax.axis_size("dp") == 4:
-        done, sent = line_sums(len(makers), lambda n, ties: makers[n](ties))
-        later = after(got["gin"], sent[0])
+        done, sent = line_sums(len(makers), OFFLOADED, lambda n, ties: makers[n](ties))
+        later = after(got["gin"], sent)
     else:
         done = []
         for make in makers:
@@ -809,12 +861,12 @@
             done.append(lax.ppermute(lax.psum(added(mine, other_core(theirs)), "dp"), PLANE, DELIVER))
         later = got["gin"]
     input_grad = spread(later, is_first).astype(F32)
-    out_grad = jnp.stack([done[5][:half], done[0][:half]])[None].astype(F32)
-    query_grad = jnp.stack([done[5][half : 2 * half], done[0][half : 2 * half]]).astype(F32)
+    hid_out_grad = jnp.stack([done[2], done[0]])[None].astype(F32)
+    in_grad = jnp.stack([done[3], done[1]])[None].astype(F32)
+    out_grad = jnp.stack([done[5][:half], done[4][:half]])[None].astype(F32)
+    query_grad = jnp.stack([done[5][half : 2 * half], done[4][half : 2 * half]]).astype(F32)
     query_grad = jnp.swapaxes(query_grad, 1, 2)[None]
     kv_grad = jnp.swapaxes(done[5][2 * half :].astype(F32), 0, 1)[None]
-    in_grad = jnp.stack([done[4], done[2]])[None].astype(F32)
-    hid_out_grad = jnp.stack([done[3], done[1]])[None].astype(F32)
 
     query = jnp.sum(got["acc"], axis=2)
     inner = jnp.sum(got["accu"], axis=2)

time: 1510 us -> 1340 us (0.89)
  waiting for transfers between devices: 750 us -> 583 us
  Pallas kernels: 352 us -> 293 us
  starting transfers between devices: 168 us -> 207 us
  other arithmetic: 97.5 us -> 114 us
    ppermute x24, waiting for transfers between devices: 222 us -> 125 us  [the longest x12 107 us: routed(): moved = lax.ppermute(value, PLANE, [(a, b) for a, b in routes if a != b])]
    ppermute x6, starting transfers between devices: 30.1 us -> 68.9 us  [line_sums(): first.append(added(term, lax.ppermute(term, 'dp', [(0, 1), (3, 2)])))]
    ppermute x6, waiting for transfers between devices: 265 us -> 228 us  [local(): hop = lax.ppermute(hop, PLANE, BEHIND)]
    pallas_call x7, Pallas kernels: 198 us -> 167 us  [bwd_call(): pl.pallas_call(functools.partial(bwd_kernel, rows, chunks, fresh), out_sh...]
    pallas_call x7, Pallas kernels: 154 us -> 126 us  [fwd_call(): pl.pallas_call(functools.partial(fwd_kernel, rows, fresh), out_shape=[mak...]
    ppermute x4, waiting for transfers between devices: 53.9 us -> 36.5 us  [local(): swapped = [lax.ppermute(w, 'dp', pairs) for w in fetched]]
    convert_element_type x16 -> x17, other arithmetic: 41.8 us -> 54.2 us  [added(): return (left.astype(F32) + right.astype(F32)).astype(BF16)]
  transfers between devices with their start and end apart: 68 -> 68, of which waited for: 36 -> 31; matrix products, arithmetic and copies ran while one was open for 13% -> 16% of each run, Pallas kernels for 8% -> 7%
where the time goes in v4:
time: 1340 us; the launch traced here: 1330 us
  waiting for transfers between devices  583 us (44%)
  Pallas kernels  293 us (22%)
  starting transfers between devices  207 us (15%)
  other arithmetic  114 us (9%)
  matrix products  61.6 us (5%)
  local copies, waits for them, and re-layouts  53.1 us (4%)
  between operations  16 us (1%)
    ppermute x6, waiting for transfers between devices, local(): hop = lax.ppermute(hop, PLANE, BEHIND)  228 us
    pallas_call x7, Pallas kernels, bwd_call(): pl.pallas_call(functools.partial(bwd_kernel, rows, chunks, fresh), out_sh...  167 us
    ppermute x6, waiting for transfers between devices, line_sums(): first.append(added(term, lax.ppermute(term, 'dp', [(0, 1), (3, 2)])))  160 us
    pallas_call x7, Pallas kernels, fwd_call(): pl.pallas_call(functools.partial(fwd_kernel, rows, fresh), out_shape=[mak...  126 us
    ppermute x12, waiting for transfers between devices, routed(): moved = lax.ppermute(value, PLANE, [(a, b) for a, b in routes if a != b])  107 us
    ppermute x6, starting transfers between devices, line_sums(): first.append(added(term, lax.ppermute(term, 'dp', [(0, 1), (3, 2)])))  68.9 us
    dot_general x17, matrix products, dot(): lax.dot_general(left, right, (dims, ((), ())), preferred_element_type=F32)  61.6 us
    convert_element_type x17, other arithmetic, added(): return (left.astype(F32) + right.astype(F32)).astype(BF16)  54.2 us
  transfers between devices with their start and end apart: 68, of which 31 were waited for; matrix products, arithmetic and copies ran while one was open for 16% of the time, Pallas kernels for 7%

profile of v4, /device:TPU:1, one launch (start us, length us, event | category | flops | bytes accessed | tf_op | source)
XLA Modules:
  0.0 1327.4 jit_solution(14934698373005046656)
XLA Ops:
  9.2 4.7 collective-permute-start
  17.4 23.4 %collective-permute-done = bf16[1536,768]{1,0:T(8,128)(2,1)} collective-permute-done((bf16[1536,768]{1,0:T(8,128)(2,1)S(1)}, bf16[1536,768]{1,0:T(8,128)(2,1)}, u32[]{:S(2)}, u32[]{:S(2)}) %collective-permute-start) | collective-permute-done | bytes 2359328 | tf_op jit(solution)/shard_map/ppermute | solution.py:671
  44.9 27.4 %collective-permute-done.13 = bf16[768,1536]{1,0:T(8,128)(2,1)} collective-permute-done((bf16[768,1536]{1,0:T(8,128)(2,1)}, bf16[768,1536]{1,0:T(8,128)(2,1)}, u32[]{:S(2)}, u32[]{:S(2)}) %collective-permute-start.13) | collective-permute-done | bytes 2359328 | tf_op jit(solution)/shard_map/ppermute | solution.py:671
  85.0 4.6 collective-permute-start.1
  99.2 4.3 collective-permute-done.4
  104.2 5.7 collective-permute-done.9
  110.5 24.5 %collective-permute-done.14.refs_18_ = bf16[768,1536]{1,0:T(8,128)(2,1)} collective-permute-done((bf16[768,1536]{1,0:T(8,128)(2,1)}, bf16[768,1536]{1,0:T(8,128)(2,1)}, u32[]{:S(2)}, u32[]{:S(2)}) %collective-permute-start.14) | collective-permute-done | bytes 2359328 | tf_op jit(solution)/shard_map/ppermute | solution.py:760
  135.5 5.7 collective-permute-done.5.refs_10_
  141.2 6.3 collective-permute-done.10.refs_14_
  170.7 26.6 %section_forward.7 = (f32[2,1024,768]{2,1,0:T(8,128)}, bf16[2,1024,768]{2,1,0:T(8,128)(2,1)}, bf16[2,1024,768]{2,1,0:T(8,128)(2,1)}, bf16[2,1024,768]{2,1,0:T(8,...) custom-call(s32[5]{0:T(128)} %stack.251.refs_0_, ...), custom_call_target="tpu_custom_call" | custom-call | tf_op jit(solution)/shard_map/section_forward/pallas_call | solution.py:341
  199.4 9.5 collective-permute-done.19.refs_1_
  209.7 27.1 %section_forward.8 = (f32[2,1024,768]{2,1,0:T(8,128)}, bf16[2,1024,768]{2,1,0:T(8,128)(2,1)}, bf16[2,1024,768]{2,1,0:T(8,128)(2,1)}, bf16[2,1024,768]{2,1,0:T(8,...) custom-call(s32[5]{0:T(128)} %stack.247.refs_0_, ...), custom_call_target="tpu_custom_call", output_to_operand_aliasing={{0}: (25, {}), {1}: (26, {}), {2}: (27, {}), {3}: (28, {}),... | custom-call | tf_op jit(solution)/shard_map/section_forward/pallas_call | solution.py:341
  236.8 4.3 collective-permute-start.20
  241.7 6.3 collective-permute-done.20.refs_1_
  248.7 32.8 %section_forward.9 = (f32[2,1024,768]{2,1,0:T(8,128)}, bf16[2,1024,768]{2,1,0:T(8,128)(2,1)}, bf16[2,1024,768]{2,1,0:T(8,128)(2,1)}, bf16[2,1024,768]{2,1,0:T(8,...) custom-call(s32[5]{0:T(128)} %stack.243.refs_0_, ...), custom_call_target="tpu_custom_call", output_to_operand_aliasing={{0}: (25, {}), {1}: (26, {}), {2}: (27, {}), {3}: (28, {}),... | custom-call | tf_op jit(solution)/shard_map/section_forward/pallas_call | solution.py:341
  283.5 5.7 collective-permute-done.21.refs_1_
  289.9 32.9 %section_forward.10 = (f32[2,1024,768]{2,1,0:T(8,128)}, bf16[2,1024,768]{2,1,0:T(8,128)(2,1)}, bf16[2,1024,768]{2,1,0:T(8,128)(2,1)}, bf16[2,1024,768]{2,1,0:T(8...) custom-call(s32[5]{0:T(128)} %stack.239.refs_0_, ...), custom_call_target="tpu_custom_call", output_to_operand_aliasing={{0}: (25, {}), {1}: (26, {}), {2}: (27, {}), {3}: (28, {}),... | custom-call | tf_op jit(solution)/shard_map/section_forward/pallas_call | solution.py:341
  322.8 4.2 collective-permute-start.22
  327.7 4.7 collective-permute-done.22.refs_1_
  335.3 34.9 %collective-permute-start.23 = (bf16[256,768]{1,0:T(8,128)(2,1)}, bf16[256,768]{1,0:T(8,128)(2,1)S(1)}, u32[]{:S(2)}, u32[]{:S(2)}) collective-permute-start(bf16[256,768]{1,0:T(8,128)(2,1)} %get-tuple-element.288), channel_id=1, source_target_pairs={{0,1},{8,9},{1,17},{9,25},{17,16},{25,24},{2,3},{10,11},{3,19},{11... | collective-permute-start | bytes 1179656 | tf_op jit(solution)/shard_map/ppermute | solution.py:798
  370.8 4.4 collective-permute-done.23.refs_1_
  394.1 36.6 %collective-permute-done.25.refs_2_ = bf16[256,768]{1,0:T(8,128)(2,1)S(1)} collective-permute-done((bf16[256,768]{1,0:T(8,128)(2,1)}, bf16[256,768]{1,0:T(8,128)(2,1)S(1)}, u32[]{:S(2)}, u32[]{:S(2)}) %collective-permute-start.25) | collective-permute-done | bytes 393248 | tf_op jit(solution)/shard_map/ppermute | solution.py:816
  435.3 7.2 collective-permute-done.26.refs_2_
  447.1 162.7 %collective-permute-done.27.refs_2_ = bf16[256,768]{1,0:T(8,128)(2,1)S(1)} collective-permute-done((bf16[256,768]{1,0:T(8,128)(2,1)}, bf16[256,768]{1,0:T(8,128)(2,1)S(1)}, u32[]{:S(2)}, u32[]{:S(2)}) %collective-permute-start.27) | collective-permute-done | bytes 393248 | tf_op jit(solution)/shard_map/ppermute | solution.py:816
  610.6 44.6 %section_backward.10 = (bf16[2,1024,768]{2,1,0:T(8,128)(2,1)}, bf16[2,1024,3072]{2,1,0:T(8,128)(2,1)}, bf16[2,1024,768]{2,1,0:T(8,128)(2,1)}, bf16[1024,128]{1,0...) custom-call(s32[5]{0:T(128)} %stack.257.refs_0_, ...), custom_call_target="tpu_custom_call", output_to_operand_aliasing={{0}: (34, {}), {1}: (35, {}), {2}: (36, {}), {3}: (37, {}),... | custom-call | tf_op jit(solution)/shard_map/section_backward/pallas_call | solution.py:609
  657.0 8.3 collective-permute-done.28.refs_2_
  666.0 45.0 %section_backward.11 = (bf16[2,1024,768]{2,1,0:T(8,128)(2,1)}, bf16[2,1024,3072]{2,1,0:T(8,128)(2,1)}, bf16[2,1024,768]{2,1,0:T(8,128)(2,1)}, bf16[1024,128]{1,0...) custom-call(s32[5]{0:T(128)} %stack.256.refs_0_, ...), custom_call_target="tpu_custom_call", output_to_operand_aliasing={{0}: (34, {}), {1}: (35, {}), {2}: (36, {}), {3}: (37, {}),... | custom-call | tf_op jit(solution)/shard_map/section_backward/pallas_call | solution.py:609
  713.0 6.8 collective-permute-done.29.refs_2_
  720.5 35.3 %section_backward.12 = (bf16[2,1024,768]{2,1,0:T(8,128)(2,1)}, bf16[2,1024,3072]{2,1,0:T(8,128)(2,1)}, bf16[2,1024,768]{2,1,0:T(8,128)(2,1)}, bf16[1024,128]{1,0...) custom-call(s32[5]{0:T(128)} %stack.255.refs_0_, ...), custom_call_target="tpu_custom_call", output_to_operand_aliasing={{0}: (34, {}), {1}: (35, {}), {2}: (36, {}), {3}: (37, {}),... | custom-call | tf_op jit(solution)/shard_map/section_backward/pallas_call | solution.py:609
  757.8 6.8 collective-permute-done.30.refs_2_
  765.4 35.6 %section_backward.13 = (bf16[2,1024,768]{2,1,0:T(8,128)(2,1)}, bf16[2,1024,3072]{2,1,0:T(8,128)(2,1)}, bf16[2,1024,768]{2,1,0:T(8,128)(2,1)}, bf16[1024,128]{1,0...) custom-call(s32[5]{0:T(128)} %stack.254.refs_0_, ...), custom_call_target="tpu_custom_call", output_to_operand_aliasing={{0}: (34, {}), {1}: (35, {}), {2}: (36, {}), {3}: (37, {}),... | custom-call | tf_op jit(solution)/shard_map/section_backward/pallas_call | solution.py:609
  801.0 5.2 convolution_convert_fusion.4
  806.2 12.2 collective-permute-start.35
  818.3 4.6 convolution_convert_fusion.5
  822.9 5.8 convolution_convert_fusion.6
  830.9 4.5 collective-permute-start.36
  840.6 4.8 convolution_convert_fusion.7
  852.2 32.3 %collective-permute-done.36 = bf16[1536,768]{1,0:T(8,128)(2,1)} collective-permute-done((bf16[1536,768]{1,0:T(8,128)(2,1)}, bf16[1536,768]{1,0:T(8,128)(2,1)}, u32[]{:S(2)}, u32[]{:S(2)}) %collective-permute-start.36) | collective-permute-done | bytes 2359328 | tf_op jit(solution)/shard_map/ppermute | solution.py:720
  884.5 4.4 add_convert_fusion.8
  888.8 6.1 convolution_convert_fusion
  903.5 31.5 %collective-permute-done.32 = bf16[768,1536]{1,0:T(8,128)(2,1)} collective-permute-done((bf16[768,1536]{1,0:T(8,128)(2,1)}, bf16[768,1536]{1,0:T(8,128)(2,1)}, u32[]{:S(2)}, u32[]{:S(2)}) %collective-permute-start.32) | collective-permute-done | bytes 2359328 | tf_op jit(solution)/shard_map/ppermute | solution.py:720
  935.0 4.4 add_convert_fusion.10
  941.5 4.6 convolution_convert_fusion.1
  949.9 7.7 collective-permute-start.41
  966.3 4.7 convolution_convert_fusion.2
  973.0 4.4 add_convert_fusion.1
  978.7 30.0 %collective-permute-done.41 = bf16[1536,768]{1,0:T(8,128)(2,1)} collective-permute-done((bf16[1536,768]{1,0:T(8,128)(2,1)}, bf16[1536,768]{1,0:T(8,128)(2,1)}, u32[]{:S(2)}, u32[]{:S(2)}) %collective-permute-start.41) | collective-permute-done | bytes 2359328 | tf_op jit(solution)/shard_map/ppermute | solution.py:720
  1010.7 4.4 add_convert_fusion.3
  1015.1 17.4 %collective-permute-done.54 = bf16[1536,768]{1,0:T(8,128)(2,1)} collective-permute-done((bf16[1536,768]{1,0:T(8,128)(2,1)}, bf16[1536,768]{1,0:T(8,128)(2,1)}, u32[]{:S(2)}, u32[]{:S(2)}) %collective-permute-start.54) | collective-permute-done | bytes 2359328 | tf_op jit(solution)/shard_map/ppermute | solution.py:671
  1039.7 5.9 add_convert_fusion.6
  1068.8 4.1 select_select_fusion.2
  1072.9 50.1 %collective-permute-done.56 = bf16[768,768]{1,0:T(8,128)(2,1)} collective-permute-done((bf16[768,768]{1,0:T(8,128)(2,1)}, bf16[768,768]{1,0:T(8,128)(2,1)}, u32[]{:S(2)}, u32[]{:S(2)}) %collective-permute-start.56) | collective-permute-done | bytes 1179680 | tf_op jit(solution)/shard_map/ppermute | solution.py:720
  1127.7 4.4 add_convert_fusion.5
  1134.4 4.4 add_convert_fusion.2
  1161.0 48.6 %collective-permute-start.47 = (bf16[896,768]{1,0:T(8,128)(2,1)S(1)}, bf16[896,768]{1,0:T(8,128)(2,1)S(1)}, u32[]{:S(2)}, u32[]{:S(2)}) collective-permute-start(bf16[896,768]{1,0:T(8,128)(2,1)S(1)} %add_convert_fusion.14), channel_id=1, source_target_pairs={{0,2},{6,4},{1,3},{7,5},{8,10},{14,12},{9,11},{15,13},{16,18},{22,... | collective-permute-start | bytes 4128776 | tf_op jit(solution)/shard_map/ppermute | solution.py:720
  1217.4 4.1 select_select_fusion.1
  1221.5 15.7 %collective-permute-done.47 = bf16[896,768]{1,0:T(8,128)(2,1)S(1)} collective-permute-done((bf16[896,768]{1,0:T(8,128)(2,1)S(1)}, bf16[896,768]{1,0:T(8,128)(2,1)S(1)}, u32[]{:S(2)}, u32[]{:S(2)}) %collective-permute-start.47) | collective-permute-done | bytes 1376288 | tf_op jit(solution)/shard_map/ppermute | solution.py:720
  1251.6 4.1 collective-permute-start.52
  1255.7 4.4 maximum_convert_fusion.1
  1260.1 11.0 collective-permute-done.61
  1271.1 20.9 %collective-permute-done.62 = bf16[768,1536]{1,0:T(8,128)(2,1)} collective-permute-done((bf16[768,1536]{1,0:T(8,128)(2,1)S(1)}, bf16[768,1536]{1,0:T(8,128)(2,1)}, u32[]{:S(2)}, u32[]{:S(2)}) %collective-permute-start.62) | collective-permute-done | bytes 2359328 | tf_op jit(solution)/shard_map/ppermute | solution.py:671
  1294.6 4.4 maximum_convert_fusion
  1299.0 7.1 collective-permute-done.51
  1306.1 7.8 collective-permute-done.52
  (346 shorter events, 236.7 us)
Async XLA Ops:
  7.2 162.8 %all-gather.3.cloned.1.call-start = ((), (), s32[]{:S(2)}) async-start(), calls=%async_computation.2 | async-start | bytes 3538944 | tf_op jit(solution)/shard_map/all_gather | solution.py:779
  9.2 31.6 %collective-permute-start = (bf16[1536,768]{1,0:T(8,128)(2,1)S(1)}, bf16[1536,768]{1,0:T(8,128)(2,1)}, u32[]{:S(2)}, u32[]{:S(2)}) collective-permute-start(bf16[1536,768]{1,0:T(8,128)(2,1)S(1)} %dynamic-slice_bitcast_fusion.1), channel_id=1, source_target_pairs={{1,8},{8,1},{16,17},{17,25},{24,16},{25,24},{3,10},{10,3},{18,19},... | collective-permute-start | bytes 7077896 | tf_op jit(solution)/shard_map/ppermute | solution.py:671
  15.5 56.8 %collective-permute-start.13 = (bf16[768,1536]{1,0:T(8,128)(2,1)}, bf16[768,1536]{1,0:T(8,128)(2,1)}, u32[]{:S(2)}, u32[]{:S(2)}) collective-permute-start(bf16[768,1536]{1,0:T(8,128)(2,1)} %dynamic-slice_bitcast_fusion), channel_id=1, source_target_pairs={{1,8},{8,1},{16,17},{17,25},{24,16},{25,24},{3,10},{10,3},{18,19},... | collective-permute-start | bytes 7077896 | tf_op jit(solution)/shard_map/ppermute | solution.py:671
  43.5 346.5 %all-gather.5.cloned.1.call-start = ((), (), s32[]{:S(2)}) async-start(), calls=%async_computation.4 | async-start | bytes 3538944 | tf_op jit(solution)/shard_map/all_gather | solution.py:796
  43.6 66.9 %collective-permute-start.7 = (bf16[1536,768]{1,0:T(8,128)(2,1)S(1)}, bf16[1536,768]{1,0:T(8,128)(2,1)}, u32[]{:S(2)}, u32[]{:S(2)}) collective-permute-start(bf16[1536,768]{1,0:T(8,128)(2,1)S(1)} %broadcast_select_fusion.3.refs_21_), channel_id=1, source_target_pairs={{0,2},{2,0},{4,6},{6,4},{1,3},{3,1},{5,7},{7,5},{8,10},{10,8},{12,... | collective-permute-start | bytes 7077896 | tf_op jit(solution)/shard_map/ppermute | solution.py:760
  76.4 58.6 %collective-permute-start.14 = (bf16[768,1536]{1,0:T(8,128)(2,1)}, bf16[768,1536]{1,0:T(8,128)(2,1)}, u32[]{:S(2)}, u32[]{:S(2)}) collective-permute-start(bf16[768,1536]{1,0:T(8,128)(2,1)} %broadcast_select_fusion.2.refs_17_), channel_id=1, source_target_pairs={{0,2},{2,0},{4,6},{6,4},{1,3},{3,1},{5,7},{7,5},{8,10},{10,8},{12,... | collective-permute-start | bytes 7077896 | tf_op jit(solution)/shard_map/ppermute | solution.py:760
  85.0 11.6 collective-permute-start.1
  89.6 8.9 collective-permute-start.3
  91.8 11.8 collective-permute-start.4
  96.5 13.3 %collective-permute-start.9 = (bf16[384,768]{1,0:T(8,128)(2,1)S(1)}, bf16[384,768]{1,0:T(8,128)(2,1)S(1)}, u32[]{:S(2)}, u32[]{:S(2)}) collective-permute-start(bf16[384,768]{1,0:T(8,128)(2,1)S(1)} %dynamic-slice_bitcast_fusion.2), channel_id=1, source_target_pairs={{1,8},{8,1},{16,17},{17,25},{24,16},{25,24},{3,10},{10,3},{18,19},... | collective-permute-start | bytes 1769480 | tf_op jit(solution)/shard_map/ppermute | solution.py:671
  99.2 58.0 %collective-permute-start.15 = (bf16[768,1536]{1,0:T(8,128)(2,1)}, bf16[768,1536]{1,0:T(8,128)(2,1)}, u32[]{:S(2)}, u32[]{:S(2)}) collective-permute-start(bf16[768,1536]{1,0:T(8,128)(2,1)} %broadcast_select_fusion.2.refs_17_), channel_id=1, source_target_pairs={{0,8},{8,0},{16,24},{24,16},{1,9},{9,1},{17,25},{25,17},{2,10},{10... | collective-permute-start | bytes 7077896 | tf_op jit(solution)/shard_map/ppermute | solution.py:678
  103.6 37.5 %collective-permute-start.5 = (bf16[768,384]{1,0:T(8,128)(2,1)S(1)}, bf16[768,384]{1,0:T(8,128)(2,1)S(1)}, u32[]{:S(2)}, u32[]{:S(2)}) collective-permute-start(bf16[768,384]{1,0:T(8,128)(2,1)S(1)} %broadcast_select_fusion.7.refs_9_), channel_id=1, source_target_pairs={{0,2},{2,0},{4,6},{6,4},{1,3},{3,1},{5,7},{7,5},{8,10},{10,8},{12,... | collective-permute-start | bytes 1769480 | tf_op jit(solution)/shard_map/ppermute | solution.py:760
  110.0 37.6 %collective-permute-start.10 = (bf16[384,768]{1,0:T(8,128)(2,1)S(1)}, bf16[384,768]{1,0:T(8,128)(2,1)S(1)}, u32[]{:S(2)}, u32[]{:S(2)}) collective-permute-start(bf16[384,768]{1,0:T(8,128)(2,1)S(1)} %broadcast_select_fusion.6.refs_13_), channel_id=1, source_target_pairs={{0,2},{2,0},{4,6},{6,4},{1,3},{3,1},{5,7},{7,5},{8,10},{10,8},{12,... | collective-permute-start | bytes 1769480 | tf_op jit(solution)/shard_map/ppermute | solution.py:760
  110.5 24.5 %collective-permute-start.2 = (f32[103,128]{1,0:T(8,128)S(1)}, f32[103,128]{1,0:T(8,128)S(1)}, u32[]{:S(2)}, u32[]{:S(2)}) collective-permute-start(f32[103,128]{1,0:T(8,128)S(1)} %broadcast_select_fusion.9), channel_id=1, source_target_pairs={{0,8},{8,0},{16,24},{24,16},{1,9},{9,1},{17,25},{25,17},{2,10},{10... | collective-permute-start | bytes 158216 | tf_op jit(solution)/shard_map/ppermute | solution.py:678
  135.0 34.9 %collective-permute-start.17 = (bf16[1536,768]{1,0:T(8,128)(2,1)S(1)}, bf16[1536,768]{1,0:T(8,128)(2,1)}, u32[]{:S(2)}, u32[]{:S(2)}) collective-permute-start(bf16[1536,768]{1,0:T(8,128)(2,1)S(1)} %broadcast_select_fusion.3.refs_21_), channel_id=1, source_target_pairs={{0,8},{8,0},{16,24},{24,16},{1,9},{9,1},{17,25},{25,17},{2,10},{10... | collective-permute-start | bytes 7077896 | tf_op jit(solution)/shard_map/ppermute | solution.py:678
  135.0 34.9 %collective-permute-start.16 = (bf16[768,1536]{1,0:T(8,128)(2,1)}, bf16[768,1536]{1,0:T(8,128)(2,1)}, u32[]{:S(2)}, u32[]{:S(2)}) collective-permute-start(bf16[768,1536]{1,0:T(8,128)(2,1)} %collective-permute-done.14.refs_18_), channel_id=1, source_target_pairs={{0,8},{8,0},{16,24},{24,16},{1,9},{9,1},{17,25},{25,17},{2,10},{10... | collective-permute-start | bytes 7077896 | tf_op jit(solution)/shard_map/ppermute | solution.py:678
  141.2 28.7 %collective-permute-start.18 = (bf16[1536,768]{1,0:T(8,128)(2,1)}, bf16[1536,768]{1,0:T(8,128)(2,1)}, u32[]{:S(2)}, u32[]{:S(2)}) collective-permute-start(bf16[1536,768]{1,0:T(8,128)(2,1)} %collective-permute-done.7.refs_22_), channel_id=1, source_target_pairs={{0,8},{8,0},{16,24},{24,16},{1,9},{9,1},{17,25},{25,17},{2,10},{10... | collective-permute-start | bytes 7077896 | tf_op jit(solution)/shard_map/ppermute | solution.py:678
  156.8 13.1 collective-permute-start.8
  157.2 12.7 collective-permute-start.12
  197.4 867.3 %all-reduce.3.cloned.1.call-start = ((), (), s32[]{:S(2)}) async-start(), calls=%async_computation.6 | async-start | bytes 196608 | tf_op jit(solution)/shard_map/psum | solution.py:878
  197.4 11.5 collective-permute-start.19
  236.8 11.2 collective-permute-start.20
  322.8 9.6 collective-permute-start.22
  335.3 39.9 %collective-permute-start.23 = (bf16[256,768]{1,0:T(8,128)(2,1)}, bf16[256,768]{1,0:T(8,128)(2,1)S(1)}, u32[]{:S(2)}, u32[]{:S(2)}) collective-permute-start(bf16[256,768]{1,0:T(8,128)(2,1)} %get-tuple-element.288), channel_id=1, source_target_pairs={{0,1},{8,9},{1,17},{9,25},{17,16},{25,24},{2,3},{10,11},{3,19},{11... | collective-permute-start | bytes 1179656 | tf_op jit(solution)/shard_map/ppermute | solution.py:798
  378.4 8.7 collective-permute-start.24
  392.2 38.5 %collective-permute-start.25 = (bf16[256,768]{1,0:T(8,128)(2,1)}, bf16[256,768]{1,0:T(8,128)(2,1)S(1)}, u32[]{:S(2)}, u32[]{:S(2)}) collective-permute-start(bf16[256,768]{1,0:T(8,128)(2,1)} %get-tuple-element.332), channel_id=1, source_target_pairs={{1,0},{9,8},{17,1},{25,9},{16,17},{24,25},{3,2},{11,10},{19,3},{27... | collective-permute-start | bytes 1179656 | tf_op jit(solution)/shard_map/ppermute | solution.py:816
  433.4 9.1 collective-permute-start.26
  445.2 164.6 %collective-permute-start.27 = (bf16[256,768]{1,0:T(8,128)(2,1)}, bf16[256,768]{1,0:T(8,128)(2,1)S(1)}, u32[]{:S(2)}, u32[]{:S(2)}) collective-permute-start(bf16[256,768]{1,0:T(8,128)(2,1)} %get-tuple-element.350), channel_id=1, source_target_pairs={{1,0},{9,8},{17,1},{25,9},{16,17},{24,25},{3,2},{11,10},{19,3},{27... | collective-permute-start | bytes 1179656 | tf_op jit(solution)/shard_map/ppermute | solution.py:816
  655.1 10.2 collective-permute-start.28
  711.1 8.7 collective-permute-start.29
  806.2 22.7 %collective-permute-start.35 = (bf16[1536,768]{1,0:T(8,128)(2,1)S(1)}, bf16[1536,768]{1,0:T(8,128)(2,1)S(1)}, u32[]{:S(2)}, u32[]{:S(2)}) collective-permute-start(bf16[1536,768]{1,0:T(8,128)(2,1)S(1)} %convolution_convert_fusion.4), channel_id=1, source_target_pairs={{0,8},{8,0},{16,24},{24,16},{1,9},{9,1},{17,25},{25,17},{2,10},{10... | collective-permute-start | bytes 7077896 | tf_op jit(solution)/shard_map/ppermute | solution.py:678
  828.7 16.7 %collective-permute-start.31 = (bf16[768,1536]{1,0:T(8,128)(2,1)}, bf16[768,1536]{1,0:T(8,128)(2,1)}, u32[]{:S(2)}, u32[]{:S(2)}) collective-permute-start(bf16[768,1536]{1,0:T(8,128)(2,1)} %convolution_convert_fusion.6), channel_id=1, source_target_pairs={{0,8},{8,0},{16,24},{24,16},{1,9},{9,1},{17,25},{25,17},{2,10},{10... | collective-permute-start | bytes 7077896 | tf_op jit(solution)/shard_map/ppermute | solution.py:678
  830.9 53.6 %collective-permute-start.36 = (bf16[1536,768]{1,0:T(8,128)(2,1)}, bf16[1536,768]{1,0:T(8,128)(2,1)}, u32[]{:S(2)}, u32[]{:S(2)}) collective-permute-start(bf16[1536,768]{1,0:T(8,128)(2,1)} %add_convert_fusion.9), channel_id=1, source_target_pairs={{0,2},{6,4},{1,3},{7,5},{8,10},{14,12},{9,11},{15,13},{16,18},{22,... | collective-permute-start | bytes 7077896 | tf_op jit(solution)/shard_map/ppermute | solution.py:720
  849.0 86.0 %collective-permute-start.32 = (bf16[768,1536]{1,0:T(8,128)(2,1)}, bf16[768,1536]{1,0:T(8,128)(2,1)}, u32[]{:S(2)}, u32[]{:S(2)}) collective-permute-start(bf16[768,1536]{1,0:T(8,128)(2,1)} %add_convert_fusion.11), channel_id=1, source_target_pairs={{0,2},{6,4},{1,3},{7,5},{8,10},{14,12},{9,11},{15,13},{16,18},{22,... | collective-permute-start | bytes 7077896 | tf_op jit(solution)/shard_map/ppermute | solution.py:720
  895.0 51.1 %collective-permute-start.40 = (bf16[1536,768]{1,0:T(8,128)(2,1)}, bf16[1536,768]{1,0:T(8,128)(2,1)}, u32[]{:S(2)}, u32[]{:S(2)}) collective-permute-start(bf16[1536,768]{1,0:T(8,128)(2,1)} %convolution_convert_fusion), channel_id=1, source_target_pairs={{0,8},{8,0},{16,24},{24,16},{1,9},{9,1},{17,25},{25,17},{2,10},{10... | collective-permute-start | bytes 7077896 | tf_op jit(solution)/shard_map/ppermute | solution.py:678
  897.1 65.7 %collective-permute-start.33 = (f32[2,12,768]{2,1,0:T(8,128)S(1)}, f32[2,12,768]{2,1,0:T(8,128)S(1)}, u32[]{:S(2)}, u32[]{:S(2)}) collective-permute-start(f32[2,12,768]{2,1,0:T(8,128)S(1)} %pad_maximum_fusion.4), channel_id=1, source_target_pairs={{0,8},{8,0},{16,24},{24,16},{1,9},{9,1},{17,25},{25,17},{2,10},{10... | collective-permute-start | bytes 221192 | tf_op jit(solution)/shard_map/ppermute | solution.py:678
  897.1 60.4 %collective-permute-start.37 = (bf16[1536,768]{1,0:T(8,128)(2,1)}, bf16[1536,768]{1,0:T(8,128)(2,1)S(1)}, u32[]{:S(2)}, u32[]{:S(2)}) collective-permute-start(bf16[1536,768]{1,0:T(8,128)(2,1)} %add_convert_fusion.8), channel_id=1, source_target_pairs={{2,4},{4,2},{3,5},{5,3},{10,12},{12,10},{11,13},{13,11},{18,20},{2... | collective-permute-start | bytes 7077896 | tf_op jit(solution)/shard_map/ppermute | solution.py:709
  939.4 33.6 %collective-permute-start.43 = (bf16[768,1536]{1,0:T(8,128)(2,1)}, bf16[768,1536]{1,0:T(8,128)(2,1)}, u32[]{:S(2)}, u32[]{:S(2)}) collective-permute-start(bf16[768,1536]{1,0:T(8,128)(2,1)} %add_convert_fusion.10), channel_id=1, source_target_pairs={{2,4},{4,2},{3,5},{5,3},{10,12},{12,10},{11,13},{13,11},{18,20},{2... | collective-permute-start | bytes 7077896 | tf_op jit(solution)/shard_map/ppermute | solution.py:709
  949.9 58.8 %collective-permute-start.41 = (bf16[1536,768]{1,0:T(8,128)(2,1)}, bf16[1536,768]{1,0:T(8,128)(2,1)}, u32[]{:S(2)}, u32[]{:S(2)}) collective-permute-start(bf16[1536,768]{1,0:T(8,128)(2,1)} %add_convert_fusion.4), channel_id=1, source_target_pairs={{0,2},{6,4},{1,3},{7,5},{8,10},{14,12},{9,11},{15,13},{16,18},{22,... | collective-permute-start | bytes 7077896 | tf_op jit(solution)/shard_map/ppermute | solution.py:720
  959.6 55.5 %collective-permute-start.53 = (bf16[1536,768]{1,0:T(8,128)(2,1)}, bf16[1536,768]{1,0:T(8,128)(2,1)}, u32[]{:S(2)}, u32[]{:S(2)}) collective-permute-start(bf16[1536,768]{1,0:T(8,128)(2,1)} %add_convert_fusion.7), channel_id=1, source_target_pairs={{2,0},{4,6},{10,1},{12,7},{3,8},{5,14},{11,9},{13,15},{19,16},{21,... | collective-permute-start | bytes 7077896 | tf_op jit(solution)/shard_map/ppermute | solution.py:698
  960.9 71.6 %collective-permute-start.54 = (bf16[1536,768]{1,0:T(8,128)(2,1)}, bf16[1536,768]{1,0:T(8,128)(2,1)}, u32[]{:S(2)}, u32[]{:S(2)}) collective-permute-start(bf16[1536,768]{1,0:T(8,128)(2,1)} %add_convert_fusion.7), channel_id=1, source_target_pairs={{8,1},{1,8},{17,16},{25,17},{16,24},{24,25},{10,3},{3,10},{19,18},... | collective-permute-start | bytes 7077896 | tf_op jit(solution)/shard_map/ppermute | solution.py:671
  963.5 280.6 %reduce-scatter.5.cloned.1.call-start = ((), (), s32[]{:S(2)}) async-start(), calls=%async_computation.5 | async-start | bytes 3538944 | tf_op jit(solution)/shard_map/reduce_scatter | solution.py:804
  971.1 68.7 %collective-permute-start.38 = (bf16[768,1536]{1,0:T(8,128)(2,1)S(1)}, bf16[768,1536]{1,0:T(8,128)(2,1)S(1)}, u32[]{:S(2)}, u32[]{:S(2)}) collective-permute-start(bf16[768,1536]{1,0:T(8,128)(2,1)S(1)} %convolution_convert_fusion.2), channel_id=1, source_target_pairs={{0,8},{8,0},{16,24},{24,16},{1,9},{9,1},{17,25},{25,17},{2,10},{10... | collective-permute-start | bytes 7077896 | tf_op jit(solution)/shard_map/ppermute | solution.py:678
  977.4 87.3 %collective-permute-start.44 = (bf16[768,1536]{1,0:T(8,128)(2,1)}, bf16[768,1536]{1,0:T(8,128)(2,1)}, u32[]{:S(2)}, u32[]{:S(2)}) collective-permute-start(bf16[768,1536]{1,0:T(8,128)(2,1)} %add_convert_fusion.1), channel_id=1, source_target_pairs={{2,0},{4,6},{10,1},{12,7},{3,8},{5,14},{11,9},{13,15},{19,16},{21,... | collective-permute-start | bytes 7077896 | tf_op jit(solution)/shard_map/ppermute | solution.py:698
  1008.7 60.1 %collective-permute-start.45 = (bf16[768,1536]{1,0:T(8,128)(2,1)}, bf16[768,1536]{1,0:T(8,128)(2,1)}, u32[]{:S(2)}, u32[]{:S(2)}) collective-permute-start(bf16[768,1536]{1,0:T(8,128)(2,1)} %add_convert_fusion.1), channel_id=1, source_target_pairs={{8,1},{1,8},{17,16},{25,17},{16,24},{24,25},{10,3},{3,10},{19,18},... | collective-permute-start | bytes 7077896 | tf_op jit(solution)/shard_map/ppermute | solution.py:671
  1039.7 16.6 %collective-permute-start.55 = (bf16[768,768]{1,0:T(8,128)(2,1)}, bf16[768,768]{1,0:T(8,128)(2,1)}, u32[]{:S(2)}, u32[]{:S(2)}) collective-permute-start(bf16[768,768]{1,0:T(8,128)(2,1)} %pad_maximum_fusion.2), channel_id=1, source_target_pairs={{0,8},{8,0},{16,24},{24,16},{1,9},{9,1},{17,25},{25,17},{2,10},{10... | collective-permute-start | bytes 3538952 | tf_op jit(solution)/shard_map/ppermute | solution.py:678
  1045.6 82.1 %collective-permute-start.39 = (bf16[768,1536]{1,0:T(8,128)(2,1)}, bf16[768,1536]{1,0:T(8,128)(2,1)}, u32[]{:S(2)}, u32[]{:S(2)}) collective-permute-start(bf16[768,1536]{1,0:T(8,128)(2,1)} %add_convert_fusion.6), channel_id=1, source_target_pairs={{0,2},{6,4},{1,3},{7,5},{8,10},{14,12},{9,11},{15,13},{16,18},{22,... | collective-permute-start | bytes 7077896 | tf_op jit(solution)/shard_map/ppermute | solution.py:720
  1051.5 269.1 %reduce-scatter.3.cloned.1.call-start = ((), (), s32[]{:S(2)}) async-start(), calls=%async_computation.3 | async-start | bytes 3538944 | tf_op jit(solution)/shard_map/reduce_scatter | solution.py:804
  1054.1 80.2 %collective-permute-start.42 = (bf16[1536,768]{1,0:T(8,128)(2,1)}, bf16[1536,768]{1,0:T(8,128)(2,1)}, u32[]{:S(2)}, u32[]{:S(2)}) collective-permute-start(bf16[1536,768]{1,0:T(8,128)(2,1)} %add_convert_fusion.3), channel_id=1, source_target_pairs={{2,4},{4,2},{3,5},{5,3},{10,12},{12,10},{11,13},{13,11},{18,20},{2... | collective-permute-start | bytes 7077896 | tf_op jit(solution)/shard_map/ppermute | solution.py:709
  1059.1 64.0 %collective-permute-start.56 = (bf16[768,768]{1,0:T(8,128)(2,1)}, bf16[768,768]{1,0:T(8,128)(2,1)}, u32[]{:S(2)}, u32[]{:S(2)}) collective-permute-start(bf16[768,768]{1,0:T(8,128)(2,1)} %add_convert_fusion.17), channel_id=1, source_target_pairs={{0,2},{6,4},{1,3},{7,5},{8,10},{14,12},{9,11},{15,13},{16,18},{22,... | collective-permute-start | bytes 3538952 | tf_op jit(solution)/shard_map/ppermute | solution.py:720
  1064.7 80.9 %collective-permute-start.34 = (f32[2,12,768]{2,1,0:T(8,128)}, f32[2,12,768]{2,1,0:T(8,128)S(1)}, u32[]{:S(2)}, u32[]{:S(2)}) collective-permute-start(f32[2,12,768]{2,1,0:T(8,128)} %all-reduce.3.cloned.1.call-done), channel_id=1, source_target_pairs={{0,0},{8,1},{1,8},{9,9},{17,16},{25,17},{16,24},{24,25},{2,2},{10,... | collective-permute-start | bytes 221192 | tf_op jit(solution)/shard_map/ppermute | solution.py:878
  1126.1 27.1 %collective-permute-start.57 = (bf16[768,768]{1,0:T(8,128)(2,1)}, bf16[768,768]{1,0:T(8,128)(2,1)}, u32[]{:S(2)}, u32[]{:S(2)}) collective-permute-start(bf16[768,768]{1,0:T(8,128)(2,1)} %add_convert_fusion.16), channel_id=1, source_target_pairs={{2,4},{4,2},{3,5},{5,3},{10,12},{12,10},{11,13},{13,11},{18,20},{2... | collective-permute-start | bytes 3538952 | tf_op jit(solution)/shard_map/ppermute | solution.py:709
  1132.1 28.8 %collective-permute-start.60 = (bf16[768,1536]{1,0:T(8,128)(2,1)}, bf16[768,1536]{1,0:T(8,128)(2,1)}, u32[]{:S(2)}, u32[]{:S(2)}) collective-permute-start(bf16[768,1536]{1,0:T(8,128)(2,1)} %add_convert_fusion.5), channel_id=1, source_target_pairs={{2,4},{4,2},{3,5},{5,3},{10,12},{12,10},{11,13},{13,11},{18,20},{2... | collective-permute-start | bytes 7077896 | tf_op jit(solution)/shard_map/ppermute | solution.py:709
  1138.8 73.8 %collective-permute-start.48 = (bf16[1536,768]{1,0:T(8,128)(2,1)}, bf16[1536,768]{1,0:T(8,128)(2,1)}, u32[]{:S(2)}, u32[]{:S(2)}) collective-permute-start(bf16[1536,768]{1,0:T(8,128)(2,1)} %add_convert_fusion.2), channel_id=1, source_target_pairs={{2,0},{4,6},{10,1},{12,7},{3,8},{5,14},{11,9},{13,15},{19,16},{21,... | collective-permute-start | bytes 7077896 | tf_op jit(solution)/shard_map/ppermute | solution.py:698
  1140.2 73.7 %collective-permute-start.49 = (bf16[1536,768]{1,0:T(8,128)(2,1)}, bf16[1536,768]{1,0:T(8,128)(2,1)}, u32[]{:S(2)}, u32[]{:S(2)}) collective-permute-start(bf16[1536,768]{1,0:T(8,128)(2,1)} %add_convert_fusion.2), channel_id=1, source_target_pairs={{8,1},{1,8},{17,16},{25,17},{16,24},{24,25},{10,3},{3,10},{19,18},... | collective-permute-start | bytes 7077896 | tf_op jit(solution)/shard_map/ppermute | solution.py:671
  1145.6 10.8 collective-permute-start.46
  1155.1 90.9 %collective-permute-start.58 = (bf16[768,768]{1,0:T(8,128)(2,1)S(1)}, bf16[768,768]{1,0:T(8,128)(2,1)}, u32[]{:S(2)}, u32[]{:S(2)}) collective-permute-start(bf16[768,768]{1,0:T(8,128)(2,1)S(1)} %add_convert_fusion.15), channel_id=1, source_target_pairs={{2,0},{4,6},{10,1},{12,7},{3,8},{5,14},{11,9},{13,15},{19,16},{21,... | collective-permute-start | bytes 3538952 | tf_op jit(solution)/shard_map/ppermute | solution.py:698
  1156.5 89.7 %collective-permute-start.59 = (bf16[768,768]{1,0:T(8,128)(2,1)S(1)}, bf16[768,768]{1,0:T(8,128)(2,1)}, u32[]{:S(2)}, u32[]{:S(2)}) collective-permute-start(bf16[768,768]{1,0:T(8,128)(2,1)S(1)} %add_convert_fusion.15), channel_id=1, source_target_pairs={{8,1},{1,8},{17,16},{25,17},{16,24},{24,25},{10,3},{3,10},{19,18},... | collective-permute-start | bytes 3538952 | tf_op jit(solution)/shard_map/ppermute | solution.py:671
  1161.0 76.2 %collective-permute-start.47 = (bf16[896,768]{1,0:T(8,128)(2,1)S(1)}, bf16[896,768]{1,0:T(8,128)(2,1)S(1)}, u32[]{:S(2)}, u32[]{:S(2)}) collective-permute-start(bf16[896,768]{1,0:T(8,128)(2,1)S(1)} %add_convert_fusion.14), channel_id=1, source_target_pairs={{0,2},{6,4},{1,3},{7,5},{8,10},{14,12},{9,11},{15,13},{16,18},{22,... | collective-permute-start | bytes 4128776 | tf_op jit(solution)/shard_map/ppermute | solution.py:720
  1212.6 58.4 %collective-permute-start.61 = (bf16[768,1536]{1,0:T(8,128)(2,1)S(1)}, bf16[768,1536]{1,0:T(8,128)(2,1)}, u32[]{:S(2)}, u32[]{:S(2)}) collective-permute-start(bf16[768,1536]{1,0:T(8,128)(2,1)S(1)} %add_convert_fusion), channel_id=1, source_target_pairs={{2,0},{4,6},{10,1},{12,7},{3,8},{5,14},{11,9},{13,15},{19,16},{21,... | collective-permute-start | bytes 7077896 | tf_op jit(solution)/shard_map/ppermute | solution.py:698
  1213.9 78.0 %collective-permute-start.62 = (bf16[768,1536]{1,0:T(8,128)(2,1)S(1)}, bf16[768,1536]{1,0:T(8,128)(2,1)}, u32[]{:S(2)}, u32[]{:S(2)}) collective-permute-start(bf16[768,1536]{1,0:T(8,128)(2,1)S(1)} %add_convert_fusion), channel_id=1, source_target_pairs={{8,1},{1,8},{17,16},{25,17},{16,24},{24,25},{10,3},{3,10},{19,18},... | collective-permute-start | bytes 7077896 | tf_op jit(solution)/shard_map/ppermute | solution.py:671
  1238.8 9.3 collective-permute-start.50
  1250.3 55.8 %collective-permute-start.51 = (bf16[896,768]{1,0:T(8,128)(2,1)S(1)}, bf16[896,768]{1,0:T(8,128)(2,1)S(1)}, u32[]{:S(2)}, u32[]{:S(2)}) collective-permute-start(bf16[896,768]{1,0:T(8,128)(2,1)S(1)} %add_convert_fusion.12), channel_id=1, source_target_pairs={{2,0},{4,6},{10,1},{12,7},{3,8},{5,14},{11,9},{13,15},{19,16},{21,... | collective-permute-start | bytes 4128776 | tf_op jit(solution)/shard_map/ppermute | solution.py:698
  1251.6 62.2 %collective-permute-start.52 = (bf16[896,768]{1,0:T(8,128)(2,1)S(1)}, bf16[896,768]{1,0:T(8,128)(2,1)S(1)}, u32[]{:S(2)}, u32[]{:S(2)}) collective-permute-start(bf16[896,768]{1,0:T(8,128)(2,1)S(1)} %add_convert_fusion.12), channel_id=1, source_target_pairs={{8,1},{1,8},{17,16},{25,17},{16,24},{24,25},{10,3},{3,10},{19,18},... | collective-permute-start | bytes 4128776 | tf_op jit(solution)/shard_map/ppermute | solution.py:671
  (62 other events, 935.0 us)
Sparse Core Ops, SparseCore 0:
  43.6 36.8 all-gather.2
  197.5 35.5 all-gather.4
  963.6 34.4 all-reduce.2
  1051.7 44.0 reduce-scatter.4
  1151.3 74.1 reduce-scatter.2

commit v5 on v4

--- a/solution.py
+++ b/solution.py
@@ -11,7 +11,6 @@
 EPS = 1e-05
 LANES = 128
 ROWS = 256
-OFFLOADED = 0
 NORM_ROWS = 64
 SPAN = 512
 VMEM_LIMIT = 60 * 2**20
@@ -659,19 +658,33 @@
 FETCH, DELIVER, AHEAD, BEHIND = plane_routes()
 
 
-def end_routes():
-    def place(plane_index, z):
-        section, tensor = plane_index // 2, plane_index % 2
-        return (section * 4 + z) * 2 + tensor
-
-    return [(place(a, z), place(b, end)) for a, b in DELIVER for z, end in ((1, 0), (2, 3))]
+def same_chip(a, b):
+    return a // 4 == b // 4 and a % 2 == b % 2
+
+
+def among(places):
+    here = lax.axis_index(PLANE)
+    return sum((here == a).astype(jnp.int32) for a in places) > 0
+
+
+def both_slots(whole, parity):
+    own, other = (lax.dynamic_index_in_dim(whole, p, 0, keepdims=False) for p in (parity, 1 - parity))
+    near = routed(own, FETCH)
+    size = lax.axis_size("dp")
+    linked = [b for a, b in FETCH if not same_chip(a, b)]
+
+    def place(b, z):
+        return (b // 2 * size + z) * 2 + b % 2
+
+    passed = lax.ppermute(near, ("section", "dp", "tensor"), [(place(b, z ^ 1), place(b, z)) for b in linked for z in range(size)])
+    moved = lax.ppermute(other, PLANE, [(a, b) for a, b in FETCH if a != b and same_chip(a, b)])
+    far = jnp.where(among([b for a, b in FETCH if a == b]), other, jnp.where(among(linked), passed, moved))
+    return near, far
 
 
 def routed(value, routes):
     moved = lax.ppermute(value, PLANE, [(a, b) for a, b in routes if a != b])
-    here = lax.axis_index(PLANE)
-    stays = sum((here == a).astype(jnp.int32) for a, b in routes if a == b) > 0
-    return jnp.where(stays, value, moved)
+    return jnp.where(among([a for a, b in routes if a == b]), value, moved)
 
 
 def other_core(value):
@@ -686,45 +699,31 @@
     return lax.optimization_barrier((value, *others))[0]
 
 
-def line_sums(count, offloaded, make):
+def line_sums(count, make):
     position = lax.axis_index("dp")
     at_end = (position == 0) | (position == 3)
-    owners = end_routes()
-    sums, terms, first, second, done = [], [], [], [], []
-
-    def finish(n):
-        whole = second[n]
-        near = routed(whole, DELIVER)
-        far = lax.ppermute(whole, ("section", "dp", "tensor"), owners)
-        done.append(jnp.where(at_end, far, near))
-
-    steps_left = count - offloaded
-
-    def middle(n):
-        part = first[n]
-        if n >= 2:
-            finish(n - 2)
+    terms, arrived, first, second, third, done = [], [], [], [], [], []
+
+    def tied(value, *links):
+        values = [chain[n] for chain, n in links if n >= 0]
+        return after(value, *values) if values else value
+
+    def advance(n):
+        first.append(added(tied(terms[n], (second, n - 1)), arrived[n]))
+        across = lax.ppermute(first[n], "dp", [(1, 2), (2, 1)])
+        second.append(added(tied(first[n], (third, n - 1), (done, n - 2)), across))
+        third.append(jnp.where(at_end, lax.ppermute(second[n], "dp", [(1, 0), (2, 3)]), second[n]))
+        done.append(routed(third[n], DELIVER))
+
+    for n in range(count):
         if n >= 3:
-            part = after(part, done[n - 3])
-        second.append(added(part, lax.ppermute(part, "dp", [(1, 2), (2, 1)])))
-
-    for r in range(count):
-        n = r - offloaded
-        ties = terms[:] if n == 0 else [chain[i] for chain, i in ((first, n - 2), (second, n - 3), (done, n - 4)) if i >= 0]
-        mine, theirs = make(r, ties)
-        term = added(mine, other_core(theirs))
-        if n < 0:
-            terms.append(term)
-            sums.append(lax.psum(term, "dp"))
-            continue
-        first.append(added(term, lax.ppermute(term, "dp", [(0, 1), (3, 2)])))
-        if n >= 1:
-            middle(n - 1)
-    for n in range(len(second), steps_left):
-        middle(n)
-    while len(done) < steps_left:
-        finish(len(done))
-    return [routed(value, DELIVER) for value in sums] + done, first[1]
+            advance(n - 3)
+        mine, theirs = make(n, terms[-2:-1])
+        terms.append(tied(added(mine, other_core(theirs)), (first, n - 3), (second, n - 3)))
+        arrived.append(lax.ppermute(terms[n], "dp", [(0, 1), (3, 2)]))
+    for n in range(max(count - 3, 0), count):
+        advance(n)
+    return done, first[1]
 
 
 def local(
@@ -754,10 +753,8 @@
     ticks = chunks + 3
 
     parity = lax.axis_index("dp") % 2
-    pairs = [(i, i ^ 1) for i in range(lax.axis_size("dp"))]
     wholes = (w_in, w_query, w_out, w_hid_out)
-    fetched = [routed(lax.dynamic_index_in_dim(w[0], parity, 0, keepdims=False), FETCH) for w in wholes]
-    swapped = [lax.ppermute(w, "dp", pairs) for w in fetched]
+    fetched, swapped = zip(*(both_slots(w[0], parity) for w in wholes))
     vectors = jnp.concatenate([v.reshape(-1) for v in (ln_gain, ln_bias, out_bias, b_kv, b_query, b_in)]).reshape(-1, LANES)
     vectors, own_kv = routed(vectors, FETCH), routed(w_kv[0], FETCH)
     early = (fetched[3], vectors, own_kv)
@@ -844,15 +841,15 @@
         return [product(part(kept["h2"], slot, 0, width), part(grad, slot, k * hid, hid)) for k in range(2)]
 
     makers = (
+        lambda ties: outer(1, ties),
         lambda ties: inner_out(1, ties),
         lambda ties: inner_in(1, ties),
         lambda ties: inner_out(0, ties),
         lambda ties: inner_in(0, ties),
-        lambda ties: outer(1, ties),
         lambda ties: outer(0, ties),
     )
     if lax.axis_size("dp") == 4:
-        done, sent = line_sums(len(makers), OFFLOADED, lambda n, ties: makers[n](ties))
+        done, sent = line_sums(len(makers), lambda n, ties: makers[n](ties))
         later = after(got["gin"], sent)
     else:
         done = []
@@ -861,10 +858,10 @@
             done.append(lax.ppermute(lax.psum(added(mine, other_core(theirs)), "dp"), PLANE, DELIVER))
         later = got["gin"]
     input_grad = spread(later, is_first).astype(F32)
-    hid_out_grad = jnp.stack([done[2], done[0]])[None].astype(F32)
-    in_grad = jnp.stack([done[3], done[1]])[None].astype(F32)
-    out_grad = jnp.stack([done[5][:half], done[4][:half]])[None].astype(F32)
-    query_grad = jnp.stack([done[5][half : 2 * half], done[4][half : 2 * half]]).astype(F32)
+    hid_out_grad = jnp.stack([done[3], done[1]])[None].astype(F32)
+    in_grad = jnp.stack([done[4], done[2]])[None].astype(F32)
+    out_grad = jnp.stack([done[5][:half], done[0][:half]])[None].astype(F32)
+    query_grad = jnp.stack([done[5][half : 2 * half], done[0][half : 2 * half]]).astype(F32)
     query_grad = jnp.swapaxes(query_grad, 1, 2)[None]
     kv_grad = jnp.swapaxes(done[5][2 * half :].astype(F32), 0, 1)[None]
 

time: 1340 us -> 1290 us (0.963)
  waiting for transfers between devices: 583 us -> 558 us
  starting transfers between devices: 207 us -> 186 us
    ppermute x12, waiting for transfers between devices: 107 us -> 46.2 us  [routed(): moved = lax.ppermute(value, PLANE, [(a, b) for a, b in routes if a != b])]
    ppermute x22 -> x26, waiting for transfers between devices: 214 us -> 239 us  [the longest x6 123 us: advance(): lax.ppermute(second[n], 'dp', [(1, 0), (2, 3)])]
    ppermute x22 -> x26, starting transfers between devices: 90.9 us -> 69.3 us  [the longest x6 32.9 us: line_sums(): arrived.append(lax.ppermute(terms[n], 'dp', [(0, 1), (3, 2)]))]
    select_n x11 -> x21, other arithmetic: 21.8 us -> 41 us  [the longest x11 20.4 us: routed(): return jnp.where(among([a for a, b in routes if a == b]), value, moved)]
    convert_element_type x17 -> x16, other arithmetic: 54.2 us -> 38.3 us  [added(): return (left.astype(F32) + right.astype(F32)).astype(BF16)]
  transfers between devices with their start and end apart: 68 -> 72, of which waited for: 31 -> 33; matrix products, arithmetic and copies ran while one was open for 16% -> 15% of each run, Pallas kernels for 7% -> 8%
where the time goes in v5:
time: 1290 us; the launch traced here: 1270 us
  waiting for transfers between devices  558 us (43%)
  Pallas kernels  292 us (23%)
  starting transfers between devices  186 us (14%)
  other arithmetic  113 us (9%)
  local copies, waits for them, and re-layouts  56.5 us (4%)
  matrix products  52.6 us (4%)
  between operations  16.5 us (1%)
    ppermute x6, waiting for transfers between devices, local(): hop = lax.ppermute(hop, PLANE, BEHIND)  229 us
    pallas_call x7, Pallas kernels, bwd_call(): pl.pallas_call(functools.partial(bwd_kernel, rows, chunks, fresh), out_sh...  167 us
    pallas_call x7, Pallas kernels, fwd_call(): pl.pallas_call(functools.partial(fwd_kernel, rows, fresh), out_shape=[mak...  126 us
    ppermute x6, waiting for transfers between devices, advance(): lax.ppermute(second[n], 'dp', [(1, 0), (2, 3)])  123 us
    ppermute x6, waiting for transfers between devices, line_sums(): arrived.append(lax.ppermute(terms[n], 'dp', [(0, 1), (3, 2)]))  109 us
    dot_general x17, matrix products, dot(): lax.dot_general(left, right, (dims, ((), ())), preferred_element_type=F32)  52.6 us
    ppermute x6, starting transfers between devices, local(): hop = lax.ppermute(hop, PLANE, AHEAD)  50.3 us
    ppermute x12, waiting for transfers between devices, routed(): moved = lax.ppermute(value, PLANE, [(a, b) for a, b in routes if a != b])  46.2 us
  transfers between devices with their start and end apart: 72, of which 33 were waited for; matrix products, arithmetic and copies ran while one was open for 15% of the time, Pallas kernels for 8%

profile of v5, /device:TPU:1, one launch (start us, length us, event | category | flops | bytes accessed | tf_op | source)
XLA Modules:
  0.0 1275.0 jit_solution(2920357088674878383)
XLA Ops:
  7.3 4.2 dynamic-slice_bitcast_fusion.2
  11.5 4.7 collective-permute-start
  34.2 8.7 collective-permute-done
  48.9 19.2 %collective-permute-done.16 = bf16[768,1536]{1,0:T(8,128)(2,1)} collective-permute-done((bf16[768,1536]{1,0:T(8,128)(2,1)}, bf16[768,1536]{1,0:T(8,128)(2,1)}, u32[]{:S(2)}, u32[]{:S(2)}) %collective-permute-start.16) | collective-permute-done | bytes 2359328 | tf_op jit(solution)/shard_map/ppermute | solution.py:686
  87.9 7.8 collective-permute-done.11
  115.2 4.6 collective-permute-done.12
  144.3 26.7 %section_forward.7 = (f32[2,1024,768]{2,1,0:T(8,128)}, bf16[2,1024,768]{2,1,0:T(8,128)(2,1)}, bf16[2,1024,768]{2,1,0:T(8,128)(2,1)}, bf16[2,1024,768]{2,1,0:T(8,...) custom-call(s32[5]{0:T(128)} %stack.251.refs_0_, ...), custom_call_target="tpu_custom_call" | custom-call | tf_op jit(solution)/shard_map/section_forward/pallas_call | solution.py:340
  173.2 10.9 collective-permute-done.23.refs_1_
  184.8 26.6 %section_forward.8 = (f32[2,1024,768]{2,1,0:T(8,128)}, bf16[2,1024,768]{2,1,0:T(8,128)(2,1)}, bf16[2,1024,768]{2,1,0:T(8,128)(2,1)}, bf16[2,1024,768]{2,1,0:T(8,...) custom-call(s32[5]{0:T(128)} %stack.247.refs_0_, ...), custom_call_target="tpu_custom_call", output_to_operand_aliasing={{0}: (25, {}), {1}: (26, {}), {2}: (27, {}), {3}: (28, {}),... | custom-call | tf_op jit(solution)/shard_map/section_forward/pallas_call | solution.py:340
  211.4 4.3 collective-permute-start.24
  216.4 7.2 collective-permute-done.24.refs_1_
  224.4 32.8 %section_forward.9 = (f32[2,1024,768]{2,1,0:T(8,128)}, bf16[2,1024,768]{2,1,0:T(8,128)(2,1)}, bf16[2,1024,768]{2,1,0:T(8,128)(2,1)}, bf16[2,1024,768]{2,1,0:T(8,...) custom-call(s32[5]{0:T(128)} %stack.243.refs_0_, ...), custom_call_target="tpu_custom_call", output_to_operand_aliasing={{0}: (25, {}), {1}: (26, {}), {2}: (27, {}), {3}: (28, {}),... | custom-call | tf_op jit(solution)/shard_map/section_forward/pallas_call | solution.py:340
  259.1 6.6 collective-permute-done.25.refs_1_
  266.4 33.2 %section_forward.10 = (f32[2,1024,768]{2,1,0:T(8,128)}, bf16[2,1024,768]{2,1,0:T(8,128)(2,1)}, bf16[2,1024,768]{2,1,0:T(8,128)(2,1)}, bf16[2,1024,768]{2,1,0:T(8...) custom-call(s32[5]{0:T(128)} %stack.239.refs_0_, ...), custom_call_target="tpu_custom_call", output_to_operand_aliasing={{0}: (25, {}), {1}: (26, {}), {2}: (27, {}), {3}: (28, {}),... | custom-call | tf_op jit(solution)/shard_map/section_forward/pallas_call | solution.py:340
  299.6 4.2 collective-permute-start.26
  304.4 5.7 collective-permute-done.26.refs_1_
  312.9 34.9 %collective-permute-start.27 = (bf16[256,768]{1,0:T(8,128)(2,1)}, bf16[256,768]{1,0:T(8,128)(2,1)S(1)}, u32[]{:S(2)}, u32[]{:S(2)}) collective-permute-start(bf16[256,768]{1,0:T(8,128)(2,1)} %get-tuple-element.298), channel_id=1, source_target_pairs={{0,1},{8,9},{1,17},{9,25},{17,16},{25,24},{2,3},{10,11},{3,19},{11... | collective-permute-start | bytes 1179656 | tf_op jit(solution)/shard_map/ppermute | solution.py:795
  348.4 4.7 collective-permute-done.27.refs_1_
  356.2 4.0 collective-permute-start.28
  372.2 36.8 %collective-permute-done.29.refs_2_ = bf16[256,768]{1,0:T(8,128)(2,1)S(1)} collective-permute-done((bf16[256,768]{1,0:T(8,128)(2,1)}, bf16[256,768]{1,0:T(8,128)(2,1)S(1)}, u32[]{:S(2)}, u32[]{:S(2)}) %collective-permute-start.29) | collective-permute-done | bytes 393248 | tf_op jit(solution)/shard_map/ppermute | solution.py:813
  413.7 7.2 collective-permute-done.30.refs_2_
  425.5 162.9 %collective-permute-done.31.refs_2_ = bf16[256,768]{1,0:T(8,128)(2,1)S(1)} collective-permute-done((bf16[256,768]{1,0:T(8,128)(2,1)}, bf16[256,768]{1,0:T(8,128)(2,1)S(1)}, u32[]{:S(2)}, u32[]{:S(2)}) %collective-permute-start.31) | collective-permute-done | bytes 393248 | tf_op jit(solution)/shard_map/ppermute | solution.py:813
  589.2 44.5 %section_backward.10 = (bf16[2,1024,768]{2,1,0:T(8,128)(2,1)}, bf16[2,1024,3072]{2,1,0:T(8,128)(2,1)}, bf16[2,1024,768]{2,1,0:T(8,128)(2,1)}, bf16[1024,128]{1,0...) custom-call(s32[5]{0:T(128)} %stack.257.refs_0_, ...), custom_call_target="tpu_custom_call", output_to_operand_aliasing={{0}: (34, {}), {1}: (35, {}), {2}: (36, {}), {3}: (37, {}),... | custom-call | tf_op jit(solution)/shard_map/section_backward/pallas_call | solution.py:608
  635.6 8.3 collective-permute-done.32.refs_2_
  644.6 45.0 %section_backward.11 = (bf16[2,1024,768]{2,1,0:T(8,128)(2,1)}, bf16[2,1024,3072]{2,1,0:T(8,128)(2,1)}, bf16[2,1024,768]{2,1,0:T(8,128)(2,1)}, bf16[1024,128]{1,0...) custom-call(s32[5]{0:T(128)} %stack.256.refs_0_, ...), custom_call_target="tpu_custom_call", output_to_operand_aliasing={{0}: (34, {}), {1}: (35, {}), {2}: (36, {}), {3}: (37, {}),... | custom-call | tf_op jit(solution)/shard_map/section_backward/pallas_call | solution.py:608
  691.5 6.8 collective-permute-done.33.refs_2_
  699.1 35.3 %section_backward.12 = (bf16[2,1024,768]{2,1,0:T(8,128)(2,1)}, bf16[2,1024,3072]{2,1,0:T(8,128)(2,1)}, bf16[2,1024,768]{2,1,0:T(8,128)(2,1)}, bf16[1024,128]{1,0...) custom-call(s32[5]{0:T(128)} %stack.255.refs_0_, ...), custom_call_target="tpu_custom_call", output_to_operand_aliasing={{0}: (34, {}), {1}: (35, {}), {2}: (36, {}), {3}: (37, {}),... | custom-call | tf_op jit(solution)/shard_map/section_backward/pallas_call | solution.py:608
  736.4 6.8 collective-permute-done.34.refs_2_
  743.9 35.8 %section_backward.13 = (bf16[2,1024,768]{2,1,0:T(8,128)(2,1)}, bf16[2,1024,3072]{2,1,0:T(8,128)(2,1)}, bf16[2,1024,768]{2,1,0:T(8,128)(2,1)}, bf16[1024,128]{1,0...) custom-call(s32[5]{0:T(128)} %stack.254.refs_0_, ...), custom_call_target="tpu_custom_call", output_to_operand_aliasing={{0}: (34, {}), {1}: (35, {}), {2}: (36, {}), {3}: (37, {}),... | custom-call | tf_op jit(solution)/shard_map/section_backward/pallas_call | solution.py:608
  779.7 5.2 convolution_convert_fusion.6
  784.9 11.0 collective-permute-start.35
  800.5 4.6 convolution_convert_fusion.7
  811.8 5.8 convolution_convert_fusion.2
  818.3 13.5 %collective-permute-done.37 = bf16[768,768]{1,0:T(8,128)(2,1)S(1)} collective-permute-done((bf16[768,768]{1,0:T(8,128)(2,1)S(1)}, bf16[768,768]{1,0:T(8,128)(2,1)S(1)}, u32[]{:S(2)}, u32[]{:S(2)}) %collective-permute-start.37) | collective-permute-done | bytes 1179680 | tf_op jit(solution)/shard_map/ppermute | solution.py:723
  837.9 44.6 %collective-permute-done.39 = bf16[1536,768]{1,0:T(8,128)(2,1)} collective-permute-done((bf16[1536,768]{1,0:T(8,128)(2,1)}, bf16[1536,768]{1,0:T(8,128)(2,1)}, u32[]{:S(2)}, u32[]{:S(2)}) %collective-permute-start.39) | collective-permute-done | bytes 2359328 | tf_op jit(solution)/shard_map/ppermute | solution.py:723
  882.5 4.4 add_convert_fusion.10
  889.1 6.1 add_convert_fusion.8
  895.2 8.4 collective-permute-start.47
  909.6 6.4 convolution_convert_fusion.4
  918.0 16.2 %collective-permute-done.45 = bf16[768,768]{1,0:T(8,128)(2,1)} collective-permute-done((bf16[768,768]{1,0:T(8,128)(2,1)}, bf16[768,768]{1,0:T(8,128)(2,1)}, u32[]{:S(2)}, u32[]{:S(2)}) %collective-permute-start.45) | collective-permute-done | bytes 1179680 | tf_op jit(solution)/shard_map/ppermute | solution.py:715
  940.2 11.3 collective-permute-done.47
  956.9 5.3 convolution_convert_fusion.5
  966.7 4.1 collective-permute-start.52
  970.8 4.0 convolution_convert_fusion
  976.3 4.0 collective-permute-done.49
  981.5 17.2 %collective-permute-done.48 = bf16[1536,768]{1,0:T(8,128)(2,1)S(1)} collective-permute-done((bf16[1536,768]{1,0:T(8,128)(2,1)S(1)}, bf16[1536,768]{1,0:T(8,128)(2,1)S(1)}, u32[]{:S(2)}, u32[]{:S(2)}) %collective-permute-start.48) | collective-permute-done | bytes 2359328 | tf_op jit(solution)/shard_map/ppermute | solution.py:715
  1009.0 10.7 collective-permute-done.52
  1022.7 5.2 add_convert_fusion.4
  1027.9 7.4 collective-permute-start.56
  1035.3 25.7 %collective-permute-done.53 = bf16[768,1536]{1,0:T(8,128)(2,1)S(1)} collective-permute-done((bf16[768,1536]{1,0:T(8,128)(2,1)S(1)}, bf16[768,1536]{1,0:T(8,128)(2,1)S(1)}, u32[]{:S(2)}, u32[]{:S(2)}) %collective-permute-start.53) | collective-permute-done | bytes 2359328 | tf_op jit(solution)/shard_map/ppermute | solution.py:715
  1072.5 9.4 collective-permute-done.56
  1082.0 4.4 add_convert_fusion.1
  1096.2 3.7 collective-permute-start.43
  1100.0 30.4 %collective-permute-done.57 = bf16[1536,768]{1,0:T(8,128)(2,1)} collective-permute-done((bf16[1536,768]{1,0:T(8,128)(2,1)}, bf16[1536,768]{1,0:T(8,128)(2,1)}, u32[]{:S(2)}, u32[]{:S(2)}) %collective-permute-start.57) | collective-permute-done | bytes 2359328 | tf_op jit(solution)/shard_map/ppermute | solution.py:715
  1137.3 4.5 add_convert_fusion
  1144.5 8.5 collective-permute-start.60
  1155.0 3.6 collective-permute-start.41
  1158.6 19.6 %collective-permute-done.60 = bf16[896,768]{1,0:T(8,128)(2,1)S(1)} collective-permute-done((bf16[896,768]{1,0:T(8,128)(2,1)S(1)}, bf16[896,768]{1,0:T(8,128)(2,1)S(1)}, u32[]{:S(2)}, u32[]{:S(2)}) %collective-permute-start.60) | collective-permute-done | bytes 1376288 | tf_op jit(solution)/shard_map/ppermute | solution.py:723
  1181.4 7.6 collective-permute-done.41
  1189.1 7.0 collective-permute-done.61
  1213.8 26.1 %collective-permute-done.64 = bf16[896,768]{1,0:T(8,128)(2,1)} collective-permute-done((bf16[896,768]{1,0:T(8,128)(2,1)}, bf16[896,768]{1,0:T(8,128)(2,1)}, u32[]{:S(2)}, u32[]{:S(2)}) %collective-permute-start.64) | collective-permute-done | bytes 1376288 | tf_op jit(solution)/shard_map/ppermute | solution.py:715
  1243.3 4.4 maximum_convert_fusion.1
  1250.1 4.4 maximum_convert_fusion
  1254.4 6.6 collective-permute-done.65
  (382 shorter events, 256.9 us)
Async XLA Ops:
  7.2 136.2 %all-gather.3.cloned.1.call-start = ((), (), s32[]{:S(2)}) async-start(), calls=%async_computation.2 | async-start | bytes 3538944 | tf_op jit(solution)/shard_map/all_gather | solution.py:776
  11.5 31.3 %collective-permute-start = (bf16[1536,768]{1,0:T(8,128)(2,1)S(1)}, bf16[1536,768]{1,0:T(8,128)(2,1)}, u32[]{:S(2)}, u32[]{:S(2)}) collective-permute-start(bf16[1536,768]{1,0:T(8,128)(2,1)S(1)} %get-tuple-element.454), channel_id=1, source_target_pairs={{1,8},{8,1},{16,17},{17,25},{24,16},{25,24},{3,10},{10,3},{18,19},... | collective-permute-start | bytes 7077896 | tf_op jit(solution)/shard_map/ppermute | solution.py:686
  18.7 49.4 %collective-permute-start.16 = (bf16[768,1536]{1,0:T(8,128)(2,1)}, bf16[768,1536]{1,0:T(8,128)(2,1)}, u32[]{:S(2)}, u32[]{:S(2)}) collective-permute-start(bf16[768,1536]{1,0:T(8,128)(2,1)} %get-tuple-element.452), channel_id=1, source_target_pairs={{1,8},{8,1},{16,17},{17,25},{24,16},{25,24},{3,10},{10,3},{18,19},... | collective-permute-start | bytes 7077896 | tf_op jit(solution)/shard_map/ppermute | solution.py:686
  26.5 48.6 %collective-permute-start.1 = (f32[103,128]{1,0:T(8,128)}, f32[103,128]{1,0:T(8,128)}, u32[]{:S(2)}, u32[]{:S(2)}) collective-permute-start(f32[103,128]{1,0:T(8,128)} %bitcast.19), channel_id=1, source_target_pairs={{1,8},{8,1},{16,17},{17,25},{24,16},{25,24},{3,10},{10,3},{18,19},... | collective-permute-start | bytes 158216 | tf_op jit(solution)/shard_map/ppermute | solution.py:686
  30.2 47.1 %collective-permute-start.3 = (bf16[768,128]{1,0:T(8,128)(2,1)}, bf16[768,128]{1,0:T(8,128)(2,1)}, u32[]{:S(2)}, u32[]{:S(2)}) collective-permute-start(bf16[768,128]{1,0:T(8,128)(2,1)} %bitcast.24), channel_id=1, source_target_pairs={{1,8},{8,1},{16,17},{17,25},{24,16},{25,24},{3,10},{10,3},{18,19},... | collective-permute-start | bytes 589832 | tf_op jit(solution)/shard_map/ppermute | solution.py:686
  32.1 64.3 %collective-permute-start.9 = (bf16[1536,768]{1,0:T(8,128)(2,1)}, bf16[1536,768]{1,0:T(8,128)(2,1)}, u32[]{:S(2)}, u32[]{:S(2)}) collective-permute-start(bf16[1536,768]{1,0:T(8,128)(2,1)} %get-tuple-element.453), channel_id=1, source_target_pairs={{17,25},{24,16},{19,27},{26,18},{21,29},{28,20},{23,31},{30,22}} | collective-permute-start | bytes 7077896 | tf_op jit(solution)/shard_map/ppermute | solution.py:680
  44.8 52.4 %collective-permute-start.8 = (bf16[1536,768]{1,0:T(8,128)(2,1)S(1)}, bf16[1536,768]{1,0:T(8,128)(2,1)}, u32[]{:S(2)}, u32[]{:S(2)}) collective-permute-start(bf16[1536,768]{1,0:T(8,128)(2,1)S(1)} %broadcast_select_fusion.10.refs_21_), channel_id=1, source_target_pairs={{10,8},{8,10},{14,12},{12,14},{3,1},{1,3},{7,5},{5,7},{19,17},{17,... | collective-permute-start | bytes 7077896 | tf_op jit(solution)/shard_map/ppermute | solution.py:679
  68.1 13.7 %collective-permute-start.4 = (bf16[768,384]{1,0:T(8,128)(2,1)S(1)}, bf16[768,384]{1,0:T(8,128)(2,1)S(1)}, u32[]{:S(2)}, u32[]{:S(2)}) collective-permute-start(bf16[768,384]{1,0:T(8,128)(2,1)S(1)} %get-tuple-element.462), channel_id=1, source_target_pairs={{1,8},{8,1},{16,17},{17,25},{24,16},{25,24},{3,10},{10,3},{18,19},... | collective-permute-start | bytes 1769480 | tf_op jit(solution)/shard_map/ppermute | solution.py:686
  75.1 27.5 %collective-permute-start.18 = (bf16[768,1536]{1,0:T(8,128)(2,1)}, bf16[768,1536]{1,0:T(8,128)(2,1)}, u32[]{:S(2)}, u32[]{:S(2)}) collective-permute-start(bf16[768,1536]{1,0:T(8,128)(2,1)} %get-tuple-element.451), channel_id=1, source_target_pairs={{17,25},{24,16},{19,27},{26,18},{21,29},{28,20},{23,31},{30,22}} | collective-permute-start | bytes 7077896 | tf_op jit(solution)/shard_map/ppermute | solution.py:680
  77.2 30.2 %collective-permute-start.17 = (bf16[768,1536]{1,0:T(8,128)(2,1)}, bf16[768,1536]{1,0:T(8,128)(2,1)}, u32[]{:S(2)}, u32[]{:S(2)}) collective-permute-start(bf16[768,1536]{1,0:T(8,128)(2,1)} %broadcast_select_fusion.7.refs_17_), channel_id=1, source_target_pairs={{10,8},{8,10},{14,12},{12,14},{3,1},{1,3},{7,5},{5,7},{19,17},{17,... | collective-permute-start | bytes 7077896 | tf_op jit(solution)/shard_map/ppermute | solution.py:679
  80.5 287.6 %all-gather.5.cloned.1.call-start = ((), (), s32[]{:S(2)}) async-start(), calls=%async_computation.4 | async-start | bytes 3538944 | tf_op jit(solution)/shard_map/all_gather | solution.py:793
  81.9 13.8 %collective-permute-start.11 = (bf16[384,768]{1,0:T(8,128)(2,1)S(1)}, bf16[384,768]{1,0:T(8,128)(2,1)S(1)}, u32[]{:S(2)}, u32[]{:S(2)}) collective-permute-start(bf16[384,768]{1,0:T(8,128)(2,1)S(1)} %get-tuple-element.460), channel_id=1, source_target_pairs={{1,8},{8,1},{16,17},{17,25},{24,16},{25,24},{3,10},{10,3},{18,19},... | collective-permute-start | bytes 1769480 | tf_op jit(solution)/shard_map/ppermute | solution.py:686
  95.7 15.1 %collective-permute-start.6 = (bf16[768,384]{1,0:T(8,128)(2,1)}, bf16[768,384]{1,0:T(8,128)(2,1)S(1)}, u32[]{:S(2)}, u32[]{:S(2)}) collective-permute-start(bf16[768,384]{1,0:T(8,128)(2,1)} %get-tuple-element.461), channel_id=1, source_target_pairs={{17,25},{24,16},{19,27},{26,18},{21,29},{28,20},{23,31},{30,22}} | collective-permute-start | bytes 1769480 | tf_op jit(solution)/shard_map/ppermute | solution.py:680
  96.5 15.7 %collective-permute-start.13 = (bf16[384,768]{1,0:T(8,128)(2,1)S(1)}, bf16[384,768]{1,0:T(8,128)(2,1)S(1)}, u32[]{:S(2)}, u32[]{:S(2)}) collective-permute-start(bf16[384,768]{1,0:T(8,128)(2,1)S(1)} %get-tuple-element.459), channel_id=1, source_target_pairs={{17,25},{24,16},{19,27},{26,18},{21,29},{28,20},{23,31},{30,22}} | collective-permute-start | bytes 1769480 | tf_op jit(solution)/shard_map/ppermute | solution.py:680
  100.7 13.1 %collective-permute-start.5 = (bf16[768,384]{1,0:T(8,128)(2,1)S(1)}, bf16[768,384]{1,0:T(8,128)(2,1)S(1)}, u32[]{:S(2)}, u32[]{:S(2)}) collective-permute-start(bf16[768,384]{1,0:T(8,128)(2,1)S(1)} %broadcast_select_fusion.18.refs_9_), channel_id=1, source_target_pairs={{10,8},{8,10},{14,12},{12,14},{3,1},{1,3},{7,5},{5,7},{19,17},{17,... | collective-permute-start | bytes 1769480 | tf_op jit(solution)/shard_map/ppermute | solution.py:679
  102.6 17.1 %collective-permute-start.12 = (bf16[384,768]{1,0:T(8,128)(2,1)S(1)}, bf16[384,768]{1,0:T(8,128)(2,1)}, u32[]{:S(2)}, u32[]{:S(2)}) collective-permute-start(bf16[384,768]{1,0:T(8,128)(2,1)S(1)} %broadcast_select_fusion.17.refs_13_), channel_id=1, source_target_pairs={{10,8},{8,10},{14,12},{12,14},{3,1},{1,3},{7,5},{5,7},{19,17},{17,... | collective-permute-start | bytes 1769480 | tf_op jit(solution)/shard_map/ppermute | solution.py:679
  107.4 22.9 %collective-permute-start.19 = (bf16[768,1536]{1,0:T(8,128)(2,1)}, bf16[768,1536]{1,0:T(8,128)(2,1)}, u32[]{:S(2)}, u32[]{:S(2)}) collective-permute-start(bf16[768,1536]{1,0:T(8,128)(2,1)} %broadcast_select_fusion.7.refs_17_), channel_id=1, source_target_pairs={{0,8},{8,0},{16,24},{24,16},{1,9},{9,1},{17,25},{25,17},{2,10},{10... | collective-permute-start | bytes 7077896 | tf_op jit(solution)/shard_map/ppermute | solution.py:691
  110.8 32.5 %collective-permute-start.21 = (bf16[1536,768]{1,0:T(8,128)(2,1)S(1)}, bf16[1536,768]{1,0:T(8,128)(2,1)}, u32[]{:S(2)}, u32[]{:S(2)}) collective-permute-start(bf16[1536,768]{1,0:T(8,128)(2,1)S(1)} %broadcast_select_fusion.10.refs_21_), channel_id=1, source_target_pairs={{0,8},{8,0},{16,24},{24,16},{1,9},{9,1},{17,25},{25,17},{2,10},{10... | collective-permute-start | bytes 7077896 | tf_op jit(solution)/shard_map/ppermute | solution.py:691
  112.2 31.2 %collective-permute-start.20 = (bf16[768,1536]{1,0:T(8,128)(2,1)}, bf16[768,1536]{1,0:T(8,128)(2,1)}, u32[]{:S(2)}, u32[]{:S(2)}) collective-permute-start(bf16[768,1536]{1,0:T(8,128)(2,1)} %select_select_fusion.refs_18_), channel_id=1, source_target_pairs={{0,8},{8,0},{16,24},{24,16},{1,9},{9,1},{17,25},{25,17},{2,10},{10... | collective-permute-start | bytes 7077896 | tf_op jit(solution)/shard_map/ppermute | solution.py:691
  113.7 29.6 %collective-permute-start.22 = (bf16[1536,768]{1,0:T(8,128)(2,1)}, bf16[1536,768]{1,0:T(8,128)(2,1)}, u32[]{:S(2)}, u32[]{:S(2)}) collective-permute-start(bf16[1536,768]{1,0:T(8,128)(2,1)} %select_select_fusion.1.refs_22_), channel_id=1, source_target_pairs={{0,8},{8,0},{16,24},{24,16},{1,9},{9,1},{17,25},{25,17},{2,10},{10... | collective-permute-start | bytes 7077896 | tf_op jit(solution)/shard_map/ppermute | solution.py:691
  130.3 13.0 %collective-permute-start.10 = (bf16[768,384]{1,0:T(8,128)(2,1)S(1)}, bf16[768,384]{1,0:T(8,128)(2,1)S(1)}, u32[]{:S(2)}, u32[]{:S(2)}) collective-permute-start(bf16[768,384]{1,0:T(8,128)(2,1)S(1)} %select_select_fusion.3.refs_10_), channel_id=1, source_target_pairs={{0,8},{8,0},{16,24},{24,16},{1,9},{9,1},{17,25},{25,17},{2,10},{10... | collective-permute-start | bytes 1769480 | tf_op jit(solution)/shard_map/ppermute | solution.py:691
  130.3 13.0 %collective-permute-start.15 = (bf16[384,768]{1,0:T(8,128)(2,1)}, bf16[384,768]{1,0:T(8,128)(2,1)}, u32[]{:S(2)}, u32[]{:S(2)}) collective-permute-start(bf16[384,768]{1,0:T(8,128)(2,1)} %select_select_fusion.2.refs_14_), channel_id=1, source_target_pairs={{0,8},{8,0},{16,24},{24,16},{1,9},{9,1},{17,25},{25,17},{2,10},{10... | collective-permute-start | bytes 1769480 | tf_op jit(solution)/shard_map/ppermute | solution.py:691
  171.0 983.9 %all-reduce.3.cloned.1.call-start = ((), (), s32[]{:S(2)}) async-start(), calls=%async_computation.6 | async-start | bytes 196608 | tf_op jit(solution)/shard_map/psum | solution.py:875
  171.1 13.0 %collective-permute-start.23 = (bf16[256,768]{1,0:T(8,128)(2,1)}, bf16[256,768]{1,0:T(8,128)(2,1)S(1)}, u32[]{:S(2)}, u32[]{:S(2)}) collective-permute-start(bf16[256,768]{1,0:T(8,128)(2,1)} %get-tuple-element.234), channel_id=1, source_target_pairs={{0,1},{8,9},{1,17},{9,25},{17,16},{25,24},{2,3},{10,11},{3,19},{11... | collective-permute-start | bytes 1179656 | tf_op jit(solution)/shard_map/ppermute | solution.py:795
  211.4 12.2 collective-permute-start.24
  299.6 10.5 collective-permute-start.26
  312.9 40.3 %collective-permute-start.27 = (bf16[256,768]{1,0:T(8,128)(2,1)}, bf16[256,768]{1,0:T(8,128)(2,1)S(1)}, u32[]{:S(2)}, u32[]{:S(2)}) collective-permute-start(bf16[256,768]{1,0:T(8,128)(2,1)} %get-tuple-element.298), channel_id=1, source_target_pairs={{0,1},{8,9},{1,17},{9,25},{17,16},{25,24},{2,3},{10,11},{3,19},{11... | collective-permute-start | bytes 1179656 | tf_op jit(solution)/shard_map/ppermute | solution.py:795
  356.2 9.0 collective-permute-start.28
  370.3 38.7 %collective-permute-start.29 = (bf16[256,768]{1,0:T(8,128)(2,1)}, bf16[256,768]{1,0:T(8,128)(2,1)S(1)}, u32[]{:S(2)}, u32[]{:S(2)}) collective-permute-start(bf16[256,768]{1,0:T(8,128)(2,1)} %get-tuple-element.342), channel_id=1, source_target_pairs={{1,0},{9,8},{17,1},{25,9},{16,17},{24,25},{3,2},{11,10},{19,3},{27... | collective-permute-start | bytes 1179656 | tf_op jit(solution)/shard_map/ppermute | solution.py:813
  411.8 9.1 collective-permute-start.30
  423.6 164.9 %collective-permute-start.31 = (bf16[256,768]{1,0:T(8,128)(2,1)}, bf16[256,768]{1,0:T(8,128)(2,1)S(1)}, u32[]{:S(2)}, u32[]{:S(2)}) collective-permute-start(bf16[256,768]{1,0:T(8,128)(2,1)} %get-tuple-element.360), channel_id=1, source_target_pairs={{1,0},{9,8},{17,1},{25,9},{16,17},{24,25},{3,2},{11,10},{19,3},{27... | collective-permute-start | bytes 1179656 | tf_op jit(solution)/shard_map/ppermute | solution.py:813
  633.6 10.2 collective-permute-start.32
  784.9 22.2 %collective-permute-start.35 = (bf16[1536,768]{1,0:T(8,128)(2,1)S(1)}, bf16[1536,768]{1,0:T(8,128)(2,1)S(1)}, u32[]{:S(2)}, u32[]{:S(2)}) collective-permute-start(bf16[1536,768]{1,0:T(8,128)(2,1)S(1)} %convolution_convert_fusion.6), channel_id=1, source_target_pairs={{0,8},{8,0},{16,24},{24,16},{1,9},{9,1},{17,25},{25,17},{2,10},{10... | collective-permute-start | bytes 7077896 | tf_op jit(solution)/shard_map/ppermute | solution.py:691
  805.3 26.5 %collective-permute-start.37 = (bf16[768,768]{1,0:T(8,128)(2,1)S(1)}, bf16[768,768]{1,0:T(8,128)(2,1)S(1)}, u32[]{:S(2)}, u32[]{:S(2)}) collective-permute-start(bf16[768,768]{1,0:T(8,128)(2,1)S(1)} %add_convert_fusion.17), channel_id=1, source_target_pairs={{0,2},{6,4},{1,3},{7,5},{8,10},{14,12},{9,11},{15,13},{16,18},{22,... | collective-permute-start | bytes 3538952 | tf_op jit(solution)/shard_map/ppermute | solution.py:723
  809.1 73.4 %collective-permute-start.39 = (bf16[1536,768]{1,0:T(8,128)(2,1)}, bf16[1536,768]{1,0:T(8,128)(2,1)}, u32[]{:S(2)}, u32[]{:S(2)}) collective-permute-start(bf16[1536,768]{1,0:T(8,128)(2,1)} %add_convert_fusion.11), channel_id=1, source_target_pairs={{0,2},{6,4},{1,3},{7,5},{8,10},{14,12},{9,11},{15,13},{16,18},{22,... | collective-permute-start | bytes 7077896 | tf_op jit(solution)/shard_map/ppermute | solution.py:723
  817.6 71.5 %collective-permute-start.44 = (bf16[768,1536]{1,0:T(8,128)(2,1)}, bf16[768,1536]{1,0:T(8,128)(2,1)}, u32[]{:S(2)}, u32[]{:S(2)}) collective-permute-start(bf16[768,1536]{1,0:T(8,128)(2,1)} %convolution_convert_fusion.2), channel_id=1, source_target_pairs={{0,8},{8,0},{16,24},{24,16},{1,9},{9,1},{17,25},{25,17},{2,10},{10... | collective-permute-start | bytes 7077896 | tf_op jit(solution)/shard_map/ppermute | solution.py:691
  886.9 48.8 %collective-permute-start.46 = (bf16[1536,768]{1,0:T(8,128)(2,1)}, bf16[1536,768]{1,0:T(8,128)(2,1)}, u32[]{:S(2)}, u32[]{:S(2)}) collective-permute-start(bf16[1536,768]{1,0:T(8,128)(2,1)} %add_convert_fusion.10), channel_id=1, source_target_pairs={{2,4},{4,2},{3,5},{5,3},{10,12},{12,10},{11,13},{13,11},{18,20},{2... | collective-permute-start | bytes 7077896 | tf_op jit(solution)/shard_map/ppermute | solution.py:713
  895.2 56.2 %collective-permute-start.47 = (bf16[768,1536]{1,0:T(8,128)(2,1)}, bf16[768,1536]{1,0:T(8,128)(2,1)}, u32[]{:S(2)}, u32[]{:S(2)}) collective-permute-start(bf16[768,1536]{1,0:T(8,128)(2,1)} %add_convert_fusion.8), channel_id=1, source_target_pairs={{0,2},{6,4},{1,3},{7,5},{8,10},{14,12},{9,11},{15,13},{16,18},{22,... | collective-permute-start | bytes 7077896 | tf_op jit(solution)/shard_map/ppermute | solution.py:723
  906.4 27.8 %collective-permute-start.45 = (bf16[768,768]{1,0:T(8,128)(2,1)}, bf16[768,768]{1,0:T(8,128)(2,1)}, u32[]{:S(2)}, u32[]{:S(2)}) collective-permute-start(bf16[768,768]{1,0:T(8,128)(2,1)} %add_convert_fusion.15), channel_id=1, source_target_pairs={{2,0},{4,6},{3,1},{5,7},{10,8},{12,14},{11,9},{13,15},{18,16},{20,... | collective-permute-start | bytes 3538952 | tf_op jit(solution)/shard_map/ppermute | solution.py:715
  916.0 48.4 %collective-permute-start.42 = (bf16[1536,768]{1,0:T(8,128)(2,1)}, bf16[1536,768]{1,0:T(8,128)(2,1)}, u32[]{:S(2)}, u32[]{:S(2)}) collective-permute-start(bf16[1536,768]{1,0:T(8,128)(2,1)} %convolution_convert_fusion.4), channel_id=1, source_target_pairs={{0,8},{8,0},{16,24},{24,16},{1,9},{9,1},{17,25},{25,17},{2,10},{10... | collective-permute-start | bytes 7077896 | tf_op jit(solution)/shard_map/ppermute | solution.py:691
  938.6 60.1 %collective-permute-start.48 = (bf16[1536,768]{1,0:T(8,128)(2,1)S(1)}, bf16[1536,768]{1,0:T(8,128)(2,1)S(1)}, u32[]{:S(2)}, u32[]{:S(2)}) collective-permute-start(bf16[1536,768]{1,0:T(8,128)(2,1)S(1)} %add_convert_fusion.7), channel_id=1, source_target_pairs={{2,0},{4,6},{3,1},{5,7},{10,8},{12,14},{11,9},{13,15},{18,16},{20,... | collective-permute-start | bytes 7077896 | tf_op jit(solution)/shard_map/ppermute | solution.py:715
  954.6 44.3 %collective-permute-start.50 = (bf16[768,1536]{1,0:T(8,128)(2,1)S(1)}, bf16[768,1536]{1,0:T(8,128)(2,1)}, u32[]{:S(2)}, u32[]{:S(2)}) collective-permute-start(bf16[768,1536]{1,0:T(8,128)(2,1)S(1)} %add_convert_fusion.6), channel_id=1, source_target_pairs={{2,4},{4,2},{3,5},{5,3},{10,12},{12,10},{11,13},{13,11},{18,20},{2... | collective-permute-start | bytes 7077896 | tf_op jit(solution)/shard_map/ppermute | solution.py:713
  962.2 18.1 %collective-permute-start.49 = (bf16[768,768]{1,0:T(8,128)(2,1)S(1)}, bf16[768,768]{1,0:T(8,128)(2,1)S(1)}, u32[]{:S(2)}, u32[]{:S(2)}) collective-permute-start(bf16[768,768]{1,0:T(8,128)(2,1)S(1)} %broadcast_select_fusion.16), channel_id=1, source_target_pairs={{8,1},{1,8},{17,16},{25,17},{16,24},{24,25},{10,3},{3,10},{19,18},... | collective-permute-start | bytes 3538952 | tf_op jit(solution)/shard_map/ppermute | solution.py:686
  966.7 53.0 %collective-permute-start.52 = (bf16[1536,768]{1,0:T(8,128)(2,1)S(1)}, bf16[1536,768]{1,0:T(8,128)(2,1)S(1)}, u32[]{:S(2)}, u32[]{:S(2)}) collective-permute-start(bf16[1536,768]{1,0:T(8,128)(2,1)S(1)} %add_convert_fusion.9), channel_id=1, source_target_pairs={{0,2},{6,4},{1,3},{7,5},{8,10},{14,12},{9,11},{15,13},{16,18},{22,... | collective-permute-start | bytes 7077896 | tf_op jit(solution)/shard_map/ppermute | solution.py:723
  974.8 47.9 %collective-permute-start.51 = (bf16[768,1536]{1,0:T(8,128)(2,1)}, bf16[768,1536]{1,0:T(8,128)(2,1)}, u32[]{:S(2)}, u32[]{:S(2)}) collective-permute-start(bf16[768,1536]{1,0:T(8,128)(2,1)} %convolution_convert_fusion), channel_id=1, source_target_pairs={{0,8},{8,0},{16,24},{24,16},{1,9},{9,1},{17,25},{25,17},{2,10},{10... | collective-permute-start | bytes 7077896 | tf_op jit(solution)/shard_map/ppermute | solution.py:691
  1001.4 59.6 %collective-permute-start.53 = (bf16[768,1536]{1,0:T(8,128)(2,1)S(1)}, bf16[768,1536]{1,0:T(8,128)(2,1)S(1)}, u32[]{:S(2)}, u32[]{:S(2)}) collective-permute-start(bf16[768,1536]{1,0:T(8,128)(2,1)S(1)} %add_convert_fusion.5), channel_id=1, source_target_pairs={{2,0},{4,6},{3,1},{5,7},{10,8},{12,14},{11,9},{13,15},{18,16},{20,... | collective-permute-start | bytes 7077896 | tf_op jit(solution)/shard_map/ppermute | solution.py:715
  1002.7 67.0 %collective-permute-start.40 = (f32[2,12,768]{2,1,0:T(8,128)S(1)}, f32[2,12,768]{2,1,0:T(8,128)S(1)}, u32[]{:S(2)}, u32[]{:S(2)}) collective-permute-start(f32[2,12,768]{2,1,0:T(8,128)S(1)} %pad_maximum_fusion.4), channel_id=1, source_target_pairs={{0,8},{8,0},{16,24},{24,16},{1,9},{9,1},{17,25},{25,17},{2,10},{10... | collective-permute-start | bytes 221192 | tf_op jit(solution)/shard_map/ppermute | solution.py:691
  1007.0 55.6 %collective-permute-start.54 = (bf16[1536,768]{1,0:T(8,128)(2,1)S(1)}, bf16[1536,768]{1,0:T(8,128)(2,1)}, u32[]{:S(2)}, u32[]{:S(2)}) collective-permute-start(bf16[1536,768]{1,0:T(8,128)(2,1)S(1)} %broadcast_select_fusion.5), channel_id=1, source_target_pairs={{8,1},{1,8},{17,16},{25,17},{16,24},{24,25},{10,3},{3,10},{19,18},... | collective-permute-start | bytes 7077896 | tf_op jit(solution)/shard_map/ppermute | solution.py:686
  1020.3 45.7 %collective-permute-start.55 = (bf16[1536,768]{1,0:T(8,128)(2,1)S(1)}, bf16[1536,768]{1,0:T(8,128)(2,1)S(1)}, u32[]{:S(2)}, u32[]{:S(2)}) collective-permute-start(bf16[1536,768]{1,0:T(8,128)(2,1)S(1)} %add_convert_fusion.3), channel_id=1, source_target_pairs={{2,4},{4,2},{3,5},{5,3},{10,12},{12,10},{11,13},{13,11},{18,20},{2... | collective-permute-start | bytes 7077896 | tf_op jit(solution)/shard_map/ppermute | solution.py:713
  1027.9 54.1 %collective-permute-start.56 = (bf16[768,1536]{1,0:T(8,128)(2,1)}, bf16[768,1536]{1,0:T(8,128)(2,1)}, u32[]{:S(2)}, u32[]{:S(2)}) collective-permute-start(bf16[768,1536]{1,0:T(8,128)(2,1)} %add_convert_fusion.4), channel_id=1, source_target_pairs={{0,2},{6,4},{1,3},{7,5},{8,10},{14,12},{9,11},{15,13},{16,18},{22,... | collective-permute-start | bytes 7077896 | tf_op jit(solution)/shard_map/ppermute | solution.py:723
  1068.0 62.4 %collective-permute-start.57 = (bf16[1536,768]{1,0:T(8,128)(2,1)}, bf16[1536,768]{1,0:T(8,128)(2,1)}, u32[]{:S(2)}, u32[]{:S(2)}) collective-permute-start(bf16[1536,768]{1,0:T(8,128)(2,1)} %add_convert_fusion.2), channel_id=1, source_target_pairs={{2,0},{4,6},{3,1},{5,7},{10,8},{12,14},{11,9},{13,15},{18,16},{20,... | collective-permute-start | bytes 7077896 | tf_op jit(solution)/shard_map/ppermute | solution.py:715
  1070.4 141.3 %reduce-scatter.5.cloned.1.call-start = ((), (), s32[]{:S(2)}) async-start(), calls=%async_computation.5 | async-start | bytes 3538944 | tf_op jit(solution)/shard_map/reduce_scatter | solution.py:801
  1070.5 63.5 %collective-permute-start.58 = (bf16[768,1536]{1,0:T(8,128)(2,1)}, bf16[768,1536]{1,0:T(8,128)(2,1)}, u32[]{:S(2)}, u32[]{:S(2)}) collective-permute-start(bf16[768,1536]{1,0:T(8,128)(2,1)} %broadcast_select_fusion.3), channel_id=1, source_target_pairs={{8,1},{1,8},{17,16},{25,17},{16,24},{24,25},{10,3},{3,10},{19,18},... | collective-permute-start | bytes 7077896 | tf_op jit(solution)/shard_map/ppermute | solution.py:686
  1086.4 50.9 %collective-permute-start.59 = (bf16[768,1536]{1,0:T(8,128)(2,1)}, bf16[768,1536]{1,0:T(8,128)(2,1)}, u32[]{:S(2)}, u32[]{:S(2)}) collective-permute-start(bf16[768,1536]{1,0:T(8,128)(2,1)} %add_convert_fusion.1), channel_id=1, source_target_pairs={{2,4},{4,2},{3,5},{5,3},{10,12},{12,10},{11,13},{13,11},{18,20},{2... | collective-permute-start | bytes 7077896 | tf_op jit(solution)/shard_map/ppermute | solution.py:713
  1091.9 176.1 %reduce-scatter.3.cloned.1.call-start = ((), (), s32[]{:S(2)}) async-start(), calls=%async_computation.3 | async-start | bytes 3538944 | tf_op jit(solution)/shard_map/reduce_scatter | solution.py:801
  1096.2 47.8 %collective-permute-start.43 = (bf16[896,768]{1,0:T(8,128)(2,1)S(1)}, bf16[896,768]{1,0:T(8,128)(2,1)S(1)}, u32[]{:S(2)}, u32[]{:S(2)}) collective-permute-start(bf16[896,768]{1,0:T(8,128)(2,1)S(1)} %pad_maximum_fusion), channel_id=1, source_target_pairs={{0,8},{8,0},{16,24},{24,16},{1,9},{9,1},{17,25},{25,17},{2,10},{10... | collective-permute-start | bytes 4128776 | tf_op jit(solution)/shard_map/ppermute | solution.py:691
  1141.8 54.3 %collective-permute-start.61 = (bf16[768,1536]{1,0:T(8,128)(2,1)}, bf16[768,1536]{1,0:T(8,128)(2,1)}, u32[]{:S(2)}, u32[]{:S(2)}) collective-permute-start(bf16[768,1536]{1,0:T(8,128)(2,1)} %add_convert_fusion), channel_id=1, source_target_pairs={{2,0},{4,6},{3,1},{5,7},{10,8},{12,14},{11,9},{13,15},{18,16},{20,... | collective-permute-start | bytes 7077896 | tf_op jit(solution)/shard_map/ppermute | solution.py:715
  1144.5 33.8 %collective-permute-start.60 = (bf16[896,768]{1,0:T(8,128)(2,1)S(1)}, bf16[896,768]{1,0:T(8,128)(2,1)S(1)}, u32[]{:S(2)}, u32[]{:S(2)}) collective-permute-start(bf16[896,768]{1,0:T(8,128)(2,1)S(1)} %add_convert_fusion.14), channel_id=1, source_target_pairs={{0,2},{6,4},{1,3},{7,5},{8,10},{14,12},{9,11},{15,13},{16,18},{22,... | collective-permute-start | bytes 4128776 | tf_op jit(solution)/shard_map/ppermute | solution.py:723
  1153.0 47.1 %collective-permute-start.62 = (bf16[1536,768]{1,0:T(8,128)(2,1)}, bf16[1536,768]{1,0:T(8,128)(2,1)}, u32[]{:S(2)}, u32[]{:S(2)}) collective-permute-start(bf16[1536,768]{1,0:T(8,128)(2,1)} %broadcast_select_fusion.4), channel_id=1, source_target_pairs={{8,1},{1,8},{17,16},{25,17},{16,24},{24,25},{10,3},{3,10},{19,18},... | collective-permute-start | bytes 7077896 | tf_op jit(solution)/shard_map/ppermute | solution.py:686
  1155.0 34.1 %collective-permute-start.41 = (f32[2,12,768]{2,1,0:T(8,128)}, f32[2,12,768]{2,1,0:T(8,128)S(1)}, u32[]{:S(2)}, u32[]{:S(2)}) collective-permute-start(f32[2,12,768]{2,1,0:T(8,128)} %all-reduce.3.cloned.1.call-done), channel_id=1, source_target_pairs={{0,0},{8,1},{1,8},{9,9},{17,16},{25,17},{16,24},{24,25},{2,2},{10,... | collective-permute-start | bytes 221192 | tf_op jit(solution)/shard_map/ppermute | solution.py:875
  1179.6 23.9 %collective-permute-start.63 = (bf16[896,768]{1,0:T(8,128)(2,1)}, bf16[896,768]{1,0:T(8,128)(2,1)}, u32[]{:S(2)}, u32[]{:S(2)}) collective-permute-start(bf16[896,768]{1,0:T(8,128)(2,1)} %add_convert_fusion.13), channel_id=1, source_target_pairs={{2,4},{4,2},{3,5},{5,3},{10,12},{12,10},{11,13},{13,11},{18,20},{2... | collective-permute-start | bytes 4128776 | tf_op jit(solution)/shard_map/ppermute | solution.py:713
  1198.2 49.5 %collective-permute-start.66 = (bf16[768,1536]{1,0:T(8,128)(2,1)S(1)}, bf16[768,1536]{1,0:T(8,128)(2,1)}, u32[]{:S(2)}, u32[]{:S(2)}) collective-permute-start(bf16[768,1536]{1,0:T(8,128)(2,1)S(1)} %broadcast_select_fusion.2), channel_id=1, source_target_pairs={{8,1},{1,8},{17,16},{25,17},{16,24},{24,25},{10,3},{3,10},{19,18},... | collective-permute-start | bytes 7077896 | tf_op jit(solution)/shard_map/ppermute | solution.py:686
  1206.8 33.1 %collective-permute-start.64 = (bf16[896,768]{1,0:T(8,128)(2,1)}, bf16[896,768]{1,0:T(8,128)(2,1)}, u32[]{:S(2)}, u32[]{:S(2)}) collective-permute-start(bf16[896,768]{1,0:T(8,128)(2,1)} %add_convert_fusion.12), channel_id=1, source_target_pairs={{2,0},{4,6},{3,1},{5,7},{10,8},{12,14},{11,9},{13,15},{18,16},{20,... | collective-permute-start | bytes 4128776 | tf_op jit(solution)/shard_map/ppermute | solution.py:715
  1241.4 19.6 %collective-permute-start.65 = (bf16[896,768]{1,0:T(8,128)(2,1)S(1)}, bf16[896,768]{1,0:T(8,128)(2,1)S(1)}, u32[]{:S(2)}, u32[]{:S(2)}) collective-permute-start(bf16[896,768]{1,0:T(8,128)(2,1)S(1)} %broadcast_select_fusion.13), channel_id=1, source_target_pairs={{8,1},{1,8},{17,16},{25,17},{16,24},{24,25},{10,3},{3,10},{19,18},... | collective-permute-start | bytes 4128776 | tf_op jit(solution)/shard_map/ppermute | solution.py:686
  (75 other events, 749.5 us)
Sparse Core Ops, SparseCore 0:
  80.6 39.1 all-gather.2
  171.1 33.6 all-gather.4
  1070.5 42.4 all-reduce.2
  1117.2 54.3 reduce-scatter.4
  1189.2 49.4 reduce-scatter.2

commit v6 on v5

--- a/solution.py
+++ b/solution.py
@@ -13,6 +13,7 @@
 ROWS = 256
 NORM_ROWS = 64
 SPAN = 512
+WAYS = 3
 VMEM_LIMIT = 60 * 2**20
 ANY = pl.BlockSpec(memory_space=pl.ANY)
 SMEM = pl.BlockSpec(memory_space=pltpu.SMEM)
@@ -54,12 +55,11 @@
 
 def staged(total, stages):
     def turns(t):
-        for half in range(2):
-            for k, stage in enumerate(stages):
-                u = 2 * t + half - k
-                stage(jnp.clip(u, 0, total - 1), (half - k) % 2, u >= 0)
-
-    steps((total + len(stages)) // 2, turns)
+        for stage in stages:
+            for way in range(WAYS):
+                stage(WAYS * t + way, way)
+
+    steps(total // WAYS, turns)
 
 
 def fold(values):
@@ -128,7 +128,7 @@
     at = 9 + N_W + (0 if fresh else n_state)
     st = dict(zip(FWD_STATE, refs[at : at + n_state]))
     hop_out = refs[at + n_state]
-    (x_s, xf_s, h1_s, h2_s, q_s, qt_s, o_s, ot_s, a_s, g_s, l_s, kd_s, vd_s, kt_s, vt_s, vtc_s, s0_s, s1_s, e0_s, e1_s, top_s, sum_s, part_s, *weights, sems, once, wsems) = refs[at + n_state + 1 :]
+    (x_s, xf_s, h1_s, h2_s, q_s, qt_s, o_s, ot_s, a_s, g_s, l_s, kd_s, vd_s, kt_s, vt_s, vtc_s, s0_s, s1_s, s2_s, e0_s, e1_s, e2_s, top_s, sum_s, part_s, *weights, sems, once, wsems) = refs[at + n_state + 1 :]
     wq, wo, wi, wh = (weights[2 * i : 2 * i + 2] for i in range(4))
     width = xf_s.shape[2]
     half, hid = wq[0].shape[2], wi[0].shape[2]
@@ -224,22 +224,22 @@
             def unit(u):
                 return (u >= pairs).astype(jnp.int32), jnp.where(u >= pairs, u - pairs, u)
 
-            def scores(u, slot, live):
+            def scores(u, slot):
                 span, i = unit(u)
-                (s0_s, s1_s)[slot][...] = dot(kd_s[block_of(span, SPAN), :HD], qt_s[j, i])
-
-            def soften(u, slot, live):
+                (s0_s, s1_s, s2_s)[slot][...] = dot(kd_s[block_of(span, SPAN), :HD], qt_s[j, i])
+
+            def soften(u, slot):
                 span, i = unit(u)
-                score = jnp.where(hidden_from(span, rows, m), -1e30, (s0_s, s1_s)[slot][...])
+                score = jnp.where(hidden_from(span, rows, m), -1e30, (s0_s, s1_s, s2_s)[slot][...])
                 top = jnp.max(score, axis=0, keepdims=True)
                 expo = jnp.exp(score - top)
                 top_s[u] = top
                 sum_s[u] = jnp.sum(expo, axis=0, keepdims=True)
-                (e0_s, e1_s)[slot][...] = expo.astype(BF16)
-
-            def weigh(u, slot, live):
+                (e0_s, e1_s, e2_s)[slot][...] = expo.astype(BF16)
+
+            def weigh(u, slot):
                 span, i = unit(u)
-                part_s[u] = dot(vt_s[:, block_of(span, SPAN)], (e0_s, e1_s)[slot][...])
+                part_s[u] = dot(vt_s[:, block_of(span, SPAN)], (e0_s, e1_s, e2_s)[slot][...])
 
             staged(jnp.where(many, 2 * pairs, pairs), (scores, soften, weigh))
 
@@ -327,6 +327,8 @@
         pltpu.VMEM((HD, rows), BF16),
         pltpu.VMEM((SPAN, 2 * rows), F32),
         pltpu.VMEM((SPAN, 2 * rows), F32),
+        pltpu.VMEM((SPAN, 2 * rows), F32),
+        pltpu.VMEM((SPAN, 2 * rows), BF16),
         pltpu.VMEM((SPAN, 2 * rows), BF16),
         pltpu.VMEM((SPAN, 2 * rows), BF16),
         pltpu.VMEM((2 * pairs, 1, 2 * rows), F32),
@@ -359,7 +361,7 @@
     at += n_read + (0 if fresh else n_state)
     st = dict(zip(BWD_STATE, refs[at : at + n_state]))
     hop_out = refs[at + n_state]
-    (in_s, dy_s, x_s, q_s, qt_s, ot_s, g_s, l_s, kd_s, vd_s, kt_s, db_s, do_s, du_s, dq_s, dqt_s, dkv_s, dkw_s, dh1_s, dh2_s, acc_s, accu_s, two_s, dot_s, d_s, s0_s, s1_s, dp0_s, dp1_s, both0_s, both1_s, *weights, sems, outs, once, wsems) = refs[at + n_state + 1 :]
+    (in_s, dy_s, x_s, q_s, qt_s, ot_s, g_s, l_s, kd_s, vd_s, kt_s, db_s, do_s, du_s, dq_s, dqt_s, dkv_s, dkw_s, dh1_s, dh2_s, acc_s, accu_s, two_s, dot_s, d_s, s0_s, s1_s, s2_s, dp0_s, dp1_s, dp2_s, both0_s, both1_s, both2_s, *weights, sems, outs, once, wsems) = refs[at + n_state + 1 :]
     wq, wo, wi, wh = (weights[2 * i : 2 * i + 2] for i in range(4))
     width = dy_s.shape[1]
     half, hid = wq[0].shape[2], wi[0].shape[2]
@@ -463,25 +465,25 @@
             def unit(u):
                 return (u >= pairs).astype(jnp.int32), jnp.where(u >= pairs, u - pairs, u)
 
-            def scores(u, slot, live):
+            def scores(u, slot):
                 span, i = unit(u)
-                (s0_s, s1_s)[slot][...] = dot(kd_s[block_of(span, SPAN), :HD], qt_s[j, i])
-                (dp0_s, dp1_s)[slot][...] = dot(vd_s[block_of(span, SPAN), :HD], dot_s[i])
-
-            def soften(u, slot, live):
+                (s0_s, s1_s, s2_s)[slot][...] = dot(kd_s[block_of(span, SPAN), :HD], qt_s[j, i])
+                (dp0_s, dp1_s, dp2_s)[slot][...] = dot(vd_s[block_of(span, SPAN), :HD], dot_s[i])
+
+            def soften(u, slot):
                 span, i = unit(u)
-                probs = jnp.where(hidden_from(span, rows, m), 0.0, jnp.exp((s0_s, s1_s)[slot][...] - l_s[j, i]))
-                both = (both0_s, both1_s)[slot]
-                both[:, : 2 * rows] = (probs * ((dp0_s, dp1_s)[slot][...] - d_s[i])).astype(BF16)
+                probs = jnp.where(hidden_from(span, rows, m), 0.0, jnp.exp((s0_s, s1_s, s2_s)[slot][...] - l_s[j, i]))
+                both = (both0_s, both1_s, both2_s)[slot]
+                both[:, : 2 * rows] = (probs * ((dp0_s, dp1_s, dp2_s)[slot][...] - d_s[i])).astype(BF16)
                 both[:, 2 * rows :] = probs.astype(BF16)
 
-            def weigh(u, slot, live):
+            def weigh(u, slot):
                 span, i = unit(u)
                 place = block_of(span, SPAN)
-                dqt_s[u] = dot(kt_s[:, place], (both0_s, both1_s)[slot][:, : 2 * rows])
-                part = dot((both0_s, both1_s)[slot][...], two_s[i])
-
-                dkw_s[place, :] += jnp.where(live, part, 0.0)
+                dqt_s[u] = dot(kt_s[:, place], (both0_s, both1_s, both2_s)[slot][:, : 2 * rows])
+                part = dot((both0_s, both1_s, both2_s)[slot][...], two_s[i])
+
+                dkw_s[place, :] += part
 
             many = m * rows >= SPAN
             staged(jnp.where(many, 2 * pairs, pairs), (scores, soften, weigh))
@@ -596,6 +598,9 @@
         pltpu.VMEM((SPAN, 2 * rows), F32),
         pltpu.VMEM((SPAN, 2 * rows), F32),
         pltpu.VMEM((SPAN, 2 * rows), F32),
+        pltpu.VMEM((SPAN, 2 * rows), F32),
+        pltpu.VMEM((SPAN, 2 * rows), F32),
+        pltpu.VMEM((SPAN, 4 * rows), BF16),
         pltpu.VMEM((SPAN, 4 * rows), BF16),
         pltpu.VMEM((SPAN, 4 * rows), BF16),
         *weight_scratch(weights),

time: 1290 us -> 1250 us (0.969)
  Pallas kernels: 292 us -> 275 us
  transfers between devices with their start and end apart: 72 -> 72, of which waited for: 33 -> 33; matrix products, arithmetic and copies ran while one was open for 15% -> 16% of each run, Pallas kernels for 8% -> 7%
where the time goes in v6:
time: 1250 us; the launch traced here: 1240 us
  waiting for transfers between devices  548 us (44%)
  Pallas kernels  275 us (22%)
  starting transfers between devices  183 us (15%)
  other arithmetic  113 us (9%)
  local copies, waits for them, and re-layouts  56.5 us (5%)
  matrix products  52.6 us (4%)
  between operations  16.2 us (1%)
    ppermute x6, waiting for transfers between devices, local(): hop = lax.ppermute(hop, PLANE, BEHIND)  219 us
    pallas_call x7, Pallas kernels, bwd_call(): pl.pallas_call(functools.partial(bwd_kernel, rows, chunks, fresh), out_sh...  160 us
    ppermute x6, waiting for transfers between devices, advance(): lax.ppermute(second[n], 'dp', [(1, 0), (2, 3)])  123 us
    pallas_call x7, Pallas kernels, fwd_call(): pl.pallas_call(functools.partial(fwd_kernel, rows, fresh), out_shape=[mak...  115 us
    ppermute x6, waiting for transfers between devices, line_sums(): arrived.append(lax.ppermute(terms[n], 'dp', [(0, 1), (3, 2)]))  109 us
    dot_general x17, matrix products, dot(): lax.dot_general(left, right, (dims, ((), ())), preferred_element_type=F32)  52.6 us
    ppermute x6, starting transfers between devices, local(): hop = lax.ppermute(hop, PLANE, AHEAD)  47.1 us
    ppermute x12, waiting for transfers between devices, routed(): moved = lax.ppermute(value, PLANE, [(a, b) for a, b in routes if a != b])  46 us
  transfers between devices with their start and end apart: 72, of which 33 were waited for; matrix products, arithmetic and copies ran while one was open for 16% of the time, Pallas kernels for 7%

profile of v6, /device:TPU:1, one launch (start us, length us, event | category | flops | bytes accessed | tf_op | source)
XLA Modules:
  0.0 1244.6 jit_solution(2754142762435466398)
XLA Ops:
  7.3 4.2 dynamic-slice_bitcast_fusion.2
  11.5 4.7 collective-permute-start
  34.2 8.7 collective-permute-done
  48.9 19.2 %collective-permute-done.16 = bf16[768,1536]{1,0:T(8,128)(2,1)} collective-permute-done((bf16[768,1536]{1,0:T(8,128)(2,1)}, bf16[768,1536]{1,0:T(8,128)(2,1)}, u32[]{:S(2)}, u32[]{:S(2)}) %collective-permute-start.16) | collective-permute-done | bytes 2359328 | tf_op jit(solution)/shard_map/ppermute | solution.py:691
  87.9 7.8 collective-permute-done.11
  115.2 4.6 collective-permute-done.12
  144.3 24.4 %section_forward.7 = (f32[2,1024,768]{2,1,0:T(8,128)}, bf16[2,1024,768]{2,1,0:T(8,128)(2,1)}, bf16[2,1024,768]{2,1,0:T(8,128)(2,1)}, bf16[2,1024,768]{2,1,0:T(8,...) custom-call(s32[5]{0:T(128)} %stack.251.refs_0_, ...), custom_call_target="tpu_custom_call" | custom-call | tf_op jit(solution)/shard_map/section_forward/pallas_call | solution.py:342
  170.7 11.1 collective-permute-done.23.refs_1_
  182.5 24.1 %section_forward.8 = (f32[2,1024,768]{2,1,0:T(8,128)}, bf16[2,1024,768]{2,1,0:T(8,128)(2,1)}, bf16[2,1024,768]{2,1,0:T(8,128)(2,1)}, bf16[2,1024,768]{2,1,0:T(8,...) custom-call(s32[5]{0:T(128)} %stack.247.refs_0_, ...), custom_call_target="tpu_custom_call", output_to_operand_aliasing={{0}: (25, {}), {1}: (26, {}), {2}: (27, {}), {3}: (28, {}),... | custom-call | tf_op jit(solution)/shard_map/section_forward/pallas_call | solution.py:342
  206.6 4.4 collective-permute-start.24
  211.6 7.2 collective-permute-done.24.refs_1_
  219.6 30.2 %section_forward.9 = (f32[2,1024,768]{2,1,0:T(8,128)}, bf16[2,1024,768]{2,1,0:T(8,128)(2,1)}, bf16[2,1024,768]{2,1,0:T(8,128)(2,1)}, bf16[2,1024,768]{2,1,0:T(8,...) custom-call(s32[5]{0:T(128)} %stack.243.refs_0_, ...), custom_call_target="tpu_custom_call", output_to_operand_aliasing={{0}: (25, {}), {1}: (26, {}), {2}: (27, {}), {3}: (28, {}),... | custom-call | tf_op jit(solution)/shard_map/section_forward/pallas_call | solution.py:342
  251.7 6.6 collective-permute-done.25.refs_1_
  259.0 29.8 %section_forward.10 = (f32[2,1024,768]{2,1,0:T(8,128)}, bf16[2,1024,768]{2,1,0:T(8,128)(2,1)}, bf16[2,1024,768]{2,1,0:T(8,128)(2,1)}, bf16[2,1024,768]{2,1,0:T(8...) custom-call(s32[5]{0:T(128)} %stack.239.refs_0_, ...), custom_call_target="tpu_custom_call", output_to_operand_aliasing={{0}: (25, {}), {1}: (26, {}), {2}: (27, {}), {3}: (28, {}),... | custom-call | tf_op jit(solution)/shard_map/section_forward/pallas_call | solution.py:342
  288.8 4.2 collective-permute-start.26
  293.6 5.7 collective-permute-done.26.refs_1_
  302.3 31.9 %collective-permute-start.27 = (bf16[256,768]{1,0:T(8,128)(2,1)}, bf16[256,768]{1,0:T(8,128)(2,1)S(1)}, u32[]{:S(2)}, u32[]{:S(2)}) collective-permute-start(bf16[256,768]{1,0:T(8,128)(2,1)} %get-tuple-element.298), channel_id=1, source_target_pairs={{0,1},{8,9},{1,17},{9,25},{17,16},{25,24},{2,3},{10,11},{3,19},{11... | collective-permute-start | bytes 1179656 | tf_op jit(solution)/shard_map/ppermute | solution.py:800
  334.8 4.7 collective-permute-done.27.refs_1_
  342.3 4.0 collective-permute-start.28
  358.4 33.8 %collective-permute-done.29.refs_2_ = bf16[256,768]{1,0:T(8,128)(2,1)S(1)} collective-permute-done((bf16[256,768]{1,0:T(8,128)(2,1)}, bf16[256,768]{1,0:T(8,128)(2,1)S(1)}, u32[]{:S(2)}, u32[]{:S(2)}) %collective-permute-start.29) | collective-permute-done | bytes 393248 | tf_op jit(solution)/shard_map/ppermute | solution.py:818
  397.2 7.2 collective-permute-done.30.refs_2_
  409.0 155.9 %collective-permute-done.31.refs_2_ = bf16[256,768]{1,0:T(8,128)(2,1)S(1)} collective-permute-done((bf16[256,768]{1,0:T(8,128)(2,1)}, bf16[256,768]{1,0:T(8,128)(2,1)S(1)}, u32[]{:S(2)}, u32[]{:S(2)}) %collective-permute-start.31) | collective-permute-done | bytes 393248 | tf_op jit(solution)/shard_map/ppermute | solution.py:818
  565.7 43.2 %section_backward.10 = (bf16[2,1024,768]{2,1,0:T(8,128)(2,1)}, bf16[2,1024,3072]{2,1,0:T(8,128)(2,1)}, bf16[2,1024,768]{2,1,0:T(8,128)(2,1)}, bf16[1024,128]{1,0...) custom-call(s32[5]{0:T(128)} %stack.257.refs_0_, ...), custom_call_target="tpu_custom_call", output_to_operand_aliasing={{0}: (34, {}), {1}: (35, {}), {2}: (36, {}), {3}: (37, {}),... | custom-call | tf_op jit(solution)/shard_map/section_backward/pallas_call | solution.py:613
  610.8 8.2 collective-permute-done.32.refs_2_
  619.8 43.7 %section_backward.11 = (bf16[2,1024,768]{2,1,0:T(8,128)(2,1)}, bf16[2,1024,3072]{2,1,0:T(8,128)(2,1)}, bf16[2,1024,768]{2,1,0:T(8,128)(2,1)}, bf16[1024,128]{1,0...) custom-call(s32[5]{0:T(128)} %stack.256.refs_0_, ...), custom_call_target="tpu_custom_call", output_to_operand_aliasing={{0}: (34, {}), {1}: (35, {}), {2}: (36, {}), {3}: (37, {}),... | custom-call | tf_op jit(solution)/shard_map/section_backward/pallas_call | solution.py:613
  665.4 6.8 collective-permute-done.33.refs_2_
  673.0 33.5 %section_backward.12 = (bf16[2,1024,768]{2,1,0:T(8,128)(2,1)}, bf16[2,1024,3072]{2,1,0:T(8,128)(2,1)}, bf16[2,1024,768]{2,1,0:T(8,128)(2,1)}, bf16[1024,128]{1,0...) custom-call(s32[5]{0:T(128)} %stack.255.refs_0_, ...), custom_call_target="tpu_custom_call", output_to_operand_aliasing={{0}: (34, {}), {1}: (35, {}), {2}: (36, {}), {3}: (37, {}),... | custom-call | tf_op jit(solution)/shard_map/section_backward/pallas_call | solution.py:613
  708.4 6.8 collective-permute-done.34.refs_2_
  716.0 33.2 %section_backward.13 = (bf16[2,1024,768]{2,1,0:T(8,128)(2,1)}, bf16[2,1024,3072]{2,1,0:T(8,128)(2,1)}, bf16[2,1024,768]{2,1,0:T(8,128)(2,1)}, bf16[1024,128]{1,0...) custom-call(s32[5]{0:T(128)} %stack.254.refs_0_, ...), custom_call_target="tpu_custom_call", output_to_operand_aliasing={{0}: (34, {}), {1}: (35, {}), {2}: (36, {}), {3}: (37, {}),... | custom-call | tf_op jit(solution)/shard_map/section_backward/pallas_call | solution.py:613
  749.2 5.2 convolution_convert_fusion.6
  754.4 11.0 collective-permute-start.35
  769.9 4.6 convolution_convert_fusion.7
  781.5 5.8 convolution_convert_fusion.2
  788.0 13.5 %collective-permute-done.37 = bf16[768,768]{1,0:T(8,128)(2,1)S(1)} collective-permute-done((bf16[768,768]{1,0:T(8,128)(2,1)S(1)}, bf16[768,768]{1,0:T(8,128)(2,1)S(1)}, u32[]{:S(2)}, u32[]{:S(2)}) %collective-permute-start.37) | collective-permute-done | bytes 1179680 | tf_op jit(solution)/shard_map/ppermute | solution.py:728
  807.6 44.6 %collective-permute-done.39 = bf16[1536,768]{1,0:T(8,128)(2,1)} collective-permute-done((bf16[1536,768]{1,0:T(8,128)(2,1)}, bf16[1536,768]{1,0:T(8,128)(2,1)}, u32[]{:S(2)}, u32[]{:S(2)}) %collective-permute-start.39) | collective-permute-done | bytes 2359328 | tf_op jit(solution)/shard_map/ppermute | solution.py:728
  852.1 4.4 add_convert_fusion.10
  858.7 6.1 add_convert_fusion.8
  864.9 8.5 collective-permute-start.47
  879.3 6.4 convolution_convert_fusion.4
  887.7 16.2 %collective-permute-done.45 = bf16[768,768]{1,0:T(8,128)(2,1)} collective-permute-done((bf16[768,768]{1,0:T(8,128)(2,1)}, bf16[768,768]{1,0:T(8,128)(2,1)}, u32[]{:S(2)}, u32[]{:S(2)}) %collective-permute-start.45) | collective-permute-done | bytes 1179680 | tf_op jit(solution)/shard_map/ppermute | solution.py:720
  909.8 11.3 collective-permute-done.47
  926.6 5.3 convolution_convert_fusion.5
  936.3 4.3 collective-permute-start.52
  940.7 4.0 convolution_convert_fusion
  946.2 3.8 collective-permute-done.49
  951.2 17.2 %collective-permute-done.48 = bf16[1536,768]{1,0:T(8,128)(2,1)S(1)} collective-permute-done((bf16[1536,768]{1,0:T(8,128)(2,1)S(1)}, bf16[1536,768]{1,0:T(8,128)(2,1)S(1)}, u32[]{:S(2)}, u32[]{:S(2)}) %collective-permute-start.48) | collective-permute-done | bytes 2359328 | tf_op jit(solution)/shard_map/ppermute | solution.py:720
  978.6 10.7 collective-permute-done.52
  992.4 5.2 add_convert_fusion.4
  997.6 7.4 collective-permute-start.56
  1005.0 25.7 %collective-permute-done.53 = bf16[768,1536]{1,0:T(8,128)(2,1)S(1)} collective-permute-done((bf16[768,1536]{1,0:T(8,128)(2,1)S(1)}, bf16[768,1536]{1,0:T(8,128)(2,1)S(1)}, u32[]{:S(2)}, u32[]{:S(2)}) %collective-permute-start.53) | collective-permute-done | bytes 2359328 | tf_op jit(solution)/shard_map/ppermute | solution.py:720
  1042.2 9.5 collective-permute-done.56
  1051.7 4.4 add_convert_fusion.1
  1065.9 3.7 collective-permute-start.43
  1069.6 30.4 %collective-permute-done.57 = bf16[1536,768]{1,0:T(8,128)(2,1)} collective-permute-done((bf16[1536,768]{1,0:T(8,128)(2,1)}, bf16[1536,768]{1,0:T(8,128)(2,1)}, u32[]{:S(2)}, u32[]{:S(2)}) %collective-permute-start.57) | collective-permute-done | bytes 2359328 | tf_op jit(solution)/shard_map/ppermute | solution.py:720
  1106.9 4.5 add_convert_fusion
  1114.1 8.5 collective-permute-start.60
  1124.6 3.6 collective-permute-start.41
  1128.3 19.7 %collective-permute-done.60 = bf16[896,768]{1,0:T(8,128)(2,1)S(1)} collective-permute-done((bf16[896,768]{1,0:T(8,128)(2,1)S(1)}, bf16[896,768]{1,0:T(8,128)(2,1)S(1)}, u32[]{:S(2)}, u32[]{:S(2)}) %collective-permute-start.60) | collective-permute-done | bytes 1376288 | tf_op jit(solution)/shard_map/ppermute | solution.py:728
  1151.2 7.6 collective-permute-done.41
  1158.8 7.0 collective-permute-done.61
  1183.6 26.2 %collective-permute-done.64 = bf16[896,768]{1,0:T(8,128)(2,1)} collective-permute-done((bf16[896,768]{1,0:T(8,128)(2,1)}, bf16[896,768]{1,0:T(8,128)(2,1)}, u32[]{:S(2)}, u32[]{:S(2)}) %collective-permute-start.64) | collective-permute-done | bytes 1376288 | tf_op jit(solution)/shard_map/ppermute | solution.py:720
  1213.2 4.4 maximum_convert_fusion.1
  1219.9 4.4 maximum_convert_fusion
  1224.3 6.6 collective-permute-done.65
  (382 shorter events, 257.3 us)
Async XLA Ops:
  7.2 136.2 %all-gather.3.cloned.1.call-start = ((), (), s32[]{:S(2)}) async-start(), calls=%async_computation.2 | async-start | bytes 3538944 | tf_op jit(solution)/shard_map/all_gather | solution.py:781
  11.5 31.3 %collective-permute-start = (bf16[1536,768]{1,0:T(8,128)(2,1)S(1)}, bf16[1536,768]{1,0:T(8,128)(2,1)}, u32[]{:S(2)}, u32[]{:S(2)}) collective-permute-start(bf16[1536,768]{1,0:T(8,128)(2,1)S(1)} %get-tuple-element.454), channel_id=1, source_target_pairs={{1,8},{8,1},{16,17},{17,25},{24,16},{25,24},{3,10},{10,3},{18,19},... | collective-permute-start | bytes 7077896 | tf_op jit(solution)/shard_map/ppermute | solution.py:691
  18.7 49.4 %collective-permute-start.16 = (bf16[768,1536]{1,0:T(8,128)(2,1)}, bf16[768,1536]{1,0:T(8,128)(2,1)}, u32[]{:S(2)}, u32[]{:S(2)}) collective-permute-start(bf16[768,1536]{1,0:T(8,128)(2,1)} %get-tuple-element.452), channel_id=1, source_target_pairs={{1,8},{8,1},{16,17},{17,25},{24,16},{25,24},{3,10},{10,3},{18,19},... | collective-permute-start | bytes 7077896 | tf_op jit(solution)/shard_map/ppermute | solution.py:691
  26.5 48.6 %collective-permute-start.1 = (f32[103,128]{1,0:T(8,128)}, f32[103,128]{1,0:T(8,128)}, u32[]{:S(2)}, u32[]{:S(2)}) collective-permute-start(f32[103,128]{1,0:T(8,128)} %bitcast.19), channel_id=1, source_target_pairs={{1,8},{8,1},{16,17},{17,25},{24,16},{25,24},{3,10},{10,3},{18,19},... | collective-permute-start | bytes 158216 | tf_op jit(solution)/shard_map/ppermute | solution.py:691
  30.2 47.1 %collective-permute-start.3 = (bf16[768,128]{1,0:T(8,128)(2,1)}, bf16[768,128]{1,0:T(8,128)(2,1)}, u32[]{:S(2)}, u32[]{:S(2)}) collective-permute-start(bf16[768,128]{1,0:T(8,128)(2,1)} %bitcast.24), channel_id=1, source_target_pairs={{1,8},{8,1},{16,17},{17,25},{24,16},{25,24},{3,10},{10,3},{18,19},... | collective-permute-start | bytes 589832 | tf_op jit(solution)/shard_map/ppermute | solution.py:691
  32.1 64.3 %collective-permute-start.9 = (bf16[1536,768]{1,0:T(8,128)(2,1)}, bf16[1536,768]{1,0:T(8,128)(2,1)}, u32[]{:S(2)}, u32[]{:S(2)}) collective-permute-start(bf16[1536,768]{1,0:T(8,128)(2,1)} %get-tuple-element.453), channel_id=1, source_target_pairs={{17,25},{24,16},{19,27},{26,18},{21,29},{28,20},{23,31},{30,22}} | collective-permute-start | bytes 7077896 | tf_op jit(solution)/shard_map/ppermute | solution.py:685
  44.8 52.4 %collective-permute-start.8 = (bf16[1536,768]{1,0:T(8,128)(2,1)S(1)}, bf16[1536,768]{1,0:T(8,128)(2,1)}, u32[]{:S(2)}, u32[]{:S(2)}) collective-permute-start(bf16[1536,768]{1,0:T(8,128)(2,1)S(1)} %broadcast_select_fusion.10.refs_21_), channel_id=1, source_target_pairs={{10,8},{8,10},{14,12},{12,14},{3,1},{1,3},{7,5},{5,7},{19,17},{17,... | collective-permute-start | bytes 7077896 | tf_op jit(solution)/shard_map/ppermute | solution.py:684
  68.1 13.7 %collective-permute-start.4 = (bf16[768,384]{1,0:T(8,128)(2,1)S(1)}, bf16[768,384]{1,0:T(8,128)(2,1)S(1)}, u32[]{:S(2)}, u32[]{:S(2)}) collective-permute-start(bf16[768,384]{1,0:T(8,128)(2,1)S(1)} %get-tuple-element.462), channel_id=1, source_target_pairs={{1,8},{8,1},{16,17},{17,25},{24,16},{25,24},{3,10},{10,3},{18,19},... | collective-permute-start | bytes 1769480 | tf_op jit(solution)/shard_map/ppermute | solution.py:691
  75.1 27.5 %collective-permute-start.18 = (bf16[768,1536]{1,0:T(8,128)(2,1)}, bf16[768,1536]{1,0:T(8,128)(2,1)}, u32[]{:S(2)}, u32[]{:S(2)}) collective-permute-start(bf16[768,1536]{1,0:T(8,128)(2,1)} %get-tuple-element.451), channel_id=1, source_target_pairs={{17,25},{24,16},{19,27},{26,18},{21,29},{28,20},{23,31},{30,22}} | collective-permute-start | bytes 7077896 | tf_op jit(solution)/shard_map/ppermute | solution.py:685
  77.2 30.2 %collective-permute-start.17 = (bf16[768,1536]{1,0:T(8,128)(2,1)}, bf16[768,1536]{1,0:T(8,128)(2,1)}, u32[]{:S(2)}, u32[]{:S(2)}) collective-permute-start(bf16[768,1536]{1,0:T(8,128)(2,1)} %broadcast_select_fusion.7.refs_17_), channel_id=1, source_target_pairs={{10,8},{8,10},{14,12},{12,14},{3,1},{1,3},{7,5},{5,7},{19,17},{17,... | collective-permute-start | bytes 7077896 | tf_op jit(solution)/shard_map/ppermute | solution.py:684
  80.5 274.0 %all-gather.5.cloned.1.call-start = ((), (), s32[]{:S(2)}) async-start(), calls=%async_computation.4 | async-start | bytes 3538944 | tf_op jit(solution)/shard_map/all_gather | solution.py:798
  81.9 13.8 %collective-permute-start.11 = (bf16[384,768]{1,0:T(8,128)(2,1)S(1)}, bf16[384,768]{1,0:T(8,128)(2,1)S(1)}, u32[]{:S(2)}, u32[]{:S(2)}) collective-permute-start(bf16[384,768]{1,0:T(8,128)(2,1)S(1)} %get-tuple-element.460), channel_id=1, source_target_pairs={{1,8},{8,1},{16,17},{17,25},{24,16},{25,24},{3,10},{10,3},{18,19},... | collective-permute-start | bytes 1769480 | tf_op jit(solution)/shard_map/ppermute | solution.py:691
  95.7 15.1 %collective-permute-start.6 = (bf16[768,384]{1,0:T(8,128)(2,1)}, bf16[768,384]{1,0:T(8,128)(2,1)S(1)}, u32[]{:S(2)}, u32[]{:S(2)}) collective-permute-start(bf16[768,384]{1,0:T(8,128)(2,1)} %get-tuple-element.461), channel_id=1, source_target_pairs={{17,25},{24,16},{19,27},{26,18},{21,29},{28,20},{23,31},{30,22}} | collective-permute-start | bytes 1769480 | tf_op jit(solution)/shard_map/ppermute | solution.py:685
  96.5 15.7 %collective-permute-start.13 = (bf16[384,768]{1,0:T(8,128)(2,1)S(1)}, bf16[384,768]{1,0:T(8,128)(2,1)S(1)}, u32[]{:S(2)}, u32[]{:S(2)}) collective-permute-start(bf16[384,768]{1,0:T(8,128)(2,1)S(1)} %get-tuple-element.459), channel_id=1, source_target_pairs={{17,25},{24,16},{19,27},{26,18},{21,29},{28,20},{23,31},{30,22}} | collective-permute-start | bytes 1769480 | tf_op jit(solution)/shard_map/ppermute | solution.py:685
  100.7 13.1 %collective-permute-start.5 = (bf16[768,384]{1,0:T(8,128)(2,1)S(1)}, bf16[768,384]{1,0:T(8,128)(2,1)S(1)}, u32[]{:S(2)}, u32[]{:S(2)}) collective-permute-start(bf16[768,384]{1,0:T(8,128)(2,1)S(1)} %broadcast_select_fusion.18.refs_9_), channel_id=1, source_target_pairs={{10,8},{8,10},{14,12},{12,14},{3,1},{1,3},{7,5},{5,7},{19,17},{17,... | collective-permute-start | bytes 1769480 | tf_op jit(solution)/shard_map/ppermute | solution.py:684
  102.6 17.1 %collective-permute-start.12 = (bf16[384,768]{1,0:T(8,128)(2,1)S(1)}, bf16[384,768]{1,0:T(8,128)(2,1)}, u32[]{:S(2)}, u32[]{:S(2)}) collective-permute-start(bf16[384,768]{1,0:T(8,128)(2,1)S(1)} %broadcast_select_fusion.17.refs_13_), channel_id=1, source_target_pairs={{10,8},{8,10},{14,12},{12,14},{3,1},{1,3},{7,5},{5,7},{19,17},{17,... | collective-permute-start | bytes 1769480 | tf_op jit(solution)/shard_map/ppermute | solution.py:684
  107.4 22.9 %collective-permute-start.19 = (bf16[768,1536]{1,0:T(8,128)(2,1)}, bf16[768,1536]{1,0:T(8,128)(2,1)}, u32[]{:S(2)}, u32[]{:S(2)}) collective-permute-start(bf16[768,1536]{1,0:T(8,128)(2,1)} %broadcast_select_fusion.7.refs_17_), channel_id=1, source_target_pairs={{0,8},{8,0},{16,24},{24,16},{1,9},{9,1},{17,25},{25,17},{2,10},{10... | collective-permute-start | bytes 7077896 | tf_op jit(solution)/shard_map/ppermute | solution.py:696
  110.8 32.5 %collective-permute-start.21 = (bf16[1536,768]{1,0:T(8,128)(2,1)S(1)}, bf16[1536,768]{1,0:T(8,128)(2,1)}, u32[]{:S(2)}, u32[]{:S(2)}) collective-permute-start(bf16[1536,768]{1,0:T(8,128)(2,1)S(1)} %broadcast_select_fusion.10.refs_21_), channel_id=1, source_target_pairs={{0,8},{8,0},{16,24},{24,16},{1,9},{9,1},{17,25},{25,17},{2,10},{10... | collective-permute-start | bytes 7077896 | tf_op jit(solution)/shard_map/ppermute | solution.py:696
  112.2 31.2 %collective-permute-start.20 = (bf16[768,1536]{1,0:T(8,128)(2,1)}, bf16[768,1536]{1,0:T(8,128)(2,1)}, u32[]{:S(2)}, u32[]{:S(2)}) collective-permute-start(bf16[768,1536]{1,0:T(8,128)(2,1)} %select_select_fusion.refs_18_), channel_id=1, source_target_pairs={{0,8},{8,0},{16,24},{24,16},{1,9},{9,1},{17,25},{25,17},{2,10},{10... | collective-permute-start | bytes 7077896 | tf_op jit(solution)/shard_map/ppermute | solution.py:696
  113.7 29.6 %collective-permute-start.22 = (bf16[1536,768]{1,0:T(8,128)(2,1)}, bf16[1536,768]{1,0:T(8,128)(2,1)}, u32[]{:S(2)}, u32[]{:S(2)}) collective-permute-start(bf16[1536,768]{1,0:T(8,128)(2,1)} %select_select_fusion.1.refs_22_), channel_id=1, source_target_pairs={{0,8},{8,0},{16,24},{24,16},{1,9},{9,1},{17,25},{25,17},{2,10},{10... | collective-permute-start | bytes 7077896 | tf_op jit(solution)/shard_map/ppermute | solution.py:696
  130.3 13.0 %collective-permute-start.10 = (bf16[768,384]{1,0:T(8,128)(2,1)S(1)}, bf16[768,384]{1,0:T(8,128)(2,1)S(1)}, u32[]{:S(2)}, u32[]{:S(2)}) collective-permute-start(bf16[768,384]{1,0:T(8,128)(2,1)S(1)} %select_select_fusion.3.refs_10_), channel_id=1, source_target_pairs={{0,8},{8,0},{16,24},{24,16},{1,9},{9,1},{17,25},{25,17},{2,10},{10... | collective-permute-start | bytes 1769480 | tf_op jit(solution)/shard_map/ppermute | solution.py:696
  130.3 13.0 %collective-permute-start.15 = (bf16[384,768]{1,0:T(8,128)(2,1)}, bf16[384,768]{1,0:T(8,128)(2,1)}, u32[]{:S(2)}, u32[]{:S(2)}) collective-permute-start(bf16[384,768]{1,0:T(8,128)(2,1)} %select_select_fusion.2.refs_14_), channel_id=1, source_target_pairs={{0,8},{8,0},{16,24},{24,16},{1,9},{9,1},{17,25},{25,17},{2,10},{10... | collective-permute-start | bytes 1769480 | tf_op jit(solution)/shard_map/ppermute | solution.py:696
  168.7 955.9 %all-reduce.3.cloned.1.call-start = ((), (), s32[]{:S(2)}) async-start(), calls=%async_computation.6 | async-start | bytes 196608 | tf_op jit(solution)/shard_map/psum | solution.py:880
  168.8 13.0 %collective-permute-start.23 = (bf16[256,768]{1,0:T(8,128)(2,1)}, bf16[256,768]{1,0:T(8,128)(2,1)S(1)}, u32[]{:S(2)}, u32[]{:S(2)}) collective-permute-start(bf16[256,768]{1,0:T(8,128)(2,1)} %get-tuple-element.234), channel_id=1, source_target_pairs={{0,1},{8,9},{1,17},{9,25},{17,16},{25,24},{2,3},{10,11},{3,19},{11... | collective-permute-start | bytes 1179656 | tf_op jit(solution)/shard_map/ppermute | solution.py:800
  206.6 12.2 collective-permute-start.24
  288.8 10.5 collective-permute-start.26
  302.3 37.2 %collective-permute-start.27 = (bf16[256,768]{1,0:T(8,128)(2,1)}, bf16[256,768]{1,0:T(8,128)(2,1)S(1)}, u32[]{:S(2)}, u32[]{:S(2)}) collective-permute-start(bf16[256,768]{1,0:T(8,128)(2,1)} %get-tuple-element.298), channel_id=1, source_target_pairs={{0,1},{8,9},{1,17},{9,25},{17,16},{25,24},{2,3},{10,11},{3,19},{11... | collective-permute-start | bytes 1179656 | tf_op jit(solution)/shard_map/ppermute | solution.py:800
  342.3 9.0 collective-permute-start.28
  356.5 35.7 %collective-permute-start.29 = (bf16[256,768]{1,0:T(8,128)(2,1)}, bf16[256,768]{1,0:T(8,128)(2,1)S(1)}, u32[]{:S(2)}, u32[]{:S(2)}) collective-permute-start(bf16[256,768]{1,0:T(8,128)(2,1)} %get-tuple-element.342), channel_id=1, source_target_pairs={{1,0},{9,8},{17,1},{25,9},{16,17},{24,25},{3,2},{11,10},{19,3},{27... | collective-permute-start | bytes 1179656 | tf_op jit(solution)/shard_map/ppermute | solution.py:818
  395.3 9.1 collective-permute-start.30
  407.1 157.8 %collective-permute-start.31 = (bf16[256,768]{1,0:T(8,128)(2,1)}, bf16[256,768]{1,0:T(8,128)(2,1)S(1)}, u32[]{:S(2)}, u32[]{:S(2)}) collective-permute-start(bf16[256,768]{1,0:T(8,128)(2,1)} %get-tuple-element.360), channel_id=1, source_target_pairs={{1,0},{9,8},{17,1},{25,9},{16,17},{24,25},{3,2},{11,10},{19,3},{27... | collective-permute-start | bytes 1179656 | tf_op jit(solution)/shard_map/ppermute | solution.py:818
  608.9 10.1 collective-permute-start.32
  754.4 22.3 %collective-permute-start.35 = (bf16[1536,768]{1,0:T(8,128)(2,1)S(1)}, bf16[1536,768]{1,0:T(8,128)(2,1)S(1)}, u32[]{:S(2)}, u32[]{:S(2)}) collective-permute-start(bf16[1536,768]{1,0:T(8,128)(2,1)S(1)} %convolution_convert_fusion.6), channel_id=1, source_target_pairs={{0,8},{8,0},{16,24},{24,16},{1,9},{9,1},{17,25},{25,17},{2,10},{10... | collective-permute-start | bytes 7077896 | tf_op jit(solution)/shard_map/ppermute | solution.py:696
  774.8 26.7 %collective-permute-start.37 = (bf16[768,768]{1,0:T(8,128)(2,1)S(1)}, bf16[768,768]{1,0:T(8,128)(2,1)S(1)}, u32[]{:S(2)}, u32[]{:S(2)}) collective-permute-start(bf16[768,768]{1,0:T(8,128)(2,1)S(1)} %add_convert_fusion.17), channel_id=1, source_target_pairs={{0,2},{6,4},{1,3},{7,5},{8,10},{14,12},{9,11},{15,13},{16,18},{22,... | collective-permute-start | bytes 3538952 | tf_op jit(solution)/shard_map/ppermute | solution.py:728
  778.7 73.4 %collective-permute-start.39 = (bf16[1536,768]{1,0:T(8,128)(2,1)}, bf16[1536,768]{1,0:T(8,128)(2,1)}, u32[]{:S(2)}, u32[]{:S(2)}) collective-permute-start(bf16[1536,768]{1,0:T(8,128)(2,1)} %add_convert_fusion.11), channel_id=1, source_target_pairs={{0,2},{6,4},{1,3},{7,5},{8,10},{14,12},{9,11},{15,13},{16,18},{22,... | collective-permute-start | bytes 7077896 | tf_op jit(solution)/shard_map/ppermute | solution.py:728
  787.2 71.5 %collective-permute-start.44 = (bf16[768,1536]{1,0:T(8,128)(2,1)}, bf16[768,1536]{1,0:T(8,128)(2,1)}, u32[]{:S(2)}, u32[]{:S(2)}) collective-permute-start(bf16[768,1536]{1,0:T(8,128)(2,1)} %convolution_convert_fusion.2), channel_id=1, source_target_pairs={{0,8},{8,0},{16,24},{24,16},{1,9},{9,1},{17,25},{25,17},{2,10},{10... | collective-permute-start | bytes 7077896 | tf_op jit(solution)/shard_map/ppermute | solution.py:696
  856.5 48.8 %collective-permute-start.46 = (bf16[1536,768]{1,0:T(8,128)(2,1)}, bf16[1536,768]{1,0:T(8,128)(2,1)}, u32[]{:S(2)}, u32[]{:S(2)}) collective-permute-start(bf16[1536,768]{1,0:T(8,128)(2,1)} %add_convert_fusion.10), channel_id=1, source_target_pairs={{2,4},{4,2},{3,5},{5,3},{10,12},{12,10},{11,13},{13,11},{18,20},{2... | collective-permute-start | bytes 7077896 | tf_op jit(solution)/shard_map/ppermute | solution.py:718
  864.9 56.3 %collective-permute-start.47 = (bf16[768,1536]{1,0:T(8,128)(2,1)}, bf16[768,1536]{1,0:T(8,128)(2,1)}, u32[]{:S(2)}, u32[]{:S(2)}) collective-permute-start(bf16[768,1536]{1,0:T(8,128)(2,1)} %add_convert_fusion.8), channel_id=1, source_target_pairs={{0,2},{6,4},{1,3},{7,5},{8,10},{14,12},{9,11},{15,13},{16,18},{22,... | collective-permute-start | bytes 7077896 | tf_op jit(solution)/shard_map/ppermute | solution.py:728
  876.1 27.8 %collective-permute-start.45 = (bf16[768,768]{1,0:T(8,128)(2,1)}, bf16[768,768]{1,0:T(8,128)(2,1)}, u32[]{:S(2)}, u32[]{:S(2)}) collective-permute-start(bf16[768,768]{1,0:T(8,128)(2,1)} %add_convert_fusion.15), channel_id=1, source_target_pairs={{2,0},{4,6},{3,1},{5,7},{10,8},{12,14},{11,9},{13,15},{18,16},{20,... | collective-permute-start | bytes 3538952 | tf_op jit(solution)/shard_map/ppermute | solution.py:720
  885.7 48.4 %collective-permute-start.42 = (bf16[1536,768]{1,0:T(8,128)(2,1)}, bf16[1536,768]{1,0:T(8,128)(2,1)}, u32[]{:S(2)}, u32[]{:S(2)}) collective-permute-start(bf16[1536,768]{1,0:T(8,128)(2,1)} %convolution_convert_fusion.4), channel_id=1, source_target_pairs={{0,8},{8,0},{16,24},{24,16},{1,9},{9,1},{17,25},{25,17},{2,10},{10... | collective-permute-start | bytes 7077896 | tf_op jit(solution)/shard_map/ppermute | solution.py:696
  908.3 60.1 %collective-permute-start.48 = (bf16[1536,768]{1,0:T(8,128)(2,1)S(1)}, bf16[1536,768]{1,0:T(8,128)(2,1)S(1)}, u32[]{:S(2)}, u32[]{:S(2)}) collective-permute-start(bf16[1536,768]{1,0:T(8,128)(2,1)S(1)} %add_convert_fusion.7), channel_id=1, source_target_pairs={{2,0},{4,6},{3,1},{5,7},{10,8},{12,14},{11,9},{13,15},{18,16},{20,... | collective-permute-start | bytes 7077896 | tf_op jit(solution)/shard_map/ppermute | solution.py:720
  924.3 44.3 %collective-permute-start.50 = (bf16[768,1536]{1,0:T(8,128)(2,1)S(1)}, bf16[768,1536]{1,0:T(8,128)(2,1)}, u32[]{:S(2)}, u32[]{:S(2)}) collective-permute-start(bf16[768,1536]{1,0:T(8,128)(2,1)S(1)} %add_convert_fusion.6), channel_id=1, source_target_pairs={{2,4},{4,2},{3,5},{5,3},{10,12},{12,10},{11,13},{13,11},{18,20},{2... | collective-permute-start | bytes 7077896 | tf_op jit(solution)/shard_map/ppermute | solution.py:718
  931.9 18.1 %collective-permute-start.49 = (bf16[768,768]{1,0:T(8,128)(2,1)S(1)}, bf16[768,768]{1,0:T(8,128)(2,1)S(1)}, u32[]{:S(2)}, u32[]{:S(2)}) collective-permute-start(bf16[768,768]{1,0:T(8,128)(2,1)S(1)} %broadcast_select_fusion.16), channel_id=1, source_target_pairs={{8,1},{1,8},{17,16},{25,17},{16,24},{24,25},{10,3},{3,10},{19,18},... | collective-permute-start | bytes 3538952 | tf_op jit(solution)/shard_map/ppermute | solution.py:691
  936.3 53.0 %collective-permute-start.52 = (bf16[1536,768]{1,0:T(8,128)(2,1)S(1)}, bf16[1536,768]{1,0:T(8,128)(2,1)S(1)}, u32[]{:S(2)}, u32[]{:S(2)}) collective-permute-start(bf16[1536,768]{1,0:T(8,128)(2,1)S(1)} %add_convert_fusion.9), channel_id=1, source_target_pairs={{0,2},{6,4},{1,3},{7,5},{8,10},{14,12},{9,11},{15,13},{16,18},{22,... | collective-permute-start | bytes 7077896 | tf_op jit(solution)/shard_map/ppermute | solution.py:728
  944.7 47.7 %collective-permute-start.51 = (bf16[768,1536]{1,0:T(8,128)(2,1)}, bf16[768,1536]{1,0:T(8,128)(2,1)}, u32[]{:S(2)}, u32[]{:S(2)}) collective-permute-start(bf16[768,1536]{1,0:T(8,128)(2,1)} %convolution_convert_fusion), channel_id=1, source_target_pairs={{0,8},{8,0},{16,24},{24,16},{1,9},{9,1},{17,25},{25,17},{2,10},{10... | collective-permute-start | bytes 7077896 | tf_op jit(solution)/shard_map/ppermute | solution.py:696
  971.1 59.6 %collective-permute-start.53 = (bf16[768,1536]{1,0:T(8,128)(2,1)S(1)}, bf16[768,1536]{1,0:T(8,128)(2,1)S(1)}, u32[]{:S(2)}, u32[]{:S(2)}) collective-permute-start(bf16[768,1536]{1,0:T(8,128)(2,1)S(1)} %add_convert_fusion.5), channel_id=1, source_target_pairs={{2,0},{4,6},{3,1},{5,7},{10,8},{12,14},{11,9},{13,15},{18,16},{20,... | collective-permute-start | bytes 7077896 | tf_op jit(solution)/shard_map/ppermute | solution.py:720
  972.4 67.0 %collective-permute-start.40 = (f32[2,12,768]{2,1,0:T(8,128)S(1)}, f32[2,12,768]{2,1,0:T(8,128)S(1)}, u32[]{:S(2)}, u32[]{:S(2)}) collective-permute-start(f32[2,12,768]{2,1,0:T(8,128)S(1)} %pad_maximum_fusion.4), channel_id=1, source_target_pairs={{0,8},{8,0},{16,24},{24,16},{1,9},{9,1},{17,25},{25,17},{2,10},{10... | collective-permute-start | bytes 221192 | tf_op jit(solution)/shard_map/ppermute | solution.py:696
  976.7 55.6 %collective-permute-start.54 = (bf16[1536,768]{1,0:T(8,128)(2,1)S(1)}, bf16[1536,768]{1,0:T(8,128)(2,1)}, u32[]{:S(2)}, u32[]{:S(2)}) collective-permute-start(bf16[1536,768]{1,0:T(8,128)(2,1)S(1)} %broadcast_select_fusion.5), channel_id=1, source_target_pairs={{8,1},{1,8},{17,16},{25,17},{16,24},{24,25},{10,3},{3,10},{19,18},... | collective-permute-start | bytes 7077896 | tf_op jit(solution)/shard_map/ppermute | solution.py:691
  989.9 45.7 %collective-permute-start.55 = (bf16[1536,768]{1,0:T(8,128)(2,1)S(1)}, bf16[1536,768]{1,0:T(8,128)(2,1)S(1)}, u32[]{:S(2)}, u32[]{:S(2)}) collective-permute-start(bf16[1536,768]{1,0:T(8,128)(2,1)S(1)} %add_convert_fusion.3), channel_id=1, source_target_pairs={{2,4},{4,2},{3,5},{5,3},{10,12},{12,10},{11,13},{13,11},{18,20},{2... | collective-permute-start | bytes 7077896 | tf_op jit(solution)/shard_map/ppermute | solution.py:718
  997.6 54.1 %collective-permute-start.56 = (bf16[768,1536]{1,0:T(8,128)(2,1)}, bf16[768,1536]{1,0:T(8,128)(2,1)}, u32[]{:S(2)}, u32[]{:S(2)}) collective-permute-start(bf16[768,1536]{1,0:T(8,128)(2,1)} %add_convert_fusion.4), channel_id=1, source_target_pairs={{0,2},{6,4},{1,3},{7,5},{8,10},{14,12},{9,11},{15,13},{16,18},{22,... | collective-permute-start | bytes 7077896 | tf_op jit(solution)/shard_map/ppermute | solution.py:728
  1037.7 62.4 %collective-permute-start.57 = (bf16[1536,768]{1,0:T(8,128)(2,1)}, bf16[1536,768]{1,0:T(8,128)(2,1)}, u32[]{:S(2)}, u32[]{:S(2)}) collective-permute-start(bf16[1536,768]{1,0:T(8,128)(2,1)} %add_convert_fusion.2), channel_id=1, source_target_pairs={{2,0},{4,6},{3,1},{5,7},{10,8},{12,14},{11,9},{13,15},{18,16},{20,... | collective-permute-start | bytes 7077896 | tf_op jit(solution)/shard_map/ppermute | solution.py:720
  1040.1 141.4 %reduce-scatter.5.cloned.1.call-start = ((), (), s32[]{:S(2)}) async-start(), calls=%async_computation.5 | async-start | bytes 3538944 | tf_op jit(solution)/shard_map/reduce_scatter | solution.py:806
  1040.2 63.5 %collective-permute-start.58 = (bf16[768,1536]{1,0:T(8,128)(2,1)}, bf16[768,1536]{1,0:T(8,128)(2,1)}, u32[]{:S(2)}, u32[]{:S(2)}) collective-permute-start(bf16[768,1536]{1,0:T(8,128)(2,1)} %broadcast_select_fusion.3), channel_id=1, source_target_pairs={{8,1},{1,8},{17,16},{25,17},{16,24},{24,25},{10,3},{3,10},{19,18},... | collective-permute-start | bytes 7077896 | tf_op jit(solution)/shard_map/ppermute | solution.py:691
  1056.1 50.9 %collective-permute-start.59 = (bf16[768,1536]{1,0:T(8,128)(2,1)}, bf16[768,1536]{1,0:T(8,128)(2,1)}, u32[]{:S(2)}, u32[]{:S(2)}) collective-permute-start(bf16[768,1536]{1,0:T(8,128)(2,1)} %add_convert_fusion.1), channel_id=1, source_target_pairs={{2,4},{4,2},{3,5},{5,3},{10,12},{12,10},{11,13},{13,11},{18,20},{2... | collective-permute-start | bytes 7077896 | tf_op jit(solution)/shard_map/ppermute | solution.py:718
  1061.6 176.2 %reduce-scatter.3.cloned.1.call-start = ((), (), s32[]{:S(2)}) async-start(), calls=%async_computation.3 | async-start | bytes 3538944 | tf_op jit(solution)/shard_map/reduce_scatter | solution.py:806
  1065.9 47.8 %collective-permute-start.43 = (bf16[896,768]{1,0:T(8,128)(2,1)S(1)}, bf16[896,768]{1,0:T(8,128)(2,1)S(1)}, u32[]{:S(2)}, u32[]{:S(2)}) collective-permute-start(bf16[896,768]{1,0:T(8,128)(2,1)S(1)} %pad_maximum_fusion), channel_id=1, source_target_pairs={{0,8},{8,0},{16,24},{24,16},{1,9},{9,1},{17,25},{25,17},{2,10},{10... | collective-permute-start | bytes 4128776 | tf_op jit(solution)/shard_map/ppermute | solution.py:696
  1111.5 54.3 %collective-permute-start.61 = (bf16[768,1536]{1,0:T(8,128)(2,1)}, bf16[768,1536]{1,0:T(8,128)(2,1)}, u32[]{:S(2)}, u32[]{:S(2)}) collective-permute-start(bf16[768,1536]{1,0:T(8,128)(2,1)} %add_convert_fusion), channel_id=1, source_target_pairs={{2,0},{4,6},{3,1},{5,7},{10,8},{12,14},{11,9},{13,15},{18,16},{20,... | collective-permute-start | bytes 7077896 | tf_op jit(solution)/shard_map/ppermute | solution.py:720
  1114.1 33.8 %collective-permute-start.60 = (bf16[896,768]{1,0:T(8,128)(2,1)S(1)}, bf16[896,768]{1,0:T(8,128)(2,1)S(1)}, u32[]{:S(2)}, u32[]{:S(2)}) collective-permute-start(bf16[896,768]{1,0:T(8,128)(2,1)S(1)} %add_convert_fusion.14), channel_id=1, source_target_pairs={{0,2},{6,4},{1,3},{7,5},{8,10},{14,12},{9,11},{15,13},{16,18},{22,... | collective-permute-start | bytes 4128776 | tf_op jit(solution)/shard_map/ppermute | solution.py:728
  1122.7 47.1 %collective-permute-start.62 = (bf16[1536,768]{1,0:T(8,128)(2,1)}, bf16[1536,768]{1,0:T(8,128)(2,1)}, u32[]{:S(2)}, u32[]{:S(2)}) collective-permute-start(bf16[1536,768]{1,0:T(8,128)(2,1)} %broadcast_select_fusion.4), channel_id=1, source_target_pairs={{8,1},{1,8},{17,16},{25,17},{16,24},{24,25},{10,3},{3,10},{19,18},... | collective-permute-start | bytes 7077896 | tf_op jit(solution)/shard_map/ppermute | solution.py:691
  1124.6 34.1 %collective-permute-start.41 = (f32[2,12,768]{2,1,0:T(8,128)}, f32[2,12,768]{2,1,0:T(8,128)S(1)}, u32[]{:S(2)}, u32[]{:S(2)}) collective-permute-start(f32[2,12,768]{2,1,0:T(8,128)} %all-reduce.3.cloned.1.call-done), channel_id=1, source_target_pairs={{0,0},{8,1},{1,8},{9,9},{17,16},{25,17},{16,24},{24,25},{2,2},{10,... | collective-permute-start | bytes 221192 | tf_op jit(solution)/shard_map/ppermute | solution.py:880
  1149.4 23.9 %collective-permute-start.63 = (bf16[896,768]{1,0:T(8,128)(2,1)}, bf16[896,768]{1,0:T(8,128)(2,1)}, u32[]{:S(2)}, u32[]{:S(2)}) collective-permute-start(bf16[896,768]{1,0:T(8,128)(2,1)} %add_convert_fusion.13), channel_id=1, source_target_pairs={{2,4},{4,2},{3,5},{5,3},{10,12},{12,10},{11,13},{13,11},{18,20},{2... | collective-permute-start | bytes 4128776 | tf_op jit(solution)/shard_map/ppermute | solution.py:718
  1167.9 49.7 %collective-permute-start.66 = (bf16[768,1536]{1,0:T(8,128)(2,1)S(1)}, bf16[768,1536]{1,0:T(8,128)(2,1)}, u32[]{:S(2)}, u32[]{:S(2)}) collective-permute-start(bf16[768,1536]{1,0:T(8,128)(2,1)S(1)} %broadcast_select_fusion.2), channel_id=1, source_target_pairs={{8,1},{1,8},{17,16},{25,17},{16,24},{24,25},{10,3},{3,10},{19,18},... | collective-permute-start | bytes 7077896 | tf_op jit(solution)/shard_map/ppermute | solution.py:691
  1176.5 33.3 %collective-permute-start.64 = (bf16[896,768]{1,0:T(8,128)(2,1)}, bf16[896,768]{1,0:T(8,128)(2,1)}, u32[]{:S(2)}, u32[]{:S(2)}) collective-permute-start(bf16[896,768]{1,0:T(8,128)(2,1)} %add_convert_fusion.12), channel_id=1, source_target_pairs={{2,0},{4,6},{3,1},{5,7},{10,8},{12,14},{11,9},{13,15},{18,16},{20,... | collective-permute-start | bytes 4128776 | tf_op jit(solution)/shard_map/ppermute | solution.py:720
  1211.3 19.6 %collective-permute-start.65 = (bf16[896,768]{1,0:T(8,128)(2,1)S(1)}, bf16[896,768]{1,0:T(8,128)(2,1)S(1)}, u32[]{:S(2)}, u32[]{:S(2)}) collective-permute-start(bf16[896,768]{1,0:T(8,128)(2,1)S(1)} %broadcast_select_fusion.13), channel_id=1, source_target_pairs={{8,1},{1,8},{17,16},{25,17},{16,24},{24,25},{10,3},{3,10},{19,18},... | collective-permute-start | bytes 4128776 | tf_op jit(solution)/shard_map/ppermute | solution.py:691
  (75 other events, 750.3 us)
Sparse Core Ops, SparseCore 0:
  80.6 39.1 all-gather.2
  168.8 33.7 all-gather.4
  1040.2 42.3 all-reduce.2
  1086.8 57.1 reduce-scatter.4
  1158.9 49.4 reduce-scatter.2

commit v7 on v6

--- a/solution.py
+++ b/solution.py
@@ -11,7 +11,7 @@
 EPS = 1e-05
 LANES = 128
 ROWS = 256
-NORM_ROWS = 64
+NORM_ROWS = 256
 SPAN = 512
 WAYS = 3
 VMEM_LIMIT = 60 * 2**20

time: 1250 us -> 1240 us (level)
  waiting for transfers between devices: 548 us -> 535 us
    ppermute x6, waiting for transfers between devices: 219 us -> 206 us  [local(): hop = lax.ppermute(hop, PLANE, BEHIND)]
where the time goes in v7:
time: 1240 us; the launch traced here: 1230 us
  waiting for transfers between devices  535 us (43%)
  Pallas kernels  273 us (22%)
  starting transfers between devices  182 us (15%)
  other arithmetic  113 us (9%)
  local copies, waits for them, and re-layouts  56.5 us (5%)
  matrix products  52.6 us (4%)
  between operations  16.3 us (1%)
    ppermute x6, waiting for transfers between devices, local(): hop = lax.ppermute(hop, PLANE, BEHIND)  206 us
    pallas_call x7, Pallas kernels, bwd_call(): pl.pallas_call(functools.partial(bwd_kernel, rows, chunks, fresh), out_sh...  163 us
    ppermute x6, waiting for transfers between devices, advance(): lax.ppermute(second[n], 'dp', [(1, 0), (2, 3)])  123 us
    pallas_call x7, Pallas kernels, fwd_call(): pl.pallas_call(functools.partial(fwd_kernel, rows, fresh), out_shape=[mak...  111 us
    ppermute x6, waiting for transfers between devices, line_sums(): arrived.append(lax.ppermute(terms[n], 'dp', [(0, 1), (3, 2)]))  109 us
    dot_general x17, matrix products, dot(): lax.dot_general(left, right, (dims, ((), ())), preferred_element_type=F32)  52.6 us
    ppermute x12, waiting for transfers between devices, routed(): moved = lax.ppermute(value, PLANE, [(a, b) for a, b in routes if a != b])  46.3 us
    ppermute x6, starting transfers between devices, local(): hop = lax.ppermute(hop, PLANE, AHEAD)  46 us
  transfers between devices with their start and end apart: 72, of which 33 were waited for; matrix products, arithmetic and copies ran while one was open for 16% of the time, Pallas kernels for 7%

profile of v7, /device:TPU:1, one launch (start us, length us, event | category | flops | bytes accessed | tf_op | source)
XLA Modules:
  0.0 1228.5 jit_solution(16345732669328585554)
XLA Ops:
  7.3 4.2 dynamic-slice_bitcast_fusion.2
  11.5 4.7 collective-permute-start
  34.2 8.7 collective-permute-done
  48.9 19.2 %collective-permute-done.16 = bf16[768,1536]{1,0:T(8,128)(2,1)} collective-permute-done((bf16[768,1536]{1,0:T(8,128)(2,1)}, bf16[768,1536]{1,0:T(8,128)(2,1)}, u32[]{:S(2)}, u32[]{:S(2)}) %collective-permute-start.16) | collective-permute-done | bytes 2359328 | tf_op jit(solution)/shard_map/ppermute | solution.py:691
  87.9 7.8 collective-permute-done.11
  115.2 4.6 collective-permute-done.12
  144.3 23.3 %section_forward.7 = (f32[2,1024,768]{2,1,0:T(8,128)}, bf16[2,1024,768]{2,1,0:T(8,128)(2,1)}, bf16[2,1024,768]{2,1,0:T(8,128)(2,1)}, bf16[2,1024,768]{2,1,0:T(8,...) custom-call(s32[5]{0:T(128)} %stack.251.refs_0_, ...), custom_call_target="tpu_custom_call" | custom-call | tf_op jit(solution)/shard_map/section_forward/pallas_call | solution.py:342
  169.6 11.0 collective-permute-done.23.refs_1_
  181.4 23.0 %section_forward.8 = (f32[2,1024,768]{2,1,0:T(8,128)}, bf16[2,1024,768]{2,1,0:T(8,128)(2,1)}, bf16[2,1024,768]{2,1,0:T(8,128)(2,1)}, bf16[2,1024,768]{2,1,0:T(8,...) custom-call(s32[5]{0:T(128)} %stack.247.refs_0_, ...), custom_call_target="tpu_custom_call", output_to_operand_aliasing={{0}: (25, {}), {1}: (26, {}), {2}: (27, {}), {3}: (28, {}),... | custom-call | tf_op jit(solution)/shard_map/section_forward/pallas_call | solution.py:342
  204.4 4.4 collective-permute-start.24
  209.3 7.2 collective-permute-done.24.refs_1_
  217.3 29.1 %section_forward.9 = (f32[2,1024,768]{2,1,0:T(8,128)}, bf16[2,1024,768]{2,1,0:T(8,128)(2,1)}, bf16[2,1024,768]{2,1,0:T(8,128)(2,1)}, bf16[2,1024,768]{2,1,0:T(8,...) custom-call(s32[5]{0:T(128)} %stack.243.refs_0_, ...), custom_call_target="tpu_custom_call", output_to_operand_aliasing={{0}: (25, {}), {1}: (26, {}), {2}: (27, {}), {3}: (28, {}),... | custom-call | tf_op jit(solution)/shard_map/section_forward/pallas_call | solution.py:342
  248.3 6.5 collective-permute-done.25.refs_1_
  255.5 28.7 %section_forward.10 = (f32[2,1024,768]{2,1,0:T(8,128)}, bf16[2,1024,768]{2,1,0:T(8,128)(2,1)}, bf16[2,1024,768]{2,1,0:T(8,128)(2,1)}, bf16[2,1024,768]{2,1,0:T(8...) custom-call(s32[5]{0:T(128)} %stack.239.refs_0_, ...), custom_call_target="tpu_custom_call", output_to_operand_aliasing={{0}: (25, {}), {1}: (26, {}), {2}: (27, {}), {3}: (28, {}),... | custom-call | tf_op jit(solution)/shard_map/section_forward/pallas_call | solution.py:342
  284.2 4.2 collective-permute-start.26
  289.0 5.6 collective-permute-done.26.refs_1_
  297.6 30.8 %collective-permute-start.27 = (bf16[256,768]{1,0:T(8,128)(2,1)}, bf16[256,768]{1,0:T(8,128)(2,1)S(1)}, u32[]{:S(2)}, u32[]{:S(2)}) collective-permute-start(bf16[256,768]{1,0:T(8,128)(2,1)} %get-tuple-element.298), channel_id=1, source_target_pairs={{0,1},{8,9},{1,17},{9,25},{17,16},{25,24},{2,3},{10,11},{3,19},{11... | collective-permute-start | bytes 1179656 | tf_op jit(solution)/shard_map/ppermute | solution.py:800
  329.0 4.7 collective-permute-done.27.refs_1_
  336.5 4.0 collective-permute-start.28
  348.8 9.5 section_backward.7
  360.2 32.7 %collective-permute-done.29.refs_2_ = bf16[256,768]{1,0:T(8,128)(2,1)S(1)} collective-permute-done((bf16[256,768]{1,0:T(8,128)(2,1)}, bf16[256,768]{1,0:T(8,128)(2,1)S(1)}, u32[]{:S(2)}, u32[]{:S(2)}) %collective-permute-start.29) | collective-permute-done | bytes 393248 | tf_op jit(solution)/shard_map/ppermute | solution.py:818
  397.6 7.2 collective-permute-done.30.refs_2_
  409.6 144.1 %collective-permute-done.31.refs_2_ = bf16[256,768]{1,0:T(8,128)(2,1)S(1)} collective-permute-done((bf16[256,768]{1,0:T(8,128)(2,1)}, bf16[256,768]{1,0:T(8,128)(2,1)S(1)}, u32[]{:S(2)}, u32[]{:S(2)}) %collective-permute-start.31) | collective-permute-done | bytes 393248 | tf_op jit(solution)/shard_map/ppermute | solution.py:818
  554.4 41.9 %section_backward.10 = (bf16[2,1024,768]{2,1,0:T(8,128)(2,1)}, bf16[2,1024,3072]{2,1,0:T(8,128)(2,1)}, bf16[2,1024,768]{2,1,0:T(8,128)(2,1)}, bf16[1024,128]{1,0...) custom-call(s32[5]{0:T(128)} %stack.257.refs_0_, ...), custom_call_target="tpu_custom_call", output_to_operand_aliasing={{0}: (34, {}), {1}: (35, {}), {2}: (36, {}), {3}: (37, {}),... | custom-call | tf_op jit(solution)/shard_map/section_backward/pallas_call | solution.py:613
  598.2 8.2 collective-permute-done.32.refs_2_
  607.1 43.0 %section_backward.11 = (bf16[2,1024,768]{2,1,0:T(8,128)(2,1)}, bf16[2,1024,3072]{2,1,0:T(8,128)(2,1)}, bf16[2,1024,768]{2,1,0:T(8,128)(2,1)}, bf16[1024,128]{1,0...) custom-call(s32[5]{0:T(128)} %stack.256.refs_0_, ...), custom_call_target="tpu_custom_call", output_to_operand_aliasing={{0}: (34, {}), {1}: (35, {}), {2}: (36, {}), {3}: (37, {}),... | custom-call | tf_op jit(solution)/shard_map/section_backward/pallas_call | solution.py:613
  652.1 6.8 collective-permute-done.33.refs_2_
  659.7 31.9 %section_backward.12 = (bf16[2,1024,768]{2,1,0:T(8,128)(2,1)}, bf16[2,1024,3072]{2,1,0:T(8,128)(2,1)}, bf16[2,1024,768]{2,1,0:T(8,128)(2,1)}, bf16[1024,128]{1,0...) custom-call(s32[5]{0:T(128)} %stack.255.refs_0_, ...), custom_call_target="tpu_custom_call", output_to_operand_aliasing={{0}: (34, {}), {1}: (35, {}), {2}: (36, {}), {3}: (37, {}),... | custom-call | tf_op jit(solution)/shard_map/section_backward/pallas_call | solution.py:613
  693.5 6.8 collective-permute-done.34.refs_2_
  701.0 32.1 %section_backward.13 = (bf16[2,1024,768]{2,1,0:T(8,128)(2,1)}, bf16[2,1024,3072]{2,1,0:T(8,128)(2,1)}, bf16[2,1024,768]{2,1,0:T(8,128)(2,1)}, bf16[1024,128]{1,0...) custom-call(s32[5]{0:T(128)} %stack.254.refs_0_, ...), custom_call_target="tpu_custom_call", output_to_operand_aliasing={{0}: (34, {}), {1}: (35, {}), {2}: (36, {}), {3}: (37, {}),... | custom-call | tf_op jit(solution)/shard_map/section_backward/pallas_call | solution.py:613
  733.2 5.2 convolution_convert_fusion.6
  738.4 11.0 collective-permute-start.35
  754.0 4.6 convolution_convert_fusion.7
  765.9 5.8 convolution_convert_fusion.2
  772.5 13.5 %collective-permute-done.37 = bf16[768,768]{1,0:T(8,128)(2,1)S(1)} collective-permute-done((bf16[768,768]{1,0:T(8,128)(2,1)S(1)}, bf16[768,768]{1,0:T(8,128)(2,1)S(1)}, u32[]{:S(2)}, u32[]{:S(2)}) %collective-permute-start.37) | collective-permute-done | bytes 1179680 | tf_op jit(solution)/shard_map/ppermute | solution.py:728
  792.3 44.4 %collective-permute-done.39 = bf16[1536,768]{1,0:T(8,128)(2,1)} collective-permute-done((bf16[1536,768]{1,0:T(8,128)(2,1)}, bf16[1536,768]{1,0:T(8,128)(2,1)}, u32[]{:S(2)}, u32[]{:S(2)}) %collective-permute-start.39) | collective-permute-done | bytes 2359328 | tf_op jit(solution)/shard_map/ppermute | solution.py:728
  836.6 4.4 add_convert_fusion.10
  843.2 6.1 add_convert_fusion.8
  849.4 8.1 collective-permute-start.47
  863.3 6.4 convolution_convert_fusion.4
  871.8 16.2 %collective-permute-done.45 = bf16[768,768]{1,0:T(8,128)(2,1)} collective-permute-done((bf16[768,768]{1,0:T(8,128)(2,1)}, bf16[768,768]{1,0:T(8,128)(2,1)}, u32[]{:S(2)}, u32[]{:S(2)}) %collective-permute-start.45) | collective-permute-done | bytes 1179680 | tf_op jit(solution)/shard_map/ppermute | solution.py:720
  893.9 11.3 collective-permute-done.47
  910.6 5.3 convolution_convert_fusion.5
  920.4 4.1 collective-permute-start.52
  924.5 4.0 convolution_convert_fusion
  930.0 4.0 collective-permute-done.49
  935.2 17.2 %collective-permute-done.48 = bf16[1536,768]{1,0:T(8,128)(2,1)S(1)} collective-permute-done((bf16[1536,768]{1,0:T(8,128)(2,1)S(1)}, bf16[1536,768]{1,0:T(8,128)(2,1)S(1)}, u32[]{:S(2)}, u32[]{:S(2)}) %collective-permute-start.48) | collective-permute-done | bytes 2359328 | tf_op jit(solution)/shard_map/ppermute | solution.py:720
  962.7 10.7 collective-permute-done.52
  976.5 5.2 add_convert_fusion.4
  981.7 7.4 collective-permute-start.56
  989.1 25.7 %collective-permute-done.53 = bf16[768,1536]{1,0:T(8,128)(2,1)S(1)} collective-permute-done((bf16[768,1536]{1,0:T(8,128)(2,1)S(1)}, bf16[768,1536]{1,0:T(8,128)(2,1)S(1)}, u32[]{:S(2)}, u32[]{:S(2)}) %collective-permute-start.53) | collective-permute-done | bytes 2359328 | tf_op jit(solution)/shard_map/ppermute | solution.py:720
  1026.3 9.4 collective-permute-done.56
  1035.7 4.4 add_convert_fusion.1
  1050.0 3.7 collective-permute-start.43
  1053.7 30.4 %collective-permute-done.57 = bf16[1536,768]{1,0:T(8,128)(2,1)} collective-permute-done((bf16[1536,768]{1,0:T(8,128)(2,1)}, bf16[1536,768]{1,0:T(8,128)(2,1)}, u32[]{:S(2)}, u32[]{:S(2)}) %collective-permute-start.57) | collective-permute-done | bytes 2359328 | tf_op jit(solution)/shard_map/ppermute | solution.py:720
  1091.0 4.5 add_convert_fusion
  1098.2 8.5 collective-permute-start.60
  1112.4 19.6 %collective-permute-done.60 = bf16[896,768]{1,0:T(8,128)(2,1)S(1)} collective-permute-done((bf16[896,768]{1,0:T(8,128)(2,1)S(1)}, bf16[896,768]{1,0:T(8,128)(2,1)S(1)}, u32[]{:S(2)}, u32[]{:S(2)}) %collective-permute-start.60) | collective-permute-done | bytes 1376288 | tf_op jit(solution)/shard_map/ppermute | solution.py:728
  1135.2 7.6 collective-permute-done.41
  1142.9 7.0 collective-permute-done.61
  1167.6 26.1 %collective-permute-done.64 = bf16[896,768]{1,0:T(8,128)(2,1)} collective-permute-done((bf16[896,768]{1,0:T(8,128)(2,1)}, bf16[896,768]{1,0:T(8,128)(2,1)}, u32[]{:S(2)}, u32[]{:S(2)}) %collective-permute-start.64) | collective-permute-done | bytes 1376288 | tf_op jit(solution)/shard_map/ppermute | solution.py:720
  1197.1 4.4 maximum_convert_fusion.1
  1203.9 4.4 maximum_convert_fusion
  1208.2 6.6 collective-permute-done.65
  (382 shorter events, 259.6 us)
Async XLA Ops:
  7.2 136.2 %all-gather.3.cloned.1.call-start = ((), (), s32[]{:S(2)}) async-start(), calls=%async_computation.2 | async-start | bytes 3538944 | tf_op jit(solution)/shard_map/all_gather | solution.py:781
  11.5 31.3 %collective-permute-start = (bf16[1536,768]{1,0:T(8,128)(2,1)S(1)}, bf16[1536,768]{1,0:T(8,128)(2,1)}, u32[]{:S(2)}, u32[]{:S(2)}) collective-permute-start(bf16[1536,768]{1,0:T(8,128)(2,1)S(1)} %get-tuple-element.454), channel_id=1, source_target_pairs={{1,8},{8,1},{16,17},{17,25},{24,16},{25,24},{3,10},{10,3},{18,19},... | collective-permute-start | bytes 7077896 | tf_op jit(solution)/shard_map/ppermute | solution.py:691
  18.7 49.4 %collective-permute-start.16 = (bf16[768,1536]{1,0:T(8,128)(2,1)}, bf16[768,1536]{1,0:T(8,128)(2,1)}, u32[]{:S(2)}, u32[]{:S(2)}) collective-permute-start(bf16[768,1536]{1,0:T(8,128)(2,1)} %get-tuple-element.452), channel_id=1, source_target_pairs={{1,8},{8,1},{16,17},{17,25},{24,16},{25,24},{3,10},{10,3},{18,19},... | collective-permute-start | bytes 7077896 | tf_op jit(solution)/shard_map/ppermute | solution.py:691
  26.5 48.6 %collective-permute-start.1 = (f32[103,128]{1,0:T(8,128)}, f32[103,128]{1,0:T(8,128)}, u32[]{:S(2)}, u32[]{:S(2)}) collective-permute-start(f32[103,128]{1,0:T(8,128)} %bitcast.19), channel_id=1, source_target_pairs={{1,8},{8,1},{16,17},{17,25},{24,16},{25,24},{3,10},{10,3},{18,19},... | collective-permute-start | bytes 158216 | tf_op jit(solution)/shard_map/ppermute | solution.py:691
  30.2 47.1 %collective-permute-start.3 = (bf16[768,128]{1,0:T(8,128)(2,1)}, bf16[768,128]{1,0:T(8,128)(2,1)}, u32[]{:S(2)}, u32[]{:S(2)}) collective-permute-start(bf16[768,128]{1,0:T(8,128)(2,1)} %bitcast.24), channel_id=1, source_target_pairs={{1,8},{8,1},{16,17},{17,25},{24,16},{25,24},{3,10},{10,3},{18,19},... | collective-permute-start | bytes 589832 | tf_op jit(solution)/shard_map/ppermute | solution.py:691
  32.1 64.3 %collective-permute-start.9 = (bf16[1536,768]{1,0:T(8,128)(2,1)}, bf16[1536,768]{1,0:T(8,128)(2,1)}, u32[]{:S(2)}, u32[]{:S(2)}) collective-permute-start(bf16[1536,768]{1,0:T(8,128)(2,1)} %get-tuple-element.453), channel_id=1, source_target_pairs={{17,25},{24,16},{19,27},{26,18},{21,29},{28,20},{23,31},{30,22}} | collective-permute-start | bytes 7077896 | tf_op jit(solution)/shard_map/ppermute | solution.py:685
  44.8 52.4 %collective-permute-start.8 = (bf16[1536,768]{1,0:T(8,128)(2,1)S(1)}, bf16[1536,768]{1,0:T(8,128)(2,1)}, u32[]{:S(2)}, u32[]{:S(2)}) collective-permute-start(bf16[1536,768]{1,0:T(8,128)(2,1)S(1)} %broadcast_select_fusion.10.refs_21_), channel_id=1, source_target_pairs={{10,8},{8,10},{14,12},{12,14},{3,1},{1,3},{7,5},{5,7},{19,17},{17,... | collective-permute-start | bytes 7077896 | tf_op jit(solution)/shard_map/ppermute | solution.py:684
  68.1 13.7 %collective-permute-start.4 = (bf16[768,384]{1,0:T(8,128)(2,1)S(1)}, bf16[768,384]{1,0:T(8,128)(2,1)S(1)}, u32[]{:S(2)}, u32[]{:S(2)}) collective-permute-start(bf16[768,384]{1,0:T(8,128)(2,1)S(1)} %get-tuple-element.462), channel_id=1, source_target_pairs={{1,8},{8,1},{16,17},{17,25},{24,16},{25,24},{3,10},{10,3},{18,19},... | collective-permute-start | bytes 1769480 | tf_op jit(solution)/shard_map/ppermute | solution.py:691
  75.1 27.5 %collective-permute-start.18 = (bf16[768,1536]{1,0:T(8,128)(2,1)}, bf16[768,1536]{1,0:T(8,128)(2,1)}, u32[]{:S(2)}, u32[]{:S(2)}) collective-permute-start(bf16[768,1536]{1,0:T(8,128)(2,1)} %get-tuple-element.451), channel_id=1, source_target_pairs={{17,25},{24,16},{19,27},{26,18},{21,29},{28,20},{23,31},{30,22}} | collective-permute-start | bytes 7077896 | tf_op jit(solution)/shard_map/ppermute | solution.py:685
  77.2 30.2 %collective-permute-start.17 = (bf16[768,1536]{1,0:T(8,128)(2,1)}, bf16[768,1536]{1,0:T(8,128)(2,1)}, u32[]{:S(2)}, u32[]{:S(2)}) collective-permute-start(bf16[768,1536]{1,0:T(8,128)(2,1)} %broadcast_select_fusion.7.refs_17_), channel_id=1, source_target_pairs={{10,8},{8,10},{14,12},{12,14},{3,1},{1,3},{7,5},{5,7},{19,17},{17,... | collective-permute-start | bytes 7077896 | tf_op jit(solution)/shard_map/ppermute | solution.py:684
  80.5 268.3 %all-gather.5.cloned.1.call-start = ((), (), s32[]{:S(2)}) async-start(), calls=%async_computation.4 | async-start | bytes 3538944 | tf_op jit(solution)/shard_map/all_gather | solution.py:798
  81.9 13.8 %collective-permute-start.11 = (bf16[384,768]{1,0:T(8,128)(2,1)S(1)}, bf16[384,768]{1,0:T(8,128)(2,1)S(1)}, u32[]{:S(2)}, u32[]{:S(2)}) collective-permute-start(bf16[384,768]{1,0:T(8,128)(2,1)S(1)} %get-tuple-element.460), channel_id=1, source_target_pairs={{1,8},{8,1},{16,17},{17,25},{24,16},{25,24},{3,10},{10,3},{18,19},... | collective-permute-start | bytes 1769480 | tf_op jit(solution)/shard_map/ppermute | solution.py:691
  95.7 15.1 %collective-permute-start.6 = (bf16[768,384]{1,0:T(8,128)(2,1)}, bf16[768,384]{1,0:T(8,128)(2,1)S(1)}, u32[]{:S(2)}, u32[]{:S(2)}) collective-permute-start(bf16[768,384]{1,0:T(8,128)(2,1)} %get-tuple-element.461), channel_id=1, source_target_pairs={{17,25},{24,16},{19,27},{26,18},{21,29},{28,20},{23,31},{30,22}} | collective-permute-start | bytes 1769480 | tf_op jit(solution)/shard_map/ppermute | solution.py:685
  96.5 15.7 %collective-permute-start.13 = (bf16[384,768]{1,0:T(8,128)(2,1)S(1)}, bf16[384,768]{1,0:T(8,128)(2,1)S(1)}, u32[]{:S(2)}, u32[]{:S(2)}) collective-permute-start(bf16[384,768]{1,0:T(8,128)(2,1)S(1)} %get-tuple-element.459), channel_id=1, source_target_pairs={{17,25},{24,16},{19,27},{26,18},{21,29},{28,20},{23,31},{30,22}} | collective-permute-start | bytes 1769480 | tf_op jit(solution)/shard_map/ppermute | solution.py:685
  100.7 13.1 %collective-permute-start.5 = (bf16[768,384]{1,0:T(8,128)(2,1)S(1)}, bf16[768,384]{1,0:T(8,128)(2,1)S(1)}, u32[]{:S(2)}, u32[]{:S(2)}) collective-permute-start(bf16[768,384]{1,0:T(8,128)(2,1)S(1)} %broadcast_select_fusion.18.refs_9_), channel_id=1, source_target_pairs={{10,8},{8,10},{14,12},{12,14},{3,1},{1,3},{7,5},{5,7},{19,17},{17,... | collective-permute-start | bytes 1769480 | tf_op jit(solution)/shard_map/ppermute | solution.py:684
  102.6 17.1 %collective-permute-start.12 = (bf16[384,768]{1,0:T(8,128)(2,1)S(1)}, bf16[384,768]{1,0:T(8,128)(2,1)}, u32[]{:S(2)}, u32[]{:S(2)}) collective-permute-start(bf16[384,768]{1,0:T(8,128)(2,1)S(1)} %broadcast_select_fusion.17.refs_13_), channel_id=1, source_target_pairs={{10,8},{8,10},{14,12},{12,14},{3,1},{1,3},{7,5},{5,7},{19,17},{17,... | collective-permute-start | bytes 1769480 | tf_op jit(solution)/shard_map/ppermute | solution.py:684
  107.4 22.9 %collective-permute-start.19 = (bf16[768,1536]{1,0:T(8,128)(2,1)}, bf16[768,1536]{1,0:T(8,128)(2,1)}, u32[]{:S(2)}, u32[]{:S(2)}) collective-permute-start(bf16[768,1536]{1,0:T(8,128)(2,1)} %broadcast_select_fusion.7.refs_17_), channel_id=1, source_target_pairs={{0,8},{8,0},{16,24},{24,16},{1,9},{9,1},{17,25},{25,17},{2,10},{10... | collective-permute-start | bytes 7077896 | tf_op jit(solution)/shard_map/ppermute | solution.py:696
  110.8 32.5 %collective-permute-start.21 = (bf16[1536,768]{1,0:T(8,128)(2,1)S(1)}, bf16[1536,768]{1,0:T(8,128)(2,1)}, u32[]{:S(2)}, u32[]{:S(2)}) collective-permute-start(bf16[1536,768]{1,0:T(8,128)(2,1)S(1)} %broadcast_select_fusion.10.refs_21_), channel_id=1, source_target_pairs={{0,8},{8,0},{16,24},{24,16},{1,9},{9,1},{17,25},{25,17},{2,10},{10... | collective-permute-start | bytes 7077896 | tf_op jit(solution)/shard_map/ppermute | solution.py:696
  112.2 31.2 %collective-permute-start.20 = (bf16[768,1536]{1,0:T(8,128)(2,1)}, bf16[768,1536]{1,0:T(8,128)(2,1)}, u32[]{:S(2)}, u32[]{:S(2)}) collective-permute-start(bf16[768,1536]{1,0:T(8,128)(2,1)} %select_select_fusion.refs_18_), channel_id=1, source_target_pairs={{0,8},{8,0},{16,24},{24,16},{1,9},{9,1},{17,25},{25,17},{2,10},{10... | collective-permute-start | bytes 7077896 | tf_op jit(solution)/shard_map/ppermute | solution.py:696
  113.7 29.6 %collective-permute-start.22 = (bf16[1536,768]{1,0:T(8,128)(2,1)}, bf16[1536,768]{1,0:T(8,128)(2,1)}, u32[]{:S(2)}, u32[]{:S(2)}) collective-permute-start(bf16[1536,768]{1,0:T(8,128)(2,1)} %select_select_fusion.1.refs_22_), channel_id=1, source_target_pairs={{0,8},{8,0},{16,24},{24,16},{1,9},{9,1},{17,25},{25,17},{2,10},{10... | collective-permute-start | bytes 7077896 | tf_op jit(solution)/shard_map/ppermute | solution.py:696
  130.3 13.0 %collective-permute-start.10 = (bf16[768,384]{1,0:T(8,128)(2,1)S(1)}, bf16[768,384]{1,0:T(8,128)(2,1)S(1)}, u32[]{:S(2)}, u32[]{:S(2)}) collective-permute-start(bf16[768,384]{1,0:T(8,128)(2,1)S(1)} %select_select_fusion.3.refs_10_), channel_id=1, source_target_pairs={{0,8},{8,0},{16,24},{24,16},{1,9},{9,1},{17,25},{25,17},{2,10},{10... | collective-permute-start | bytes 1769480 | tf_op jit(solution)/shard_map/ppermute | solution.py:696
  130.3 13.0 %collective-permute-start.15 = (bf16[384,768]{1,0:T(8,128)(2,1)}, bf16[384,768]{1,0:T(8,128)(2,1)}, u32[]{:S(2)}, u32[]{:S(2)}) collective-permute-start(bf16[384,768]{1,0:T(8,128)(2,1)} %select_select_fusion.2.refs_14_), channel_id=1, source_target_pairs={{0,8},{8,0},{16,24},{24,16},{1,9},{9,1},{17,25},{25,17},{2,10},{10... | collective-permute-start | bytes 1769480 | tf_op jit(solution)/shard_map/ppermute | solution.py:696
  167.6 941.1 %all-reduce.3.cloned.1.call-start = ((), (), s32[]{:S(2)}) async-start(), calls=%async_computation.6 | async-start | bytes 196608 | tf_op jit(solution)/shard_map/psum | solution.py:880
  167.7 13.0 %collective-permute-start.23 = (bf16[256,768]{1,0:T(8,128)(2,1)}, bf16[256,768]{1,0:T(8,128)(2,1)S(1)}, u32[]{:S(2)}, u32[]{:S(2)}) collective-permute-start(bf16[256,768]{1,0:T(8,128)(2,1)} %get-tuple-element.234), channel_id=1, source_target_pairs={{0,1},{8,9},{1,17},{9,25},{17,16},{25,24},{2,3},{10,11},{3,19},{11... | collective-permute-start | bytes 1179656 | tf_op jit(solution)/shard_map/ppermute | solution.py:800
  204.4 12.1 collective-permute-start.24
  284.2 10.4 collective-permute-start.26
  297.6 36.1 %collective-permute-start.27 = (bf16[256,768]{1,0:T(8,128)(2,1)}, bf16[256,768]{1,0:T(8,128)(2,1)S(1)}, u32[]{:S(2)}, u32[]{:S(2)}) collective-permute-start(bf16[256,768]{1,0:T(8,128)(2,1)} %get-tuple-element.298), channel_id=1, source_target_pairs={{0,1},{8,9},{1,17},{9,25},{17,16},{25,24},{2,3},{10,11},{3,19},{11... | collective-permute-start | bytes 1179656 | tf_op jit(solution)/shard_map/ppermute | solution.py:800
  336.5 9.0 collective-permute-start.28
  358.3 34.6 %collective-permute-start.29 = (bf16[256,768]{1,0:T(8,128)(2,1)}, bf16[256,768]{1,0:T(8,128)(2,1)S(1)}, u32[]{:S(2)}, u32[]{:S(2)}) collective-permute-start(bf16[256,768]{1,0:T(8,128)(2,1)} %get-tuple-element.342), channel_id=1, source_target_pairs={{1,0},{9,8},{17,1},{25,9},{16,17},{24,25},{3,2},{11,10},{19,3},{27... | collective-permute-start | bytes 1179656 | tf_op jit(solution)/shard_map/ppermute | solution.py:818
  395.7 9.1 collective-permute-start.30
  407.7 146.0 %collective-permute-start.31 = (bf16[256,768]{1,0:T(8,128)(2,1)}, bf16[256,768]{1,0:T(8,128)(2,1)S(1)}, u32[]{:S(2)}, u32[]{:S(2)}) collective-permute-start(bf16[256,768]{1,0:T(8,128)(2,1)} %get-tuple-element.360), channel_id=1, source_target_pairs={{1,0},{9,8},{17,1},{25,9},{16,17},{24,25},{3,2},{11,10},{19,3},{27... | collective-permute-start | bytes 1179656 | tf_op jit(solution)/shard_map/ppermute | solution.py:818
  596.3 10.1 collective-permute-start.32
  738.4 22.8 %collective-permute-start.35 = (bf16[1536,768]{1,0:T(8,128)(2,1)S(1)}, bf16[1536,768]{1,0:T(8,128)(2,1)S(1)}, u32[]{:S(2)}, u32[]{:S(2)}) collective-permute-start(bf16[1536,768]{1,0:T(8,128)(2,1)S(1)} %convolution_convert_fusion.6), channel_id=1, source_target_pairs={{0,8},{8,0},{16,24},{24,16},{1,9},{9,1},{17,25},{25,17},{2,10},{10... | collective-permute-start | bytes 7077896 | tf_op jit(solution)/shard_map/ppermute | solution.py:696
  758.8 27.1 %collective-permute-start.37 = (bf16[768,768]{1,0:T(8,128)(2,1)S(1)}, bf16[768,768]{1,0:T(8,128)(2,1)S(1)}, u32[]{:S(2)}, u32[]{:S(2)}) collective-permute-start(bf16[768,768]{1,0:T(8,128)(2,1)S(1)} %add_convert_fusion.17), channel_id=1, source_target_pairs={{0,2},{6,4},{1,3},{7,5},{8,10},{14,12},{9,11},{15,13},{16,18},{22,... | collective-permute-start | bytes 3538952 | tf_op jit(solution)/shard_map/ppermute | solution.py:728
  763.2 73.4 %collective-permute-start.39 = (bf16[1536,768]{1,0:T(8,128)(2,1)}, bf16[1536,768]{1,0:T(8,128)(2,1)}, u32[]{:S(2)}, u32[]{:S(2)}) collective-permute-start(bf16[1536,768]{1,0:T(8,128)(2,1)} %add_convert_fusion.11), channel_id=1, source_target_pairs={{0,2},{6,4},{1,3},{7,5},{8,10},{14,12},{9,11},{15,13},{16,18},{22,... | collective-permute-start | bytes 7077896 | tf_op jit(solution)/shard_map/ppermute | solution.py:728
  771.7 71.5 %collective-permute-start.44 = (bf16[768,1536]{1,0:T(8,128)(2,1)}, bf16[768,1536]{1,0:T(8,128)(2,1)}, u32[]{:S(2)}, u32[]{:S(2)}) collective-permute-start(bf16[768,1536]{1,0:T(8,128)(2,1)} %convolution_convert_fusion.2), channel_id=1, source_target_pairs={{0,8},{8,0},{16,24},{24,16},{1,9},{9,1},{17,25},{25,17},{2,10},{10... | collective-permute-start | bytes 7077896 | tf_op jit(solution)/shard_map/ppermute | solution.py:696
  841.0 48.4 %collective-permute-start.46 = (bf16[1536,768]{1,0:T(8,128)(2,1)}, bf16[1536,768]{1,0:T(8,128)(2,1)}, u32[]{:S(2)}, u32[]{:S(2)}) collective-permute-start(bf16[1536,768]{1,0:T(8,128)(2,1)} %add_convert_fusion.10), channel_id=1, source_target_pairs={{2,4},{4,2},{3,5},{5,3},{10,12},{12,10},{11,13},{13,11},{18,20},{2... | collective-permute-start | bytes 7077896 | tf_op jit(solution)/shard_map/ppermute | solution.py:718
  849.4 55.9 %collective-permute-start.47 = (bf16[768,1536]{1,0:T(8,128)(2,1)}, bf16[768,1536]{1,0:T(8,128)(2,1)}, u32[]{:S(2)}, u32[]{:S(2)}) collective-permute-start(bf16[768,1536]{1,0:T(8,128)(2,1)} %add_convert_fusion.8), channel_id=1, source_target_pairs={{0,2},{6,4},{1,3},{7,5},{8,10},{14,12},{9,11},{15,13},{16,18},{22,... | collective-permute-start | bytes 7077896 | tf_op jit(solution)/shard_map/ppermute | solution.py:728
  860.2 27.8 %collective-permute-start.45 = (bf16[768,768]{1,0:T(8,128)(2,1)}, bf16[768,768]{1,0:T(8,128)(2,1)}, u32[]{:S(2)}, u32[]{:S(2)}) collective-permute-start(bf16[768,768]{1,0:T(8,128)(2,1)} %add_convert_fusion.15), channel_id=1, source_target_pairs={{2,0},{4,6},{3,1},{5,7},{10,8},{12,14},{11,9},{13,15},{18,16},{20,... | collective-permute-start | bytes 3538952 | tf_op jit(solution)/shard_map/ppermute | solution.py:720
  869.8 48.4 %collective-permute-start.42 = (bf16[1536,768]{1,0:T(8,128)(2,1)}, bf16[1536,768]{1,0:T(8,128)(2,1)}, u32[]{:S(2)}, u32[]{:S(2)}) collective-permute-start(bf16[1536,768]{1,0:T(8,128)(2,1)} %convolution_convert_fusion.4), channel_id=1, source_target_pairs={{0,8},{8,0},{16,24},{24,16},{1,9},{9,1},{17,25},{25,17},{2,10},{10... | collective-permute-start | bytes 7077896 | tf_op jit(solution)/shard_map/ppermute | solution.py:696
  892.4 60.1 %collective-permute-start.48 = (bf16[1536,768]{1,0:T(8,128)(2,1)S(1)}, bf16[1536,768]{1,0:T(8,128)(2,1)S(1)}, u32[]{:S(2)}, u32[]{:S(2)}) collective-permute-start(bf16[1536,768]{1,0:T(8,128)(2,1)S(1)} %add_convert_fusion.7), channel_id=1, source_target_pairs={{2,0},{4,6},{3,1},{5,7},{10,8},{12,14},{11,9},{13,15},{18,16},{20,... | collective-permute-start | bytes 7077896 | tf_op jit(solution)/shard_map/ppermute | solution.py:720
  908.4 44.3 %collective-permute-start.50 = (bf16[768,1536]{1,0:T(8,128)(2,1)S(1)}, bf16[768,1536]{1,0:T(8,128)(2,1)}, u32[]{:S(2)}, u32[]{:S(2)}) collective-permute-start(bf16[768,1536]{1,0:T(8,128)(2,1)S(1)} %add_convert_fusion.6), channel_id=1, source_target_pairs={{2,4},{4,2},{3,5},{5,3},{10,12},{12,10},{11,13},{13,11},{18,20},{2... | collective-permute-start | bytes 7077896 | tf_op jit(solution)/shard_map/ppermute | solution.py:718
  916.0 18.1 %collective-permute-start.49 = (bf16[768,768]{1,0:T(8,128)(2,1)S(1)}, bf16[768,768]{1,0:T(8,128)(2,1)S(1)}, u32[]{:S(2)}, u32[]{:S(2)}) collective-permute-start(bf16[768,768]{1,0:T(8,128)(2,1)S(1)} %broadcast_select_fusion.16), channel_id=1, source_target_pairs={{8,1},{1,8},{17,16},{25,17},{16,24},{24,25},{10,3},{3,10},{19,18},... | collective-permute-start | bytes 3538952 | tf_op jit(solution)/shard_map/ppermute | solution.py:691
  920.4 53.0 %collective-permute-start.52 = (bf16[1536,768]{1,0:T(8,128)(2,1)S(1)}, bf16[1536,768]{1,0:T(8,128)(2,1)S(1)}, u32[]{:S(2)}, u32[]{:S(2)}) collective-permute-start(bf16[1536,768]{1,0:T(8,128)(2,1)S(1)} %add_convert_fusion.9), channel_id=1, source_target_pairs={{0,2},{6,4},{1,3},{7,5},{8,10},{14,12},{9,11},{15,13},{16,18},{22,... | collective-permute-start | bytes 7077896 | tf_op jit(solution)/shard_map/ppermute | solution.py:728
  928.5 48.0 %collective-permute-start.51 = (bf16[768,1536]{1,0:T(8,128)(2,1)}, bf16[768,1536]{1,0:T(8,128)(2,1)}, u32[]{:S(2)}, u32[]{:S(2)}) collective-permute-start(bf16[768,1536]{1,0:T(8,128)(2,1)} %convolution_convert_fusion), channel_id=1, source_target_pairs={{0,8},{8,0},{16,24},{24,16},{1,9},{9,1},{17,25},{25,17},{2,10},{10... | collective-permute-start | bytes 7077896 | tf_op jit(solution)/shard_map/ppermute | solution.py:696
  955.1 59.6 %collective-permute-start.53 = (bf16[768,1536]{1,0:T(8,128)(2,1)S(1)}, bf16[768,1536]{1,0:T(8,128)(2,1)S(1)}, u32[]{:S(2)}, u32[]{:S(2)}) collective-permute-start(bf16[768,1536]{1,0:T(8,128)(2,1)S(1)} %add_convert_fusion.5), channel_id=1, source_target_pairs={{2,0},{4,6},{3,1},{5,7},{10,8},{12,14},{11,9},{13,15},{18,16},{20,... | collective-permute-start | bytes 7077896 | tf_op jit(solution)/shard_map/ppermute | solution.py:720
  956.5 67.0 %collective-permute-start.40 = (f32[2,12,768]{2,1,0:T(8,128)S(1)}, f32[2,12,768]{2,1,0:T(8,128)S(1)}, u32[]{:S(2)}, u32[]{:S(2)}) collective-permute-start(f32[2,12,768]{2,1,0:T(8,128)S(1)} %pad_maximum_fusion.4), channel_id=1, source_target_pairs={{0,8},{8,0},{16,24},{24,16},{1,9},{9,1},{17,25},{25,17},{2,10},{10... | collective-permute-start | bytes 221192 | tf_op jit(solution)/shard_map/ppermute | solution.py:696
  960.8 55.6 %collective-permute-start.54 = (bf16[1536,768]{1,0:T(8,128)(2,1)S(1)}, bf16[1536,768]{1,0:T(8,128)(2,1)}, u32[]{:S(2)}, u32[]{:S(2)}) collective-permute-start(bf16[1536,768]{1,0:T(8,128)(2,1)S(1)} %broadcast_select_fusion.5), channel_id=1, source_target_pairs={{8,1},{1,8},{17,16},{25,17},{16,24},{24,25},{10,3},{3,10},{19,18},... | collective-permute-start | bytes 7077896 | tf_op jit(solution)/shard_map/ppermute | solution.py:691
  974.0 45.7 %collective-permute-start.55 = (bf16[1536,768]{1,0:T(8,128)(2,1)S(1)}, bf16[1536,768]{1,0:T(8,128)(2,1)S(1)}, u32[]{:S(2)}, u32[]{:S(2)}) collective-permute-start(bf16[1536,768]{1,0:T(8,128)(2,1)S(1)} %add_convert_fusion.3), channel_id=1, source_target_pairs={{2,4},{4,2},{3,5},{5,3},{10,12},{12,10},{11,13},{13,11},{18,20},{2... | collective-permute-start | bytes 7077896 | tf_op jit(solution)/shard_map/ppermute | solution.py:718
  981.7 54.1 %collective-permute-start.56 = (bf16[768,1536]{1,0:T(8,128)(2,1)}, bf16[768,1536]{1,0:T(8,128)(2,1)}, u32[]{:S(2)}, u32[]{:S(2)}) collective-permute-start(bf16[768,1536]{1,0:T(8,128)(2,1)} %add_convert_fusion.4), channel_id=1, source_target_pairs={{0,2},{6,4},{1,3},{7,5},{8,10},{14,12},{9,11},{15,13},{16,18},{22,... | collective-permute-start | bytes 7077896 | tf_op jit(solution)/shard_map/ppermute | solution.py:728
  1021.8 62.4 %collective-permute-start.57 = (bf16[1536,768]{1,0:T(8,128)(2,1)}, bf16[1536,768]{1,0:T(8,128)(2,1)}, u32[]{:S(2)}, u32[]{:S(2)}) collective-permute-start(bf16[1536,768]{1,0:T(8,128)(2,1)} %add_convert_fusion.2), channel_id=1, source_target_pairs={{2,0},{4,6},{3,1},{5,7},{10,8},{12,14},{11,9},{13,15},{18,16},{20,... | collective-permute-start | bytes 7077896 | tf_op jit(solution)/shard_map/ppermute | solution.py:720
  1024.2 141.3 %reduce-scatter.5.cloned.1.call-start = ((), (), s32[]{:S(2)}) async-start(), calls=%async_computation.5 | async-start | bytes 3538944 | tf_op jit(solution)/shard_map/reduce_scatter | solution.py:806
  1024.2 63.5 %collective-permute-start.58 = (bf16[768,1536]{1,0:T(8,128)(2,1)}, bf16[768,1536]{1,0:T(8,128)(2,1)}, u32[]{:S(2)}, u32[]{:S(2)}) collective-permute-start(bf16[768,1536]{1,0:T(8,128)(2,1)} %broadcast_select_fusion.3), channel_id=1, source_target_pairs={{8,1},{1,8},{17,16},{25,17},{16,24},{24,25},{10,3},{3,10},{19,18},... | collective-permute-start | bytes 7077896 | tf_op jit(solution)/shard_map/ppermute | solution.py:691
  1040.1 50.9 %collective-permute-start.59 = (bf16[768,1536]{1,0:T(8,128)(2,1)}, bf16[768,1536]{1,0:T(8,128)(2,1)}, u32[]{:S(2)}, u32[]{:S(2)}) collective-permute-start(bf16[768,1536]{1,0:T(8,128)(2,1)} %add_convert_fusion.1), channel_id=1, source_target_pairs={{2,4},{4,2},{3,5},{5,3},{10,12},{12,10},{11,13},{13,11},{18,20},{2... | collective-permute-start | bytes 7077896 | tf_op jit(solution)/shard_map/ppermute | solution.py:718
  1045.7 176.1 %reduce-scatter.3.cloned.1.call-start = ((), (), s32[]{:S(2)}) async-start(), calls=%async_computation.3 | async-start | bytes 3538944 | tf_op jit(solution)/shard_map/reduce_scatter | solution.py:806
  1050.0 47.8 %collective-permute-start.43 = (bf16[896,768]{1,0:T(8,128)(2,1)S(1)}, bf16[896,768]{1,0:T(8,128)(2,1)S(1)}, u32[]{:S(2)}, u32[]{:S(2)}) collective-permute-start(bf16[896,768]{1,0:T(8,128)(2,1)S(1)} %pad_maximum_fusion), channel_id=1, source_target_pairs={{0,8},{8,0},{16,24},{24,16},{1,9},{9,1},{17,25},{25,17},{2,10},{10... | collective-permute-start | bytes 4128776 | tf_op jit(solution)/shard_map/ppermute | solution.py:696
  1095.6 54.3 %collective-permute-start.61 = (bf16[768,1536]{1,0:T(8,128)(2,1)}, bf16[768,1536]{1,0:T(8,128)(2,1)}, u32[]{:S(2)}, u32[]{:S(2)}) collective-permute-start(bf16[768,1536]{1,0:T(8,128)(2,1)} %add_convert_fusion), channel_id=1, source_target_pairs={{2,0},{4,6},{3,1},{5,7},{10,8},{12,14},{11,9},{13,15},{18,16},{20,... | collective-permute-start | bytes 7077896 | tf_op jit(solution)/shard_map/ppermute | solution.py:720
  1098.2 33.8 %collective-permute-start.60 = (bf16[896,768]{1,0:T(8,128)(2,1)S(1)}, bf16[896,768]{1,0:T(8,128)(2,1)S(1)}, u32[]{:S(2)}, u32[]{:S(2)}) collective-permute-start(bf16[896,768]{1,0:T(8,128)(2,1)S(1)} %add_convert_fusion.14), channel_id=1, source_target_pairs={{0,2},{6,4},{1,3},{7,5},{8,10},{14,12},{9,11},{15,13},{16,18},{22,... | collective-permute-start | bytes 4128776 | tf_op jit(solution)/shard_map/ppermute | solution.py:728
  1106.8 47.1 %collective-permute-start.62 = (bf16[1536,768]{1,0:T(8,128)(2,1)}, bf16[1536,768]{1,0:T(8,128)(2,1)}, u32[]{:S(2)}, u32[]{:S(2)}) collective-permute-start(bf16[1536,768]{1,0:T(8,128)(2,1)} %broadcast_select_fusion.4), channel_id=1, source_target_pairs={{8,1},{1,8},{17,16},{25,17},{16,24},{24,25},{10,3},{3,10},{19,18},... | collective-permute-start | bytes 7077896 | tf_op jit(solution)/shard_map/ppermute | solution.py:691
  1108.7 34.1 %collective-permute-start.41 = (f32[2,12,768]{2,1,0:T(8,128)}, f32[2,12,768]{2,1,0:T(8,128)S(1)}, u32[]{:S(2)}, u32[]{:S(2)}) collective-permute-start(f32[2,12,768]{2,1,0:T(8,128)} %all-reduce.3.cloned.1.call-done), channel_id=1, source_target_pairs={{0,0},{8,1},{1,8},{9,9},{17,16},{25,17},{16,24},{24,25},{2,2},{10,... | collective-permute-start | bytes 221192 | tf_op jit(solution)/shard_map/ppermute | solution.py:880
  1133.4 23.9 %collective-permute-start.63 = (bf16[896,768]{1,0:T(8,128)(2,1)}, bf16[896,768]{1,0:T(8,128)(2,1)}, u32[]{:S(2)}, u32[]{:S(2)}) collective-permute-start(bf16[896,768]{1,0:T(8,128)(2,1)} %add_convert_fusion.13), channel_id=1, source_target_pairs={{2,4},{4,2},{3,5},{5,3},{10,12},{12,10},{11,13},{13,11},{18,20},{2... | collective-permute-start | bytes 4128776 | tf_op jit(solution)/shard_map/ppermute | solution.py:718
  1151.9 49.5 %collective-permute-start.66 = (bf16[768,1536]{1,0:T(8,128)(2,1)S(1)}, bf16[768,1536]{1,0:T(8,128)(2,1)}, u32[]{:S(2)}, u32[]{:S(2)}) collective-permute-start(bf16[768,1536]{1,0:T(8,128)(2,1)S(1)} %broadcast_select_fusion.2), channel_id=1, source_target_pairs={{8,1},{1,8},{17,16},{25,17},{16,24},{24,25},{10,3},{3,10},{19,18},... | collective-permute-start | bytes 7077896 | tf_op jit(solution)/shard_map/ppermute | solution.py:691
  1160.5 33.1 %collective-permute-start.64 = (bf16[896,768]{1,0:T(8,128)(2,1)}, bf16[896,768]{1,0:T(8,128)(2,1)}, u32[]{:S(2)}, u32[]{:S(2)}) collective-permute-start(bf16[896,768]{1,0:T(8,128)(2,1)} %add_convert_fusion.12), channel_id=1, source_target_pairs={{2,0},{4,6},{3,1},{5,7},{10,8},{12,14},{11,9},{13,15},{18,16},{20,... | collective-permute-start | bytes 4128776 | tf_op jit(solution)/shard_map/ppermute | solution.py:720
  1195.2 19.6 %collective-permute-start.65 = (bf16[896,768]{1,0:T(8,128)(2,1)S(1)}, bf16[896,768]{1,0:T(8,128)(2,1)S(1)}, u32[]{:S(2)}, u32[]{:S(2)}) collective-permute-start(bf16[896,768]{1,0:T(8,128)(2,1)S(1)} %broadcast_select_fusion.13), channel_id=1, source_target_pairs={{8,1},{1,8},{17,16},{25,17},{16,24},{24,25},{10,3},{3,10},{19,18},... | collective-permute-start | bytes 4128776 | tf_op jit(solution)/shard_map/ppermute | solution.py:691
  (75 other events, 748.3 us)
Sparse Core Ops, SparseCore 0:
  80.6 39.1 all-gather.2
  167.7 33.7 all-gather.4
  1024.3 42.4 all-reduce.2
  1071.0 54.3 reduce-scatter.4
  1143.0 50.1 reduce-scatter.2
